TPU v7x, 32 devices: a whole 2x2x4 slice. The times are simulated.
32 devices in a mesh: groups: 2 (over y), user: 4 (over z), item: 2 (over x), rep: 2 (over core).
Axes of the slice: x: 2, y: 2, z: 4, core: 2. Of those that a mesh axis runs over, the one named last changes fastest.
Arguments:
- user_emb: bfloat16 [64, 16384], P(None, ('groups', 'user')), parts along dimension 1, may hold values from -2 to 2
- item_emb: bfloat16 [64, 8192], P(None, ('groups', 'item')), parts along dimension 1, may hold values from -2 to 2
- user_deg: int32 [16384], P(('groups', 'user')), parts along dimension 0, may hold values from 16 to 256
- item_deg: int32 [8192], P(('groups', 'item')), parts along dimension 0, may hold values from 16 to 256
- block_vals: bfloat16 [9216, 128, 128], P(('groups', 'user', 'item', 'rep')), parts along dimension 0, may hold values from 0 to 1
- block_row: int32 [9216], P(('groups', 'user', 'item', 'rep')), parts along dimension 0, may hold values from 0 to 15
- block_col: int32 [9216], P(('groups', 'user', 'item', 'rep')), parts along dimension 0, may hold values from 0 to 15
- block_count: int32 [32], P(('groups', 'user', 'item', 'rep')), parts along dimension 0, may hold values from 36 to 288, as said below
- trip_user: int32 [8192], P(('groups', 'user', 'item', 'rep')), parts along dimension 0, may hold values from 0 to 2047
- trip_pos: int32 [8192], P(('groups', 'user', 'item', 'rep')), parts along dimension 0, may hold values from 0 to 2047
- trip_neg: int32 [8192], P(('groups', 'user', 'item', 'rep')), parts along dimension 0, may hold values from 0 to 2047
Outputs:
- grad_user: float32 [64, 16384], P(None, ('groups', 'user')), parts along dimension 1
- grad_item: float32 [64, 8192], P(None, ('groups', 'item')), parts along dimension 1
There are 2 independent parts, one for each index of `groups`. A program takes and returns all parts, laid end to end along the dimension named above; each array names one. Nothing has to cross between parts.
Inputs may be any that keep to these rules, and one draw needn't show every extreme that they name: `block_count`: every draw has a device with exactly 288 live slots; slots at or past a device's count hold arbitrary values and are left out of R.
All inputs are finite; a program needn't handle non-finite values.
Results may differ from a plain program's by a relative error of at most 0.00076.
Values sent between devices are 32-bit elements; how exact they have to be, the bound alone decides.
No kernel may reach another device: no remote copies, remote signals or barrier semaphores. Data moves between devices by JAX's collectives and lax.ppermute only.
A program may use at most 128 MiB of HBM per device.

v0:
```python
import functools

import jax
import jax.numpy as jnp
from jax import lax
from jax.experimental import pallas as pl
from jax.experimental.pallas import tpu as pltpu
from jax.sharding import PartitionSpec as P

F32 = jnp.float32
BF16 = jnp.bfloat16
PACK = 4
GROUP = 4
ID_ROWS = 64
HEAVY = 10 ** 11

VMEM = pl.BlockSpec(memory_space=pltpu.VMEM)
SMEM = pl.BlockSpec(memory_space=pltpu.SMEM)
ANY = pl.BlockSpec(memory_space=pl.ANY)
HBM = pl.BlockSpec(memory_space=pltpu.HBM)


def call(kernel, outs, ins, specs, scratch=(), flops=0, moved=0, room=16):
    return pl.pallas_call(
        kernel,
        out_shape=outs,
        in_specs=specs,
        out_specs=jax.tree.map(lambda _: VMEM, outs),
        scratch_shapes=list(scratch),
        cost_estimate=pl.CostEstimate(flops=flops, bytes_accessed=moved, transcendentals=0),
        compiler_params=pltpu.CompilerParams(vmem_limit_bytes=room * 1024 * 1024),
    )(*ins)


def shape(*dims):
    return jax.ShapeDtypeStruct(dims, F32)


def split3(values):
    high = values.astype(BF16)
    rest = values - high.astype(F32)
    middle = rest.astype(BF16)
    low = (rest - middle.astype(F32)).astype(BF16)
    return high, middle, low


def hot(ids, start, tile):
    if len(ids) == 2:
        same = ids[0] == ids[1]
        ids = [jnp.where(same, -1, each) for each in ids]
    ids = [each.astype(jnp.int16) for each in ids]
    place = lax.broadcasted_iota(jnp.int16, (tile, ids[0].shape[1]), 0) + jnp.int16(start)
    chosen = jnp.zeros(place.shape, BF16)
    for each, sign in zip(ids, (1, -1)):
        chosen = jnp.where(place == each, jnp.asarray(sign, BF16), chosen)
    return chosen


def sort_slots(keys, sources, count, blocks):
    lanes = keys.shape[1]
    rows = 2 * blocks
    place = lax.broadcasted_iota(jnp.int32, (1, lanes), 1)
    live = place < count
    mine = (lax.broadcasted_iota(jnp.int32, (rows, lanes), 0) == keys) & live
    mine = jnp.where(mine, 1.0, 0.0)
    earlier = lax.broadcasted_iota(jnp.int32, (lanes, lanes), 0) < lax.broadcasted_iota(
        jnp.int32, (lanes, lanes), 1)
    before = jnp.dot(mine.astype(BF16), jnp.where(earlier, 1.0, 0.0).astype(BF16),
                     preferred_element_type=F32)
    packs = jnp.floor((jnp.sum(mine, axis=1, keepdims=True) + (PACK - 1)) * (1.0 / PACK))
    packs = jnp.broadcast_to(packs, (rows, 128))
    lower = lax.broadcasted_iota(jnp.int32, (rows, rows), 1) < lax.broadcasted_iota(
        jnp.int32, (rows, rows), 0)
    first = jnp.dot(jnp.where(lower, 1.0, 0.0).astype(BF16), packs.astype(BF16),
                    preferred_element_type=F32)
    position = jnp.sum(mine * (first[:, :1] * PACK + before), axis=0, keepdims=True)
    position = jnp.where(live, position.astype(jnp.int32), -1)
    match = lax.broadcasted_iota(jnp.int32, (lanes, lanes), 0) == position
    row = lax.broadcasted_iota(jnp.int32, (16, lanes), 0)
    values = jnp.where(row == 0, place // 16, jnp.where(row == 1, place % 16, jnp.where(
        row == 2, sources, jnp.where(row == 3, keys, jnp.where(row == 4, 1, 0)))))
    values = jnp.where(live, values, 0).astype(F32)
    found = lax.dot_general(values.astype(BF16), jnp.where(match, 1.0, 0.0).astype(BF16),
                            (((1,), (1,)), ((), ())), preferred_element_type=F32)
    found = found.astype(jnp.int32)
    valid = found[4:5] > 0
    total = jnp.broadcast_to(jnp.sum(packs[:, :1], axis=0, keepdims=True), (1, lanes))
    row = lax.broadcasted_iota(jnp.int32, (4, lanes), 0)
    slot = found[0:1] * 16 + found[1:2]
    source = jnp.where(valid, found[2:3], blocks)
    target = jnp.where(valid, found[3:4], 0)
    return jnp.where(row == 0, slot, jnp.where(row == 1, source, jnp.where(
        row == 2, target, total.astype(jnp.int32))))


def multiply_blocks(order, vals, source, total, across):
    _, width, size = source.shape
    total[...] = jnp.zeros_like(total)
    contract = (((1,), (1,)), ((), ())) if across else (((1,), (0,)), ((), ()))

    def group(index, _):
        targets, terms = [], []
        for step in range(GROUP):
            left, right = [], []
            for half in range(2):
                first = ((index * GROUP + step) * 2 + half) * PACK
                places = [first + each for each in range(PACK)]
                left.append(jnp.concatenate([source[order[1, each]] for each in places], axis=1))
                right.append(jnp.concatenate([vals[order[0, each]] for each in places],
                                             axis=1 if across else 0))
                targets.append(order[2, first])
            both = lax.dot_general(
                jnp.concatenate(left, axis=0), jnp.concatenate(right, axis=0 if across else 1),
                contract, preferred_element_type=F32,
            )
            terms += [both[:width, :size], both[width:, size:]]
        for target, term in zip(targets, terms):
            total[target] += term
        return 0

    lax.fori_loop(0, (order[3, 0] + 2 * GROUP - 1) // (2 * GROUP), group, 0)


def begin(out):
    out[...] = jnp.zeros_like(out)


def stack_ids(user, positive, negative, after, out):
    out[...] = jnp.zeros_like(out)
    for row, ids in enumerate((user, positive, negative)):
        out[row:row + 1, :] = ids[...]


def prepare(count, rows, columns, user_emb, item_emb, user_deg, item_deg, after,
            user_source, item_source, user_scale, item_scale, item_order, user_order, keys):
    live = count[0]
    slots = rows.shape[0]
    keys[...] = jnp.zeros_like(keys)
    keys[0:1, 0:slots] = rows[...].reshape(1, slots)
    keys[1:2, 0:slots] = columns[...].reshape(1, slots)
    users, items = keys[0:1, :], keys[1:2, :]
    item_order[...] = sort_slots(items, users, live, item_scale.shape[0])
    user_order[...] = sort_slots(users, items, live, user_scale.shape[0])
    for emb, deg, scale, into in ((user_emb, user_deg, user_scale, user_source),
                                  (item_emb, item_deg, item_scale, item_source)):
        scale[...] = lax.rsqrt(deg[...].astype(F32))
        blocks, size = scale.shape
        for block in range(blocks):
            piece = emb[:, block * size:(block + 1) * size].astype(F32)
            into[block] = (scale[block:block + 1, :] * piece).astype(BF16)
        into[blocks] = jnp.zeros(into.shape[1:], BF16)


def first_pass(across, order, vals, source, *refs):
    multiply_blocks(order, vals, source, refs[-1], across)


def fold(stacked, width):
    return (
        stacked[:width] + stacked[width:2 * width] + stacked[2 * width:3 * width]
    )


def rows_of(ref, rows):
    return [ref[row:row + 1, :] for row in rows]


def pick(table, ids, tile):
    total = None
    for start in range(0, table.shape[1], tile):
        term = jnp.dot(
            table[:, start:start + tile], hot(ids, start, tile),
            preferred_element_type=F32,
        )
        total = term if total is None else total + term
    return total


def gather(rows, peers, mine, other, scale, after, *refs):
    ids, outs, table = refs[:peers], refs[peers:2 * peers], refs[2 * peers]
    blocks, width, size = mine.shape
    for block in range(blocks):
        span = slice(block * size, (block + 1) * size)
        here = scale[block:block + 1, :] * (mine[block] + other[block])
        for part, piece in enumerate(split3(here)):
            table[part * width:(part + 1) * width, span] = piece
    for peer in range(peers):
        outs[peer][...] = fold(pick(table, rows_of(ids[peer], rows), 2 * size), width)


def scatter(pieces, ids, table, blocks, size, put):
    width = table.shape[1] // 3
    tile = 2 * size
    for place, piece in enumerate(pieces):
        for part, value in enumerate(split3(piece[:width, :])):
            table[place, part * width:(part + 1) * width, :] = value
    for start in range(0, blocks * size, tile):
        total = None
        for place, rows in enumerate(ids):
            term = lax.dot_general(
                table[place], hot(rows, start, tile), (((1,), (1,)), ((), ())),
                preferred_element_type=F32,
            )
            total = term if total is None else total + term
        total = fold(total, width)
        for offset in range(0, tile, size):
            put((start + offset) // size, total[:, offset:offset + size])


def scatter_items(peers, after, *refs):
    pieces, ids, out, table = refs[:peers], refs[peers:2 * peers], refs[2 * peers], refs[-1]
    blocks, _, size = out.shape

    def put(block, value):
        out[block] = value

    scatter(pieces, [rows_of(ref, [1, 2]) for ref in ids], table, blocks, size, put)


def gather_base(user_emb, item_emb, ids, user_out, item_out):
    tile = ids.shape[1]
    user_out[...] = pick(user_emb, rows_of(ids, [0]), tile)
    item_out[...] = pick(item_emb, rows_of(ids, [1, 2]), tile)


def add_all(refs):
    total = refs[0][...]
    for ref in refs[1:]:
        total = total + ref[...]
    return total


def slopes(user_parts, item_parts, ids, *refs):
    users, items = refs[:user_parts], refs[user_parts:user_parts + item_parts]
    pieces, pushed = refs[user_parts + item_parts:]
    width = pushed.shape[0]
    user_rows = 0.5 * add_all(users)
    difference = 0.5 * add_all(items)
    margin = jnp.sum(user_rows * difference, axis=0, keepdims=True)
    slope = -jax.nn.sigmoid(-margin)
    pieces[:width, :] = slope * difference
    pieces[width:, :] = jnp.broadcast_to(ids[0:1, :].astype(F32), (8, ids.shape[1]))
    pushed[...] = slope * user_rows


def halves(total, keep, send):
    me = lax.axis_index("rep")
    half = keep.shape[1]
    for block in range(keep.shape[0]):
        keep[block] = total[block, pl.ds(pl.multiple_of(me * half, half), half), :]
        send[block] = total[block, pl.ds(pl.multiple_of((1 - me) * half, half), half), :]


def second_items(parts, order, source_scale, target_scale, vals, *refs):
    pieces = refs[:parts]
    half_grad, keep, send, source, total, table = refs[parts:]
    blocks, width, size = half_grad.shape

    def put(block, grad):
        half_grad[block] = 0.5 * grad
        source[block] = (source_scale[block:block + 1, :] * grad * 0.5).astype(BF16)

    ids = [[piece[width:width + 1, :].astype(jnp.int32)] for piece in pieces]
    scatter(pieces, ids, table, blocks, size, put)
    source[blocks] = jnp.zeros((width, size), BF16)
    multiply_blocks(order, vals, source, total, False)
    for block in range(total.shape[0]):
        total[block] = target_scale[block:block + 1, :] * total[block]
    halves(total, keep, send)


def second_users(order, mine, other, source_scale, target_scale, vals, after,
                 half_grad, out, source, total):
    blocks, width, size = mine.shape
    for block in range(blocks):
        grad = mine[block] + other[block]
        half_grad[block] = 0.5 * grad
        source[block] = (source_scale[block:block + 1, :] * grad * 0.5).astype(BF16)
    source[blocks] = jnp.zeros((width, size), BF16)
    multiply_blocks(order, vals, source, total, True)
    for block in range(out.shape[0]):
        out[block] = target_scale[block:block + 1, :] * total[block]


def halves_after(total, after, keep, send):
    halves(total, keep, send)


def add_deal(offsets, keep, received, after, *outs):
    me = lax.axis_index("user")
    per = outs[0].shape[0]
    for out, offset in zip(outs, offsets):
        there = (me ^ offset) * per
        for block in range(per):
            out[block] = keep[there + block] + received[there + block]


def sum_parts(*refs):
    refs[-1][...] = add_all(refs[:-1])


def sum_after(after, *refs):
    sum_parts(*refs)


def pack(*refs):
    for place, ref in enumerate(refs[:-1]):
        refs[-1][place] = ref[...]


def finish(offsets, user_half_grad, user_mine, user_other, item_half_grad, item_mine, item_other,
           user_out, item_out):
    finish_users(user_half_grad, user_mine, user_other, user_out)
    finish_items(offsets, item_half_grad, item_mine, item_other, item_out)


def finish_users(half_grad, mine, other, out):
    me = lax.axis_index("rep")
    blocks, width, size = half_grad.shape
    half = width // 2
    for block in range(blocks):
        span = slice(block * size, (block + 1) * size)
        for rank, part in ((me, mine), (1 - me, other)):
            rows = pl.ds(pl.multiple_of(rank * half, half), half)
            out[rows, span] = half_grad[block, rows, :] + part[block]


def finish_items(offsets, half_grad, mine, other, out):
    me = lax.axis_index("rep")
    place = lax.axis_index("user")
    blocks, width, size = half_grad.shape
    half = width // 2
    per = blocks // len(offsets)
    for index, offset in enumerate(offsets):
        there = (place ^ offset) * per
        for block in range(per):
            span = pl.ds(pl.multiple_of((there + block) * size, size), size)
            for rank, part in ((me, mine), (1 - me, other)):
                rows = pl.ds(pl.multiple_of(rank * half, half), half)
                out[rows, span] = half_grad[there + block, rows, :] + part[index, block]


def swap(values, axis="rep", peers=2, offset=1):
    return lax.ppermute(values, axis, [(i, i ^ offset) for i in range(peers)])


def on_device(users, items, user_emb, item_emb, user_deg, item_deg, block_vals, block_row,
              block_col, block_count, trip_user, trip_pos, trip_neg):
    width = user_emb.shape[0]
    slots, size, _ = block_vals.shape
    user_blocks = user_emb.shape[1] // size
    item_blocks = item_emb.shape[1] // size
    trips = trip_user.shape[0]
    half = width // 2
    user_deg = user_deg.reshape(user_blocks, size)
    item_deg = item_deg.reshape(item_blocks, size)

    product_flops = 2 * slots * size * size * width
    product_bytes = slots * size * size * 2
    started = call(begin, shape(8, size), (), [], (), 16 * product_flops, product_bytes)
    ids = call(
        stack_ids, jax.ShapeDtypeStruct((ID_ROWS, trips), jnp.int32),
        [each.reshape(1, trips) for each in (trip_user, trip_pos, trip_neg)] + [started],
        [VMEM, VMEM, VMEM, ANY],
    )
    ids_user = [ids] + [swap(ids, "item", items, o) for o in range(1, items)]
    near = list(range(1, users))
    far = near[::-1]
    ids_item = [ids] + [swap(ids, "user", users, o) for o in far]
    lanes = -(-slots // size) * size

    order_shape = jax.ShapeDtypeStruct((4, lanes), jnp.int32)

    def source_shape(blocks):
        return jax.ShapeDtypeStruct((blocks + 1, width, size), BF16)

    (user_source, item_source, user_scale, item_scale, item_order, user_order) = call(
        prepare,
        [source_shape(user_blocks), source_shape(item_blocks), shape(user_blocks, size),
         shape(item_blocks, size), order_shape, order_shape],
        (block_count, block_row, block_col, user_emb, item_emb, user_deg, item_deg, ids),
        [SMEM, VMEM, VMEM, VMEM, VMEM, VMEM, VMEM, ANY],
        [pltpu.VMEM((8, lanes), jnp.int32)], product_flops, product_bytes,
    )
    item_table = call(
        functools.partial(first_pass, False), shape(item_blocks, width, size),
        (item_order, block_vals, user_source, ids), [SMEM, VMEM, VMEM, ANY], (),
        product_flops, product_bytes,
    )
    ids_here = [*ids_item[1:], *ids_user[1:]]
    user_table = call(
        functools.partial(first_pass, True), shape(user_blocks, width, size),
        (user_order, block_vals, item_source, item_table, *ids_here),
        [SMEM, VMEM, VMEM] + [ANY] * (1 + len(ids_here)), (),
        product_flops, product_bytes,
    )

    hot_flops = 2 * 3 * width * trips * size

    def reduced(rows, table, scale, peer_ids, axis, offsets, after):
        peers, blocks = len(peer_ids), scale.shape[0]
        dealt = call(
            functools.partial(gather, rows, peers), [shape(width, trips)] * peers,
            (table, swap(table), scale, after, *peer_ids), [VMEM] * 3 + [ANY] + [VMEM] * peers,
            [pltpu.VMEM((3 * width, blocks * size), BF16)],
            peers * blocks * hot_flops, 8 * blocks * width * size,
        )
        return [dealt[0]] + [swap(part, axis, peers, o) for part, o in zip(dealt[1:], offsets)]

    item_parts = reduced([1, 2], item_table, item_scale, ids_item, "user", far, ids)
    user_parts = reduced([0], user_table, user_scale, ids_user, "item", list(range(1, items)), item_parts[0])
    user_base, item_base = call(
        gather_base, [shape(width, trips)] * 2, (user_emb, item_emb, ids),
        [VMEM, VMEM, VMEM], (), 4 * width * trips * size * (user_blocks + item_blocks),
        2 * width * size * (user_blocks + item_blocks),
    )
    user_parts.append(user_base)
    item_parts.append(item_base)
    pieces, pushed = call(
        functools.partial(slopes, len(user_parts), len(item_parts)),
        [shape(width + 8, trips), shape(width, trips)],
        (ids, *user_parts, *item_parts), [VMEM] * (1 + len(user_parts) + len(item_parts)),
        moved=4 * width * trips * (len(user_parts) + len(item_parts) + 2),
    )

    arrays = [pieces, swap(pieces)]
    for offset in range(1, items):
        arrays.append(swap(pieces, "item", items, offset))
        arrays.append(lax.ppermute(pieces, ("item", "rep"), [
            (i, i ^ (2 * offset + 1)) for i in range(2 * items)]))
    user_half_grad, item_keep, item_send = call(
        functools.partial(second_items, len(arrays)),
        [shape(user_blocks, width, size)] + [shape(item_blocks, half, size)] * 2,
        (item_order, user_scale, item_scale, block_vals, *arrays),
        [SMEM] + [VMEM] * (3 + len(arrays)),
        [pltpu.VMEM((user_blocks + 1, width, size), BF16),
         pltpu.VMEM((item_blocks, width, size), F32),
         pltpu.VMEM((len(arrays), 3 * width, trips), BF16)],
        product_flops, product_bytes,
    )
    arrays = [pushed] + [swap(pushed, "user", users, o) for o in near]
    item_grad = call(
        functools.partial(scatter_items, users), shape(item_blocks, width, size),
        (item_send, *arrays, ids, *ids_item[:0:-1]), [ANY] + [VMEM] * (2 * users),
        [pltpu.VMEM((users, 3 * width, trips), BF16)], HEAVY, 0,
    )

    per = item_blocks // users
    dealt = call(
        functools.partial(add_deal, [0, *far]), [shape(per, half, size)] * users,
        (item_keep, swap(item_send), item_grad), [VMEM, VMEM, ANY], (), HEAVY,
    )
    item_half_grad, user_back = call(
        second_users, [shape(item_blocks, width, size), shape(user_blocks, width, size)],
        (user_order, item_grad, swap(item_grad), item_scale, user_scale, block_vals, dealt[0]),
        [SMEM] + [VMEM] * 5 + [ANY],
        [pltpu.VMEM((item_blocks + 1, width, size), BF16),
         pltpu.VMEM((user_blocks, width, size), F32)],
        product_flops, product_bytes,
    )
    parts = [dealt[0]] + [swap(part, "user", users, o) for part, o in zip(dealt[1:], far)]
    item_own = call(sum_after, shape(per, half, size), (user_back, *parts),
                    [ANY] + [VMEM] * users,
               moved=4 * (users + 1) * per * half * size)
    item_mine = call(pack, shape(users, per, half, size),
                     (item_own, *[swap(item_own, "user", users, o) for o in near]),
                     [VMEM] * users, moved=8 * item_blocks * half * size)
    item_other = swap(item_mine)

    user_keep, user_send = call(
        halves_after, [shape(user_blocks, half, size)] * 2, (user_back, item_own), [VMEM, ANY],
        moved=8 * user_blocks * width * size,
    )
    own = call(sum_parts, shape(user_blocks, half, size), (user_keep, swap(user_send)),
               [VMEM, VMEM], moved=12 * user_blocks * half * size)
    mine = call(sum_parts, shape(user_blocks, half, size),
                (own, *[swap(own, "item", items, o) for o in range(1, items)]),
                [VMEM] * items, moved=12 * user_blocks * half * size)
    return call(
        functools.partial(finish, [0, *near]),
        (shape(width, user_blocks * size), shape(width, item_blocks * size)),
        (user_half_grad, mine, swap(mine), item_half_grad, item_mine, item_other),
        [VMEM] * 6, moved=12 * (user_blocks + item_blocks) * width * size,
    )


def solution(mesh):
    return jax.shard_map(
        functools.partial(on_device, mesh.shape["user"], mesh.shape["item"]),
        mesh=mesh,
        in_specs=(
            P(None, ("groups", "user")),
            P(None, ("groups", "item")),
            P(("groups", "user")),
            P(("groups", "item")),
            P(("groups", "user", "item", "rep"), None, None),
            P(("groups", "user", "item", "rep")),
            P(("groups", "user", "item", "rep")),
            P(("groups", "user", "item", "rep")),
            P(("groups", "user", "item", "rep")),
            P(("groups", "user", "item", "rep")),
            P(("groups", "user", "item", "rep")),
        ),
        out_specs=(P(None, ("groups", "user")), P(None, ("groups", "item"))),
        check_vma=False,
    )
```

profile of v0, /device:TPU:0, one launch (start us, length us, event | category | flops | bytes accessed | tf_op | source)
XLA Modules:
  0.0 66.8 jit_solution(14475955745702399993)
XLA Ops:
  0.7 0.0 copy-start
  0.7 0.6 copy-done.6
  1.3 0.0 copy-done.5
  1.3 0.0 copy-done.4
  1.4 3.0 %collective-permute-start.3 = (s32[64,256]{1,0:T(8,128)S(1)}, s32[64,256]{1,0:T(8,128)S(1)}, u32[]{:S(2)}, u32[]{:S(2)}) collective-permute-start(s32[64,256]{1,0:T(8,128)S(1)} %shard_map.123.after.refs_0_.ids.refs_4_), channel_id=1, source_target_pairs={{0,2},{2,0},{1,3},{3,1},{4,6},{6,4},{5,7},{7,5},{8,10},{10,8},{9,1... | collective-permute-start | bytes 196616 | tf_op jit(solution)/shard_map/ppermute | solution.py:344
  4.3 1.6 %collective-permute-start.2 = (s32[64,256]{1,0:T(8,128)S(1)}, s32[64,256]{1,0:T(8,128)S(1)}, u32[]{:S(2)}, u32[]{:S(2)}) collective-permute-start(s32[64,256]{1,0:T(8,128)S(1)} %shard_map.123.after.refs_0_.ids.refs_4_), channel_id=1, source_target_pairs={{0,4},{4,0},{8,12},{12,8},{1,5},{5,1},{9,13},{13,9},{2,6},{6,2},{1... | collective-permute-start | bytes 196616 | tf_op jit(solution)/shard_map/ppermute | solution.py:344
  5.9 2.6 %collective-permute-start.1 = (s32[64,256]{1,0:T(8,128)S(1)}, s32[64,256]{1,0:T(8,128)S(1)}, u32[]{:S(2)}, u32[]{:S(2)}) collective-permute-start(s32[64,256]{1,0:T(8,128)S(1)} %shard_map.123.after.refs_0_.ids.refs_4_), channel_id=1, source_target_pairs={{0,8},{4,12},{8,0},{12,4},{1,9},{5,13},{9,1},{13,5},{2,10},{6,14},... | collective-permute-start | bytes 196616 | tf_op jit(solution)/shard_map/ppermute | solution.py:344
  8.5 0.2 collective-permute-start
  9.4 0.9 %shard_map.124 = (bf16[17,64,128]{2,1,0:T(8,128)(2,1)S(1)}, bf16[17,64,128]{2,1,0:T(8,128)(2,1)S(1)}, f32[16,128]{1,0:T(8,128)S(1)}, f32[16,128]{1,0:T(8,128)S(1...) custom-call(s32[1]{0:T(128)S(6)} %copy.13.count, s32[288]{0:T(512)S(1)} %copy-done.11, s32[288]{0:T(512)S(1)} %copy-done.12, ...), custom_call_target="tpu_custom_call" | custom-call | flops 603979776 | bytes 9437184 | tf_op jit(solution)/shard_map/pallas_call | solution.py:24
  10.4 0.0 copy-start.2
  10.4 2.0 %shard_map.125.refs_0_.mine = f32[16,64,128]{2,1,0:T(8,128)S(1)} custom-call(s32[4,384]{1,0:T(4,128)S(1)} %get-tuple-element.29.order, bf16[288,128,128]{2,1,0:T(8,128)(2,1)S(1)} %copy-done, bf16[17,64,128]{2,1,0:T(8,128)(2,1)S(1)} %get-tuple-element.34.source, s32[64,256]{1,0:T(8,128)S(1)} %shard_map.123.after.refs_0_.ids.refs_4_), custom_call_target="tpu_custom_call" | custom-call | flops 603979776 | bytes 9437184 | tf_op jit(solution)/shard_map/pallas_call | solution.py:24
  12.5 0.1 collective-permute-start.5
  12.5 0.0 collective-permute-done.2.refs_3_.refs_5_
  12.6 0.4 collective-permute-done.1.refs_2_.refs_6_
  12.9 1.7 %collective-permute-done.refs_1_.refs_7_ = s32[64,256]{1,0:T(8,128)S(1)} collective-permute-done((s32[64,256]{1,0:T(8,128)S(1)}, s32[64,256]{1,0:T(8,128)S(1)}, u32[]{:S(2)}, u32[]{:S(2)}) %collective-permute-start) | collective-permute-done | bytes 65568 | tf_op jit(solution)/shard_map/ppermute | solution.py:344
  14.6 2.6 %shard_map.126.mine = f32[16,64,128]{2,1,0:T(8,128)S(1)} custom-call(s32[4,384]{1,0:T(4,128)S(1)} %get-tuple-element.32.order, bf16[288,128,128]{2,1,0:T(8,128)(2,1)S(1)} %copy-done, bf16[17,64,128]{2,1,0:T(8,128)(2,1)S(1)} %get-tuple-element.33.source, f32[16,64,128]{2,1,0:T(8,128)S(1)} %shard_map.125.refs_0_.mine, ...), custom_call_target="tpu_custom_call" | custom-call | flops 603979776 | bytes 9437184 | tf_op jit(solution)/shard_map/pallas_call | solution.py:24
  17.2 0.1 collective-permute-start.4
  17.3 0.0 collective-permute-done.5.other
  17.3 1.2 %shard_map.127 = (f32[64,256]{1,0:T(8,128)S(1)}, f32[64,256]{1,0:T(8,128)S(1)}, f32[64,256]{1,0:T(8,128)S(1)}, f32[64,256]{1,0:T(8,128)S(1)}) custom-call(f32[16,64,128]{2,1,0:T(8,128)S(1)} %shard_map.125.refs_0_.mine, f32[16,64,128]{2,1,0:T(8,128)S(1)} %collective-permute-done.5.other, f32[16,128]{1,0:T(8,128)S(1)} %get-tuple-element.31.scale.target_scale.source_scale, ...), custom_call_target="tpu_custom_call" | custom-call | flops 805306368 | bytes 1048576 | tf_op jit(solution)/shard_map/pallas_call | solution.py:24
  18.5 1.7 %collective-permute-start.7 = (f32[64,256]{1,0:T(8,128)S(1)}, f32[64,256]{1,0:T(8,128)S(1)}, u32[]{:S(2)}, u32[]{:S(2)}) collective-permute-start(f32[64,256]{1,0:T(8,128)S(1)} %get-tuple-element.39), channel_id=1, source_target_pairs={{0,12},{4,8},{8,4},{12,0},{1,13},{5,9},{9,5},{13,1},{2,14},{6,10},... | collective-permute-start | bytes 196616 | tf_op jit(solution)/shard_map/ppermute | solution.py:344
  20.2 0.0 collective-permute-start.8
  20.2 2.8 %collective-permute-start.9 = (f32[64,256]{1,0:T(8,128)S(1)}, f32[64,256]{1,0:T(8,128)S(1)}, u32[]{:S(2)}, u32[]{:S(2)}) collective-permute-start(f32[64,256]{1,0:T(8,128)S(1)} %get-tuple-element.41), channel_id=1, source_target_pairs={{0,4},{4,0},{8,12},{12,8},{1,5},{5,1},{9,13},{13,9},{2,6},{6,2},{1... | collective-permute-start | bytes 196616 | tf_op jit(solution)/shard_map/ppermute | solution.py:344
  23.0 0.6 shard_map.128
  23.6 2.1 %collective-permute-start.6 = (f32[64,256]{1,0:T(8,128)S(1)}, f32[64,256]{1,0:T(8,128)S(1)}, u32[]{:S(2)}, u32[]{:S(2)}) collective-permute-start(f32[64,256]{1,0:T(8,128)S(1)} %get-tuple-element.37), channel_id=1, source_target_pairs={{0,2},{2,0},{1,3},{3,1},{4,6},{6,4},{5,7},{7,5},{8,10},{10,8},{9,1... | collective-permute-start | bytes 196616 | tf_op jit(solution)/shard_map/ppermute | solution.py:344
  25.8 0.5 shard_map.129
  26.2 0.0 collective-permute-done.7.refs_4_
  26.2 1.5 %collective-permute-done.8.refs_5_ = f32[64,256]{1,0:T(8,128)S(1)} collective-permute-done((f32[64,256]{1,0:T(8,128)S(1)}, f32[64,256]{1,0:T(8,128)S(1)}, u32[]{:S(2)}, u32[]{:S(2)}) %collective-permute-start.8) | collective-permute-done | bytes 65568 | tf_op jit(solution)/shard_map/ppermute | solution.py:344
  27.7 0.3 collective-permute-done.6.refs_1_
  28.0 0.1 shard_map.130
  28.1 0.4 collective-permute-start.12
  28.5 1.8 %collective-permute-start.11 = (f32[72,256]{1,0:T(8,128)S(1)}, f32[72,256]{1,0:T(8,128)S(1)}, u32[]{:S(2)}, u32[]{:S(2)}) collective-permute-start(f32[72,256]{1,0:T(8,128)S(1)} %get-tuple-element.43.refs_0_), channel_id=1, source_target_pairs={{0,2},{2,0},{1,3},{3,1},{4,6},{6,4},{5,7},{7,5},{8,10},{10,8},{9,1... | collective-permute-start | bytes 221192 | tf_op jit(solution)/shard_map/ppermute | solution.py:344
  30.3 0.0 collective-permute-start.10
  30.3 3.7 %collective-permute-start.15 = (f32[64,256]{1,0:T(8,128)S(1)}, f32[64,256]{1,0:T(8,128)S(1)}, u32[]{:S(2)}, u32[]{:S(2)}) collective-permute-start(f32[64,256]{1,0:T(8,128)S(1)} %get-tuple-element.46.refs_0_), channel_id=1, source_target_pairs={{0,12},{4,8},{8,4},{12,0},{1,13},{5,9},{9,5},{13,1},{2,14},{6,10},... | collective-permute-start | bytes 196616 | tf_op jit(solution)/shard_map/ppermute | solution.py:344
  34.0 0.0 collective-permute-done.12.refs_3_
  34.0 0.7 %collective-permute-start.13 = (f32[64,256]{1,0:T(8,128)S(1)}, f32[64,256]{1,0:T(8,128)S(1)}, u32[]{:S(2)}, u32[]{:S(2)}) collective-permute-start(f32[64,256]{1,0:T(8,128)S(1)} %get-tuple-element.46.refs_0_), channel_id=1, source_target_pairs={{0,4},{4,0},{8,12},{12,8},{1,5},{5,1},{9,13},{13,9},{2,6},{6,2},{1... | collective-permute-start | bytes 196616 | tf_op jit(solution)/shard_map/ppermute | solution.py:344
  34.7 0.0 collective-permute-done.11.refs_2_
  34.7 0.0 collective-permute-done.10.refs_1_
  34.7 3.6 %shard_map.131 = (f32[16,64,128]{2,1,0:T(8,128)S(1)}, f32[16,32,128]{2,1,0:T(8,128)S(1)}, f32[16,32,128]{2,1,0:T(8,128)S(1)}) custom-call(s32[4,384]{1,0:T(4,128)S(1)} %get-tuple-element.29.order, f32[16,128]{1,0:T(8,128)S(1)} %get-tuple-element.30.scale.source_scale.target_scale, f32[16,128]{1,0:T(8,128)S(1)} %get-tuple-element.31.scale.target_scale.source_scale, ...), custom_call_target="tpu_custom_call" | custom-call | flops 603979776 | bytes 9437184 | tf_op jit(solution)/shard_map/pallas_call | solution.py:24
  38.3 0.1 collective-permute-start.17
  38.4 0.0 collective-permute-done.15.refs_3_
  38.4 1.4 %collective-permute-done.14.refs_2_ = f32[64,256]{1,0:T(8,128)S(1)} collective-permute-done((f32[64,256]{1,0:T(8,128)S(1)}, f32[64,256]{1,0:T(8,128)S(1)}, u32[]{:S(2)}, u32[]{:S(2)}) %collective-permute-start.14) | collective-permute-done | bytes 65568 | tf_op jit(solution)/shard_map/ppermute | solution.py:344
  39.8 1.5 %shard_map.132.after.mine = f32[16,64,128]{2,1,0:T(8,128)S(1)} custom-call(f32[16,32,128]{2,1,0:T(8,128)S(1)} %get-tuple-element.45.after, f32[64,256]{1,0:T(8,128)S(1)} %get-tuple-element.46.refs_0_, f32[64,256]{1,0:T(8,128)S(1)} %collective-permute-done.13.refs_1_, f32[64,256]{1,0:T(8,128)S(1)} %collective-permute-done.14.refs_2_, ...), custom_call_target="tpu_custom_call" | custom-call | flops 99999997952 | tf_op jit(solution)/shard_map/pallas_call | solution.py:24
  41.3 0.1 collective-permute-start.16
  41.4 0.0 collective-permute-done.17.received
  41.4 0.0 copy-start.1
  41.4 0.0 copy-start.3
  41.5 2.8 %collective-permute-start.18 = (f32[4,32,128]{2,1,0:T(8,128)S(1)}, f32[4,32,128]{2,1,0:T(8,128)S(1)}, u32[]{:S(2)}, u32[]{:S(2)}) collective-permute-start(f32[4,32,128]{2,1,0:T(8,128)S(1)} %get-tuple-element.50), channel_id=1, source_target_pairs={{0,12},{4,8},{8,4},{12,0},{1,13},{5,9},{9,5},{13,1},{2,14},{6,10},... | collective-permute-start | bytes 196616 | tf_op jit(solution)/shard_map/ppermute | solution.py:344
  44.3 0.3 collective-permute-start.19
  44.5 1.4 %collective-permute-start.20 = (f32[4,32,128]{2,1,0:T(8,128)S(1)}, f32[4,32,128]{2,1,0:T(8,128)S(1)}, u32[]{:S(2)}, u32[]{:S(2)}) collective-permute-start(f32[4,32,128]{2,1,0:T(8,128)S(1)} %get-tuple-element.52), channel_id=1, source_target_pairs={{0,4},{4,0},{8,12},{12,8},{1,5},{5,1},{9,13},{13,9},{2,6},{6,2},{1... | collective-permute-start | bytes 196616 | tf_op jit(solution)/shard_map/ppermute | solution.py:344
  45.9 2.7 %shard_map.134 = (f32[16,64,128]{2,1,0:T(8,128)S(1)}, f32[16,64,128]{2,1,0:T(8,128)S(1)}) custom-call(s32[4,384]{1,0:T(4,128)S(1)} %copy-done.3, f32[16,64,128]{2,1,0:T(8,128)S(1)} %shard_map.132.after.mine, f32[16,64,128]{2,1,0:T(8,128)S(1)} %collective-permute-done.16.other, f32[16,128]{1,0:T(8,128)S(1)} %get-tuple-element.31.scale.target_scale.source_scale, ...), custom_call_target="tpu_custom_call" | custom-call | flops 603979776 | bytes 9437184 | tf_op jit(solution)/shard_map/pallas_call | solution.py:24
  48.7 0.0 collective-permute-done.18.refs_1_
  48.7 2.5 %collective-permute-done.19.refs_2_ = f32[4,32,128]{2,1,0:T(8,128)S(1)} collective-permute-done((f32[4,32,128]{2,1,0:T(8,128)S(1)}, f32[4,32,128]{2,1,0:T(8,128)S(1)}, u32[]{:S(2)}, u32[]{:S(2)}) %collective-permute-start.19) | collective-permute-done | bytes 65568 | tf_op jit(solution)/shard_map/ppermute | solution.py:344
  51.3 0.1 collective-permute-start.21
  51.3 1.5 %collective-permute-done.21.refs_1_ = f32[16,32,128]{2,1,0:T(8,128)S(1)} collective-permute-done((f32[16,32,128]{2,1,0:T(8,128)S(1)}, f32[16,32,128]{2,1,0:T(8,128)S(1)}, u32[]{:S(2)}, u32[]{:S(2)}) %collective-permute-start.21) | collective-permute-done | bytes 262176 | tf_op jit(solution)/shard_map/ppermute | solution.py:344
  52.9 1.4 %collective-permute-start.22 = (f32[16,32,128]{2,1,0:T(8,128)S(1)}, f32[16,32,128]{2,1,0:T(8,128)S(1)}, u32[]{:S(2)}, u32[]{:S(2)}) collective-permute-start(f32[16,32,128]{2,1,0:T(8,128)S(1)} %shard_map.137.refs_0_), channel_id=1, source_target_pairs={{0,2},{2,0},{1,3},{3,1},{4,6},{6,4},{5,7},{7,5},{8,10},{10,8},{9,1... | collective-permute-start | bytes 786440 | tf_op jit(solution)/shard_map/ppermute | solution.py:344
  54.3 3.6 %collective-permute-start.26 = (f32[4,32,128]{2,1,0:T(8,128)S(1)}, f32[4,32,128]{2,1,0:T(8,128)S(1)}, u32[]{:S(2)}, u32[]{:S(2)}) collective-permute-start(f32[4,32,128]{2,1,0:T(8,128)S(1)} %shard_map.135.after.refs_0_), channel_id=1, source_target_pairs={{0,12},{4,8},{8,4},{12,0},{1,13},{5,9},{9,5},{13,1},{2,14},{6,10},... | collective-permute-start | bytes 196616 | tf_op jit(solution)/shard_map/ppermute | solution.py:344
  57.9 0.8 %collective-permute-start.24 = (f32[4,32,128]{2,1,0:T(8,128)S(1)}, f32[4,32,128]{2,1,0:T(8,128)S(1)}, u32[]{:S(2)}, u32[]{:S(2)}) collective-permute-start(f32[4,32,128]{2,1,0:T(8,128)S(1)} %shard_map.135.after.refs_0_), channel_id=1, source_target_pairs={{0,4},{4,0},{8,12},{12,8},{1,5},{5,1},{9,13},{13,9},{2,6},{6,2},{1... | collective-permute-start | bytes 196616 | tf_op jit(solution)/shard_map/ppermute | solution.py:344
  58.7 2.5 %collective-permute-done.26.refs_3_ = f32[4,32,128]{2,1,0:T(8,128)S(1)} collective-permute-done((f32[4,32,128]{2,1,0:T(8,128)S(1)}, f32[4,32,128]{2,1,0:T(8,128)S(1)}, u32[]{:S(2)}, u32[]{:S(2)}) %collective-permute-start.26) | collective-permute-done | bytes 65568 | tf_op jit(solution)/shard_map/ppermute | solution.py:344
  61.2 2.6 %collective-permute-done.25.refs_2_ = f32[4,32,128]{2,1,0:T(8,128)S(1)} collective-permute-done((f32[4,32,128]{2,1,0:T(8,128)S(1)}, f32[4,32,128]{2,1,0:T(8,128)S(1)}, u32[]{:S(2)}, u32[]{:S(2)}) %collective-permute-start.25) | collective-permute-done | bytes 65568 | tf_op jit(solution)/shard_map/ppermute | solution.py:344
  63.8 0.1 collective-permute-start.27
  63.9 0.5 collective-permute-start.23
  64.5 0.9 %collective-permute-done.27.item_other = f32[4,4,32,128]{3,2,1,0:T(8,128)S(1)} collective-permute-done((f32[4,4,32,128]{3,2,1,0:T(8,128)S(1)}, f32[4,4,32,128]{3,2,1,0:T(8,128)S(1)}, u32[]{:S(2)}, u32[]{:S(2)}) %collective-permute-start.27) | collective-permute-done | bytes 262176 | tf_op jit(solution)/shard_map/ppermute | solution.py:344
  65.4 0.4 collective-permute-done.23.user_other
  65.7 1.1 %shard_map.140 = (f32[64,2048]{1,0:T(8,128)}, f32[64,2048]{1,0:T(8,128)}) custom-call(f32[16,64,128]{2,1,0:T(8,128)S(1)} %get-tuple-element.44.user_half_grad, f32[16,32,128]{2,1,0:T(8,128)S(1)} %shard_map.138.user_mine, f32[16,32,128]{2,1,0:T(8,128)S(1)} %collective-permute-done.23.user_other, f32[16,64,128]{2,1,0:T(8,128)S(1)} %get-tuple-element.55.item_half_grad, ...), custom_call_target="tpu_custom_call" | custom-call | bytes 3145728 | tf_op jit(solution)/shard_map/pallas_call | solution.py:24
  (37 shorter events, 0.3 us)
Async XLA Ops:
  0.6 0.7 %copy-start.6 = (s32[256]{0:T(256)S(1)}, s32[256]{0:T(256)}, u32[]{:S(2)}) copy-start(s32[256]{0:T(256)} %param.21) | copy-start | bytes 3076
  0.6 0.7 %copy-start.5 = (s32[256]{0:T(256)S(1)}, s32[256]{0:T(256)}, u32[]{:S(2)}) copy-start(s32[256]{0:T(256)} %param.20) | copy-start | bytes 3076
  0.7 0.7 %copy-start.4 = (s32[256]{0:T(256)S(1)}, s32[256]{0:T(256)}, u32[]{:S(2)}) copy-start(s32[256]{0:T(256)} %param.19) | copy-start | bytes 3076
  0.7 8.7 %copy-start.8 = (bf16[64,2048]{1,0:T(8,128)(2,1)S(1)}, bf16[64,2048]{1,0:T(8,128)(2,1)}, u32[]{:S(2)}) copy-start(bf16[64,2048]{1,0:T(8,128)(2,1)} %item_emb.3) | copy-start | bytes 786436
  0.7 8.7 %copy-start.7 = (bf16[64,2048]{1,0:T(8,128)(2,1)S(1)}, bf16[64,2048]{1,0:T(8,128)(2,1)}, u32[]{:S(2)}) copy-start(bf16[64,2048]{1,0:T(8,128)(2,1)} %user_emb.3) | copy-start | bytes 786436
  0.7 8.7 %copy-start.12 = (s32[288]{0:T(512)S(1)}, s32[288]{0:T(512)}, u32[]{:S(2)}) copy-start(s32[288]{0:T(512)} %columns.1) | copy-start | bytes 3460
  0.7 8.7 %copy-start.11 = (s32[288]{0:T(512)S(1)}, s32[288]{0:T(512)}, u32[]{:S(2)}) copy-start(s32[288]{0:T(512)} %rows.1) | copy-start | bytes 3460
  0.7 8.7 %copy-start.10 = (s32[2048]{0:T(1024)S(1)}, s32[2048]{0:T(1024)}, u32[]{:S(2)}) copy-start(s32[2048]{0:T(1024)} %param.14) | copy-start | bytes 24580
  0.7 8.7 %copy-start.9 = (s32[2048]{0:T(1024)S(1)}, s32[2048]{0:T(1024)}, u32[]{:S(2)}) copy-start(s32[2048]{0:T(1024)} %param.13) | copy-start | bytes 24580
  0.7 9.7 %copy-start = (bf16[288,128,128]{2,1,0:T(8,128)(2,1)S(1)}, bf16[288,128,128]{2,1,0:T(8,128)(2,1)}, u32[]{:S(2)}) copy-start(bf16[288,128,128]{2,1,0:T(8,128)(2,1)} %vals.7) | copy-start | bytes 28311556
  1.4 11.2 %collective-permute-start.3 = (s32[64,256]{1,0:T(8,128)S(1)}, s32[64,256]{1,0:T(8,128)S(1)}, u32[]{:S(2)}, u32[]{:S(2)}) collective-permute-start(s32[64,256]{1,0:T(8,128)S(1)} %shard_map.123.after.refs_0_.ids.refs_4_), channel_id=1, source_target_pairs={{0,2},{2,0},{1,3},{3,1},{4,6},{6,4},{5,7},{7,5},{8,10},{10,8},{9,1... | collective-permute-start | bytes 196616 | tf_op jit(solution)/shard_map/ppermute | solution.py:344
  4.3 8.2 %collective-permute-start.2 = (s32[64,256]{1,0:T(8,128)S(1)}, s32[64,256]{1,0:T(8,128)S(1)}, u32[]{:S(2)}, u32[]{:S(2)}) collective-permute-start(s32[64,256]{1,0:T(8,128)S(1)} %shard_map.123.after.refs_0_.ids.refs_4_), channel_id=1, source_target_pairs={{0,4},{4,0},{8,12},{12,8},{1,5},{5,1},{9,13},{13,9},{2,6},{6,2},{1... | collective-permute-start | bytes 196616 | tf_op jit(solution)/shard_map/ppermute | solution.py:344
  5.9 7.0 %collective-permute-start.1 = (s32[64,256]{1,0:T(8,128)S(1)}, s32[64,256]{1,0:T(8,128)S(1)}, u32[]{:S(2)}, u32[]{:S(2)}) collective-permute-start(s32[64,256]{1,0:T(8,128)S(1)} %shard_map.123.after.refs_0_.ids.refs_4_), channel_id=1, source_target_pairs={{0,8},{4,12},{8,0},{12,4},{1,9},{5,13},{9,1},{13,5},{2,10},{6,14},... | collective-permute-start | bytes 196616 | tf_op jit(solution)/shard_map/ppermute | solution.py:344
  8.5 6.1 %collective-permute-start = (s32[64,256]{1,0:T(8,128)S(1)}, s32[64,256]{1,0:T(8,128)S(1)}, u32[]{:S(2)}, u32[]{:S(2)}) collective-permute-start(s32[64,256]{1,0:T(8,128)S(1)} %shard_map.123.after.refs_0_.ids.refs_4_), channel_id=1, source_target_pairs={{0,12},{4,8},{8,4},{12,0},{1,13},{5,9},{9,5},{13,1},{2,14},{6,10},... | collective-permute-start | bytes 196616 | tf_op jit(solution)/shard_map/ppermute | solution.py:344
  10.4 6.8 %copy-start.2 = (s32[4,384]{1,0:T(4,128)}, s32[4,384]{1,0:T(4,128)S(1)}, u32[]{:S(2)}) copy-start(s32[4,384]{1,0:T(4,128)S(1)} %get-tuple-element.32.order) | copy-start | bytes 18436
  12.5 4.8 %collective-permute-start.5 = (f32[16,64,128]{2,1,0:T(8,128)S(1)}, f32[16,64,128]{2,1,0:T(8,128)S(1)}, u32[]{:S(2)}, u32[]{:S(2)}) collective-permute-start(f32[16,64,128]{2,1,0:T(8,128)S(1)} %shard_map.125.refs_0_.mine), channel_id=1, source_target_pairs={{0,1},{1,0},{2,3},{3,2},{4,5},{5,4},{6,7},{7,6},{8,9},{9,8},{10,11... | collective-permute-start | bytes 1572872 | tf_op jit(solution)/shard_map/ppermute | solution.py:344
  17.2 5.8 %collective-permute-start.4 = (f32[16,64,128]{2,1,0:T(8,128)S(1)}, f32[16,64,128]{2,1,0:T(8,128)S(1)}, u32[]{:S(2)}, u32[]{:S(2)}) collective-permute-start(f32[16,64,128]{2,1,0:T(8,128)S(1)} %shard_map.126.mine), channel_id=1, source_target_pairs={{0,1},{1,0},{2,3},{3,2},{4,5},{5,4},{6,7},{7,6},{8,9},{9,8},{10,11... | collective-permute-start | bytes 1572872 | tf_op jit(solution)/shard_map/ppermute | solution.py:344
  18.5 7.7 %collective-permute-start.7 = (f32[64,256]{1,0:T(8,128)S(1)}, f32[64,256]{1,0:T(8,128)S(1)}, u32[]{:S(2)}, u32[]{:S(2)}) collective-permute-start(f32[64,256]{1,0:T(8,128)S(1)} %get-tuple-element.39), channel_id=1, source_target_pairs={{0,12},{4,8},{8,4},{12,0},{1,13},{5,9},{9,5},{13,1},{2,14},{6,10},... | collective-permute-start | bytes 196616 | tf_op jit(solution)/shard_map/ppermute | solution.py:344
  20.2 7.5 %collective-permute-start.8 = (f32[64,256]{1,0:T(8,128)S(1)}, f32[64,256]{1,0:T(8,128)S(1)}, u32[]{:S(2)}, u32[]{:S(2)}) collective-permute-start(f32[64,256]{1,0:T(8,128)S(1)} %get-tuple-element.40), channel_id=1, source_target_pairs={{0,8},{4,12},{8,0},{12,4},{1,9},{5,13},{9,1},{13,5},{2,10},{6,14},... | collective-permute-start | bytes 196616 | tf_op jit(solution)/shard_map/ppermute | solution.py:344
  20.2 7.5 %collective-permute-start.9 = (f32[64,256]{1,0:T(8,128)S(1)}, f32[64,256]{1,0:T(8,128)S(1)}, u32[]{:S(2)}, u32[]{:S(2)}) collective-permute-start(f32[64,256]{1,0:T(8,128)S(1)} %get-tuple-element.41), channel_id=1, source_target_pairs={{0,4},{4,0},{8,12},{12,8},{1,5},{5,1},{9,13},{13,9},{2,6},{6,2},{1... | collective-permute-start | bytes 196616 | tf_op jit(solution)/shard_map/ppermute | solution.py:344
  23.6 4.4 %collective-permute-start.6 = (f32[64,256]{1,0:T(8,128)S(1)}, f32[64,256]{1,0:T(8,128)S(1)}, u32[]{:S(2)}, u32[]{:S(2)}) collective-permute-start(f32[64,256]{1,0:T(8,128)S(1)} %get-tuple-element.37), channel_id=1, source_target_pairs={{0,2},{2,0},{1,3},{3,1},{4,6},{6,4},{5,7},{7,5},{8,10},{10,8},{9,1... | collective-permute-start | bytes 196616 | tf_op jit(solution)/shard_map/ppermute | solution.py:344
  28.1 5.9 %collective-permute-start.12 = (f32[72,256]{1,0:T(8,128)S(1)}, f32[72,256]{1,0:T(8,128)S(1)}, u32[]{:S(2)}, u32[]{:S(2)}) collective-permute-start(f32[72,256]{1,0:T(8,128)S(1)} %get-tuple-element.43.refs_0_), channel_id=1, source_target_pairs={{0,3},{1,2},{2,1},{3,0},{4,7},{5,6},{6,5},{7,4},{8,11},{9,10},{10,... | collective-permute-start | bytes 221192 | tf_op jit(solution)/shard_map/ppermute | solution.py:429
  28.5 6.2 %collective-permute-start.11 = (f32[72,256]{1,0:T(8,128)S(1)}, f32[72,256]{1,0:T(8,128)S(1)}, u32[]{:S(2)}, u32[]{:S(2)}) collective-permute-start(f32[72,256]{1,0:T(8,128)S(1)} %get-tuple-element.43.refs_0_), channel_id=1, source_target_pairs={{0,2},{2,0},{1,3},{3,1},{4,6},{6,4},{5,7},{7,5},{8,10},{10,8},{9,1... | collective-permute-start | bytes 221192 | tf_op jit(solution)/shard_map/ppermute | solution.py:344
  30.3 4.4 %collective-permute-start.10 = (f32[72,256]{1,0:T(8,128)S(1)}, f32[72,256]{1,0:T(8,128)S(1)}, u32[]{:S(2)}, u32[]{:S(2)}) collective-permute-start(f32[72,256]{1,0:T(8,128)S(1)} %get-tuple-element.43.refs_0_), channel_id=1, source_target_pairs={{0,1},{1,0},{2,3},{3,2},{4,5},{5,4},{6,7},{7,6},{8,9},{9,8},{10,11... | collective-permute-start | bytes 221192 | tf_op jit(solution)/shard_map/ppermute | solution.py:344
  30.3 8.1 %collective-permute-start.15 = (f32[64,256]{1,0:T(8,128)S(1)}, f32[64,256]{1,0:T(8,128)S(1)}, u32[]{:S(2)}, u32[]{:S(2)}) collective-permute-start(f32[64,256]{1,0:T(8,128)S(1)} %get-tuple-element.46.refs_0_), channel_id=1, source_target_pairs={{0,12},{4,8},{8,4},{12,0},{1,13},{5,9},{9,5},{13,1},{2,14},{6,10},... | collective-permute-start | bytes 196616 | tf_op jit(solution)/shard_map/ppermute | solution.py:344
  34.0 5.8 %collective-permute-start.14 = (f32[64,256]{1,0:T(8,128)S(1)}, f32[64,256]{1,0:T(8,128)S(1)}, u32[]{:S(2)}, u32[]{:S(2)}) collective-permute-start(f32[64,256]{1,0:T(8,128)S(1)} %get-tuple-element.46.refs_0_), channel_id=1, source_target_pairs={{0,8},{4,12},{8,0},{12,4},{1,9},{5,13},{9,1},{13,5},{2,10},{6,14},... | collective-permute-start | bytes 196616 | tf_op jit(solution)/shard_map/ppermute | solution.py:344
  34.0 5.8 %collective-permute-start.13 = (f32[64,256]{1,0:T(8,128)S(1)}, f32[64,256]{1,0:T(8,128)S(1)}, u32[]{:S(2)}, u32[]{:S(2)}) collective-permute-start(f32[64,256]{1,0:T(8,128)S(1)} %get-tuple-element.46.refs_0_), channel_id=1, source_target_pairs={{0,4},{4,0},{8,12},{12,8},{1,5},{5,1},{9,13},{13,9},{2,6},{6,2},{1... | collective-permute-start | bytes 196616 | tf_op jit(solution)/shard_map/ppermute | solution.py:344
  38.3 3.1 %collective-permute-start.17 = (f32[16,32,128]{2,1,0:T(8,128)S(1)}, f32[16,32,128]{2,1,0:T(8,128)S(1)}, u32[]{:S(2)}, u32[]{:S(2)}) collective-permute-start(f32[16,32,128]{2,1,0:T(8,128)S(1)} %get-tuple-element.45.after), channel_id=1, source_target_pairs={{0,1},{1,0},{2,3},{3,2},{4,5},{5,4},{6,7},{7,6},{8,9},{9,8},{10,11... | collective-permute-start | bytes 786440 | tf_op jit(solution)/shard_map/ppermute | solution.py:344
  41.3 4.6 %collective-permute-start.16 = (f32[16,64,128]{2,1,0:T(8,128)S(1)}, f32[16,64,128]{2,1,0:T(8,128)S(1)}, u32[]{:S(2)}, u32[]{:S(2)}) collective-permute-start(f32[16,64,128]{2,1,0:T(8,128)S(1)} %shard_map.132.after.mine), channel_id=1, source_target_pairs={{0,1},{1,0},{2,3},{3,2},{4,5},{5,4},{6,7},{7,6},{8,9},{9,8},{10,11... | collective-permute-start | bytes 1572872 | tf_op jit(solution)/shard_map/ppermute | solution.py:344
  41.4 4.5 %copy-start.1 = (bf16[288,128,128]{2,1,0:T(8,128)(2,1)S(1)}, bf16[288,128,128]{2,1,0:T(8,128)(2,1)}, u32[]{:S(2)}) copy-start(bf16[288,128,128]{2,1,0:T(8,128)(2,1)} %vals.7) | copy-start | bytes 28311556
  41.4 4.5 %copy-start.3 = (s32[4,384]{1,0:T(4,128)S(1)}, s32[4,384]{1,0:T(4,128)}, u32[]{:S(2)}) copy-start(s32[4,384]{1,0:T(4,128)} %copy-done.2) | copy-start | bytes 18436
  41.5 7.2 %collective-permute-start.18 = (f32[4,32,128]{2,1,0:T(8,128)S(1)}, f32[4,32,128]{2,1,0:T(8,128)S(1)}, u32[]{:S(2)}, u32[]{:S(2)}) collective-permute-start(f32[4,32,128]{2,1,0:T(8,128)S(1)} %get-tuple-element.50), channel_id=1, source_target_pairs={{0,12},{4,8},{8,4},{12,0},{1,13},{5,9},{9,5},{13,1},{2,14},{6,10},... | collective-permute-start | bytes 196616 | tf_op jit(solution)/shard_map/ppermute | solution.py:344
  44.3 6.9 %collective-permute-start.19 = (f32[4,32,128]{2,1,0:T(8,128)S(1)}, f32[4,32,128]{2,1,0:T(8,128)S(1)}, u32[]{:S(2)}, u32[]{:S(2)}) collective-permute-start(f32[4,32,128]{2,1,0:T(8,128)S(1)} %get-tuple-element.51), channel_id=1, source_target_pairs={{0,8},{4,12},{8,0},{12,4},{1,9},{5,13},{9,1},{13,5},{2,10},{6,14},... | collective-permute-start | bytes 196616 | tf_op jit(solution)/shard_map/ppermute | solution.py:344
  44.5 6.6 %collective-permute-start.20 = (f32[4,32,128]{2,1,0:T(8,128)S(1)}, f32[4,32,128]{2,1,0:T(8,128)S(1)}, u32[]{:S(2)}, u32[]{:S(2)}) collective-permute-start(f32[4,32,128]{2,1,0:T(8,128)S(1)} %get-tuple-element.52), channel_id=1, source_target_pairs={{0,4},{4,0},{8,12},{12,8},{1,5},{5,1},{9,13},{13,9},{2,6},{6,2},{1... | collective-permute-start | bytes 196616 | tf_op jit(solution)/shard_map/ppermute | solution.py:344
  51.3 1.6 %collective-permute-start.21 = (f32[16,32,128]{2,1,0:T(8,128)S(1)}, f32[16,32,128]{2,1,0:T(8,128)S(1)}, u32[]{:S(2)}, u32[]{:S(2)}) collective-permute-start(f32[16,32,128]{2,1,0:T(8,128)S(1)} %get-tuple-element.54), channel_id=1, source_target_pairs={{0,1},{1,0},{2,3},{3,2},{4,5},{5,4},{6,7},{7,6},{8,9},{9,8},{10,11... | collective-permute-start | bytes 786440 | tf_op jit(solution)/shard_map/ppermute | solution.py:344
  52.9 11.0 %collective-permute-start.22 = (f32[16,32,128]{2,1,0:T(8,128)S(1)}, f32[16,32,128]{2,1,0:T(8,128)S(1)}, u32[]{:S(2)}, u32[]{:S(2)}) collective-permute-start(f32[16,32,128]{2,1,0:T(8,128)S(1)} %shard_map.137.refs_0_), channel_id=1, source_target_pairs={{0,2},{2,0},{1,3},{3,1},{4,6},{6,4},{5,7},{7,5},{8,10},{10,8},{9,1... | collective-permute-start | bytes 786440 | tf_op jit(solution)/shard_map/ppermute | solution.py:344
  54.3 6.8 %collective-permute-start.26 = (f32[4,32,128]{2,1,0:T(8,128)S(1)}, f32[4,32,128]{2,1,0:T(8,128)S(1)}, u32[]{:S(2)}, u32[]{:S(2)}) collective-permute-start(f32[4,32,128]{2,1,0:T(8,128)S(1)} %shard_map.135.after.refs_0_), channel_id=1, source_target_pairs={{0,12},{4,8},{8,4},{12,0},{1,13},{5,9},{9,5},{13,1},{2,14},{6,10},... | collective-permute-start | bytes 196616 | tf_op jit(solution)/shard_map/ppermute | solution.py:344
  57.9 5.8 %collective-permute-start.25 = (f32[4,32,128]{2,1,0:T(8,128)S(1)}, f32[4,32,128]{2,1,0:T(8,128)S(1)}, u32[]{:S(2)}, u32[]{:S(2)}) collective-permute-start(f32[4,32,128]{2,1,0:T(8,128)S(1)} %shard_map.135.after.refs_0_), channel_id=1, source_target_pairs={{0,8},{4,12},{8,0},{12,4},{1,9},{5,13},{9,1},{13,5},{2,10},{6,14},... | collective-permute-start | bytes 196616 | tf_op jit(solution)/shard_map/ppermute | solution.py:344
  57.9 5.8 %collective-permute-start.24 = (f32[4,32,128]{2,1,0:T(8,128)S(1)}, f32[4,32,128]{2,1,0:T(8,128)S(1)}, u32[]{:S(2)}, u32[]{:S(2)}) collective-permute-start(f32[4,32,128]{2,1,0:T(8,128)S(1)} %shard_map.135.after.refs_0_), channel_id=1, source_target_pairs={{0,4},{4,0},{8,12},{12,8},{1,5},{5,1},{9,13},{13,9},{2,6},{6,2},{1... | collective-permute-start | bytes 196616 | tf_op jit(solution)/shard_map/ppermute | solution.py:344
  63.8 1.6 %collective-permute-start.27 = (f32[4,4,32,128]{3,2,1,0:T(8,128)S(1)}, f32[4,4,32,128]{3,2,1,0:T(8,128)S(1)}, u32[]{:S(2)}, u32[]{:S(2)}) collective-permute-start(f32[4,4,32,128]{3,2,1,0:T(8,128)S(1)} %shard_map.139.item_mine), channel_id=1, source_target_pairs={{0,1},{1,0},{2,3},{3,2},{4,5},{5,4},{6,7},{7,6},{8,9},{9,8},{10,11... | collective-permute-start | bytes 786440 | tf_op jit(solution)/shard_map/ppermute | solution.py:344
  63.9 1.8 %collective-permute-start.23 = (f32[16,32,128]{2,1,0:T(8,128)S(1)}, f32[16,32,128]{2,1,0:T(8,128)S(1)}, u32[]{:S(2)}, u32[]{:S(2)}) collective-permute-start(f32[16,32,128]{2,1,0:T(8,128)S(1)} %shard_map.138.user_mine), channel_id=1, source_target_pairs={{0,1},{1,0},{2,3},{3,2},{4,5},{5,4},{6,7},{7,6},{8,9},{9,8},{10,11... | collective-permute-start | bytes 786440 | tf_op jit(solution)/shard_map/ppermute | solution.py:344
where the time goes:
time: 68.1 us; the launch traced here: 66.8 us
  starting transfers between devices  31.9 us (47%)
  Pallas kernels  17.1 us (25%)
  waiting for transfers between devices  15.5 us (23%)
  between operations  1.69 us (2%)
    ppermute x27, starting transfers between devices, swap(): return lax.ppermute(values, axis, [(i, i ^ offset) for i in range(peers)])  31.5 us
    pallas_call x19, Pallas kernels, call(): pl.pallas_call(kernel, out_shape=outs, in_specs=specs, out_specs=jax.tree...  17.1 us
    ppermute x27, waiting for transfers between devices, swap(): return lax.ppermute(values, axis, [(i, i ^ offset) for i in range(peers)])  15.5 us
  transfers between devices with their start and end apart: 28, of which 11 were waited for; matrix products, arithmetic and copies ran while one was open for 0% of the time, Pallas kernels for 24%

commit v1 on v0

--- a/solution.py
+++ b/solution.py
@@ -131,6 +131,13 @@
         out[row:row + 1, :] = ids[...]
 
 
+def pack_ids(places, *refs):
+    out = refs[-1]
+    out[...] = jnp.zeros_like(out)
+    for offset, (index, row) in enumerate(places):
+        out[3 * offset:3 * offset + 3, :] = refs[index][row:row + 3, :]
+
+
 def prepare(count, rows, columns, user_emb, item_emb, user_deg, item_deg, after,
             user_source, item_source, user_scale, item_scale, item_order, user_order, keys):
     live = count[0]
@@ -176,16 +183,16 @@
     return total
 
 
-def gather(rows, peers, mine, other, scale, after, *refs):
-    ids, outs, table = refs[:peers], refs[peers:2 * peers], refs[2 * peers]
+def gather(places, count, mine, other, scale, after, *refs):
+    ids, outs, table = refs[:count], refs[count:-1], refs[-1]
     blocks, width, size = mine.shape
     for block in range(blocks):
         span = slice(block * size, (block + 1) * size)
         here = scale[block:block + 1, :] * (mine[block] + other[block])
         for part, piece in enumerate(split3(here)):
             table[part * width:(part + 1) * width, span] = piece
-    for peer in range(peers):
-        outs[peer][...] = fold(pick(table, rows_of(ids[peer], rows), 2 * size), width)
+    for out, (index, rows) in zip(outs, places):
+        out[...] = fold(pick(table, rows_of(ids[index], rows), 2 * size), width)
 
 
 def scatter(pieces, ids, table, blocks, size, put):
@@ -207,14 +214,16 @@
             put((start + offset) // size, total[:, offset:offset + size])
 
 
-def scatter_items(peers, after, *refs):
-    pieces, ids, out, table = refs[:peers], refs[peers:2 * peers], refs[2 * peers], refs[-1]
+def scatter_items(places, after, *refs):
+    peers = len(places)
+    pieces, ids, out, table = refs[:peers], refs[peers:-2], refs[-2], refs[-1]
     blocks, _, size = out.shape
 
     def put(block, value):
         out[block] = value
 
-    scatter(pieces, [rows_of(ref, [1, 2]) for ref in ids], table, blocks, size, put)
+    scatter(pieces, [rows_of(ids[index], rows) for index, rows in places],
+            table, blocks, size, put)
 
 
 def gather_base(user_emb, item_emb, ids, user_out, item_out):
@@ -358,15 +367,22 @@
     product_flops = 2 * slots * size * size * width
     product_bytes = slots * size * size * 2
     started = call(begin, shape(8, size), (), [], (), 16 * product_flops, product_bytes)
+    ids_shape = jax.ShapeDtypeStruct((ID_ROWS, trips), jnp.int32)
     ids = call(
-        stack_ids, jax.ShapeDtypeStruct((ID_ROWS, trips), jnp.int32),
+        stack_ids, ids_shape,
         [each.reshape(1, trips) for each in (trip_user, trip_pos, trip_neg)] + [started],
         [VMEM, VMEM, VMEM, ANY],
     )
     ids_user = [ids] + [swap(ids, "item", items, o) for o in range(1, items)]
-    near = list(range(1, users))
-    far = near[::-1]
-    ids_item = [ids] + [swap(ids, "user", users, o) for o in far]
+    met = sorted(range(1, users), key=lambda offset: (offset != users // 2, -offset))
+    back = met[::-1]
+    ids_item, held, step = [(0, 0)], [ids], 1
+    while step < users:
+        packed = ids if step == 1 else call(
+            functools.partial(pack_ids, ids_item), ids_shape, held, [VMEM] * len(held))
+        held.append(swap(packed, "user", users, step))
+        ids_item += [(len(held) - 1, 3 * place) for place in range(step)]
+        step *= 2
     lanes = -(-slots // size) * size
 
     order_shape = jax.ShapeDtypeStruct((4, lanes), jnp.int32)
@@ -387,7 +403,7 @@
         (item_order, block_vals, user_source, ids), [SMEM, VMEM, VMEM, ANY], (),
         product_flops, product_bytes,
     )
-    ids_here = [*ids_item[1:], *ids_user[1:]]
+    ids_here = [*held[1:], *ids_user[1:]]
     user_table = call(
         functools.partial(first_pass, True), shape(user_blocks, width, size),
         (user_order, block_vals, item_source, item_table, *ids_here),
@@ -397,18 +413,25 @@
 
     hot_flops = 2 * 3 * width * trips * size
 
-    def reduced(rows, table, scale, peer_ids, axis, offsets, after):
-        peers, blocks = len(peer_ids), scale.shape[0]
+    def reduced(table, scale, arrays, places, axis, offsets, after):
+        peers, blocks = len(places), scale.shape[0]
         dealt = call(
-            functools.partial(gather, rows, peers), [shape(width, trips)] * peers,
-            (table, swap(table), scale, after, *peer_ids), [VMEM] * 3 + [ANY] + [VMEM] * peers,
+            functools.partial(gather, places, len(arrays)), [shape(width, trips)] * peers,
+            (table, swap(table), scale, after, *arrays),
+            [VMEM] * 3 + [ANY] + [VMEM] * len(arrays),
             [pltpu.VMEM((3 * width, blocks * size), BF16)],
             peers * blocks * hot_flops, 8 * blocks * width * size,
         )
         return [dealt[0]] + [swap(part, axis, peers, o) for part, o in zip(dealt[1:], offsets)]
 
-    item_parts = reduced([1, 2], item_table, item_scale, ids_item, "user", far, ids)
-    user_parts = reduced([0], user_table, user_scale, ids_user, "item", list(range(1, items)), item_parts[0])
+    def item_rows(offset):
+        index, row = ids_item[offset]
+        return index, [row + 1, row + 2]
+
+    item_parts = reduced(item_table, item_scale, held, [item_rows(o) for o in [0, *met]],
+                         "user", met, ids)
+    user_parts = reduced(user_table, user_scale, ids_user, [(o, [0]) for o in range(items)],
+                         "item", list(range(1, items)), item_parts[0])
     user_base, item_base = call(
         gather_base, [shape(width, trips)] * 2, (user_emb, item_emb, ids),
         [VMEM, VMEM, VMEM], (), 4 * width * trips * size * (user_blocks + item_blocks),
@@ -438,16 +461,17 @@
          pltpu.VMEM((len(arrays), 3 * width, trips), BF16)],
         product_flops, product_bytes,
     )
-    arrays = [pushed] + [swap(pushed, "user", users, o) for o in near]
+    arrays = [pushed] + [swap(pushed, "user", users, o) for o in back]
     item_grad = call(
-        functools.partial(scatter_items, users), shape(item_blocks, width, size),
-        (item_send, *arrays, ids, *ids_item[:0:-1]), [ANY] + [VMEM] * (2 * users),
+        functools.partial(scatter_items, [item_rows(o) for o in [0, *back]]),
+        shape(item_blocks, width, size),
+        (item_send, *arrays, *held), [ANY] + [VMEM] * (users + len(held)),
         [pltpu.VMEM((users, 3 * width, trips), BF16)], HEAVY, 0,
     )
 
     per = item_blocks // users
     dealt = call(
-        functools.partial(add_deal, [0, *far]), [shape(per, half, size)] * users,
+        functools.partial(add_deal, [0, *met]), [shape(per, half, size)] * users,
         (item_keep, swap(item_send), item_grad), [VMEM, VMEM, ANY], (), HEAVY,
     )
     item_half_grad, user_back = call(
@@ -458,12 +482,12 @@
          pltpu.VMEM((user_blocks, width, size), F32)],
         product_flops, product_bytes,
     )
-    parts = [dealt[0]] + [swap(part, "user", users, o) for part, o in zip(dealt[1:], far)]
+    parts = [dealt[0]] + [swap(part, "user", users, o) for part, o in zip(dealt[1:], met)]
     item_own = call(sum_after, shape(per, half, size), (user_back, *parts),
                     [ANY] + [VMEM] * users,
                moved=4 * (users + 1) * per * half * size)
     item_mine = call(pack, shape(users, per, half, size),
-                     (item_own, *[swap(item_own, "user", users, o) for o in near]),
+                     (item_own, *[swap(item_own, "user", users, o) for o in back]),
                      [VMEM] * users, moved=8 * item_blocks * half * size)
     item_other = swap(item_mine)
 
@@ -477,7 +501,7 @@
                 (own, *[swap(own, "item", items, o) for o in range(1, items)]),
                 [VMEM] * items, moved=12 * user_blocks * half * size)
     return call(
-        functools.partial(finish, [0, *near]),
+        functools.partial(finish, [0, *back]),
         (shape(width, user_blocks * size), shape(width, item_blocks * size)),
         (user_half_grad, mine, swap(mine), item_half_grad, item_mine, item_other),
         [VMEM] * 6, moved=12 * (user_blocks + item_blocks) * width * size,

time: 68.1 us -> 67.1 us (0.985); the launches traced: 66.8 us -> 67 us
  Pallas kernels: 17.1 us -> 13.8 us
  starting transfers between devices: 31.9 us -> 34.7 us
    pallas_call x19 -> x20, Pallas kernels: 17.1 us -> 13.8 us  [call(): pl.pallas_call(kernel, out_shape=outs, in_specs=specs, out_specs=jax.tree...]
    ppermute x27 -> x26, starting transfers between devices: 31.5 us -> 33.3 us  [swap(): return lax.ppermute(values, axis, [(i, i ^ offset) for i in range(peers)])]
    ppermute x1, starting transfers between devices: 0.43 us -> 1.49 us  [on_device(): lax.ppermute(pieces, ('item', 'rep'), [(i, i ^ 2 * offset + 1) for i in r...]
    ppermute x27 -> x26, waiting for transfers between devices: 15.5 us -> 16.1 us  [swap(): return lax.ppermute(values, axis, [(i, i ^ offset) for i in range(peers)])]
  transfers between devices with their start and end apart: 28 -> 27, of which waited for: 11 -> 11; matrix products, arithmetic and copies ran while one was open for 0% -> 0% of each run, Pallas kernels for 24% -> 19%
where the time goes in v1:
time: 67.1 us; the launch traced here: 67 us
  starting transfers between devices  34.7 us (52%)
  waiting for transfers between devices  16.1 us (24%)
  Pallas kernels  13.8 us (21%)
  between operations  1.65 us (2%)
  local copies, waits for them, and re-layouts  0.72 us (1%)
    ppermute x26, starting transfers between devices, swap(): return lax.ppermute(values, axis, [(i, i ^ offset) for i in range(peers)])  33.3 us
    ppermute x26, waiting for transfers between devices, swap(): return lax.ppermute(values, axis, [(i, i ^ offset) for i in range(peers)])  16.1 us
    pallas_call x20, Pallas kernels, call(): pl.pallas_call(kernel, out_shape=outs, in_specs=specs, out_specs=jax.tree...  13.8 us
    ppermute x1, starting transfers between devices, on_device(): lax.ppermute(pieces, ('item', 'rep'), [(i, i ^ 2 * offset + 1) for i in r...  1.49 us
  transfers between devices with their start and end apart: 27, of which 11 were waited for; matrix products, arithmetic and copies ran while one was open for 0% of the time, Pallas kernels for 19%

profile of v1, /device:TPU:0, one launch (start us, length us, event | category | flops | bytes accessed | tf_op | source)
XLA Modules:
  0.0 67.0 jit_solution(5963119704070367956)
XLA Ops:
  0.7 0.0 copy-start
  0.7 0.6 copy-done.6
  1.3 0.0 copy-done.5
  1.3 0.0 copy-done.4
  1.4 3.1 %collective-permute-start = (s32[64,256]{1,0:T(8,128)S(1)}, s32[64,256]{1,0:T(8,128)S(1)}, u32[]{:S(2)}, u32[]{:S(2)}) collective-permute-start(s32[64,256]{1,0:T(8,128)S(1)} %shard_map.123.after.refs_0_.ids.refs_4_), channel_id=1, source_target_pairs={{0,4},{4,0},{8,12},{12,8},{1,5},{5,1},{9,13},{13,9},{2,6},{6,2},{1... | collective-permute-start | bytes 196616 | tf_op jit(solution)/shard_map/ppermute | solution.py:353
  4.4 1.5 %collective-permute-start.2 = (s32[64,256]{1,0:T(8,128)S(1)}, s32[64,256]{1,0:T(8,128)S(1)}, u32[]{:S(2)}, u32[]{:S(2)}) collective-permute-start(s32[64,256]{1,0:T(8,128)S(1)} %shard_map.123.after.refs_0_.ids.refs_4_), channel_id=1, source_target_pairs={{0,2},{2,0},{1,3},{3,1},{4,6},{6,4},{5,7},{7,5},{8,10},{10,8},{9,1... | collective-permute-start | bytes 196616 | tf_op jit(solution)/shard_map/ppermute | solution.py:353
  6.6 0.9 %shard_map.124 = (bf16[17,64,128]{2,1,0:T(8,128)(2,1)S(1)}, bf16[17,64,128]{2,1,0:T(8,128)(2,1)S(1)}, f32[16,128]{1,0:T(8,128)S(1)}, f32[16,128]{1,0:T(8,128)S(1...) custom-call(s32[1]{0:T(128)S(6)} %copy.13.count, s32[288]{0:T(512)S(1)} %copy-done.11, s32[288]{0:T(512)S(1)} %copy-done.12, ...), custom_call_target="tpu_custom_call" | custom-call | flops 603979776 | bytes 9437184 | tf_op jit(solution)/shard_map/pallas_call | solution.py:24
  7.6 0.0 copy-start.2
  7.6 0.0 collective-permute-done.refs_1_.refs_5_
  7.6 2.7 %collective-permute-start.1 = (s32[64,256]{1,0:T(8,128)S(1)}, s32[64,256]{1,0:T(8,128)S(1)}, u32[]{:S(2)}, u32[]{:S(2)}) collective-permute-start(s32[64,256]{1,0:T(8,128)S(1)} %shard_map.126), channel_id=1, source_target_pairs={{0,8},{4,12},{8,0},{12,4},{1,9},{5,13},{9,1},{13,5},{2,10},{6,14},... | collective-permute-start | bytes 196616 | tf_op jit(solution)/shard_map/ppermute | solution.py:353
  10.3 1.4 %shard_map.125.refs_0_.mine = f32[16,64,128]{2,1,0:T(8,128)S(1)} custom-call(s32[4,384]{1,0:T(4,128)S(1)} %get-tuple-element.29.order, bf16[288,128,128]{2,1,0:T(8,128)(2,1)S(1)} %copy-done, bf16[17,64,128]{2,1,0:T(8,128)(2,1)S(1)} %get-tuple-element.34.source, s32[64,256]{1,0:T(8,128)S(1)} %shard_map.123.after.refs_0_.ids.refs_4_), custom_call_target="tpu_custom_call" | custom-call | flops 603979776 | bytes 9437184 | tf_op jit(solution)/shard_map/pallas_call | solution.py:24
  11.6 0.4 collective-permute-start.4
  12.1 1.5 %collective-permute-done.1.refs_2_.refs_6_ = s32[64,256]{1,0:T(8,128)S(1)} collective-permute-done((s32[64,256]{1,0:T(8,128)S(1)}, s32[64,256]{1,0:T(8,128)S(1)}, u32[]{:S(2)}, u32[]{:S(2)}) %collective-permute-start.1) | collective-permute-done | bytes 65568 | tf_op jit(solution)/shard_map/ppermute | solution.py:353
  13.5 1.6 %shard_map.127.mine = f32[16,64,128]{2,1,0:T(8,128)S(1)} custom-call(s32[4,384]{1,0:T(4,128)S(1)} %get-tuple-element.32.order, bf16[288,128,128]{2,1,0:T(8,128)(2,1)S(1)} %copy-done, bf16[17,64,128]{2,1,0:T(8,128)(2,1)S(1)} %get-tuple-element.33.source, f32[16,64,128]{2,1,0:T(8,128)S(1)} %shard_map.125.refs_0_.mine, ...), custom_call_target="tpu_custom_call" | custom-call | flops 603979776 | bytes 9437184 | tf_op jit(solution)/shard_map/pallas_call | solution.py:24
  15.2 0.2 collective-permute-start.3
  15.4 1.2 %shard_map.128 = (f32[64,256]{1,0:T(8,128)S(1)}, f32[64,256]{1,0:T(8,128)S(1)}, f32[64,256]{1,0:T(8,128)S(1)}, f32[64,256]{1,0:T(8,128)S(1)}) custom-call(f32[16,64,128]{2,1,0:T(8,128)S(1)} %shard_map.125.refs_0_.mine, f32[16,64,128]{2,1,0:T(8,128)S(1)} %collective-permute-done.4.other, f32[16,128]{1,0:T(8,128)S(1)} %get-tuple-element.31.scale.target_scale.source_scale, ...), custom_call_target="tpu_custom_call" | custom-call | flops 805306368 | bytes 1048576 | tf_op jit(solution)/shard_map/pallas_call | solution.py:24
  16.6 2.4 %collective-permute-start.6 = (f32[64,256]{1,0:T(8,128)S(1)}, f32[64,256]{1,0:T(8,128)S(1)}, u32[]{:S(2)}, u32[]{:S(2)}) collective-permute-start(f32[64,256]{1,0:T(8,128)S(1)} %get-tuple-element.39), channel_id=1, source_target_pairs={{0,8},{4,12},{8,0},{12,4},{1,9},{5,13},{9,1},{13,5},{2,10},{6,14},... | collective-permute-start | bytes 196616 | tf_op jit(solution)/shard_map/ppermute | solution.py:353
  19.1 1.8 %collective-permute-start.7 = (f32[64,256]{1,0:T(8,128)S(1)}, f32[64,256]{1,0:T(8,128)S(1)}, u32[]{:S(2)}, u32[]{:S(2)}) collective-permute-start(f32[64,256]{1,0:T(8,128)S(1)} %get-tuple-element.40), channel_id=1, source_target_pairs={{0,12},{4,8},{8,4},{12,0},{1,13},{5,9},{9,5},{13,1},{2,14},{6,10},... | collective-permute-start | bytes 196616 | tf_op jit(solution)/shard_map/ppermute | solution.py:353
  20.9 0.0 collective-permute-start.8
  20.9 0.0 collective-permute-done.3.other
  20.9 0.6 shard_map.129
  21.5 5.1 %collective-permute-start.5 = (f32[64,256]{1,0:T(8,128)S(1)}, f32[64,256]{1,0:T(8,128)S(1)}, u32[]{:S(2)}, u32[]{:S(2)}) collective-permute-start(f32[64,256]{1,0:T(8,128)S(1)} %get-tuple-element.37), channel_id=1, source_target_pairs={{0,2},{2,0},{1,3},{3,1},{4,6},{6,4},{5,7},{7,5},{8,10},{10,8},{9,1... | collective-permute-start | bytes 196616 | tf_op jit(solution)/shard_map/ppermute | solution.py:353
  26.6 0.5 shard_map.130
  27.0 0.0 collective-permute-done.7.refs_5_
  27.1 1.7 %collective-permute-done.5.refs_1_ = f32[64,256]{1,0:T(8,128)S(1)} collective-permute-done((f32[64,256]{1,0:T(8,128)S(1)}, f32[64,256]{1,0:T(8,128)S(1)}, u32[]{:S(2)}, u32[]{:S(2)}) %collective-permute-start.5) | collective-permute-done | bytes 65568 | tf_op jit(solution)/shard_map/ppermute | solution.py:353
  28.8 0.1 shard_map.131
  28.9 1.5 %collective-permute-start.11 = (f32[72,256]{1,0:T(8,128)S(1)}, f32[72,256]{1,0:T(8,128)S(1)}, u32[]{:S(2)}, u32[]{:S(2)}) collective-permute-start(f32[72,256]{1,0:T(8,128)S(1)} %get-tuple-element.43.refs_0_), channel_id=1, source_target_pairs={{0,3},{1,2},{2,1},{3,0},{4,7},{5,6},{6,5},{7,4},{8,11},{9,10},{10,... | collective-permute-start | bytes 221192 | tf_op jit(solution)/shard_map/ppermute | solution.py:452
  30.4 0.7 collective-permute-start.10
  31.0 0.0 collective-permute-start.9
  31.1 1.0 %collective-permute-start.14 = (f32[64,256]{1,0:T(8,128)S(1)}, f32[64,256]{1,0:T(8,128)S(1)}, u32[]{:S(2)}, u32[]{:S(2)}) collective-permute-start(f32[64,256]{1,0:T(8,128)S(1)} %get-tuple-element.46.refs_0_), channel_id=1, source_target_pairs={{0,8},{4,12},{8,0},{12,4},{1,9},{5,13},{9,1},{13,5},{2,10},{6,14},... | collective-permute-start | bytes 196616 | tf_op jit(solution)/shard_map/ppermute | solution.py:353
  32.0 1.7 %collective-permute-start.13 = (f32[64,256]{1,0:T(8,128)S(1)}, f32[64,256]{1,0:T(8,128)S(1)}, u32[]{:S(2)}, u32[]{:S(2)}) collective-permute-start(f32[64,256]{1,0:T(8,128)S(1)} %get-tuple-element.46.refs_0_), channel_id=1, source_target_pairs={{0,12},{4,8},{8,4},{12,0},{1,13},{5,9},{9,5},{13,1},{2,14},{6,10},... | collective-permute-start | bytes 196616 | tf_op jit(solution)/shard_map/ppermute | solution.py:353
  33.8 0.0 collective-permute-done.11.refs_3_
  33.8 0.8 %collective-permute-start.12 = (f32[64,256]{1,0:T(8,128)S(1)}, f32[64,256]{1,0:T(8,128)S(1)}, u32[]{:S(2)}, u32[]{:S(2)}) collective-permute-start(f32[64,256]{1,0:T(8,128)S(1)} %get-tuple-element.46.refs_0_), channel_id=1, source_target_pairs={{0,4},{4,0},{8,12},{12,8},{1,5},{5,1},{9,13},{13,9},{2,6},{6,2},{1... | collective-permute-start | bytes 196616 | tf_op jit(solution)/shard_map/ppermute | solution.py:353
  34.6 0.7 %collective-permute-done.10.refs_2_ = f32[72,256]{1,0:T(8,128)S(1)} collective-permute-done((f32[72,256]{1,0:T(8,128)S(1)}, f32[72,256]{1,0:T(8,128)S(1)}, u32[]{:S(2)}, u32[]{:S(2)}) %collective-permute-start.10) | collective-permute-done | bytes 73760 | tf_op jit(solution)/shard_map/ppermute | solution.py:353
  35.2 0.0 collective-permute-done.9.refs_1_
  35.2 2.9 %shard_map.132 = (f32[16,64,128]{2,1,0:T(8,128)S(1)}, f32[16,32,128]{2,1,0:T(8,128)S(1)}, f32[16,32,128]{2,1,0:T(8,128)S(1)}) custom-call(s32[4,384]{1,0:T(4,128)S(1)} %get-tuple-element.29.order, f32[16,128]{1,0:T(8,128)S(1)} %get-tuple-element.30.scale.source_scale.target_scale, f32[16,128]{1,0:T(8,128)S(1)} %get-tuple-element.31.scale.target_scale.source_scale, ...), custom_call_target="tpu_custom_call" | custom-call | flops 603979776 | bytes 9437184 | tf_op jit(solution)/shard_map/pallas_call | solution.py:24
  38.1 1.3 %collective-permute-start.16 = (f32[16,32,128]{2,1,0:T(8,128)S(1)}, f32[16,32,128]{2,1,0:T(8,128)S(1)}, u32[]{:S(2)}, u32[]{:S(2)}) collective-permute-start(f32[16,32,128]{2,1,0:T(8,128)S(1)} %get-tuple-element.45.after), channel_id=1, source_target_pairs={{0,1},{1,0},{2,3},{3,2},{4,5},{5,4},{6,7},{7,6},{8,9},{9,8},{10,11... | collective-permute-start | bytes 786440 | tf_op jit(solution)/shard_map/ppermute | solution.py:353
  39.4 0.0 collective-permute-done.14.refs_3_
  39.4 0.0 collective-permute-done.13.refs_2_
  39.4 1.0 %collective-permute-done.12.refs_1_ = f32[64,256]{1,0:T(8,128)S(1)} collective-permute-done((f32[64,256]{1,0:T(8,128)S(1)}, f32[64,256]{1,0:T(8,128)S(1)}, u32[]{:S(2)}, u32[]{:S(2)}) %collective-permute-start.12) | collective-permute-done | bytes 65568 | tf_op jit(solution)/shard_map/ppermute | solution.py:353
  40.4 1.5 %shard_map.133.after.mine = f32[16,64,128]{2,1,0:T(8,128)S(1)} custom-call(f32[16,32,128]{2,1,0:T(8,128)S(1)} %get-tuple-element.45.after, f32[64,256]{1,0:T(8,128)S(1)} %get-tuple-element.46.refs_0_, f32[64,256]{1,0:T(8,128)S(1)} %collective-permute-done.12.refs_1_, f32[64,256]{1,0:T(8,128)S(1)} %collective-permute-done.13.refs_2_, ...), custom_call_target="tpu_custom_call" | custom-call | flops 99999997952 | tf_op jit(solution)/shard_map/pallas_call | solution.py:24
  41.9 0.1 collective-permute-start.15
  42.0 0.0 collective-permute-done.16.received
  42.0 0.0 copy-start.1
  42.0 0.0 copy-start.3
  42.1 0.7 collective-permute-start.17
  42.7 2.4 %collective-permute-start.18 = (f32[4,32,128]{2,1,0:T(8,128)S(1)}, f32[4,32,128]{2,1,0:T(8,128)S(1)}, u32[]{:S(2)}, u32[]{:S(2)}) collective-permute-start(f32[4,32,128]{2,1,0:T(8,128)S(1)} %get-tuple-element.51), channel_id=1, source_target_pairs={{0,12},{4,8},{8,4},{12,0},{1,13},{5,9},{9,5},{13,1},{2,14},{6,10},... | collective-permute-start | bytes 196616 | tf_op jit(solution)/shard_map/ppermute | solution.py:353
  45.2 0.5 collective-permute-start.19
  45.6 0.1 copy-done.1
  45.7 1.8 %shard_map.135 = (f32[16,64,128]{2,1,0:T(8,128)S(1)}, f32[16,64,128]{2,1,0:T(8,128)S(1)}) custom-call(s32[4,384]{1,0:T(4,128)S(1)} %copy-done.3, f32[16,64,128]{2,1,0:T(8,128)S(1)} %shard_map.133.after.mine, f32[16,64,128]{2,1,0:T(8,128)S(1)} %collective-permute-done.15.other, f32[16,128]{1,0:T(8,128)S(1)} %get-tuple-element.31.scale.target_scale.source_scale, ...), custom_call_target="tpu_custom_call" | custom-call | flops 603979776 | bytes 9437184 | tf_op jit(solution)/shard_map/pallas_call | solution.py:24
  47.5 3.1 %collective-permute-done.17.refs_1_ = f32[4,32,128]{2,1,0:T(8,128)S(1)} collective-permute-done((f32[4,32,128]{2,1,0:T(8,128)S(1)}, f32[4,32,128]{2,1,0:T(8,128)S(1)}, u32[]{:S(2)}, u32[]{:S(2)}) %collective-permute-start.17) | collective-permute-done | bytes 65568 | tf_op jit(solution)/shard_map/ppermute | solution.py:353
  50.5 1.0 %collective-permute-done.19.refs_3_ = f32[4,32,128]{2,1,0:T(8,128)S(1)} collective-permute-done((f32[4,32,128]{2,1,0:T(8,128)S(1)}, f32[4,32,128]{2,1,0:T(8,128)S(1)}, u32[]{:S(2)}, u32[]{:S(2)}) %collective-permute-start.19) | collective-permute-done | bytes 65568 | tf_op jit(solution)/shard_map/ppermute | solution.py:353
  51.6 0.1 collective-permute-start.20
  51.6 1.5 %collective-permute-done.20.refs_1_ = f32[16,32,128]{2,1,0:T(8,128)S(1)} collective-permute-done((f32[16,32,128]{2,1,0:T(8,128)S(1)}, f32[16,32,128]{2,1,0:T(8,128)S(1)}, u32[]{:S(2)}, u32[]{:S(2)}) %collective-permute-start.20) | collective-permute-done | bytes 262176 | tf_op jit(solution)/shard_map/ppermute | solution.py:353
  53.2 2.8 %collective-permute-start.21 = (f32[16,32,128]{2,1,0:T(8,128)S(1)}, f32[16,32,128]{2,1,0:T(8,128)S(1)}, u32[]{:S(2)}, u32[]{:S(2)}) collective-permute-start(f32[16,32,128]{2,1,0:T(8,128)S(1)} %shard_map.138.refs_0_), channel_id=1, source_target_pairs={{0,2},{2,0},{1,3},{3,1},{4,6},{6,4},{5,7},{7,5},{8,10},{10,8},{9,1... | collective-permute-start | bytes 786440 | tf_op jit(solution)/shard_map/ppermute | solution.py:353
  56.0 1.7 %collective-permute-start.24 = (f32[4,32,128]{2,1,0:T(8,128)S(1)}, f32[4,32,128]{2,1,0:T(8,128)S(1)}, u32[]{:S(2)}, u32[]{:S(2)}) collective-permute-start(f32[4,32,128]{2,1,0:T(8,128)S(1)} %shard_map.136.after.refs_0_), channel_id=1, source_target_pairs={{0,12},{4,8},{8,4},{12,0},{1,13},{5,9},{9,5},{13,1},{2,14},{6,10},... | collective-permute-start | bytes 196616 | tf_op jit(solution)/shard_map/ppermute | solution.py:353
  57.7 1.8 %collective-permute-start.23 = (f32[4,32,128]{2,1,0:T(8,128)S(1)}, f32[4,32,128]{2,1,0:T(8,128)S(1)}, u32[]{:S(2)}, u32[]{:S(2)}) collective-permute-start(f32[4,32,128]{2,1,0:T(8,128)S(1)} %shard_map.136.after.refs_0_), channel_id=1, source_target_pairs={{0,4},{4,0},{8,12},{12,8},{1,5},{5,1},{9,13},{13,9},{2,6},{6,2},{1... | collective-permute-start | bytes 196616 | tf_op jit(solution)/shard_map/ppermute | solution.py:353
  59.5 3.6 %collective-permute-done.25.refs_3_ = f32[4,32,128]{2,1,0:T(8,128)S(1)} collective-permute-done((f32[4,32,128]{2,1,0:T(8,128)S(1)}, f32[4,32,128]{2,1,0:T(8,128)S(1)}, u32[]{:S(2)}, u32[]{:S(2)}) %collective-permute-start.25) | collective-permute-done | bytes 65568 | tf_op jit(solution)/shard_map/ppermute | solution.py:353
  63.1 0.7 %collective-permute-done.23.refs_1_ = f32[4,32,128]{2,1,0:T(8,128)S(1)} collective-permute-done((f32[4,32,128]{2,1,0:T(8,128)S(1)}, f32[4,32,128]{2,1,0:T(8,128)S(1)}, u32[]{:S(2)}, u32[]{:S(2)}) %collective-permute-start.23) | collective-permute-done | bytes 65568 | tf_op jit(solution)/shard_map/ppermute | solution.py:353
  63.9 0.1 collective-permute-start.26
  64.0 0.5 collective-permute-start.22
  64.6 0.9 %collective-permute-done.26.item_other = f32[4,4,32,128]{3,2,1,0:T(8,128)S(1)} collective-permute-done((f32[4,4,32,128]{3,2,1,0:T(8,128)S(1)}, f32[4,4,32,128]{3,2,1,0:T(8,128)S(1)}, u32[]{:S(2)}, u32[]{:S(2)}) %collective-permute-start.26) | collective-permute-done | bytes 262176 | tf_op jit(solution)/shard_map/ppermute | solution.py:353
  65.5 0.4 collective-permute-done.22.user_other
  65.9 1.1 %shard_map.141 = (f32[64,2048]{1,0:T(8,128)}, f32[64,2048]{1,0:T(8,128)}) custom-call(f32[16,64,128]{2,1,0:T(8,128)S(1)} %get-tuple-element.44.user_half_grad, f32[16,32,128]{2,1,0:T(8,128)S(1)} %shard_map.139.user_mine, f32[16,32,128]{2,1,0:T(8,128)S(1)} %collective-permute-done.22.user_other, f32[16,64,128]{2,1,0:T(8,128)S(1)} %get-tuple-element.55.item_half_grad, ...), custom_call_target="tpu_custom_call" | custom-call | bytes 3145728 | tf_op jit(solution)/shard_map/pallas_call | solution.py:24
  (36 shorter events, 0.3 us)
Async XLA Ops:
  0.6 0.7 %copy-start.6 = (s32[256]{0:T(256)S(1)}, s32[256]{0:T(256)}, u32[]{:S(2)}) copy-start(s32[256]{0:T(256)} %param.21) | copy-start | bytes 3076
  0.6 0.7 %copy-start.5 = (s32[256]{0:T(256)S(1)}, s32[256]{0:T(256)}, u32[]{:S(2)}) copy-start(s32[256]{0:T(256)} %param.20) | copy-start | bytes 3076
  0.7 0.7 %copy-start.4 = (s32[256]{0:T(256)S(1)}, s32[256]{0:T(256)}, u32[]{:S(2)}) copy-start(s32[256]{0:T(256)} %param.19) | copy-start | bytes 3076
  0.7 5.9 %copy-start.8 = (bf16[64,2048]{1,0:T(8,128)(2,1)S(1)}, bf16[64,2048]{1,0:T(8,128)(2,1)}, u32[]{:S(2)}) copy-start(bf16[64,2048]{1,0:T(8,128)(2,1)} %item_emb.3) | copy-start | bytes 786436
  0.7 5.9 %copy-start.7 = (bf16[64,2048]{1,0:T(8,128)(2,1)S(1)}, bf16[64,2048]{1,0:T(8,128)(2,1)}, u32[]{:S(2)}) copy-start(bf16[64,2048]{1,0:T(8,128)(2,1)} %user_emb.3) | copy-start | bytes 786436
  0.7 5.9 %copy-start.12 = (s32[288]{0:T(512)S(1)}, s32[288]{0:T(512)}, u32[]{:S(2)}) copy-start(s32[288]{0:T(512)} %columns.1) | copy-start | bytes 3460
  0.7 5.9 %copy-start.11 = (s32[288]{0:T(512)S(1)}, s32[288]{0:T(512)}, u32[]{:S(2)}) copy-start(s32[288]{0:T(512)} %rows.1) | copy-start | bytes 3460
  0.7 5.9 %copy-start.10 = (s32[2048]{0:T(1024)S(1)}, s32[2048]{0:T(1024)}, u32[]{:S(2)}) copy-start(s32[2048]{0:T(1024)} %param.14) | copy-start | bytes 24580
  0.7 5.9 %copy-start.9 = (s32[2048]{0:T(1024)S(1)}, s32[2048]{0:T(1024)}, u32[]{:S(2)}) copy-start(s32[2048]{0:T(1024)} %param.13) | copy-start | bytes 24580
  0.7 9.5 %copy-start = (bf16[288,128,128]{2,1,0:T(8,128)(2,1)S(1)}, bf16[288,128,128]{2,1,0:T(8,128)(2,1)}, u32[]{:S(2)}) copy-start(bf16[288,128,128]{2,1,0:T(8,128)(2,1)} %vals.7) | copy-start | bytes 28311556
  1.4 6.2 %collective-permute-start = (s32[64,256]{1,0:T(8,128)S(1)}, s32[64,256]{1,0:T(8,128)S(1)}, u32[]{:S(2)}, u32[]{:S(2)}) collective-permute-start(s32[64,256]{1,0:T(8,128)S(1)} %shard_map.123.after.refs_0_.ids.refs_4_), channel_id=1, source_target_pairs={{0,4},{4,0},{8,12},{12,8},{1,5},{5,1},{9,13},{13,9},{2,6},{6,2},{1... | collective-permute-start | bytes 196616 | tf_op jit(solution)/shard_map/ppermute | solution.py:353
  4.4 7.6 %collective-permute-start.2 = (s32[64,256]{1,0:T(8,128)S(1)}, s32[64,256]{1,0:T(8,128)S(1)}, u32[]{:S(2)}, u32[]{:S(2)}) collective-permute-start(s32[64,256]{1,0:T(8,128)S(1)} %shard_map.123.after.refs_0_.ids.refs_4_), channel_id=1, source_target_pairs={{0,2},{2,0},{1,3},{3,1},{4,6},{6,4},{5,7},{7,5},{8,10},{10,8},{9,1... | collective-permute-start | bytes 196616 | tf_op jit(solution)/shard_map/ppermute | solution.py:353
  7.6 7.6 %copy-start.2 = (s32[4,384]{1,0:T(4,128)}, s32[4,384]{1,0:T(4,128)S(1)}, u32[]{:S(2)}) copy-start(s32[4,384]{1,0:T(4,128)S(1)} %get-tuple-element.32.order) | copy-start | bytes 18436
  7.6 5.9 %collective-permute-start.1 = (s32[64,256]{1,0:T(8,128)S(1)}, s32[64,256]{1,0:T(8,128)S(1)}, u32[]{:S(2)}, u32[]{:S(2)}) collective-permute-start(s32[64,256]{1,0:T(8,128)S(1)} %shard_map.126), channel_id=1, source_target_pairs={{0,8},{4,12},{8,0},{12,4},{1,9},{5,13},{9,1},{13,5},{2,10},{6,14},... | collective-permute-start | bytes 196616 | tf_op jit(solution)/shard_map/ppermute | solution.py:353
  11.6 3.8 %collective-permute-start.4 = (f32[16,64,128]{2,1,0:T(8,128)S(1)}, f32[16,64,128]{2,1,0:T(8,128)S(1)}, u32[]{:S(2)}, u32[]{:S(2)}) collective-permute-start(f32[16,64,128]{2,1,0:T(8,128)S(1)} %shard_map.125.refs_0_.mine), channel_id=1, source_target_pairs={{0,1},{1,0},{2,3},{3,2},{4,5},{5,4},{6,7},{7,6},{8,9},{9,8},{10,11... | collective-permute-start | bytes 1572872 | tf_op jit(solution)/shard_map/ppermute | solution.py:353
  15.2 5.7 %collective-permute-start.3 = (f32[16,64,128]{2,1,0:T(8,128)S(1)}, f32[16,64,128]{2,1,0:T(8,128)S(1)}, u32[]{:S(2)}, u32[]{:S(2)}) collective-permute-start(f32[16,64,128]{2,1,0:T(8,128)S(1)} %shard_map.127.mine), channel_id=1, source_target_pairs={{0,1},{1,0},{2,3},{3,2},{4,5},{5,4},{6,7},{7,6},{8,9},{9,8},{10,11... | collective-permute-start | bytes 1572872 | tf_op jit(solution)/shard_map/ppermute | solution.py:353
  16.6 10.4 %collective-permute-start.6 = (f32[64,256]{1,0:T(8,128)S(1)}, f32[64,256]{1,0:T(8,128)S(1)}, u32[]{:S(2)}, u32[]{:S(2)}) collective-permute-start(f32[64,256]{1,0:T(8,128)S(1)} %get-tuple-element.39), channel_id=1, source_target_pairs={{0,8},{4,12},{8,0},{12,4},{1,9},{5,13},{9,1},{13,5},{2,10},{6,14},... | collective-permute-start | bytes 196616 | tf_op jit(solution)/shard_map/ppermute | solution.py:353
  19.1 8.0 %collective-permute-start.7 = (f32[64,256]{1,0:T(8,128)S(1)}, f32[64,256]{1,0:T(8,128)S(1)}, u32[]{:S(2)}, u32[]{:S(2)}) collective-permute-start(f32[64,256]{1,0:T(8,128)S(1)} %get-tuple-element.40), channel_id=1, source_target_pairs={{0,12},{4,8},{8,4},{12,0},{1,13},{5,9},{9,5},{13,1},{2,14},{6,10},... | collective-permute-start | bytes 196616 | tf_op jit(solution)/shard_map/ppermute | solution.py:353
  20.9 6.2 %collective-permute-start.8 = (f32[64,256]{1,0:T(8,128)S(1)}, f32[64,256]{1,0:T(8,128)S(1)}, u32[]{:S(2)}, u32[]{:S(2)}) collective-permute-start(f32[64,256]{1,0:T(8,128)S(1)} %get-tuple-element.41), channel_id=1, source_target_pairs={{0,4},{4,0},{8,12},{12,8},{1,5},{5,1},{9,13},{13,9},{2,6},{6,2},{1... | collective-permute-start | bytes 196616 | tf_op jit(solution)/shard_map/ppermute | solution.py:353
  21.5 7.3 %collective-permute-start.5 = (f32[64,256]{1,0:T(8,128)S(1)}, f32[64,256]{1,0:T(8,128)S(1)}, u32[]{:S(2)}, u32[]{:S(2)}) collective-permute-start(f32[64,256]{1,0:T(8,128)S(1)} %get-tuple-element.37), channel_id=1, source_target_pairs={{0,2},{2,0},{1,3},{3,1},{4,6},{6,4},{5,7},{7,5},{8,10},{10,8},{9,1... | collective-permute-start | bytes 196616 | tf_op jit(solution)/shard_map/ppermute | solution.py:353
  28.9 4.9 %collective-permute-start.11 = (f32[72,256]{1,0:T(8,128)S(1)}, f32[72,256]{1,0:T(8,128)S(1)}, u32[]{:S(2)}, u32[]{:S(2)}) collective-permute-start(f32[72,256]{1,0:T(8,128)S(1)} %get-tuple-element.43.refs_0_), channel_id=1, source_target_pairs={{0,3},{1,2},{2,1},{3,0},{4,7},{5,6},{6,5},{7,4},{8,11},{9,10},{10,... | collective-permute-start | bytes 221192 | tf_op jit(solution)/shard_map/ppermute | solution.py:452
  30.4 4.9 %collective-permute-start.10 = (f32[72,256]{1,0:T(8,128)S(1)}, f32[72,256]{1,0:T(8,128)S(1)}, u32[]{:S(2)}, u32[]{:S(2)}) collective-permute-start(f32[72,256]{1,0:T(8,128)S(1)} %get-tuple-element.43.refs_0_), channel_id=1, source_target_pairs={{0,2},{2,0},{1,3},{3,1},{4,6},{6,4},{5,7},{7,5},{8,10},{10,8},{9,1... | collective-permute-start | bytes 221192 | tf_op jit(solution)/shard_map/ppermute | solution.py:353
  31.0 4.2 %collective-permute-start.9 = (f32[72,256]{1,0:T(8,128)S(1)}, f32[72,256]{1,0:T(8,128)S(1)}, u32[]{:S(2)}, u32[]{:S(2)}) collective-permute-start(f32[72,256]{1,0:T(8,128)S(1)} %get-tuple-element.43.refs_0_), channel_id=1, source_target_pairs={{0,1},{1,0},{2,3},{3,2},{4,5},{5,4},{6,7},{7,6},{8,9},{9,8},{10,11... | collective-permute-start | bytes 221192 | tf_op jit(solution)/shard_map/ppermute | solution.py:353
  31.1 8.4 %collective-permute-start.14 = (f32[64,256]{1,0:T(8,128)S(1)}, f32[64,256]{1,0:T(8,128)S(1)}, u32[]{:S(2)}, u32[]{:S(2)}) collective-permute-start(f32[64,256]{1,0:T(8,128)S(1)} %get-tuple-element.46.refs_0_), channel_id=1, source_target_pairs={{0,8},{4,12},{8,0},{12,4},{1,9},{5,13},{9,1},{13,5},{2,10},{6,14},... | collective-permute-start | bytes 196616 | tf_op jit(solution)/shard_map/ppermute | solution.py:353
  32.0 7.4 %collective-permute-start.13 = (f32[64,256]{1,0:T(8,128)S(1)}, f32[64,256]{1,0:T(8,128)S(1)}, u32[]{:S(2)}, u32[]{:S(2)}) collective-permute-start(f32[64,256]{1,0:T(8,128)S(1)} %get-tuple-element.46.refs_0_), channel_id=1, source_target_pairs={{0,12},{4,8},{8,4},{12,0},{1,13},{5,9},{9,5},{13,1},{2,14},{6,10},... | collective-permute-start | bytes 196616 | tf_op jit(solution)/shard_map/ppermute | solution.py:353
  33.8 6.6 %collective-permute-start.12 = (f32[64,256]{1,0:T(8,128)S(1)}, f32[64,256]{1,0:T(8,128)S(1)}, u32[]{:S(2)}, u32[]{:S(2)}) collective-permute-start(f32[64,256]{1,0:T(8,128)S(1)} %get-tuple-element.46.refs_0_), channel_id=1, source_target_pairs={{0,4},{4,0},{8,12},{12,8},{1,5},{5,1},{9,13},{13,9},{2,6},{6,2},{1... | collective-permute-start | bytes 196616 | tf_op jit(solution)/shard_map/ppermute | solution.py:353
  38.1 3.8 %collective-permute-start.16 = (f32[16,32,128]{2,1,0:T(8,128)S(1)}, f32[16,32,128]{2,1,0:T(8,128)S(1)}, u32[]{:S(2)}, u32[]{:S(2)}) collective-permute-start(f32[16,32,128]{2,1,0:T(8,128)S(1)} %get-tuple-element.45.after), channel_id=1, source_target_pairs={{0,1},{1,0},{2,3},{3,2},{4,5},{5,4},{6,7},{7,6},{8,9},{9,8},{10,11... | collective-permute-start | bytes 786440 | tf_op jit(solution)/shard_map/ppermute | solution.py:353
  41.9 3.7 %collective-permute-start.15 = (f32[16,64,128]{2,1,0:T(8,128)S(1)}, f32[16,64,128]{2,1,0:T(8,128)S(1)}, u32[]{:S(2)}, u32[]{:S(2)}) collective-permute-start(f32[16,64,128]{2,1,0:T(8,128)S(1)} %shard_map.133.after.mine), channel_id=1, source_target_pairs={{0,1},{1,0},{2,3},{3,2},{4,5},{5,4},{6,7},{7,6},{8,9},{9,8},{10,11... | collective-permute-start | bytes 1572872 | tf_op jit(solution)/shard_map/ppermute | solution.py:353
  42.0 3.7 %copy-start.1 = (bf16[288,128,128]{2,1,0:T(8,128)(2,1)S(1)}, bf16[288,128,128]{2,1,0:T(8,128)(2,1)}, u32[]{:S(2)}) copy-start(bf16[288,128,128]{2,1,0:T(8,128)(2,1)} %vals.7) | copy-start | bytes 28311556
  42.0 3.7 %copy-start.3 = (s32[4,384]{1,0:T(4,128)S(1)}, s32[4,384]{1,0:T(4,128)}, u32[]{:S(2)}) copy-start(s32[4,384]{1,0:T(4,128)} %copy-done.2) | copy-start | bytes 18436
  42.1 8.4 %collective-permute-start.17 = (f32[4,32,128]{2,1,0:T(8,128)S(1)}, f32[4,32,128]{2,1,0:T(8,128)S(1)}, u32[]{:S(2)}, u32[]{:S(2)}) collective-permute-start(f32[4,32,128]{2,1,0:T(8,128)S(1)} %get-tuple-element.50), channel_id=1, source_target_pairs={{0,8},{4,12},{8,0},{12,4},{1,9},{5,13},{9,1},{13,5},{2,10},{6,14},... | collective-permute-start | bytes 196616 | tf_op jit(solution)/shard_map/ppermute | solution.py:353
  42.7 7.8 %collective-permute-start.18 = (f32[4,32,128]{2,1,0:T(8,128)S(1)}, f32[4,32,128]{2,1,0:T(8,128)S(1)}, u32[]{:S(2)}, u32[]{:S(2)}) collective-permute-start(f32[4,32,128]{2,1,0:T(8,128)S(1)} %get-tuple-element.51), channel_id=1, source_target_pairs={{0,12},{4,8},{8,4},{12,0},{1,13},{5,9},{9,5},{13,1},{2,14},{6,10},... | collective-permute-start | bytes 196616 | tf_op jit(solution)/shard_map/ppermute | solution.py:353
  45.2 6.3 %collective-permute-start.19 = (f32[4,32,128]{2,1,0:T(8,128)S(1)}, f32[4,32,128]{2,1,0:T(8,128)S(1)}, u32[]{:S(2)}, u32[]{:S(2)}) collective-permute-start(f32[4,32,128]{2,1,0:T(8,128)S(1)} %get-tuple-element.52), channel_id=1, source_target_pairs={{0,4},{4,0},{8,12},{12,8},{1,5},{5,1},{9,13},{13,9},{2,6},{6,2},{1... | collective-permute-start | bytes 196616 | tf_op jit(solution)/shard_map/ppermute | solution.py:353
  51.6 1.6 %collective-permute-start.20 = (f32[16,32,128]{2,1,0:T(8,128)S(1)}, f32[16,32,128]{2,1,0:T(8,128)S(1)}, u32[]{:S(2)}, u32[]{:S(2)}) collective-permute-start(f32[16,32,128]{2,1,0:T(8,128)S(1)} %get-tuple-element.54), channel_id=1, source_target_pairs={{0,1},{1,0},{2,3},{3,2},{4,5},{5,4},{6,7},{7,6},{8,9},{9,8},{10,11... | collective-permute-start | bytes 786440 | tf_op jit(solution)/shard_map/ppermute | solution.py:353
  53.2 10.8 %collective-permute-start.21 = (f32[16,32,128]{2,1,0:T(8,128)S(1)}, f32[16,32,128]{2,1,0:T(8,128)S(1)}, u32[]{:S(2)}, u32[]{:S(2)}) collective-permute-start(f32[16,32,128]{2,1,0:T(8,128)S(1)} %shard_map.138.refs_0_), channel_id=1, source_target_pairs={{0,2},{2,0},{1,3},{3,1},{4,6},{6,4},{5,7},{7,5},{8,10},{10,8},{9,1... | collective-permute-start | bytes 786440 | tf_op jit(solution)/shard_map/ppermute | solution.py:353
  56.0 7.1 %collective-permute-start.25 = (f32[4,32,128]{2,1,0:T(8,128)S(1)}, f32[4,32,128]{2,1,0:T(8,128)S(1)}, u32[]{:S(2)}, u32[]{:S(2)}) collective-permute-start(f32[4,32,128]{2,1,0:T(8,128)S(1)} %shard_map.136.after.refs_0_), channel_id=1, source_target_pairs={{0,8},{4,12},{8,0},{12,4},{1,9},{5,13},{9,1},{13,5},{2,10},{6,14},... | collective-permute-start | bytes 196616 | tf_op jit(solution)/shard_map/ppermute | solution.py:353
  56.0 7.1 %collective-permute-start.24 = (f32[4,32,128]{2,1,0:T(8,128)S(1)}, f32[4,32,128]{2,1,0:T(8,128)S(1)}, u32[]{:S(2)}, u32[]{:S(2)}) collective-permute-start(f32[4,32,128]{2,1,0:T(8,128)S(1)} %shard_map.136.after.refs_0_), channel_id=1, source_target_pairs={{0,12},{4,8},{8,4},{12,0},{1,13},{5,9},{9,5},{13,1},{2,14},{6,10},... | collective-permute-start | bytes 196616 | tf_op jit(solution)/shard_map/ppermute | solution.py:353
  57.7 6.1 %collective-permute-start.23 = (f32[4,32,128]{2,1,0:T(8,128)S(1)}, f32[4,32,128]{2,1,0:T(8,128)S(1)}, u32[]{:S(2)}, u32[]{:S(2)}) collective-permute-start(f32[4,32,128]{2,1,0:T(8,128)S(1)} %shard_map.136.after.refs_0_), channel_id=1, source_target_pairs={{0,4},{4,0},{8,12},{12,8},{1,5},{5,1},{9,13},{13,9},{2,6},{6,2},{1... | collective-permute-start | bytes 196616 | tf_op jit(solution)/shard_map/ppermute | solution.py:353
  63.9 1.6 %collective-permute-start.26 = (f32[4,4,32,128]{3,2,1,0:T(8,128)S(1)}, f32[4,4,32,128]{3,2,1,0:T(8,128)S(1)}, u32[]{:S(2)}, u32[]{:S(2)}) collective-permute-start(f32[4,4,32,128]{3,2,1,0:T(8,128)S(1)} %shard_map.140.item_mine), channel_id=1, source_target_pairs={{0,1},{1,0},{2,3},{3,2},{4,5},{5,4},{6,7},{7,6},{8,9},{9,8},{10,11... | collective-permute-start | bytes 786440 | tf_op jit(solution)/shard_map/ppermute | solution.py:353
  64.0 1.8 %collective-permute-start.22 = (f32[16,32,128]{2,1,0:T(8,128)S(1)}, f32[16,32,128]{2,1,0:T(8,128)S(1)}, u32[]{:S(2)}, u32[]{:S(2)}) collective-permute-start(f32[16,32,128]{2,1,0:T(8,128)S(1)} %shard_map.139.user_mine), channel_id=1, source_target_pairs={{0,1},{1,0},{2,3},{3,2},{4,5},{5,4},{6,7},{7,6},{8,9},{9,8},{10,11... | collective-permute-start | bytes 786440 | tf_op jit(solution)/shard_map/ppermute | solution.py:353

commit v2 on v1

--- a/solution.py
+++ b/solution.py
@@ -309,18 +309,21 @@
 
 
 def sum_after(after, *refs):
-    sum_parts(*refs)
-
-
-def pack(*refs):
-    for place, ref in enumerate(refs[:-1]):
-        refs[-1][place] = ref[...]
-
-
-def finish(offsets, user_half_grad, user_mine, user_other, item_half_grad, item_mine, item_other,
-           user_out, item_out):
+    refs[-1][0] = add_all(refs[:-1])
+
+
+def pack(first, second, out):
+    count = first.shape[0]
+    out[:count] = first[...]
+    out[count:] = second[...]
+
+
+def finish(places, user_half_grad, user_mine, user_other, item_half_grad, *refs):
+    (user_out, item_out), refs = refs[-2:], refs[:-2]
     finish_users(user_half_grad, user_mine, user_other, user_out)
-    finish_items(offsets, item_half_grad, item_mine, item_other, item_out)
+    mine, other = refs[:len(places)], refs[len(places):]
+    for offsets, mine_here, other_here in zip(places, mine, other):
+        finish_items(offsets, item_half_grad, mine_here, other_here, item_out)
 
 
 def finish_users(half_grad, mine, other, out):
@@ -339,7 +342,7 @@
     place = lax.axis_index("user")
     blocks, width, size = half_grad.shape
     half = width // 2
-    per = blocks // len(offsets)
+    per = mine.shape[1]
     for index, offset in enumerate(offsets):
         there = (place ^ offset) * per
         for block in range(per):
@@ -483,13 +486,22 @@
         product_flops, product_bytes,
     )
     parts = [dealt[0]] + [swap(part, "user", users, o) for part, o in zip(dealt[1:], met)]
-    item_own = call(sum_after, shape(per, half, size), (user_back, *parts),
+    item_own = call(sum_after, shape(1, per, half, size), (user_back, *parts),
                     [ANY] + [VMEM] * users,
                moved=4 * (users + 1) * per * half * size)
-    item_mine = call(pack, shape(users, per, half, size),
-                     (item_own, *[swap(item_own, "user", users, o) for o in back]),
-                     [VMEM] * users, moved=8 * item_blocks * half * size)
-    item_other = swap(item_mine)
+    known, offsets, step = item_own, [0], users // 2
+    item_mine = [(known, offsets)]
+    while step >= 1:
+        come = swap(known, "user", users, step)
+        item_mine = [(known, offsets), (come, [offset ^ step for offset in offsets])]
+        offsets = offsets + item_mine[1][1]
+        if step > 1:
+            known = call(pack, shape(len(offsets), per, half, size), (known, come), [VMEM] * 2,
+                         (), HEAVY)
+        step //= 2
+    item_places = [places for _, places in item_mine]
+    item_mine = [part for part, _ in item_mine]
+    item_other = [swap(part) for part in item_mine]
 
     user_keep, user_send = call(
         halves_after, [shape(user_blocks, half, size)] * 2, (user_back, item_own), [VMEM, ANY],
@@ -501,10 +513,10 @@
                 (own, *[swap(own, "item", items, o) for o in range(1, items)]),
                 [VMEM] * items, moved=12 * user_blocks * half * size)
     return call(
-        functools.partial(finish, [0, *back]),
+        functools.partial(finish, item_places),
         (shape(width, user_blocks * size), shape(width, item_blocks * size)),
-        (user_half_grad, mine, swap(mine), item_half_grad, item_mine, item_other),
-        [VMEM] * 6, moved=12 * (user_blocks + item_blocks) * width * size,
+        (user_half_grad, mine, swap(mine), item_half_grad, *item_mine, *item_other),
+        [VMEM] * (4 + 2 * len(item_mine)), moved=12 * (user_blocks + item_blocks) * width * size,
     )
 
 

time: 67.1 us -> 65.7 us (0.979); the launches traced: 67 us -> 64.7 us
  starting transfers between devices: 34.7 us -> 26.1 us
  waiting for transfers between devices: 16.1 us -> 19.8 us
  Pallas kernels: 13.8 us -> 16.4 us
    ppermute x26, starting transfers between devices: 33.3 us -> 25.6 us  [swap(): return lax.ppermute(values, axis, [(i, i ^ offset) for i in range(peers)])]
    ppermute x26, waiting for transfers between devices: 16.1 us -> 19.8 us  [swap(): return lax.ppermute(values, axis, [(i, i ^ offset) for i in range(peers)])]
    pallas_call x20, Pallas kernels: 13.8 us -> 16.4 us  [call(): pl.pallas_call(kernel, out_shape=outs, in_specs=specs, out_specs=jax.tree...]
    ppermute x1, starting transfers between devices: 1.49 us -> 0.5 us  [on_device(): lax.ppermute(pieces, ('item', 'rep'), [(i, i ^ 2 * offset + 1) for i in r...]
  transfers between devices with their start and end apart: 27 -> 27, of which waited for: 11 -> 12; matrix products, arithmetic and copies ran while one was open for 0% -> 0% of each run, Pallas kernels for 19% -> 23%
where the time goes in v2:
time: 65.7 us; the launch traced here: 64.7 us
  starting transfers between devices  26.1 us (40%)
  waiting for transfers between devices  19.8 us (30%)
  Pallas kernels  16.4 us (25%)
  between operations  1.66 us (3%)
  local copies, waits for them, and re-layouts  0.72 us (1%)
    ppermute x26, starting transfers between devices, swap(): return lax.ppermute(values, axis, [(i, i ^ offset) for i in range(peers)])  25.6 us
    ppermute x26, waiting for transfers between devices, swap(): return lax.ppermute(values, axis, [(i, i ^ offset) for i in range(peers)])  19.8 us
    pallas_call x20, Pallas kernels, call(): pl.pallas_call(kernel, out_shape=outs, in_specs=specs, out_specs=jax.tree...  16.4 us
  transfers between devices with their start and end apart: 27, of which 12 were waited for; matrix products, arithmetic and copies ran while one was open for 0% of the time, Pallas kernels for 23%

profile of v2, /device:TPU:0, one launch (start us, length us, event | category | flops | bytes accessed | tf_op | source)
XLA Modules:
  0.0 64.7 jit_solution(14431696539935252848)
XLA Ops:
  0.7 0.0 copy-start
  0.7 0.6 copy-done.6
  1.3 0.0 copy-done.5
  1.3 0.0 copy-done.4
  1.4 3.1 %collective-permute-start = (s32[64,256]{1,0:T(8,128)S(1)}, s32[64,256]{1,0:T(8,128)S(1)}, u32[]{:S(2)}, u32[]{:S(2)}) collective-permute-start(s32[64,256]{1,0:T(8,128)S(1)} %shard_map.123.after.refs_0_.ids.refs_4_), channel_id=1, source_target_pairs={{0,4},{4,0},{8,12},{12,8},{1,5},{5,1},{9,13},{13,9},{2,6},{6,2},{1... | collective-permute-start | bytes 196616 | tf_op jit(solution)/shard_map/ppermute | solution.py:356
  4.4 1.5 %collective-permute-start.2 = (s32[64,256]{1,0:T(8,128)S(1)}, s32[64,256]{1,0:T(8,128)S(1)}, u32[]{:S(2)}, u32[]{:S(2)}) collective-permute-start(s32[64,256]{1,0:T(8,128)S(1)} %shard_map.123.after.refs_0_.ids.refs_4_), channel_id=1, source_target_pairs={{0,2},{2,0},{1,3},{3,1},{4,6},{6,4},{5,7},{7,5},{8,10},{10,8},{9,1... | collective-permute-start | bytes 196616 | tf_op jit(solution)/shard_map/ppermute | solution.py:356
  6.6 0.9 %shard_map.124 = (bf16[17,64,128]{2,1,0:T(8,128)(2,1)S(1)}, bf16[17,64,128]{2,1,0:T(8,128)(2,1)S(1)}, f32[16,128]{1,0:T(8,128)S(1)}, f32[16,128]{1,0:T(8,128)S(1...) custom-call(s32[1]{0:T(128)S(6)} %copy.13.count, s32[288]{0:T(512)S(1)} %copy-done.11, s32[288]{0:T(512)S(1)} %copy-done.12, ...), custom_call_target="tpu_custom_call" | custom-call | flops 603979776 | bytes 9437184 | tf_op jit(solution)/shard_map/pallas_call | solution.py:24
  7.6 0.0 copy-start.2
  7.6 2.7 %collective-permute-start.1 = (s32[64,256]{1,0:T(8,128)S(1)}, s32[64,256]{1,0:T(8,128)S(1)}, u32[]{:S(2)}, u32[]{:S(2)}) collective-permute-start(s32[64,256]{1,0:T(8,128)S(1)} %shard_map.126), channel_id=1, source_target_pairs={{0,8},{4,12},{8,0},{12,4},{1,9},{5,13},{9,1},{13,5},{2,10},{6,14},... | collective-permute-start | bytes 196616 | tf_op jit(solution)/shard_map/ppermute | solution.py:356
  10.3 1.7 %shard_map.125.refs_0_.mine = f32[16,64,128]{2,1,0:T(8,128)S(1)} custom-call(s32[4,384]{1,0:T(4,128)S(1)} %get-tuple-element.29.order, bf16[288,128,128]{2,1,0:T(8,128)(2,1)S(1)} %copy-done, bf16[17,64,128]{2,1,0:T(8,128)(2,1)S(1)} %get-tuple-element.34.source, s32[64,256]{1,0:T(8,128)S(1)} %shard_map.123.after.refs_0_.ids.refs_4_), custom_call_target="tpu_custom_call" | custom-call | flops 603979776 | bytes 9437184 | tf_op jit(solution)/shard_map/pallas_call | solution.py:24
  12.0 0.1 collective-permute-start.4
  12.0 0.0 collective-permute-done.2.refs_3_.refs_1_
  12.1 1.5 %collective-permute-done.1.refs_2_.refs_6_ = s32[64,256]{1,0:T(8,128)S(1)} collective-permute-done((s32[64,256]{1,0:T(8,128)S(1)}, s32[64,256]{1,0:T(8,128)S(1)}, u32[]{:S(2)}, u32[]{:S(2)}) %collective-permute-start.1) | collective-permute-done | bytes 65568 | tf_op jit(solution)/shard_map/ppermute | solution.py:356
  13.5 2.6 %shard_map.127.mine = f32[16,64,128]{2,1,0:T(8,128)S(1)} custom-call(s32[4,384]{1,0:T(4,128)S(1)} %get-tuple-element.32.order, bf16[288,128,128]{2,1,0:T(8,128)(2,1)S(1)} %copy-done, bf16[17,64,128]{2,1,0:T(8,128)(2,1)S(1)} %get-tuple-element.33.source, f32[16,64,128]{2,1,0:T(8,128)S(1)} %shard_map.125.refs_0_.mine, ...), custom_call_target="tpu_custom_call" | custom-call | flops 603979776 | bytes 9437184 | tf_op jit(solution)/shard_map/pallas_call | solution.py:24
  16.2 0.1 collective-permute-start.3
  16.3 0.0 collective-permute-done.4.other
  16.3 1.2 %shard_map.128 = (f32[64,256]{1,0:T(8,128)S(1)}, f32[64,256]{1,0:T(8,128)S(1)}, f32[64,256]{1,0:T(8,128)S(1)}, f32[64,256]{1,0:T(8,128)S(1)}) custom-call(f32[16,64,128]{2,1,0:T(8,128)S(1)} %shard_map.125.refs_0_.mine, f32[16,64,128]{2,1,0:T(8,128)S(1)} %collective-permute-done.4.other, f32[16,128]{1,0:T(8,128)S(1)} %get-tuple-element.31.scale.target_scale.source_scale, ...), custom_call_target="tpu_custom_call" | custom-call | flops 805306368 | bytes 1048576 | tf_op jit(solution)/shard_map/pallas_call | solution.py:24
  17.5 1.6 %collective-permute-start.6 = (f32[64,256]{1,0:T(8,128)S(1)}, f32[64,256]{1,0:T(8,128)S(1)}, u32[]{:S(2)}, u32[]{:S(2)}) collective-permute-start(f32[64,256]{1,0:T(8,128)S(1)} %get-tuple-element.39), channel_id=1, source_target_pairs={{0,8},{4,12},{8,0},{12,4},{1,9},{5,13},{9,1},{13,5},{2,10},{6,14},... | collective-permute-start | bytes 196616 | tf_op jit(solution)/shard_map/ppermute | solution.py:356
  19.1 1.6 %collective-permute-start.7 = (f32[64,256]{1,0:T(8,128)S(1)}, f32[64,256]{1,0:T(8,128)S(1)}, u32[]{:S(2)}, u32[]{:S(2)}) collective-permute-start(f32[64,256]{1,0:T(8,128)S(1)} %get-tuple-element.40), channel_id=1, source_target_pairs={{0,12},{4,8},{8,4},{12,0},{1,13},{5,9},{9,5},{13,1},{2,14},{6,10},... | collective-permute-start | bytes 196616 | tf_op jit(solution)/shard_map/ppermute | solution.py:356
  20.7 0.5 collective-permute-start.8
  21.2 0.6 shard_map.129
  21.8 1.9 %collective-permute-start.5 = (f32[64,256]{1,0:T(8,128)S(1)}, f32[64,256]{1,0:T(8,128)S(1)}, u32[]{:S(2)}, u32[]{:S(2)}) collective-permute-start(f32[64,256]{1,0:T(8,128)S(1)} %get-tuple-element.37), channel_id=1, source_target_pairs={{0,2},{2,0},{1,3},{3,1},{4,6},{6,4},{5,7},{7,5},{8,10},{10,8},{9,1... | collective-permute-start | bytes 196616 | tf_op jit(solution)/shard_map/ppermute | solution.py:356
  23.7 0.5 shard_map.130
  24.2 1.9 %collective-permute-done.6.refs_4_ = f32[64,256]{1,0:T(8,128)S(1)} collective-permute-done((f32[64,256]{1,0:T(8,128)S(1)}, f32[64,256]{1,0:T(8,128)S(1)}, u32[]{:S(2)}, u32[]{:S(2)}) %collective-permute-start.6) | collective-permute-done | bytes 65568 | tf_op jit(solution)/shard_map/ppermute | solution.py:356
  26.2 0.0 collective-permute-done.7.refs_5_
  26.2 1.0 %collective-permute-done.8.refs_6_ = f32[64,256]{1,0:T(8,128)S(1)} collective-permute-done((f32[64,256]{1,0:T(8,128)S(1)}, f32[64,256]{1,0:T(8,128)S(1)}, u32[]{:S(2)}, u32[]{:S(2)}) %collective-permute-start.8) | collective-permute-done | bytes 65568 | tf_op jit(solution)/shard_map/ppermute | solution.py:356
  27.2 0.1 shard_map.131
  27.2 0.5 collective-permute-start.11
  27.7 1.2 %collective-permute-start.10 = (f32[72,256]{1,0:T(8,128)S(1)}, f32[72,256]{1,0:T(8,128)S(1)}, u32[]{:S(2)}, u32[]{:S(2)}) collective-permute-start(f32[72,256]{1,0:T(8,128)S(1)} %get-tuple-element.43.refs_0_), channel_id=1, source_target_pairs={{0,2},{2,0},{1,3},{3,1},{4,6},{6,4},{5,7},{7,5},{8,10},{10,8},{9,1... | collective-permute-start | bytes 221192 | tf_op jit(solution)/shard_map/ppermute | solution.py:356
  29.0 0.2 collective-permute-start.9
  29.2 1.6 %collective-permute-start.14 = (f32[64,256]{1,0:T(8,128)S(1)}, f32[64,256]{1,0:T(8,128)S(1)}, u32[]{:S(2)}, u32[]{:S(2)}) collective-permute-start(f32[64,256]{1,0:T(8,128)S(1)} %get-tuple-element.46.refs_0_), channel_id=1, source_target_pairs={{0,8},{4,12},{8,0},{12,4},{1,9},{5,13},{9,1},{13,5},{2,10},{6,14},... | collective-permute-start | bytes 196616 | tf_op jit(solution)/shard_map/ppermute | solution.py:356
  30.7 1.4 %collective-permute-start.13 = (f32[64,256]{1,0:T(8,128)S(1)}, f32[64,256]{1,0:T(8,128)S(1)}, u32[]{:S(2)}, u32[]{:S(2)}) collective-permute-start(f32[64,256]{1,0:T(8,128)S(1)} %get-tuple-element.46.refs_0_), channel_id=1, source_target_pairs={{0,12},{4,8},{8,4},{12,0},{1,13},{5,9},{9,5},{13,1},{2,14},{6,10},... | collective-permute-start | bytes 196616 | tf_op jit(solution)/shard_map/ppermute | solution.py:356
  32.2 0.5 collective-permute-start.12
  32.7 0.8 %collective-permute-done.10.refs_2_ = f32[72,256]{1,0:T(8,128)S(1)} collective-permute-done((f32[72,256]{1,0:T(8,128)S(1)}, f32[72,256]{1,0:T(8,128)S(1)}, u32[]{:S(2)}, u32[]{:S(2)}) %collective-permute-start.10) | collective-permute-done | bytes 73760 | tf_op jit(solution)/shard_map/ppermute | solution.py:356
  33.5 3.2 %shard_map.132 = (f32[16,64,128]{2,1,0:T(8,128)S(1)}, f32[16,32,128]{2,1,0:T(8,128)S(1)}, f32[16,32,128]{2,1,0:T(8,128)S(1)}) custom-call(s32[4,384]{1,0:T(4,128)S(1)} %get-tuple-element.29.order, f32[16,128]{1,0:T(8,128)S(1)} %get-tuple-element.30.scale.source_scale.target_scale, f32[16,128]{1,0:T(8,128)S(1)} %get-tuple-element.31.scale.target_scale.source_scale, ...), custom_call_target="tpu_custom_call" | custom-call | flops 603979776 | bytes 9437184 | tf_op jit(solution)/shard_map/pallas_call | solution.py:24
  36.7 0.3 collective-permute-start.16
  37.0 0.5 collective-permute-done.14.refs_3_
  37.5 0.0 collective-permute-done.13.refs_2_
  37.6 1.0 %collective-permute-done.12.refs_1_ = f32[64,256]{1,0:T(8,128)S(1)} collective-permute-done((f32[64,256]{1,0:T(8,128)S(1)}, f32[64,256]{1,0:T(8,128)S(1)}, u32[]{:S(2)}, u32[]{:S(2)}) %collective-permute-start.12) | collective-permute-done | bytes 65568 | tf_op jit(solution)/shard_map/ppermute | solution.py:356
  38.6 1.5 %shard_map.133.after.mine = f32[16,64,128]{2,1,0:T(8,128)S(1)} custom-call(f32[16,32,128]{2,1,0:T(8,128)S(1)} %get-tuple-element.45.after, f32[64,256]{1,0:T(8,128)S(1)} %get-tuple-element.46.refs_0_, f32[64,256]{1,0:T(8,128)S(1)} %collective-permute-done.12.refs_1_, f32[64,256]{1,0:T(8,128)S(1)} %collective-permute-done.13.refs_2_, ...), custom_call_target="tpu_custom_call" | custom-call | flops 99999997952 | tf_op jit(solution)/shard_map/pallas_call | solution.py:24
  40.1 0.1 collective-permute-start.15
  40.2 0.0 collective-permute-done.16.received
  40.2 0.0 copy-start.1
  40.2 0.0 copy-start.3
  40.2 1.6 %collective-permute-start.17 = (f32[4,32,128]{2,1,0:T(8,128)S(1)}, f32[4,32,128]{2,1,0:T(8,128)S(1)}, u32[]{:S(2)}, u32[]{:S(2)}) collective-permute-start(f32[4,32,128]{2,1,0:T(8,128)S(1)} %get-tuple-element.50), channel_id=1, source_target_pairs={{0,8},{4,12},{8,0},{12,4},{1,9},{5,13},{9,1},{13,5},{2,10},{6,14},... | collective-permute-start | bytes 196616 | tf_op jit(solution)/shard_map/ppermute | solution.py:356
  41.9 1.5 %collective-permute-start.18 = (f32[4,32,128]{2,1,0:T(8,128)S(1)}, f32[4,32,128]{2,1,0:T(8,128)S(1)}, u32[]{:S(2)}, u32[]{:S(2)}) collective-permute-start(f32[4,32,128]{2,1,0:T(8,128)S(1)} %get-tuple-element.51), channel_id=1, source_target_pairs={{0,12},{4,8},{8,4},{12,0},{1,13},{5,9},{9,5},{13,1},{2,14},{6,10},... | collective-permute-start | bytes 196616 | tf_op jit(solution)/shard_map/ppermute | solution.py:356
  43.3 0.5 collective-permute-start.19
  43.8 0.1 copy-done.1
  43.9 2.7 %shard_map.135 = (f32[16,64,128]{2,1,0:T(8,128)S(1)}, f32[16,64,128]{2,1,0:T(8,128)S(1)}) custom-call(s32[4,384]{1,0:T(4,128)S(1)} %copy-done.3, f32[16,64,128]{2,1,0:T(8,128)S(1)} %shard_map.133.after.mine, f32[16,64,128]{2,1,0:T(8,128)S(1)} %collective-permute-done.15.other, f32[16,128]{1,0:T(8,128)S(1)} %get-tuple-element.31.scale.target_scale.source_scale, ...), custom_call_target="tpu_custom_call" | custom-call | flops 603979776 | bytes 9437184 | tf_op jit(solution)/shard_map/pallas_call | solution.py:24
  46.6 2.1 %collective-permute-done.17.refs_1_ = f32[4,32,128]{2,1,0:T(8,128)S(1)} collective-permute-done((f32[4,32,128]{2,1,0:T(8,128)S(1)}, f32[4,32,128]{2,1,0:T(8,128)S(1)}, u32[]{:S(2)}, u32[]{:S(2)}) %collective-permute-start.17) | collective-permute-done | bytes 65568 | tf_op jit(solution)/shard_map/ppermute | solution.py:356
  48.7 0.0 collective-permute-done.18.refs_2_
  48.7 1.1 %collective-permute-done.19.refs_3_ = f32[4,32,128]{2,1,0:T(8,128)S(1)} collective-permute-done((f32[4,32,128]{2,1,0:T(8,128)S(1)}, f32[4,32,128]{2,1,0:T(8,128)S(1)}, u32[]{:S(2)}, u32[]{:S(2)}) %collective-permute-start.19) | collective-permute-done | bytes 65568 | tf_op jit(solution)/shard_map/ppermute | solution.py:356
  49.9 0.1 collective-permute-start.20
  50.0 1.5 %collective-permute-start.23 = (f32[1,4,32,128]{3,2,1,0:T(8,128)S(1)}, f32[1,4,32,128]{3,2,1,0:T(8,128)S(1)}, u32[]{:S(2)}, u32[]{:S(2)}) collective-permute-start(f32[1,4,32,128]{3,2,1,0:T(8,128)S(1)} %shard_map.136.after.first), channel_id=1, source_target_pairs={{0,8},{4,12},{8,0},{12,4},{1,9},{5,13},{9,1},{13,5},{2,10},{6,14},... | collective-permute-start | bytes 196616 | tf_op jit(solution)/shard_map/ppermute | solution.py:356
  51.5 0.0 collective-permute-done.20.refs_1_
  51.5 1.6 %collective-permute-start.21 = (f32[16,32,128]{2,1,0:T(8,128)S(1)}, f32[16,32,128]{2,1,0:T(8,128)S(1)}, u32[]{:S(2)}, u32[]{:S(2)}) collective-permute-start(f32[16,32,128]{2,1,0:T(8,128)S(1)} %shard_map.138.refs_0_), channel_id=1, source_target_pairs={{0,2},{2,0},{1,3},{3,1},{4,6},{6,4},{5,7},{7,5},{8,10},{10,8},{9,1... | collective-permute-start | bytes 786440 | tf_op jit(solution)/shard_map/ppermute | solution.py:356
  53.1 3.7 %collective-permute-done.23.second = f32[1,4,32,128]{3,2,1,0:T(8,128)S(1)} collective-permute-done((f32[1,4,32,128]{3,2,1,0:T(8,128)S(1)}, f32[1,4,32,128]{3,2,1,0:T(8,128)S(1)}, u32[]{:S(2)}, u32[]{:S(2)}) %collective-permute-start.23) | collective-permute-done | bytes 65568 | tf_op jit(solution)/shard_map/ppermute | solution.py:356
  56.8 0.1 collective-permute-start.24
  56.9 3.1 %collective-permute-done.21.refs_1_ = f32[16,32,128]{2,1,0:T(8,128)S(1)} collective-permute-done((f32[16,32,128]{2,1,0:T(8,128)S(1)}, f32[16,32,128]{2,1,0:T(8,128)S(1)}, u32[]{:S(2)}, u32[]{:S(2)}) %collective-permute-start.21) | collective-permute-done | bytes 262176 | tf_op jit(solution)/shard_map/ppermute | solution.py:356
  60.0 0.1 collective-permute-start.22
  60.1 0.5 collective-permute-start.25
  60.6 1.6 %collective-permute-done.24.refs_1_ = f32[2,4,32,128]{3,2,1,0:T(8,128)S(1)} collective-permute-done((f32[2,4,32,128]{3,2,1,0:T(8,128)S(1)}, f32[2,4,32,128]{3,2,1,0:T(8,128)S(1)}, u32[]{:S(2)}, u32[]{:S(2)}) %collective-permute-start.24) | collective-permute-done | bytes 131104 | tf_op jit(solution)/shard_map/ppermute | solution.py:356
  62.2 1.3 %collective-permute-done.26.refs_3_ = f32[2,4,32,128]{3,2,1,0:T(8,128)S(1)} collective-permute-done((f32[2,4,32,128]{3,2,1,0:T(8,128)S(1)}, f32[2,4,32,128]{3,2,1,0:T(8,128)S(1)}, u32[]{:S(2)}, u32[]{:S(2)}) %collective-permute-start.26) | collective-permute-done | bytes 131104 | tf_op jit(solution)/shard_map/ppermute | solution.py:356
  63.6 1.1 %shard_map.141 = (f32[64,2048]{1,0:T(8,128)}, f32[64,2048]{1,0:T(8,128)}) custom-call(f32[16,64,128]{2,1,0:T(8,128)S(1)} %get-tuple-element.44.user_half_grad, f32[16,32,128]{2,1,0:T(8,128)S(1)} %shard_map.139.user_mine, f32[16,32,128]{2,1,0:T(8,128)S(1)} %collective-permute-done.22.user_other, f32[16,64,128]{2,1,0:T(8,128)S(1)} %get-tuple-element.55.item_half_grad, ...), custom_call_target="tpu_custom_call" | custom-call | bytes 3145728 | tf_op jit(solution)/shard_map/pallas_call | solution.py:24
  (36 shorter events, 0.2 us)
Async XLA Ops:
  0.6 0.7 %copy-start.6 = (s32[256]{0:T(256)S(1)}, s32[256]{0:T(256)}, u32[]{:S(2)}) copy-start(s32[256]{0:T(256)} %param.21) | copy-start | bytes 3076
  0.6 0.7 %copy-start.5 = (s32[256]{0:T(256)S(1)}, s32[256]{0:T(256)}, u32[]{:S(2)}) copy-start(s32[256]{0:T(256)} %param.20) | copy-start | bytes 3076
  0.7 0.7 %copy-start.4 = (s32[256]{0:T(256)S(1)}, s32[256]{0:T(256)}, u32[]{:S(2)}) copy-start(s32[256]{0:T(256)} %param.19) | copy-start | bytes 3076
  0.7 5.9 %copy-start.8 = (bf16[64,2048]{1,0:T(8,128)(2,1)S(1)}, bf16[64,2048]{1,0:T(8,128)(2,1)}, u32[]{:S(2)}) copy-start(bf16[64,2048]{1,0:T(8,128)(2,1)} %item_emb.3) | copy-start | bytes 786436
  0.7 5.9 %copy-start.7 = (bf16[64,2048]{1,0:T(8,128)(2,1)S(1)}, bf16[64,2048]{1,0:T(8,128)(2,1)}, u32[]{:S(2)}) copy-start(bf16[64,2048]{1,0:T(8,128)(2,1)} %user_emb.3) | copy-start | bytes 786436
  0.7 5.9 %copy-start.12 = (s32[288]{0:T(512)S(1)}, s32[288]{0:T(512)}, u32[]{:S(2)}) copy-start(s32[288]{0:T(512)} %columns.1) | copy-start | bytes 3460
  0.7 5.9 %copy-start.11 = (s32[288]{0:T(512)S(1)}, s32[288]{0:T(512)}, u32[]{:S(2)}) copy-start(s32[288]{0:T(512)} %rows.1) | copy-start | bytes 3460
  0.7 5.9 %copy-start.10 = (s32[2048]{0:T(1024)S(1)}, s32[2048]{0:T(1024)}, u32[]{:S(2)}) copy-start(s32[2048]{0:T(1024)} %param.14) | copy-start | bytes 24580
  0.7 5.9 %copy-start.9 = (s32[2048]{0:T(1024)S(1)}, s32[2048]{0:T(1024)}, u32[]{:S(2)}) copy-start(s32[2048]{0:T(1024)} %param.13) | copy-start | bytes 24580
  0.7 9.5 %copy-start = (bf16[288,128,128]{2,1,0:T(8,128)(2,1)S(1)}, bf16[288,128,128]{2,1,0:T(8,128)(2,1)}, u32[]{:S(2)}) copy-start(bf16[288,128,128]{2,1,0:T(8,128)(2,1)} %vals.7) | copy-start | bytes 28311556
  1.4 6.2 %collective-permute-start = (s32[64,256]{1,0:T(8,128)S(1)}, s32[64,256]{1,0:T(8,128)S(1)}, u32[]{:S(2)}, u32[]{:S(2)}) collective-permute-start(s32[64,256]{1,0:T(8,128)S(1)} %shard_map.123.after.refs_0_.ids.refs_4_), channel_id=1, source_target_pairs={{0,4},{4,0},{8,12},{12,8},{1,5},{5,1},{9,13},{13,9},{2,6},{6,2},{1... | collective-permute-start | bytes 196616 | tf_op jit(solution)/shard_map/ppermute | solution.py:356
  4.4 7.6 %collective-permute-start.2 = (s32[64,256]{1,0:T(8,128)S(1)}, s32[64,256]{1,0:T(8,128)S(1)}, u32[]{:S(2)}, u32[]{:S(2)}) collective-permute-start(s32[64,256]{1,0:T(8,128)S(1)} %shard_map.123.after.refs_0_.ids.refs_4_), channel_id=1, source_target_pairs={{0,2},{2,0},{1,3},{3,1},{4,6},{6,4},{5,7},{7,5},{8,10},{10,8},{9,1... | collective-permute-start | bytes 196616 | tf_op jit(solution)/shard_map/ppermute | solution.py:356
  7.6 8.6 %copy-start.2 = (s32[4,384]{1,0:T(4,128)}, s32[4,384]{1,0:T(4,128)S(1)}, u32[]{:S(2)}) copy-start(s32[4,384]{1,0:T(4,128)S(1)} %get-tuple-element.32.order) | copy-start | bytes 18436
  7.6 5.9 %collective-permute-start.1 = (s32[64,256]{1,0:T(8,128)S(1)}, s32[64,256]{1,0:T(8,128)S(1)}, u32[]{:S(2)}, u32[]{:S(2)}) collective-permute-start(s32[64,256]{1,0:T(8,128)S(1)} %shard_map.126), channel_id=1, source_target_pairs={{0,8},{4,12},{8,0},{12,4},{1,9},{5,13},{9,1},{13,5},{2,10},{6,14},... | collective-permute-start | bytes 196616 | tf_op jit(solution)/shard_map/ppermute | solution.py:356
  12.0 4.3 %collective-permute-start.4 = (f32[16,64,128]{2,1,0:T(8,128)S(1)}, f32[16,64,128]{2,1,0:T(8,128)S(1)}, u32[]{:S(2)}, u32[]{:S(2)}) collective-permute-start(f32[16,64,128]{2,1,0:T(8,128)S(1)} %shard_map.125.refs_0_.mine), channel_id=1, source_target_pairs={{0,1},{1,0},{2,3},{3,2},{4,5},{5,4},{6,7},{7,6},{8,9},{9,8},{10,11... | collective-permute-start | bytes 1572872 | tf_op jit(solution)/shard_map/ppermute | solution.py:356
  16.2 5.0 %collective-permute-start.3 = (f32[16,64,128]{2,1,0:T(8,128)S(1)}, f32[16,64,128]{2,1,0:T(8,128)S(1)}, u32[]{:S(2)}, u32[]{:S(2)}) collective-permute-start(f32[16,64,128]{2,1,0:T(8,128)S(1)} %shard_map.127.mine), channel_id=1, source_target_pairs={{0,1},{1,0},{2,3},{3,2},{4,5},{5,4},{6,7},{7,6},{8,9},{9,8},{10,11... | collective-permute-start | bytes 1572872 | tf_op jit(solution)/shard_map/ppermute | solution.py:356
  17.5 8.7 %collective-permute-start.6 = (f32[64,256]{1,0:T(8,128)S(1)}, f32[64,256]{1,0:T(8,128)S(1)}, u32[]{:S(2)}, u32[]{:S(2)}) collective-permute-start(f32[64,256]{1,0:T(8,128)S(1)} %get-tuple-element.39), channel_id=1, source_target_pairs={{0,8},{4,12},{8,0},{12,4},{1,9},{5,13},{9,1},{13,5},{2,10},{6,14},... | collective-permute-start | bytes 196616 | tf_op jit(solution)/shard_map/ppermute | solution.py:356
  19.1 7.1 %collective-permute-start.7 = (f32[64,256]{1,0:T(8,128)S(1)}, f32[64,256]{1,0:T(8,128)S(1)}, u32[]{:S(2)}, u32[]{:S(2)}) collective-permute-start(f32[64,256]{1,0:T(8,128)S(1)} %get-tuple-element.40), channel_id=1, source_target_pairs={{0,12},{4,8},{8,4},{12,0},{1,13},{5,9},{9,5},{13,1},{2,14},{6,10},... | collective-permute-start | bytes 196616 | tf_op jit(solution)/shard_map/ppermute | solution.py:356
  20.7 6.5 %collective-permute-start.8 = (f32[64,256]{1,0:T(8,128)S(1)}, f32[64,256]{1,0:T(8,128)S(1)}, u32[]{:S(2)}, u32[]{:S(2)}) collective-permute-start(f32[64,256]{1,0:T(8,128)S(1)} %get-tuple-element.41), channel_id=1, source_target_pairs={{0,4},{4,0},{8,12},{12,8},{1,5},{5,1},{9,13},{13,9},{2,6},{6,2},{1... | collective-permute-start | bytes 196616 | tf_op jit(solution)/shard_map/ppermute | solution.py:356
  21.8 5.4 %collective-permute-start.5 = (f32[64,256]{1,0:T(8,128)S(1)}, f32[64,256]{1,0:T(8,128)S(1)}, u32[]{:S(2)}, u32[]{:S(2)}) collective-permute-start(f32[64,256]{1,0:T(8,128)S(1)} %get-tuple-element.37), channel_id=1, source_target_pairs={{0,2},{2,0},{1,3},{3,1},{4,6},{6,4},{5,7},{7,5},{8,10},{10,8},{9,1... | collective-permute-start | bytes 196616 | tf_op jit(solution)/shard_map/ppermute | solution.py:356
  27.2 4.9 %collective-permute-start.11 = (f32[72,256]{1,0:T(8,128)S(1)}, f32[72,256]{1,0:T(8,128)S(1)}, u32[]{:S(2)}, u32[]{:S(2)}) collective-permute-start(f32[72,256]{1,0:T(8,128)S(1)} %get-tuple-element.43.refs_0_), channel_id=1, source_target_pairs={{0,3},{1,2},{2,1},{3,0},{4,7},{5,6},{6,5},{7,4},{8,11},{9,10},{10,... | collective-permute-start | bytes 221192 | tf_op jit(solution)/shard_map/ppermute | solution.py:455
  27.7 5.7 %collective-permute-start.10 = (f32[72,256]{1,0:T(8,128)S(1)}, f32[72,256]{1,0:T(8,128)S(1)}, u32[]{:S(2)}, u32[]{:S(2)}) collective-permute-start(f32[72,256]{1,0:T(8,128)S(1)} %get-tuple-element.43.refs_0_), channel_id=1, source_target_pairs={{0,2},{2,0},{1,3},{3,1},{4,6},{6,4},{5,7},{7,5},{8,10},{10,8},{9,1... | collective-permute-start | bytes 221192 | tf_op jit(solution)/shard_map/ppermute | solution.py:356
  29.0 4.5 %collective-permute-start.9 = (f32[72,256]{1,0:T(8,128)S(1)}, f32[72,256]{1,0:T(8,128)S(1)}, u32[]{:S(2)}, u32[]{:S(2)}) collective-permute-start(f32[72,256]{1,0:T(8,128)S(1)} %get-tuple-element.43.refs_0_), channel_id=1, source_target_pairs={{0,1},{1,0},{2,3},{3,2},{4,5},{5,4},{6,7},{7,6},{8,9},{9,8},{10,11... | collective-permute-start | bytes 221192 | tf_op jit(solution)/shard_map/ppermute | solution.py:356
  29.2 8.4 %collective-permute-start.14 = (f32[64,256]{1,0:T(8,128)S(1)}, f32[64,256]{1,0:T(8,128)S(1)}, u32[]{:S(2)}, u32[]{:S(2)}) collective-permute-start(f32[64,256]{1,0:T(8,128)S(1)} %get-tuple-element.46.refs_0_), channel_id=1, source_target_pairs={{0,8},{4,12},{8,0},{12,4},{1,9},{5,13},{9,1},{13,5},{2,10},{6,14},... | collective-permute-start | bytes 196616 | tf_op jit(solution)/shard_map/ppermute | solution.py:356
  30.7 6.8 %collective-permute-start.13 = (f32[64,256]{1,0:T(8,128)S(1)}, f32[64,256]{1,0:T(8,128)S(1)}, u32[]{:S(2)}, u32[]{:S(2)}) collective-permute-start(f32[64,256]{1,0:T(8,128)S(1)} %get-tuple-element.46.refs_0_), channel_id=1, source_target_pairs={{0,12},{4,8},{8,4},{12,0},{1,13},{5,9},{9,5},{13,1},{2,14},{6,10},... | collective-permute-start | bytes 196616 | tf_op jit(solution)/shard_map/ppermute | solution.py:356
  32.2 6.4 %collective-permute-start.12 = (f32[64,256]{1,0:T(8,128)S(1)}, f32[64,256]{1,0:T(8,128)S(1)}, u32[]{:S(2)}, u32[]{:S(2)}) collective-permute-start(f32[64,256]{1,0:T(8,128)S(1)} %get-tuple-element.46.refs_0_), channel_id=1, source_target_pairs={{0,4},{4,0},{8,12},{12,8},{1,5},{5,1},{9,13},{13,9},{2,6},{6,2},{1... | collective-permute-start | bytes 196616 | tf_op jit(solution)/shard_map/ppermute | solution.py:356
  36.7 3.5 %collective-permute-start.16 = (f32[16,32,128]{2,1,0:T(8,128)S(1)}, f32[16,32,128]{2,1,0:T(8,128)S(1)}, u32[]{:S(2)}, u32[]{:S(2)}) collective-permute-start(f32[16,32,128]{2,1,0:T(8,128)S(1)} %get-tuple-element.45.after), channel_id=1, source_target_pairs={{0,1},{1,0},{2,3},{3,2},{4,5},{5,4},{6,7},{7,6},{8,9},{9,8},{10,11... | collective-permute-start | bytes 786440 | tf_op jit(solution)/shard_map/ppermute | solution.py:356
  40.1 3.7 %collective-permute-start.15 = (f32[16,64,128]{2,1,0:T(8,128)S(1)}, f32[16,64,128]{2,1,0:T(8,128)S(1)}, u32[]{:S(2)}, u32[]{:S(2)}) collective-permute-start(f32[16,64,128]{2,1,0:T(8,128)S(1)} %shard_map.133.after.mine), channel_id=1, source_target_pairs={{0,1},{1,0},{2,3},{3,2},{4,5},{5,4},{6,7},{7,6},{8,9},{9,8},{10,11... | collective-permute-start | bytes 1572872 | tf_op jit(solution)/shard_map/ppermute | solution.py:356
  40.2 3.7 %copy-start.1 = (bf16[288,128,128]{2,1,0:T(8,128)(2,1)S(1)}, bf16[288,128,128]{2,1,0:T(8,128)(2,1)}, u32[]{:S(2)}) copy-start(bf16[288,128,128]{2,1,0:T(8,128)(2,1)} %vals.7) | copy-start | bytes 28311556
  40.2 3.7 %copy-start.3 = (s32[4,384]{1,0:T(4,128)S(1)}, s32[4,384]{1,0:T(4,128)}, u32[]{:S(2)}) copy-start(s32[4,384]{1,0:T(4,128)} %copy-done.2) | copy-start | bytes 18436
  40.2 8.5 %collective-permute-start.17 = (f32[4,32,128]{2,1,0:T(8,128)S(1)}, f32[4,32,128]{2,1,0:T(8,128)S(1)}, u32[]{:S(2)}, u32[]{:S(2)}) collective-permute-start(f32[4,32,128]{2,1,0:T(8,128)S(1)} %get-tuple-element.50), channel_id=1, source_target_pairs={{0,8},{4,12},{8,0},{12,4},{1,9},{5,13},{9,1},{13,5},{2,10},{6,14},... | collective-permute-start | bytes 196616 | tf_op jit(solution)/shard_map/ppermute | solution.py:356
  41.9 6.8 %collective-permute-start.18 = (f32[4,32,128]{2,1,0:T(8,128)S(1)}, f32[4,32,128]{2,1,0:T(8,128)S(1)}, u32[]{:S(2)}, u32[]{:S(2)}) collective-permute-start(f32[4,32,128]{2,1,0:T(8,128)S(1)} %get-tuple-element.51), channel_id=1, source_target_pairs={{0,12},{4,8},{8,4},{12,0},{1,13},{5,9},{9,5},{13,1},{2,14},{6,10},... | collective-permute-start | bytes 196616 | tf_op jit(solution)/shard_map/ppermute | solution.py:356
  43.3 6.5 %collective-permute-start.19 = (f32[4,32,128]{2,1,0:T(8,128)S(1)}, f32[4,32,128]{2,1,0:T(8,128)S(1)}, u32[]{:S(2)}, u32[]{:S(2)}) collective-permute-start(f32[4,32,128]{2,1,0:T(8,128)S(1)} %get-tuple-element.52), channel_id=1, source_target_pairs={{0,4},{4,0},{8,12},{12,8},{1,5},{5,1},{9,13},{13,9},{2,6},{6,2},{1... | collective-permute-start | bytes 196616 | tf_op jit(solution)/shard_map/ppermute | solution.py:356
  49.9 1.6 %collective-permute-start.20 = (f32[16,32,128]{2,1,0:T(8,128)S(1)}, f32[16,32,128]{2,1,0:T(8,128)S(1)}, u32[]{:S(2)}, u32[]{:S(2)}) collective-permute-start(f32[16,32,128]{2,1,0:T(8,128)S(1)} %get-tuple-element.54), channel_id=1, source_target_pairs={{0,1},{1,0},{2,3},{3,2},{4,5},{5,4},{6,7},{7,6},{8,9},{9,8},{10,11... | collective-permute-start | bytes 786440 | tf_op jit(solution)/shard_map/ppermute | solution.py:356
  50.0 6.8 %collective-permute-start.23 = (f32[1,4,32,128]{3,2,1,0:T(8,128)S(1)}, f32[1,4,32,128]{3,2,1,0:T(8,128)S(1)}, u32[]{:S(2)}, u32[]{:S(2)}) collective-permute-start(f32[1,4,32,128]{3,2,1,0:T(8,128)S(1)} %shard_map.136.after.first), channel_id=1, source_target_pairs={{0,8},{4,12},{8,0},{12,4},{1,9},{5,13},{9,1},{13,5},{2,10},{6,14},... | collective-permute-start | bytes 196616 | tf_op jit(solution)/shard_map/ppermute | solution.py:356
  51.5 8.4 %collective-permute-start.21 = (f32[16,32,128]{2,1,0:T(8,128)S(1)}, f32[16,32,128]{2,1,0:T(8,128)S(1)}, u32[]{:S(2)}, u32[]{:S(2)}) collective-permute-start(f32[16,32,128]{2,1,0:T(8,128)S(1)} %shard_map.138.refs_0_), channel_id=1, source_target_pairs={{0,2},{2,0},{1,3},{3,1},{4,6},{6,4},{5,7},{7,5},{8,10},{10,8},{9,1... | collective-permute-start | bytes 786440 | tf_op jit(solution)/shard_map/ppermute | solution.py:356
  56.8 5.4 %collective-permute-start.24 = (f32[2,4,32,128]{3,2,1,0:T(8,128)S(1)}, f32[2,4,32,128]{3,2,1,0:T(8,128)S(1)}, u32[]{:S(2)}, u32[]{:S(2)}) collective-permute-start(f32[2,4,32,128]{3,2,1,0:T(8,128)S(1)} %shard_map.140.refs_0_), channel_id=1, source_target_pairs={{0,4},{4,0},{8,12},{12,8},{1,5},{5,1},{9,13},{13,9},{2,6},{6,2},{1... | collective-permute-start | bytes 393224 | tf_op jit(solution)/shard_map/ppermute | solution.py:356
  60.0 3.6 %collective-permute-start.22 = (f32[16,32,128]{2,1,0:T(8,128)S(1)}, f32[16,32,128]{2,1,0:T(8,128)S(1)}, u32[]{:S(2)}, u32[]{:S(2)}) collective-permute-start(f32[16,32,128]{2,1,0:T(8,128)S(1)} %shard_map.139.user_mine), channel_id=1, source_target_pairs={{0,1},{1,0},{2,3},{3,2},{4,5},{5,4},{6,7},{7,6},{8,9},{9,8},{10,11... | collective-permute-start | bytes 786440 | tf_op jit(solution)/shard_map/ppermute | solution.py:356
  60.1 2.1 %collective-permute-start.25 = (f32[2,4,32,128]{3,2,1,0:T(8,128)S(1)}, f32[2,4,32,128]{3,2,1,0:T(8,128)S(1)}, u32[]{:S(2)}, u32[]{:S(2)}) collective-permute-start(f32[2,4,32,128]{3,2,1,0:T(8,128)S(1)} %shard_map.140.refs_0_), channel_id=1, source_target_pairs={{0,1},{1,0},{2,3},{3,2},{4,5},{5,4},{6,7},{7,6},{8,9},{9,8},{10,11... | collective-permute-start | bytes 393224 | tf_op jit(solution)/shard_map/ppermute | solution.py:356
  62.2 1.3 %collective-permute-start.26 = (f32[2,4,32,128]{3,2,1,0:T(8,128)S(1)}, f32[2,4,32,128]{3,2,1,0:T(8,128)S(1)}, u32[]{:S(2)}, u32[]{:S(2)}) collective-permute-start(f32[2,4,32,128]{3,2,1,0:T(8,128)S(1)} %collective-permute-done.24.refs_1_), channel_id=1, source_target_pairs={{0,1},{1,0},{2,3},{3,2},{4,5},{5,4},{6,7},{7,6},{8,9},{9,8},{10,11... | collective-permute-start | bytes 393224 | tf_op jit(solution)/shard_map/ppermute | solution.py:356

commit v3 on v1

--- a/solution.py
+++ b/solution.py
@@ -10,7 +10,7 @@
 F32 = jnp.float32
 BF16 = jnp.bfloat16
 PACK = 4
-GROUP = 4
+GROUP = 8
 ID_ROWS = 64
 HEAVY = 10 ** 11
 
@@ -30,6 +30,17 @@
         cost_estimate=pl.CostEstimate(flops=flops, bytes_accessed=moved, transcendentals=0),
         compiler_params=pltpu.CompilerParams(vmem_limit_bytes=room * 1024 * 1024),
     )(*ins)
+
+
+def hold(values, *after, flops=0):
+    return pl.pallas_call(
+        nothing,
+        out_shape=jax.ShapeDtypeStruct(values.shape, values.dtype),
+        in_specs=[ANY] * (1 + len(after)),
+        out_specs=ANY,
+        input_output_aliases={0: 0},
+        cost_estimate=pl.CostEstimate(flops=flops, bytes_accessed=0, transcendentals=0),
+    )(values, *after)
 
 
 def shape(*dims):
@@ -279,7 +290,7 @@
 
 
 def second_users(order, mine, other, source_scale, target_scale, vals, after,
-                 half_grad, out, source, total):
+                 half_grad, keep, send, source, total):
     blocks, width, size = mine.shape
     for block in range(blocks):
         grad = mine[block] + other[block]
@@ -287,12 +298,13 @@
         source[block] = (source_scale[block:block + 1, :] * grad * 0.5).astype(BF16)
     source[blocks] = jnp.zeros((width, size), BF16)
     multiply_blocks(order, vals, source, total, True)
-    for block in range(out.shape[0]):
-        out[block] = target_scale[block:block + 1, :] * total[block]
-
-
-def halves_after(total, after, keep, send):
+    for block in range(total.shape[0]):
+        total[block] = target_scale[block:block + 1, :] * total[block]
     halves(total, keep, send)
+
+
+def nothing(*refs):
+    pass
 
 
 def add_deal(offsets, keep, received, after, *outs):
@@ -308,8 +320,8 @@
     refs[-1][...] = add_all(refs[:-1])
 
 
-def sum_after(after, *refs):
-    sum_parts(*refs)
+def sum_after(count, *refs):
+    sum_parts(*refs[count:])
 
 
 def pack(*refs):
@@ -337,9 +349,7 @@
 def finish_items(offsets, half_grad, mine, other, out):
     me = lax.axis_index("rep")
     place = lax.axis_index("user")
-    blocks, width, size = half_grad.shape
-    half = width // 2
-    per = blocks // len(offsets)
+    _, per, half, size = mine.shape
     for index, offset in enumerate(offsets):
         there = (place ^ offset) * per
         for block in range(per):
@@ -474,8 +484,9 @@
         functools.partial(add_deal, [0, *met]), [shape(per, half, size)] * users,
         (item_keep, swap(item_send), item_grad), [VMEM, VMEM, ANY], (), HEAVY,
     )
-    item_half_grad, user_back = call(
-        second_users, [shape(item_blocks, width, size), shape(user_blocks, width, size)],
+    item_half_grad, user_keep, user_send = call(
+        second_users,
+        [shape(item_blocks, width, size)] + [shape(user_blocks, half, size)] * 2,
         (user_order, item_grad, swap(item_grad), item_scale, user_scale, block_vals, dealt[0]),
         [SMEM] + [VMEM] * 5 + [ANY],
         [pltpu.VMEM((item_blocks + 1, width, size), BF16),
@@ -483,27 +494,30 @@
         product_flops, product_bytes,
     )
     parts = [dealt[0]] + [swap(part, "user", users, o) for part, o in zip(dealt[1:], met)]
-    item_own = call(sum_after, shape(per, half, size), (user_back, *parts),
+    item_own = call(functools.partial(sum_after, 1), shape(per, half, size), (user_keep, *parts),
                     [ANY] + [VMEM] * users,
                moved=4 * (users + 1) * per * half * size)
-    item_mine = call(pack, shape(users, per, half, size),
-                     (item_own, *[swap(item_own, "user", users, o) for o in back]),
+    item_mine, step = {0: item_own}, users // 2
+    while step >= 1:
+        for offset, part in list(item_mine.items()):
+            item_mine[offset ^ step] = swap(part, "user", users, step)
+        if step > 1:
+            item_mine[step] = hold(item_mine[step], flops=HEAVY)
+        step //= 2
+    item_places = list(item_mine)
+    item_mine = call(pack, shape(users, per, half, size), tuple(item_mine.values()),
                      [VMEM] * users, moved=8 * item_blocks * half * size)
-    item_other = swap(item_mine)
-
-    user_keep, user_send = call(
-        halves_after, [shape(user_blocks, half, size)] * 2, (user_back, item_own), [VMEM, ANY],
-        moved=8 * user_blocks * width * size,
-    )
+    user_send = hold(user_send, item_own)
+
     own = call(sum_parts, shape(user_blocks, half, size), (user_keep, swap(user_send)),
                [VMEM, VMEM], moved=12 * user_blocks * half * size)
-    mine = call(sum_parts, shape(user_blocks, half, size),
-                (own, *[swap(own, "item", items, o) for o in range(1, items)]),
-                [VMEM] * items, moved=12 * user_blocks * half * size)
+    mine = call(functools.partial(sum_after, 1), shape(user_blocks, half, size),
+                (item_mine, own, *[swap(own, "item", items, o) for o in range(1, items)]),
+                [ANY] + [VMEM] * items, moved=12 * user_blocks * half * size)
     return call(
-        functools.partial(finish, [0, *back]),
+        functools.partial(finish, item_places),
         (shape(width, user_blocks * size), shape(width, item_blocks * size)),
-        (user_half_grad, mine, swap(mine), item_half_grad, item_mine, item_other),
+        (user_half_grad, mine, swap(mine), item_half_grad, item_mine, swap(item_mine)),
         [VMEM] * 6, moved=12 * (user_blocks + item_blocks) * width * size,
     )
 

time: 67.1 us -> 67.7 us (level)
  starting transfers between devices: 34.7 us -> 25.8 us
  Pallas kernels: 13.8 us -> 18.4 us
  waiting for transfers between devices: 16.1 us -> 18.7 us
  local copies, waits for them, and re-layouts: 0.72 us -> 2.83 us
    ppermute x26, starting transfers between devices: 33.3 us -> 25.8 us  [swap(): return lax.ppermute(values, axis, [(i, i ^ offset) for i in range(peers)])]
    pallas_call x20 -> x19, Pallas kernels: 13.8 us -> 18.4 us  [call(): pl.pallas_call(kernel, out_shape=outs, in_specs=specs, out_specs=jax.tree...]
    ppermute x26, waiting for transfers between devices: 16.1 us -> 18.7 us  [swap(): return lax.ppermute(values, axis, [(i, i ^ offset) for i in range(peers)])]
    unnamed x26 -> x36, local copies, waits for them, and re-layouts: 0.72 us -> 2.83 us
    ppermute x1, starting transfers between devices: 1.49 us -> 0.07 us  [on_device(): lax.ppermute(pieces, ('item', 'rep'), [(i, i ^ 2 * offset + 1) for i in r...]
  transfers between devices with their start and end apart: 27 -> 27, of which waited for: 11 -> 11; matrix products, arithmetic and copies ran while one was open for 0% -> 0% of each run, Pallas kernels for 19% -> 26%
where the time goes in v3:
time: 67.7 us; the launch traced here: 67.4 us
  starting transfers between devices  25.8 us (38%)
  waiting for transfers between devices  18.7 us (28%)
  Pallas kernels  18.4 us (27%)
  local copies, waits for them, and re-layouts  2.83 us (4%)
  between operations  1.67 us (2%)
    ppermute x26, starting transfers between devices, swap(): return lax.ppermute(values, axis, [(i, i ^ offset) for i in range(peers)])  25.8 us
    ppermute x26, waiting for transfers between devices, swap(): return lax.ppermute(values, axis, [(i, i ^ offset) for i in range(peers)])  18.7 us
    pallas_call x19, Pallas kernels, call(): pl.pallas_call(kernel, out_shape=outs, in_specs=specs, out_specs=jax.tree...  18.4 us
    unnamed x36, local copies, waits for them, and re-layouts  2.83 us
  transfers between devices with their start and end apart: 27, of which 11 were waited for; matrix products, arithmetic and copies ran while one was open for 0% of the time, Pallas kernels for 26%

profile of v3, /device:TPU:0, one launch (start us, length us, event | category | flops | bytes accessed | tf_op | source)
XLA Modules:
  0.0 67.4 jit_solution(2140731238666435179)
XLA Ops:
  0.7 0.0 copy-start
  0.7 0.6 copy-done.11
  1.3 0.0 copy-done.10
  1.3 0.0 copy-done.9
  1.4 3.1 %collective-permute-start = (s32[64,256]{1,0:T(8,128)S(1)}, s32[64,256]{1,0:T(8,128)S(1)}, u32[]{:S(2)}, u32[]{:S(2)}) collective-permute-start(s32[64,256]{1,0:T(8,128)S(1)} %shard_map.123.after.refs_0_.ids.refs_4_), channel_id=1, source_target_pairs={{0,4},{4,0},{8,12},{12,8},{1,5},{5,1},{9,13},{13,9},{2,6},{6,2},{1... | collective-permute-start | bytes 196616 | tf_op jit(solution)/shard_map/ppermute | solution.py:363
  4.4 1.5 %collective-permute-start.2 = (s32[64,256]{1,0:T(8,128)S(1)}, s32[64,256]{1,0:T(8,128)S(1)}, u32[]{:S(2)}, u32[]{:S(2)}) collective-permute-start(s32[64,256]{1,0:T(8,128)S(1)} %shard_map.123.after.refs_0_.ids.refs_4_), channel_id=1, source_target_pairs={{0,2},{2,0},{1,3},{3,1},{4,6},{6,4},{5,7},{7,5},{8,10},{10,8},{9,1... | collective-permute-start | bytes 196616 | tf_op jit(solution)/shard_map/ppermute | solution.py:363
  6.6 0.9 %shard_map.124 = (bf16[17,64,128]{2,1,0:T(8,128)(2,1)S(1)}, bf16[17,64,128]{2,1,0:T(8,128)(2,1)S(1)}, f32[16,128]{1,0:T(8,128)S(1)}, f32[16,128]{1,0:T(8,128)S(1...) custom-call(s32[1]{0:T(128)S(6)} %copy.17.count, s32[288]{0:T(512)S(1)} %copy-done.16, s32[288]{0:T(512)S(1)} %copy-done.17, ...), custom_call_target="tpu_custom_call" | custom-call | flops 603979776 | bytes 9437184 | tf_op jit(solution)/shard_map/pallas_call | solution.py:24
  7.6 0.0 copy-start.7
  7.6 0.0 collective-permute-done.refs_1_.refs_5_
  7.6 2.7 %collective-permute-start.1 = (s32[64,256]{1,0:T(8,128)S(1)}, s32[64,256]{1,0:T(8,128)S(1)}, u32[]{:S(2)}, u32[]{:S(2)}) collective-permute-start(s32[64,256]{1,0:T(8,128)S(1)} %shard_map.126), channel_id=1, source_target_pairs={{0,8},{4,12},{8,0},{12,4},{1,9},{5,13},{9,1},{13,5},{2,10},{6,14},... | collective-permute-start | bytes 196616 | tf_op jit(solution)/shard_map/ppermute | solution.py:363
  10.3 2.2 %shard_map.125.refs_0_.mine = f32[16,64,128]{2,1,0:T(8,128)S(1)} custom-call(s32[4,384]{1,0:T(4,128)S(1)} %get-tuple-element.28.order, bf16[288,128,128]{2,1,0:T(8,128)(2,1)S(1)} %copy-done, bf16[17,64,128]{2,1,0:T(8,128)(2,1)S(1)} %get-tuple-element.33.source, s32[64,256]{1,0:T(8,128)S(1)} %shard_map.123.after.refs_0_.ids.refs_4_), custom_call_target="tpu_custom_call" | custom-call | flops 603979776 | bytes 9437184 | tf_op jit(solution)/shard_map/pallas_call | solution.py:24
  12.5 0.1 collective-permute-start.4
  12.6 0.0 collective-permute-done.2.refs_3_.refs_1_
  12.6 0.9 %collective-permute-done.1.refs_2_.refs_6_ = s32[64,256]{1,0:T(8,128)S(1)} collective-permute-done((s32[64,256]{1,0:T(8,128)S(1)}, s32[64,256]{1,0:T(8,128)S(1)}, u32[]{:S(2)}, u32[]{:S(2)}) %collective-permute-start.1) | collective-permute-done | bytes 65568 | tf_op jit(solution)/shard_map/ppermute | solution.py:363
  13.5 3.1 %shard_map.127.mine = f32[16,64,128]{2,1,0:T(8,128)S(1)} custom-call(s32[4,384]{1,0:T(4,128)S(1)} %get-tuple-element.31.order, bf16[288,128,128]{2,1,0:T(8,128)(2,1)S(1)} %copy-done, bf16[17,64,128]{2,1,0:T(8,128)(2,1)S(1)} %get-tuple-element.32.source, f32[16,64,128]{2,1,0:T(8,128)S(1)} %shard_map.125.refs_0_.mine, ...), custom_call_target="tpu_custom_call" | custom-call | flops 603979776 | bytes 9437184 | tf_op jit(solution)/shard_map/pallas_call | solution.py:24
  16.7 1.3 %collective-permute-start.3 = (f32[16,64,128]{2,1,0:T(8,128)S(1)}, f32[16,64,128]{2,1,0:T(8,128)S(1)}, u32[]{:S(2)}, u32[]{:S(2)}) collective-permute-start(f32[16,64,128]{2,1,0:T(8,128)S(1)} %shard_map.127.mine), channel_id=1, source_target_pairs={{0,1},{1,0},{2,3},{3,2},{4,5},{5,4},{6,7},{7,6},{8,9},{9,8},{10,11... | collective-permute-start | bytes 1572872 | tf_op jit(solution)/shard_map/ppermute | solution.py:363
  18.0 1.2 %shard_map.128 = (f32[64,256]{1,0:T(8,128)S(1)}, f32[64,256]{1,0:T(8,128)S(1)}, f32[64,256]{1,0:T(8,128)S(1)}, f32[64,256]{1,0:T(8,128)S(1)}) custom-call(f32[16,64,128]{2,1,0:T(8,128)S(1)} %shard_map.125.refs_0_.mine, f32[16,64,128]{2,1,0:T(8,128)S(1)} %collective-permute-done.4.other, f32[16,128]{1,0:T(8,128)S(1)} %get-tuple-element.30.scale.target_scale.source_scale, ...), custom_call_target="tpu_custom_call" | custom-call | flops 805306368 | bytes 1048576 | tf_op jit(solution)/shard_map/pallas_call | solution.py:24
  19.2 0.1 collective-permute-start.6
  19.3 2.0 %collective-permute-start.7 = (f32[64,256]{1,0:T(8,128)S(1)}, f32[64,256]{1,0:T(8,128)S(1)}, u32[]{:S(2)}, u32[]{:S(2)}) collective-permute-start(f32[64,256]{1,0:T(8,128)S(1)} %get-tuple-element.39), channel_id=1, source_target_pairs={{0,12},{4,8},{8,4},{12,0},{1,13},{5,9},{9,5},{13,1},{2,14},{6,10},... | collective-permute-start | bytes 196616 | tf_op jit(solution)/shard_map/ppermute | solution.py:363
  21.2 1.5 %collective-permute-start.8 = (f32[64,256]{1,0:T(8,128)S(1)}, f32[64,256]{1,0:T(8,128)S(1)}, u32[]{:S(2)}, u32[]{:S(2)}) collective-permute-start(f32[64,256]{1,0:T(8,128)S(1)} %get-tuple-element.40), channel_id=1, source_target_pairs={{0,4},{4,0},{8,12},{12,8},{1,5},{5,1},{9,13},{13,9},{2,6},{6,2},{1... | collective-permute-start | bytes 196616 | tf_op jit(solution)/shard_map/ppermute | solution.py:363
  22.8 0.6 shard_map.129
  23.4 0.1 collective-permute-start.5
  23.4 0.5 shard_map.130
  23.9 2.9 %collective-permute-done.6.refs_4_ = f32[64,256]{1,0:T(8,128)S(1)} collective-permute-done((f32[64,256]{1,0:T(8,128)S(1)}, f32[64,256]{1,0:T(8,128)S(1)}, u32[]{:S(2)}, u32[]{:S(2)}) %collective-permute-start.6) | collective-permute-done | bytes 65568 | tf_op jit(solution)/shard_map/ppermute | solution.py:363
  26.8 1.3 %collective-permute-done.8.refs_6_ = f32[64,256]{1,0:T(8,128)S(1)} collective-permute-done((f32[64,256]{1,0:T(8,128)S(1)}, f32[64,256]{1,0:T(8,128)S(1)}, u32[]{:S(2)}, u32[]{:S(2)}) %collective-permute-start.8) | collective-permute-done | bytes 65568 | tf_op jit(solution)/shard_map/ppermute | solution.py:363
  28.1 0.1 shard_map.131
  28.2 0.1 collective-permute-start.11
  28.3 1.7 %collective-permute-start.10 = (f32[72,256]{1,0:T(8,128)S(1)}, f32[72,256]{1,0:T(8,128)S(1)}, u32[]{:S(2)}, u32[]{:S(2)}) collective-permute-start(f32[72,256]{1,0:T(8,128)S(1)} %get-tuple-element.42.refs_0_), channel_id=1, source_target_pairs={{0,2},{2,0},{1,3},{3,1},{4,6},{6,4},{5,7},{7,5},{8,10},{10,8},{9,1... | collective-permute-start | bytes 221192 | tf_op jit(solution)/shard_map/ppermute | solution.py:363
  29.9 0.2 collective-permute-start.9
  30.1 0.8 %collective-permute-start.14 = (f32[64,256]{1,0:T(8,128)S(1)}, f32[64,256]{1,0:T(8,128)S(1)}, u32[]{:S(2)}, u32[]{:S(2)}) collective-permute-start(f32[64,256]{1,0:T(8,128)S(1)} %get-tuple-element.45.refs_0_), channel_id=1, source_target_pairs={{0,8},{4,12},{8,0},{12,4},{1,9},{5,13},{9,1},{13,5},{2,10},{6,14},... | collective-permute-start | bytes 196616 | tf_op jit(solution)/shard_map/ppermute | solution.py:363
  30.9 2.2 %collective-permute-start.13 = (f32[64,256]{1,0:T(8,128)S(1)}, f32[64,256]{1,0:T(8,128)S(1)}, u32[]{:S(2)}, u32[]{:S(2)}) collective-permute-start(f32[64,256]{1,0:T(8,128)S(1)} %get-tuple-element.45.refs_0_), channel_id=1, source_target_pairs={{0,12},{4,8},{8,4},{12,0},{1,13},{5,9},{9,5},{13,1},{2,14},{6,10},... | collective-permute-start | bytes 196616 | tf_op jit(solution)/shard_map/ppermute | solution.py:363
  33.1 0.5 collective-permute-start.12
  33.6 0.8 %collective-permute-done.10.refs_2_ = f32[72,256]{1,0:T(8,128)S(1)} collective-permute-done((f32[72,256]{1,0:T(8,128)S(1)}, f32[72,256]{1,0:T(8,128)S(1)}, u32[]{:S(2)}, u32[]{:S(2)}) %collective-permute-start.10) | collective-permute-done | bytes 73760 | tf_op jit(solution)/shard_map/ppermute | solution.py:363
  34.4 3.7 %shard_map.132 = (f32[16,64,128]{2,1,0:T(8,128)S(1)}, f32[16,32,128]{2,1,0:T(8,128)S(1)}, f32[16,32,128]{2,1,0:T(8,128)S(1)}) custom-call(s32[4,384]{1,0:T(4,128)S(1)} %get-tuple-element.28.order, f32[16,128]{1,0:T(8,128)S(1)} %get-tuple-element.29.scale.source_scale.target_scale, f32[16,128]{1,0:T(8,128)S(1)} %get-tuple-element.30.scale.target_scale.source_scale, ...), custom_call_target="tpu_custom_call" | custom-call | flops 603979776 | bytes 9437184 | tf_op jit(solution)/shard_map/pallas_call | solution.py:24
  38.1 0.9 %collective-permute-start.16 = (f32[16,32,128]{2,1,0:T(8,128)S(1)}, f32[16,32,128]{2,1,0:T(8,128)S(1)}, u32[]{:S(2)}, u32[]{:S(2)}) collective-permute-start(f32[16,32,128]{2,1,0:T(8,128)S(1)} %get-tuple-element.44.after), channel_id=1, source_target_pairs={{0,1},{1,0},{2,3},{3,2},{4,5},{5,4},{6,7},{7,6},{8,9},{9,8},{10,11... | collective-permute-start | bytes 786440 | tf_op jit(solution)/shard_map/ppermute | solution.py:363
  39.0 0.5 collective-permute-done.12.refs_1_
  39.5 1.5 %shard_map.133.after.mine = f32[16,64,128]{2,1,0:T(8,128)S(1)} custom-call(f32[16,32,128]{2,1,0:T(8,128)S(1)} %get-tuple-element.44.after, f32[64,256]{1,0:T(8,128)S(1)} %get-tuple-element.45.refs_0_, f32[64,256]{1,0:T(8,128)S(1)} %collective-permute-done.12.refs_1_, f32[64,256]{1,0:T(8,128)S(1)} %collective-permute-done.13.refs_2_, ...), custom_call_target="tpu_custom_call" | custom-call | flops 99999997952 | tf_op jit(solution)/shard_map/pallas_call | solution.py:24
  41.0 0.1 collective-permute-start.15
  41.1 0.0 copy-start.1
  41.1 0.0 copy-start.8
  41.2 0.9 %collective-permute-start.17 = (f32[4,32,128]{2,1,0:T(8,128)S(1)}, f32[4,32,128]{2,1,0:T(8,128)S(1)}, u32[]{:S(2)}, u32[]{:S(2)}) collective-permute-start(f32[4,32,128]{2,1,0:T(8,128)S(1)} %get-tuple-element.49), channel_id=1, source_target_pairs={{0,8},{4,12},{8,0},{12,4},{1,9},{5,13},{9,1},{13,5},{2,10},{6,14},... | collective-permute-start | bytes 196616 | tf_op jit(solution)/shard_map/ppermute | solution.py:363
  42.1 2.2 %collective-permute-start.18 = (f32[4,32,128]{2,1,0:T(8,128)S(1)}, f32[4,32,128]{2,1,0:T(8,128)S(1)}, u32[]{:S(2)}, u32[]{:S(2)}) collective-permute-start(f32[4,32,128]{2,1,0:T(8,128)S(1)} %get-tuple-element.50), channel_id=1, source_target_pairs={{0,12},{4,8},{8,4},{12,0},{1,13},{5,9},{9,5},{13,1},{2,14},{6,10},... | collective-permute-start | bytes 196616 | tf_op jit(solution)/shard_map/ppermute | solution.py:363
  44.3 0.5 collective-permute-start.19
  44.7 0.1 copy-done.1
  44.8 3.3 %shard_map.135 = (f32[16,64,128]{2,1,0:T(8,128)S(1)}, f32[16,32,128]{2,1,0:T(8,128)S(1)}, f32[16,32,128]{2,1,0:T(8,128)S(1)}) custom-call(s32[4,384]{1,0:T(4,128)S(1)} %copy-done.8, f32[16,64,128]{2,1,0:T(8,128)S(1)} %shard_map.133.after.mine, f32[16,64,128]{2,1,0:T(8,128)S(1)} %collective-permute-done.15.other, ...), custom_call_target="tpu_custom_call" | custom-call | flops 603979776 | bytes 9437184 | tf_op jit(solution)/shard_map/pallas_call | solution.py:24
  48.1 0.0 copy-start.4
  48.1 1.5 %collective-permute-done.17.refs_2_ = f32[4,32,128]{2,1,0:T(8,128)S(1)} collective-permute-done((f32[4,32,128]{2,1,0:T(8,128)S(1)}, f32[4,32,128]{2,1,0:T(8,128)S(1)}, u32[]{:S(2)}, u32[]{:S(2)}) %collective-permute-start.17) | collective-permute-done | bytes 65568 | tf_op jit(solution)/shard_map/ppermute | solution.py:363
  49.6 1.1 %collective-permute-done.19.refs_4_ = f32[4,32,128]{2,1,0:T(8,128)S(1)} collective-permute-done((f32[4,32,128]{2,1,0:T(8,128)S(1)}, f32[4,32,128]{2,1,0:T(8,128)S(1)}, u32[]{:S(2)}, u32[]{:S(2)}) %collective-permute-start.19) | collective-permute-done | bytes 65568 | tf_op jit(solution)/shard_map/ppermute | solution.py:363
  50.8 0.0 copy-start.2
  50.8 0.6 copy-done.2
  51.4 0.2 collective-permute-start.23
  51.6 0.7 %collective-permute-start.20 = (f32[4,32,128]{2,1,0:T(8,128)}, f32[4,32,128]{2,1,0:T(8,128)S(1)}, u32[]{:S(2)}, u32[]{:S(2)}) collective-permute-start(f32[4,32,128]{2,1,0:T(8,128)} %copy-done.2), channel_id=1, source_target_pairs={{0,8},{4,12},{8,0},{12,4},{1,9},{5,13},{9,1},{13,5},{2,10},{6,14},... | collective-permute-start | bytes 196616 | tf_op jit(solution)/shard_map/ppermute | solution.py:363
  52.3 1.4 %collective-permute-start.21 = (f32[4,32,128]{2,1,0:T(8,128)}, f32[4,32,128]{2,1,0:T(8,128)S(1)}, u32[]{:S(2)}, u32[]{:S(2)}) collective-permute-start(f32[4,32,128]{2,1,0:T(8,128)} %copy-done.2), channel_id=1, source_target_pairs={{0,4},{4,0},{8,12},{12,8},{1,5},{5,1},{9,13},{13,9},{2,6},{6,2},{1... | collective-permute-start | bytes 196616 | tf_op jit(solution)/shard_map/ppermute | solution.py:363
  53.7 0.0 copy-start.3
  53.7 0.8 %collective-permute-start.24 = (f32[16,32,128]{2,1,0:T(8,128)S(1)}, f32[16,32,128]{2,1,0:T(8,128)S(1)}, u32[]{:S(2)}, u32[]{:S(2)}) collective-permute-start(f32[16,32,128]{2,1,0:T(8,128)S(1)} %shard_map.140.refs_1_), channel_id=1, source_target_pairs={{0,2},{2,0},{1,3},{3,1},{4,6},{6,4},{5,7},{7,5},{8,10},{10,8},{9,1... | collective-permute-start | bytes 786440 | tf_op jit(solution)/shard_map/ppermute | solution.py:363
  54.5 3.9 %collective-permute-done.20.refs_0_ = f32[4,32,128]{2,1,0:T(8,128)S(1)} collective-permute-done((f32[4,32,128]{2,1,0:T(8,128)}, f32[4,32,128]{2,1,0:T(8,128)S(1)}, u32[]{:S(2)}, u32[]{:S(2)}) %collective-permute-start.20) | collective-permute-done | bytes 65568 | tf_op jit(solution)/shard_map/ppermute | solution.py:363
  58.4 0.6 copy-done.5
  59.0 4.5 %collective-permute-done.22.refs_3_ = f32[4,32,128]{2,1,0:T(8,128)S(1)} collective-permute-done((f32[4,32,128]{2,1,0:T(8,128)}, f32[4,32,128]{2,1,0:T(8,128)S(1)}, u32[]{:S(2)}, u32[]{:S(2)}) %collective-permute-start.22) | collective-permute-done | bytes 65568 | tf_op jit(solution)/shard_map/ppermute | solution.py:363
  63.5 0.8 %copy-done.6 = f32[4,32,128]{2,1,0:T(8,128)S(1)} copy-done((f32[4,32,128]{2,1,0:T(8,128)S(1)}, f32[4,32,128]{2,1,0:T(8,128)}, u32[]{:S(2)}) %copy-start.6) | copy-done | bytes 65560
  64.4 0.1 collective-permute-start.26
  64.5 0.5 collective-permute-start.25
  65.1 0.9 %collective-permute-done.26.item_other = f32[4,4,32,128]{3,2,1,0:T(8,128)S(1)} collective-permute-done((f32[4,4,32,128]{3,2,1,0:T(8,128)S(1)}, f32[4,4,32,128]{3,2,1,0:T(8,128)S(1)}, u32[]{:S(2)}, u32[]{:S(2)}) %collective-permute-start.26) | collective-permute-done | bytes 262176 | tf_op jit(solution)/shard_map/ppermute | solution.py:363
  66.0 0.4 collective-permute-done.25.user_other
  66.4 1.1 %shard_map.142 = (f32[64,2048]{1,0:T(8,128)}, f32[64,2048]{1,0:T(8,128)}) custom-call(f32[16,64,128]{2,1,0:T(8,128)S(1)} %get-tuple-element.43.user_half_grad, f32[16,32,128]{2,1,0:T(8,128)S(1)} %shard_map.141.user_mine, f32[16,32,128]{2,1,0:T(8,128)S(1)} %collective-permute-done.25.user_other, f32[16,64,128]{2,1,0:T(8,128)S(1)} %get-tuple-element.53.item_half_grad, ...), custom_call_target="tpu_custom_call" | custom-call | bytes 3145728 | tf_op jit(solution)/shard_map/pallas_call | solution.py:24
  (47 shorter events, 0.2 us)
Async XLA Ops:
  0.6 0.7 %copy-start.11 = (s32[256]{0:T(256)S(1)}, s32[256]{0:T(256)}, u32[]{:S(2)}) copy-start(s32[256]{0:T(256)} %param.21) | copy-start | bytes 3076
  0.6 0.7 %copy-start.10 = (s32[256]{0:T(256)S(1)}, s32[256]{0:T(256)}, u32[]{:S(2)}) copy-start(s32[256]{0:T(256)} %param.20) | copy-start | bytes 3076
  0.7 0.7 %copy-start.9 = (s32[256]{0:T(256)S(1)}, s32[256]{0:T(256)}, u32[]{:S(2)}) copy-start(s32[256]{0:T(256)} %param.19) | copy-start | bytes 3076
  0.7 5.9 %copy-start.13 = (bf16[64,2048]{1,0:T(8,128)(2,1)S(1)}, bf16[64,2048]{1,0:T(8,128)(2,1)}, u32[]{:S(2)}) copy-start(bf16[64,2048]{1,0:T(8,128)(2,1)} %item_emb.3) | copy-start | bytes 786436
  0.7 5.9 %copy-start.12 = (bf16[64,2048]{1,0:T(8,128)(2,1)S(1)}, bf16[64,2048]{1,0:T(8,128)(2,1)}, u32[]{:S(2)}) copy-start(bf16[64,2048]{1,0:T(8,128)(2,1)} %user_emb.3) | copy-start | bytes 786436
  0.7 5.9 %copy-start.17 = (s32[288]{0:T(512)S(1)}, s32[288]{0:T(512)}, u32[]{:S(2)}) copy-start(s32[288]{0:T(512)} %columns.1) | copy-start | bytes 3460
  0.7 5.9 %copy-start.16 = (s32[288]{0:T(512)S(1)}, s32[288]{0:T(512)}, u32[]{:S(2)}) copy-start(s32[288]{0:T(512)} %rows.1) | copy-start | bytes 3460
  0.7 5.9 %copy-start.15 = (s32[2048]{0:T(1024)S(1)}, s32[2048]{0:T(1024)}, u32[]{:S(2)}) copy-start(s32[2048]{0:T(1024)} %param.14) | copy-start | bytes 24580
  0.7 5.9 %copy-start.14 = (s32[2048]{0:T(1024)S(1)}, s32[2048]{0:T(1024)}, u32[]{:S(2)}) copy-start(s32[2048]{0:T(1024)} %param.13) | copy-start | bytes 24580
  0.7 9.5 %copy-start = (bf16[288,128,128]{2,1,0:T(8,128)(2,1)S(1)}, bf16[288,128,128]{2,1,0:T(8,128)(2,1)}, u32[]{:S(2)}) copy-start(bf16[288,128,128]{2,1,0:T(8,128)(2,1)} %vals.7) | copy-start | bytes 28311556
  1.4 6.2 %collective-permute-start = (s32[64,256]{1,0:T(8,128)S(1)}, s32[64,256]{1,0:T(8,128)S(1)}, u32[]{:S(2)}, u32[]{:S(2)}) collective-permute-start(s32[64,256]{1,0:T(8,128)S(1)} %shard_map.123.after.refs_0_.ids.refs_4_), channel_id=1, source_target_pairs={{0,4},{4,0},{8,12},{12,8},{1,5},{5,1},{9,13},{13,9},{2,6},{6,2},{1... | collective-permute-start | bytes 196616 | tf_op jit(solution)/shard_map/ppermute | solution.py:363
  4.4 8.2 %collective-permute-start.2 = (s32[64,256]{1,0:T(8,128)S(1)}, s32[64,256]{1,0:T(8,128)S(1)}, u32[]{:S(2)}, u32[]{:S(2)}) collective-permute-start(s32[64,256]{1,0:T(8,128)S(1)} %shard_map.123.after.refs_0_.ids.refs_4_), channel_id=1, source_target_pairs={{0,2},{2,0},{1,3},{3,1},{4,6},{6,4},{5,7},{7,5},{8,10},{10,8},{9,1... | collective-permute-start | bytes 196616 | tf_op jit(solution)/shard_map/ppermute | solution.py:363
  7.6 9.1 %copy-start.7 = (s32[4,384]{1,0:T(4,128)}, s32[4,384]{1,0:T(4,128)S(1)}, u32[]{:S(2)}) copy-start(s32[4,384]{1,0:T(4,128)S(1)} %get-tuple-element.31.order) | copy-start | bytes 18436
  7.6 5.9 %collective-permute-start.1 = (s32[64,256]{1,0:T(8,128)S(1)}, s32[64,256]{1,0:T(8,128)S(1)}, u32[]{:S(2)}, u32[]{:S(2)}) collective-permute-start(s32[64,256]{1,0:T(8,128)S(1)} %shard_map.126), channel_id=1, source_target_pairs={{0,8},{4,12},{8,0},{12,4},{1,9},{5,13},{9,1},{13,5},{2,10},{6,14},... | collective-permute-start | bytes 196616 | tf_op jit(solution)/shard_map/ppermute | solution.py:363
  12.5 5.5 %collective-permute-start.4 = (f32[16,64,128]{2,1,0:T(8,128)S(1)}, f32[16,64,128]{2,1,0:T(8,128)S(1)}, u32[]{:S(2)}, u32[]{:S(2)}) collective-permute-start(f32[16,64,128]{2,1,0:T(8,128)S(1)} %shard_map.125.refs_0_.mine), channel_id=1, source_target_pairs={{0,1},{1,0},{2,3},{3,2},{4,5},{5,4},{6,7},{7,6},{8,9},{9,8},{10,11... | collective-permute-start | bytes 1572872 | tf_op jit(solution)/shard_map/ppermute | solution.py:363
  16.7 6.1 %collective-permute-start.3 = (f32[16,64,128]{2,1,0:T(8,128)S(1)}, f32[16,64,128]{2,1,0:T(8,128)S(1)}, u32[]{:S(2)}, u32[]{:S(2)}) collective-permute-start(f32[16,64,128]{2,1,0:T(8,128)S(1)} %shard_map.127.mine), channel_id=1, source_target_pairs={{0,1},{1,0},{2,3},{3,2},{4,5},{5,4},{6,7},{7,6},{8,9},{9,8},{10,11... | collective-permute-start | bytes 1572872 | tf_op jit(solution)/shard_map/ppermute | solution.py:363
  19.2 7.6 %collective-permute-start.6 = (f32[64,256]{1,0:T(8,128)S(1)}, f32[64,256]{1,0:T(8,128)S(1)}, u32[]{:S(2)}, u32[]{:S(2)}) collective-permute-start(f32[64,256]{1,0:T(8,128)S(1)} %get-tuple-element.38), channel_id=1, source_target_pairs={{0,8},{4,12},{8,0},{12,4},{1,9},{5,13},{9,1},{13,5},{2,10},{6,14},... | collective-permute-start | bytes 196616 | tf_op jit(solution)/shard_map/ppermute | solution.py:363
  19.3 7.6 %collective-permute-start.7 = (f32[64,256]{1,0:T(8,128)S(1)}, f32[64,256]{1,0:T(8,128)S(1)}, u32[]{:S(2)}, u32[]{:S(2)}) collective-permute-start(f32[64,256]{1,0:T(8,128)S(1)} %get-tuple-element.39), channel_id=1, source_target_pairs={{0,12},{4,8},{8,4},{12,0},{1,13},{5,9},{9,5},{13,1},{2,14},{6,10},... | collective-permute-start | bytes 196616 | tf_op jit(solution)/shard_map/ppermute | solution.py:363
  21.2 6.9 %collective-permute-start.8 = (f32[64,256]{1,0:T(8,128)S(1)}, f32[64,256]{1,0:T(8,128)S(1)}, u32[]{:S(2)}, u32[]{:S(2)}) collective-permute-start(f32[64,256]{1,0:T(8,128)S(1)} %get-tuple-element.40), channel_id=1, source_target_pairs={{0,4},{4,0},{8,12},{12,8},{1,5},{5,1},{9,13},{13,9},{2,6},{6,2},{1... | collective-permute-start | bytes 196616 | tf_op jit(solution)/shard_map/ppermute | solution.py:363
  23.4 4.8 %collective-permute-start.5 = (f32[64,256]{1,0:T(8,128)S(1)}, f32[64,256]{1,0:T(8,128)S(1)}, u32[]{:S(2)}, u32[]{:S(2)}) collective-permute-start(f32[64,256]{1,0:T(8,128)S(1)} %get-tuple-element.36), channel_id=1, source_target_pairs={{0,2},{2,0},{1,3},{3,1},{4,6},{6,4},{5,7},{7,5},{8,10},{10,8},{9,1... | collective-permute-start | bytes 196616 | tf_op jit(solution)/shard_map/ppermute | solution.py:363
  28.2 4.9 %collective-permute-start.11 = (f32[72,256]{1,0:T(8,128)S(1)}, f32[72,256]{1,0:T(8,128)S(1)}, u32[]{:S(2)}, u32[]{:S(2)}) collective-permute-start(f32[72,256]{1,0:T(8,128)S(1)} %get-tuple-element.42.refs_0_), channel_id=1, source_target_pairs={{0,3},{1,2},{2,1},{3,0},{4,7},{5,6},{6,5},{7,4},{8,11},{9,10},{10,... | collective-permute-start | bytes 221192 | tf_op jit(solution)/shard_map/ppermute | solution.py:462
  28.3 6.1 %collective-permute-start.10 = (f32[72,256]{1,0:T(8,128)S(1)}, f32[72,256]{1,0:T(8,128)S(1)}, u32[]{:S(2)}, u32[]{:S(2)}) collective-permute-start(f32[72,256]{1,0:T(8,128)S(1)} %get-tuple-element.42.refs_0_), channel_id=1, source_target_pairs={{0,2},{2,0},{1,3},{3,1},{4,6},{6,4},{5,7},{7,5},{8,10},{10,8},{9,1... | collective-permute-start | bytes 221192 | tf_op jit(solution)/shard_map/ppermute | solution.py:363
  29.9 4.5 %collective-permute-start.9 = (f32[72,256]{1,0:T(8,128)S(1)}, f32[72,256]{1,0:T(8,128)S(1)}, u32[]{:S(2)}, u32[]{:S(2)}) collective-permute-start(f32[72,256]{1,0:T(8,128)S(1)} %get-tuple-element.42.refs_0_), channel_id=1, source_target_pairs={{0,1},{1,0},{2,3},{3,2},{4,5},{5,4},{6,7},{7,6},{8,9},{9,8},{10,11... | collective-permute-start | bytes 221192 | tf_op jit(solution)/shard_map/ppermute | solution.py:363
  30.1 8.9 %collective-permute-start.14 = (f32[64,256]{1,0:T(8,128)S(1)}, f32[64,256]{1,0:T(8,128)S(1)}, u32[]{:S(2)}, u32[]{:S(2)}) collective-permute-start(f32[64,256]{1,0:T(8,128)S(1)} %get-tuple-element.45.refs_0_), channel_id=1, source_target_pairs={{0,8},{4,12},{8,0},{12,4},{1,9},{5,13},{9,1},{13,5},{2,10},{6,14},... | collective-permute-start | bytes 196616 | tf_op jit(solution)/shard_map/ppermute | solution.py:363
  30.9 8.1 %collective-permute-start.13 = (f32[64,256]{1,0:T(8,128)S(1)}, f32[64,256]{1,0:T(8,128)S(1)}, u32[]{:S(2)}, u32[]{:S(2)}) collective-permute-start(f32[64,256]{1,0:T(8,128)S(1)} %get-tuple-element.45.refs_0_), channel_id=1, source_target_pairs={{0,12},{4,8},{8,4},{12,0},{1,13},{5,9},{9,5},{13,1},{2,14},{6,10},... | collective-permute-start | bytes 196616 | tf_op jit(solution)/shard_map/ppermute | solution.py:363
  33.1 6.4 %collective-permute-start.12 = (f32[64,256]{1,0:T(8,128)S(1)}, f32[64,256]{1,0:T(8,128)S(1)}, u32[]{:S(2)}, u32[]{:S(2)}) collective-permute-start(f32[64,256]{1,0:T(8,128)S(1)} %get-tuple-element.45.refs_0_), channel_id=1, source_target_pairs={{0,4},{4,0},{8,12},{12,8},{1,5},{5,1},{9,13},{13,9},{2,6},{6,2},{1... | collective-permute-start | bytes 196616 | tf_op jit(solution)/shard_map/ppermute | solution.py:363
  38.1 3.0 %collective-permute-start.16 = (f32[16,32,128]{2,1,0:T(8,128)S(1)}, f32[16,32,128]{2,1,0:T(8,128)S(1)}, u32[]{:S(2)}, u32[]{:S(2)}) collective-permute-start(f32[16,32,128]{2,1,0:T(8,128)S(1)} %get-tuple-element.44.after), channel_id=1, source_target_pairs={{0,1},{1,0},{2,3},{3,2},{4,5},{5,4},{6,7},{7,6},{8,9},{9,8},{10,11... | collective-permute-start | bytes 786440 | tf_op jit(solution)/shard_map/ppermute | solution.py:363
  41.0 3.7 %collective-permute-start.15 = (f32[16,64,128]{2,1,0:T(8,128)S(1)}, f32[16,64,128]{2,1,0:T(8,128)S(1)}, u32[]{:S(2)}, u32[]{:S(2)}) collective-permute-start(f32[16,64,128]{2,1,0:T(8,128)S(1)} %shard_map.133.after.mine), channel_id=1, source_target_pairs={{0,1},{1,0},{2,3},{3,2},{4,5},{5,4},{6,7},{7,6},{8,9},{9,8},{10,11... | collective-permute-start | bytes 1572872 | tf_op jit(solution)/shard_map/ppermute | solution.py:363
  41.1 3.7 %copy-start.1 = (bf16[288,128,128]{2,1,0:T(8,128)(2,1)S(1)}, bf16[288,128,128]{2,1,0:T(8,128)(2,1)}, u32[]{:S(2)}) copy-start(bf16[288,128,128]{2,1,0:T(8,128)(2,1)} %vals.7) | copy-start | bytes 28311556
  41.1 3.7 %copy-start.8 = (s32[4,384]{1,0:T(4,128)S(1)}, s32[4,384]{1,0:T(4,128)}, u32[]{:S(2)}) copy-start(s32[4,384]{1,0:T(4,128)} %copy-done.7) | copy-start | bytes 18436
  41.2 8.5 %collective-permute-start.17 = (f32[4,32,128]{2,1,0:T(8,128)S(1)}, f32[4,32,128]{2,1,0:T(8,128)S(1)}, u32[]{:S(2)}, u32[]{:S(2)}) collective-permute-start(f32[4,32,128]{2,1,0:T(8,128)S(1)} %get-tuple-element.49), channel_id=1, source_target_pairs={{0,8},{4,12},{8,0},{12,4},{1,9},{5,13},{9,1},{13,5},{2,10},{6,14},... | collective-permute-start | bytes 196616 | tf_op jit(solution)/shard_map/ppermute | solution.py:363
  42.1 7.6 %collective-permute-start.18 = (f32[4,32,128]{2,1,0:T(8,128)S(1)}, f32[4,32,128]{2,1,0:T(8,128)S(1)}, u32[]{:S(2)}, u32[]{:S(2)}) collective-permute-start(f32[4,32,128]{2,1,0:T(8,128)S(1)} %get-tuple-element.50), channel_id=1, source_target_pairs={{0,12},{4,8},{8,4},{12,0},{1,13},{5,9},{9,5},{13,1},{2,14},{6,10},... | collective-permute-start | bytes 196616 | tf_op jit(solution)/shard_map/ppermute | solution.py:363
  44.3 6.5 %collective-permute-start.19 = (f32[4,32,128]{2,1,0:T(8,128)S(1)}, f32[4,32,128]{2,1,0:T(8,128)S(1)}, u32[]{:S(2)}, u32[]{:S(2)}) collective-permute-start(f32[4,32,128]{2,1,0:T(8,128)S(1)} %get-tuple-element.51), channel_id=1, source_target_pairs={{0,4},{4,0},{8,12},{12,8},{1,5},{5,1},{9,13},{13,9},{2,6},{6,2},{1... | collective-permute-start | bytes 196616 | tf_op jit(solution)/shard_map/ppermute | solution.py:363
  48.1 2.7 %copy-start.4 = (f32[16,32,128]{2,1,0:T(8,128)}, f32[16,32,128]{2,1,0:T(8,128)S(1)}, u32[]{:S(2)}) copy-start(f32[16,32,128]{2,1,0:T(8,128)S(1)} %get-tuple-element.52.refs_0_) | copy-start | bytes 786436
  50.8 0.6 copy-start.2
  51.4 2.3 %collective-permute-start.23 = (f32[16,32,128]{2,1,0:T(8,128)}, f32[16,32,128]{2,1,0:T(8,128)S(1)}, u32[]{:S(2)}, u32[]{:S(2)}) collective-permute-start(f32[16,32,128]{2,1,0:T(8,128)} %shard_map.139), channel_id=1, source_target_pairs={{0,1},{1,0},{2,3},{3,2},{4,5},{5,4},{6,7},{7,6},{8,9},{9,8},{10,11... | collective-permute-start | bytes 786440 | tf_op jit(solution)/shard_map/ppermute | solution.py:363
  51.6 6.8 %collective-permute-start.20 = (f32[4,32,128]{2,1,0:T(8,128)}, f32[4,32,128]{2,1,0:T(8,128)S(1)}, u32[]{:S(2)}, u32[]{:S(2)}) collective-permute-start(f32[4,32,128]{2,1,0:T(8,128)} %copy-done.2), channel_id=1, source_target_pairs={{0,8},{4,12},{8,0},{12,4},{1,9},{5,13},{9,1},{13,5},{2,10},{6,14},... | collective-permute-start | bytes 196616 | tf_op jit(solution)/shard_map/ppermute | solution.py:363
  52.3 6.8 %collective-permute-start.21 = (f32[4,32,128]{2,1,0:T(8,128)}, f32[4,32,128]{2,1,0:T(8,128)S(1)}, u32[]{:S(2)}, u32[]{:S(2)}) collective-permute-start(f32[4,32,128]{2,1,0:T(8,128)} %copy-done.2), channel_id=1, source_target_pairs={{0,4},{4,0},{8,12},{12,8},{1,5},{5,1},{9,13},{13,9},{2,6},{6,2},{1... | collective-permute-start | bytes 196616 | tf_op jit(solution)/shard_map/ppermute | solution.py:363
  53.7 9.8 %copy-start.3 = (f32[4,32,128]{2,1,0:T(8,128)S(1)}, f32[4,32,128]{2,1,0:T(8,128)}, u32[]{:S(2)}) copy-start(f32[4,32,128]{2,1,0:T(8,128)} %copy-done.2) | copy-start | bytes 196612
  53.7 10.8 %collective-permute-start.24 = (f32[16,32,128]{2,1,0:T(8,128)S(1)}, f32[16,32,128]{2,1,0:T(8,128)S(1)}, u32[]{:S(2)}, u32[]{:S(2)}) collective-permute-start(f32[16,32,128]{2,1,0:T(8,128)S(1)} %shard_map.140.refs_1_), channel_id=1, source_target_pairs={{0,2},{2,0},{1,3},{3,1},{4,6},{6,4},{5,7},{7,5},{8,10},{10,8},{9,1... | collective-permute-start | bytes 786440 | tf_op jit(solution)/shard_map/ppermute | solution.py:363
  58.4 0.6 copy-start.5
  59.0 4.5 %collective-permute-start.22 = (f32[4,32,128]{2,1,0:T(8,128)}, f32[4,32,128]{2,1,0:T(8,128)S(1)}, u32[]{:S(2)}, u32[]{:S(2)}) collective-permute-start(f32[4,32,128]{2,1,0:T(8,128)} %shard_map.137.refs_1_), channel_id=1, source_target_pairs={{0,4},{4,0},{8,12},{12,8},{1,5},{5,1},{9,13},{13,9},{2,6},{6,2},{1... | collective-permute-start | bytes 196616 | tf_op jit(solution)/shard_map/ppermute | solution.py:363
  63.5 0.8 %copy-start.6 = (f32[4,32,128]{2,1,0:T(8,128)S(1)}, f32[4,32,128]{2,1,0:T(8,128)}, u32[]{:S(2)}) copy-start(f32[4,32,128]{2,1,0:T(8,128)} %shard_map.137.refs_1_) | copy-start | bytes 196612
  64.4 1.6 %collective-permute-start.26 = (f32[4,4,32,128]{3,2,1,0:T(8,128)S(1)}, f32[4,4,32,128]{3,2,1,0:T(8,128)S(1)}, u32[]{:S(2)}, u32[]{:S(2)}) collective-permute-start(f32[4,4,32,128]{3,2,1,0:T(8,128)S(1)} %shard_map.138.refs_0_.item_mine), channel_id=1, source_target_pairs={{0,1},{1,0},{2,3},{3,2},{4,5},{5,4},{6,7},{7,6},{8,9},{9,8},{10,11... | collective-permute-start | bytes 786440 | tf_op jit(solution)/shard_map/ppermute | solution.py:363
  64.5 1.8 %collective-permute-start.25 = (f32[16,32,128]{2,1,0:T(8,128)S(1)}, f32[16,32,128]{2,1,0:T(8,128)S(1)}, u32[]{:S(2)}, u32[]{:S(2)}) collective-permute-start(f32[16,32,128]{2,1,0:T(8,128)S(1)} %shard_map.141.user_mine), channel_id=1, source_target_pairs={{0,1},{1,0},{2,3},{3,2},{4,5},{5,4},{6,7},{7,6},{8,9},{9,8},{10,11... | collective-permute-start | bytes 786440 | tf_op jit(solution)/shard_map/ppermute | solution.py:363

commit v4 on v3

--- a/solution.py
+++ b/solution.py
@@ -33,14 +33,8 @@
 
 
 def hold(values, *after, flops=0):
-    return pl.pallas_call(
-        nothing,
-        out_shape=jax.ShapeDtypeStruct(values.shape, values.dtype),
-        in_specs=[ANY] * (1 + len(after)),
-        out_specs=ANY,
-        input_output_aliases={0: 0},
-        cost_estimate=pl.CostEstimate(flops=flops, bytes_accessed=0, transcendentals=0),
-    )(values, *after)
+    return call(copy, jax.ShapeDtypeStruct(values.shape, values.dtype), (values, *after),
+                [VMEM] + [ANY] * len(after), flops=flops)
 
 
 def shape(*dims):
@@ -303,8 +297,8 @@
     halves(total, keep, send)
 
 
-def nothing(*refs):
-    pass
+def copy(values, *refs):
+    refs[-1][...] = values[...]
 
 
 def add_deal(offsets, keep, received, after, *outs):

time: 67.7 us -> 64.9 us (0.959)
  waiting for transfers between devices: 18.7 us -> 16.2 us
  local copies, waits for them, and re-layouts: 2.83 us -> 0.72 us
  starting transfers between devices: 25.8 us -> 27.2 us
    ppermute x26, waiting for transfers between devices: 18.7 us -> 16.2 us  [swap(): return lax.ppermute(values, axis, [(i, i ^ offset) for i in range(peers)])]
    unnamed x36 -> x26, local copies, waits for them, and re-layouts: 2.83 us -> 0.72 us
    ppermute x26, starting transfers between devices: 25.8 us -> 27.1 us  [swap(): return lax.ppermute(values, axis, [(i, i ^ offset) for i in range(peers)])]
    pallas_call x19 -> x21, Pallas kernels: 18.4 us -> 18.5 us  [call(): pl.pallas_call(kernel, out_shape=outs, in_specs=specs, out_specs=jax.tree...]
  transfers between devices with their start and end apart: 27 -> 27, of which waited for: 11 -> 12; matrix products, arithmetic and copies ran while one was open for 0% -> 0% of each run, Pallas kernels for 26% -> 27%
where the time goes in v4:
time: 64.9 us; the launch traced here: 64.3 us
  starting transfers between devices  27.2 us (42%)
  Pallas kernels  18.5 us (29%)
  waiting for transfers between devices  16.2 us (25%)
  between operations  1.69 us (3%)
  local copies, waits for them, and re-layouts  0.72 us (1%)
    ppermute x26, starting transfers between devices, swap(): return lax.ppermute(values, axis, [(i, i ^ offset) for i in range(peers)])  27.1 us
    pallas_call x21, Pallas kernels, call(): pl.pallas_call(kernel, out_shape=outs, in_specs=specs, out_specs=jax.tree...  18.5 us
    ppermute x26, waiting for transfers between devices, swap(): return lax.ppermute(values, axis, [(i, i ^ offset) for i in range(peers)])  16.2 us
  transfers between devices with their start and end apart: 27, of which 12 were waited for; matrix products, arithmetic and copies ran while one was open for 0% of the time, Pallas kernels for 27%

profile of v4, /device:TPU:0, one launch (start us, length us, event | category | flops | bytes accessed | tf_op | source)
XLA Modules:
  0.0 64.3 jit_solution(6526022095697325367)
XLA Ops:
  0.7 0.0 copy-start
  0.7 0.6 copy-done.6
  1.3 0.0 copy-done.5
  1.3 0.0 copy-done.4
  1.4 3.1 %collective-permute-start = (s32[64,256]{1,0:T(8,128)S(1)}, s32[64,256]{1,0:T(8,128)S(1)}, u32[]{:S(2)}, u32[]{:S(2)}) collective-permute-start(s32[64,256]{1,0:T(8,128)S(1)} %shard_map.123.after.refs_0_.ids.refs_4_), channel_id=1, source_target_pairs={{0,4},{4,0},{8,12},{12,8},{1,5},{5,1},{9,13},{13,9},{2,6},{6,2},{1... | collective-permute-start | bytes 196616 | tf_op jit(solution)/shard_map/ppermute | solution.py:357
  4.4 1.5 %collective-permute-start.2 = (s32[64,256]{1,0:T(8,128)S(1)}, s32[64,256]{1,0:T(8,128)S(1)}, u32[]{:S(2)}, u32[]{:S(2)}) collective-permute-start(s32[64,256]{1,0:T(8,128)S(1)} %shard_map.123.after.refs_0_.ids.refs_4_), channel_id=1, source_target_pairs={{0,2},{2,0},{1,3},{3,1},{4,6},{6,4},{5,7},{7,5},{8,10},{10,8},{9,1... | collective-permute-start | bytes 196616 | tf_op jit(solution)/shard_map/ppermute | solution.py:357
  6.6 0.9 %shard_map.124 = (bf16[17,64,128]{2,1,0:T(8,128)(2,1)S(1)}, bf16[17,64,128]{2,1,0:T(8,128)(2,1)S(1)}, f32[16,128]{1,0:T(8,128)S(1)}, f32[16,128]{1,0:T(8,128)S(1...) custom-call(s32[1]{0:T(128)S(6)} %copy.13.count, s32[288]{0:T(512)S(1)} %copy-done.11, s32[288]{0:T(512)S(1)} %copy-done.12, ...), custom_call_target="tpu_custom_call" | custom-call | flops 603979776 | bytes 9437184 | tf_op jit(solution)/shard_map/pallas_call | solution.py:24
  7.6 0.0 copy-start.2
  7.6 2.7 %collective-permute-start.1 = (s32[64,256]{1,0:T(8,128)S(1)}, s32[64,256]{1,0:T(8,128)S(1)}, u32[]{:S(2)}, u32[]{:S(2)}) collective-permute-start(s32[64,256]{1,0:T(8,128)S(1)} %shard_map.126), channel_id=1, source_target_pairs={{0,8},{4,12},{8,0},{12,4},{1,9},{5,13},{9,1},{13,5},{2,10},{6,14},... | collective-permute-start | bytes 196616 | tf_op jit(solution)/shard_map/ppermute | solution.py:357
  10.3 2.2 %shard_map.125.refs_0_.mine = f32[16,64,128]{2,1,0:T(8,128)S(1)} custom-call(s32[4,384]{1,0:T(4,128)S(1)} %get-tuple-element.28.order, bf16[288,128,128]{2,1,0:T(8,128)(2,1)S(1)} %copy-done, bf16[17,64,128]{2,1,0:T(8,128)(2,1)S(1)} %get-tuple-element.33.source, s32[64,256]{1,0:T(8,128)S(1)} %shard_map.123.after.refs_0_.ids.refs_4_), custom_call_target="tpu_custom_call" | custom-call | flops 603979776 | bytes 9437184 | tf_op jit(solution)/shard_map/pallas_call | solution.py:24
  12.5 0.1 collective-permute-start.4
  12.6 0.0 collective-permute-done.2.refs_3_.refs_1_
  12.6 0.9 %collective-permute-done.1.refs_2_.refs_6_ = s32[64,256]{1,0:T(8,128)S(1)} collective-permute-done((s32[64,256]{1,0:T(8,128)S(1)}, s32[64,256]{1,0:T(8,128)S(1)}, u32[]{:S(2)}, u32[]{:S(2)}) %collective-permute-start.1) | collective-permute-done | bytes 65568 | tf_op jit(solution)/shard_map/ppermute | solution.py:357
  13.5 3.1 %shard_map.127.mine = f32[16,64,128]{2,1,0:T(8,128)S(1)} custom-call(s32[4,384]{1,0:T(4,128)S(1)} %get-tuple-element.31.order, bf16[288,128,128]{2,1,0:T(8,128)(2,1)S(1)} %copy-done, bf16[17,64,128]{2,1,0:T(8,128)(2,1)S(1)} %get-tuple-element.32.source, f32[16,64,128]{2,1,0:T(8,128)S(1)} %shard_map.125.refs_0_.mine, ...), custom_call_target="tpu_custom_call" | custom-call | flops 603979776 | bytes 9437184 | tf_op jit(solution)/shard_map/pallas_call | solution.py:24
  16.7 0.1 collective-permute-start.3
  16.8 1.2 %shard_map.128 = (f32[64,256]{1,0:T(8,128)S(1)}, f32[64,256]{1,0:T(8,128)S(1)}, f32[64,256]{1,0:T(8,128)S(1)}, f32[64,256]{1,0:T(8,128)S(1)}) custom-call(f32[16,64,128]{2,1,0:T(8,128)S(1)} %shard_map.125.refs_0_.mine, f32[16,64,128]{2,1,0:T(8,128)S(1)} %collective-permute-done.4.other, f32[16,128]{1,0:T(8,128)S(1)} %get-tuple-element.30.scale.target_scale.source_scale, ...), custom_call_target="tpu_custom_call" | custom-call | flops 805306368 | bytes 1048576 | tf_op jit(solution)/shard_map/pallas_call | solution.py:24
  18.0 1.2 %collective-permute-start.6 = (f32[64,256]{1,0:T(8,128)S(1)}, f32[64,256]{1,0:T(8,128)S(1)}, u32[]{:S(2)}, u32[]{:S(2)}) collective-permute-start(f32[64,256]{1,0:T(8,128)S(1)} %get-tuple-element.38), channel_id=1, source_target_pairs={{0,8},{4,12},{8,0},{12,4},{1,9},{5,13},{9,1},{13,5},{2,10},{6,14},... | collective-permute-start | bytes 196616 | tf_op jit(solution)/shard_map/ppermute | solution.py:357
  19.3 1.1 %collective-permute-start.7 = (f32[64,256]{1,0:T(8,128)S(1)}, f32[64,256]{1,0:T(8,128)S(1)}, u32[]{:S(2)}, u32[]{:S(2)}) collective-permute-start(f32[64,256]{1,0:T(8,128)S(1)} %get-tuple-element.39), channel_id=1, source_target_pairs={{0,12},{4,8},{8,4},{12,0},{1,13},{5,9},{9,5},{13,1},{2,14},{6,10},... | collective-permute-start | bytes 196616 | tf_op jit(solution)/shard_map/ppermute | solution.py:357
  20.4 1.2 %collective-permute-start.8 = (f32[64,256]{1,0:T(8,128)S(1)}, f32[64,256]{1,0:T(8,128)S(1)}, u32[]{:S(2)}, u32[]{:S(2)}) collective-permute-start(f32[64,256]{1,0:T(8,128)S(1)} %get-tuple-element.40), channel_id=1, source_target_pairs={{0,4},{4,0},{8,12},{12,8},{1,5},{5,1},{9,13},{13,9},{2,6},{6,2},{1... | collective-permute-start | bytes 196616 | tf_op jit(solution)/shard_map/ppermute | solution.py:357
  21.6 0.0 collective-permute-done.3.other
  21.6 0.6 shard_map.129
  22.2 2.1 %collective-permute-start.5 = (f32[64,256]{1,0:T(8,128)S(1)}, f32[64,256]{1,0:T(8,128)S(1)}, u32[]{:S(2)}, u32[]{:S(2)}) collective-permute-start(f32[64,256]{1,0:T(8,128)S(1)} %get-tuple-element.36), channel_id=1, source_target_pairs={{0,2},{2,0},{1,3},{3,1},{4,6},{6,4},{5,7},{7,5},{8,10},{10,8},{9,1... | collective-permute-start | bytes 196616 | tf_op jit(solution)/shard_map/ppermute | solution.py:357
  24.3 0.5 shard_map.130
  24.8 1.1 %collective-permute-done.6.refs_4_ = f32[64,256]{1,0:T(8,128)S(1)} collective-permute-done((f32[64,256]{1,0:T(8,128)S(1)}, f32[64,256]{1,0:T(8,128)S(1)}, u32[]{:S(2)}, u32[]{:S(2)}) %collective-permute-start.6) | collective-permute-done | bytes 65568 | tf_op jit(solution)/shard_map/ppermute | solution.py:357
  26.0 0.0 collective-permute-done.7.refs_5_
  26.0 1.3 %collective-permute-done.8.refs_6_ = f32[64,256]{1,0:T(8,128)S(1)} collective-permute-done((f32[64,256]{1,0:T(8,128)S(1)}, f32[64,256]{1,0:T(8,128)S(1)}, u32[]{:S(2)}, u32[]{:S(2)}) %collective-permute-start.8) | collective-permute-done | bytes 65568 | tf_op jit(solution)/shard_map/ppermute | solution.py:357
  27.3 0.1 shard_map.131
  27.4 0.1 collective-permute-start.11
  27.4 1.7 %collective-permute-start.10 = (f32[72,256]{1,0:T(8,128)S(1)}, f32[72,256]{1,0:T(8,128)S(1)}, u32[]{:S(2)}, u32[]{:S(2)}) collective-permute-start(f32[72,256]{1,0:T(8,128)S(1)} %get-tuple-element.42.refs_0_), channel_id=1, source_target_pairs={{0,2},{2,0},{1,3},{3,1},{4,6},{6,4},{5,7},{7,5},{8,10},{10,8},{9,1... | collective-permute-start | bytes 221192 | tf_op jit(solution)/shard_map/ppermute | solution.py:357
  29.1 0.2 collective-permute-start.9
  29.3 1.6 %collective-permute-start.14 = (f32[64,256]{1,0:T(8,128)S(1)}, f32[64,256]{1,0:T(8,128)S(1)}, u32[]{:S(2)}, u32[]{:S(2)}) collective-permute-start(f32[64,256]{1,0:T(8,128)S(1)} %get-tuple-element.45.refs_0_), channel_id=1, source_target_pairs={{0,8},{4,12},{8,0},{12,4},{1,9},{5,13},{9,1},{13,5},{2,10},{6,14},... | collective-permute-start | bytes 196616 | tf_op jit(solution)/shard_map/ppermute | solution.py:357
  30.9 2.3 %collective-permute-start.13 = (f32[64,256]{1,0:T(8,128)S(1)}, f32[64,256]{1,0:T(8,128)S(1)}, u32[]{:S(2)}, u32[]{:S(2)}) collective-permute-start(f32[64,256]{1,0:T(8,128)S(1)} %get-tuple-element.45.refs_0_), channel_id=1, source_target_pairs={{0,12},{4,8},{8,4},{12,0},{1,13},{5,9},{9,5},{13,1},{2,14},{6,10},... | collective-permute-start | bytes 196616 | tf_op jit(solution)/shard_map/ppermute | solution.py:357
  33.2 0.0 collective-permute-done.11.refs_3_
  33.2 0.0 collective-permute-start.12
  33.2 0.3 collective-permute-done.10.refs_2_
  33.6 3.8 %shard_map.132 = (f32[16,64,128]{2,1,0:T(8,128)S(1)}, f32[16,32,128]{2,1,0:T(8,128)S(1)}, f32[16,32,128]{2,1,0:T(8,128)S(1)}) custom-call(s32[4,384]{1,0:T(4,128)S(1)} %get-tuple-element.28.order, f32[16,128]{1,0:T(8,128)S(1)} %get-tuple-element.29.scale.source_scale.target_scale, f32[16,128]{1,0:T(8,128)S(1)} %get-tuple-element.30.scale.target_scale.source_scale, ...), custom_call_target="tpu_custom_call" | custom-call | flops 603979776 | bytes 9437184 | tf_op jit(solution)/shard_map/pallas_call | solution.py:24
  37.3 0.1 collective-permute-start.16
  37.4 0.4 collective-permute-done.14.refs_3_
  37.8 0.9 %collective-permute-done.12.refs_1_ = f32[64,256]{1,0:T(8,128)S(1)} collective-permute-done((f32[64,256]{1,0:T(8,128)S(1)}, f32[64,256]{1,0:T(8,128)S(1)}, u32[]{:S(2)}, u32[]{:S(2)}) %collective-permute-start.12) | collective-permute-done | bytes 65568 | tf_op jit(solution)/shard_map/ppermute | solution.py:357
  38.7 1.5 %shard_map.133.after.mine = f32[16,64,128]{2,1,0:T(8,128)S(1)} custom-call(f32[16,32,128]{2,1,0:T(8,128)S(1)} %get-tuple-element.44.after, f32[64,256]{1,0:T(8,128)S(1)} %get-tuple-element.45.refs_0_, f32[64,256]{1,0:T(8,128)S(1)} %collective-permute-done.12.refs_1_, f32[64,256]{1,0:T(8,128)S(1)} %collective-permute-done.13.refs_2_, ...), custom_call_target="tpu_custom_call" | custom-call | flops 99999997952 | tf_op jit(solution)/shard_map/pallas_call | solution.py:24
  40.2 0.1 collective-permute-start.15
  40.3 0.0 collective-permute-done.16.received
  40.3 0.0 copy-start.1
  40.3 0.0 copy-start.3
  40.4 1.3 %collective-permute-start.17 = (f32[4,32,128]{2,1,0:T(8,128)S(1)}, f32[4,32,128]{2,1,0:T(8,128)S(1)}, u32[]{:S(2)}, u32[]{:S(2)}) collective-permute-start(f32[4,32,128]{2,1,0:T(8,128)S(1)} %get-tuple-element.49), channel_id=1, source_target_pairs={{0,8},{4,12},{8,0},{12,4},{1,9},{5,13},{9,1},{13,5},{2,10},{6,14},... | collective-permute-start | bytes 196616 | tf_op jit(solution)/shard_map/ppermute | solution.py:357
  41.7 1.7 %collective-permute-start.18 = (f32[4,32,128]{2,1,0:T(8,128)S(1)}, f32[4,32,128]{2,1,0:T(8,128)S(1)}, u32[]{:S(2)}, u32[]{:S(2)}) collective-permute-start(f32[4,32,128]{2,1,0:T(8,128)S(1)} %get-tuple-element.50), channel_id=1, source_target_pairs={{0,12},{4,8},{8,4},{12,0},{1,13},{5,9},{9,5},{13,1},{2,14},{6,10},... | collective-permute-start | bytes 196616 | tf_op jit(solution)/shard_map/ppermute | solution.py:357
  43.4 0.5 collective-permute-start.19
  43.9 0.1 copy-done.1
  44.0 3.3 %shard_map.135 = (f32[16,64,128]{2,1,0:T(8,128)S(1)}, f32[16,32,128]{2,1,0:T(8,128)S(1)}, f32[16,32,128]{2,1,0:T(8,128)S(1)}) custom-call(s32[4,384]{1,0:T(4,128)S(1)} %copy-done.3, f32[16,64,128]{2,1,0:T(8,128)S(1)} %shard_map.133.after.mine, f32[16,64,128]{2,1,0:T(8,128)S(1)} %collective-permute-done.15.other, ...), custom_call_target="tpu_custom_call" | custom-call | flops 603979776 | bytes 9437184 | tf_op jit(solution)/shard_map/pallas_call | solution.py:24
  47.3 1.5 %collective-permute-done.17.refs_2_ = f32[4,32,128]{2,1,0:T(8,128)S(1)} collective-permute-done((f32[4,32,128]{2,1,0:T(8,128)S(1)}, f32[4,32,128]{2,1,0:T(8,128)S(1)}, u32[]{:S(2)}, u32[]{:S(2)}) %collective-permute-start.17) | collective-permute-done | bytes 65568 | tf_op jit(solution)/shard_map/ppermute | solution.py:357
  48.8 1.2 %collective-permute-done.19.refs_4_ = f32[4,32,128]{2,1,0:T(8,128)S(1)} collective-permute-done((f32[4,32,128]{2,1,0:T(8,128)S(1)}, f32[4,32,128]{2,1,0:T(8,128)S(1)}, u32[]{:S(2)}, u32[]{:S(2)}) %collective-permute-start.19) | collective-permute-done | bytes 65568 | tf_op jit(solution)/shard_map/ppermute | solution.py:357
  50.0 0.1 collective-permute-start.23
  50.1 1.4 %collective-permute-start.20 = (f32[4,32,128]{2,1,0:T(8,128)S(1)}, f32[4,32,128]{2,1,0:T(8,128)S(1)}, u32[]{:S(2)}, u32[]{:S(2)}) collective-permute-start(f32[4,32,128]{2,1,0:T(8,128)S(1)} %shard_map.136.refs_0_), channel_id=1, source_target_pairs={{0,8},{4,12},{8,0},{12,4},{1,9},{5,13},{9,1},{13,5},{2,10},{6,14},... | collective-permute-start | bytes 196616 | tf_op jit(solution)/shard_map/ppermute | solution.py:357
  51.4 1.4 %collective-permute-start.21 = (f32[4,32,128]{2,1,0:T(8,128)S(1)}, f32[4,32,128]{2,1,0:T(8,128)S(1)}, u32[]{:S(2)}, u32[]{:S(2)}) collective-permute-start(f32[4,32,128]{2,1,0:T(8,128)S(1)} %shard_map.136.refs_0_), channel_id=1, source_target_pairs={{0,4},{4,0},{8,12},{12,8},{1,5},{5,1},{9,13},{13,9},{2,6},{6,2},{1... | collective-permute-start | bytes 196616 | tf_op jit(solution)/shard_map/ppermute | solution.py:357
  52.8 0.0 collective-permute-done.23.refs_1_
  52.9 1.1 %collective-permute-start.24 = (f32[16,32,128]{2,1,0:T(8,128)S(1)}, f32[16,32,128]{2,1,0:T(8,128)S(1)}, u32[]{:S(2)}, u32[]{:S(2)}) collective-permute-start(f32[16,32,128]{2,1,0:T(8,128)S(1)} %shard_map.140.refs_1_), channel_id=1, source_target_pairs={{0,2},{2,0},{1,3},{3,1},{4,6},{6,4},{5,7},{7,5},{8,10},{10,8},{9,1... | collective-permute-start | bytes 786440 | tf_op jit(solution)/shard_map/ppermute | solution.py:357
  54.0 2.9 %collective-permute-done.20.values = f32[4,32,128]{2,1,0:T(8,128)S(1)} collective-permute-done((f32[4,32,128]{2,1,0:T(8,128)S(1)}, f32[4,32,128]{2,1,0:T(8,128)S(1)}, u32[]{:S(2)}, u32[]{:S(2)}) %collective-permute-start.20) | collective-permute-done | bytes 65568 | tf_op jit(solution)/shard_map/ppermute | solution.py:357
  56.9 0.0 collective-permute-start.22
  56.9 4.2 %collective-permute-done.22.refs_3_ = f32[4,32,128]{2,1,0:T(8,128)S(1)} collective-permute-done((f32[4,32,128]{2,1,0:T(8,128)S(1)}, f32[4,32,128]{2,1,0:T(8,128)S(1)}, u32[]{:S(2)}, u32[]{:S(2)}) %collective-permute-start.22) | collective-permute-done | bytes 65568 | tf_op jit(solution)/shard_map/ppermute | solution.py:357
  61.2 0.1 collective-permute-start.26
  61.3 0.5 collective-permute-start.25
  61.9 0.9 %collective-permute-done.26.item_other = f32[4,4,32,128]{3,2,1,0:T(8,128)S(1)} collective-permute-done((f32[4,4,32,128]{3,2,1,0:T(8,128)S(1)}, f32[4,4,32,128]{3,2,1,0:T(8,128)S(1)}, u32[]{:S(2)}, u32[]{:S(2)}) %collective-permute-start.26) | collective-permute-done | bytes 262176 | tf_op jit(solution)/shard_map/ppermute | solution.py:357
  62.8 0.4 collective-permute-done.25.user_other
  63.2 1.1 %shard_map.142 = (f32[64,2048]{1,0:T(8,128)}, f32[64,2048]{1,0:T(8,128)}) custom-call(f32[16,64,128]{2,1,0:T(8,128)S(1)} %get-tuple-element.43.user_half_grad, f32[16,32,128]{2,1,0:T(8,128)S(1)} %shard_map.141.user_mine, f32[16,32,128]{2,1,0:T(8,128)S(1)} %collective-permute-done.25.user_other, f32[16,64,128]{2,1,0:T(8,128)S(1)} %get-tuple-element.53.item_half_grad, ...), custom_call_target="tpu_custom_call" | custom-call | bytes 3145728 | tf_op jit(solution)/shard_map/pallas_call | solution.py:24
  (37 shorter events, 0.2 us)
Async XLA Ops:
  0.6 0.7 %copy-start.6 = (s32[256]{0:T(256)S(1)}, s32[256]{0:T(256)}, u32[]{:S(2)}) copy-start(s32[256]{0:T(256)} %param.21) | copy-start | bytes 3076
  0.6 0.7 %copy-start.5 = (s32[256]{0:T(256)S(1)}, s32[256]{0:T(256)}, u32[]{:S(2)}) copy-start(s32[256]{0:T(256)} %param.20) | copy-start | bytes 3076
  0.7 0.7 %copy-start.4 = (s32[256]{0:T(256)S(1)}, s32[256]{0:T(256)}, u32[]{:S(2)}) copy-start(s32[256]{0:T(256)} %param.19) | copy-start | bytes 3076
  0.7 5.9 %copy-start.8 = (bf16[64,2048]{1,0:T(8,128)(2,1)S(1)}, bf16[64,2048]{1,0:T(8,128)(2,1)}, u32[]{:S(2)}) copy-start(bf16[64,2048]{1,0:T(8,128)(2,1)} %item_emb.3) | copy-start | bytes 786436
  0.7 5.9 %copy-start.7 = (bf16[64,2048]{1,0:T(8,128)(2,1)S(1)}, bf16[64,2048]{1,0:T(8,128)(2,1)}, u32[]{:S(2)}) copy-start(bf16[64,2048]{1,0:T(8,128)(2,1)} %user_emb.3) | copy-start | bytes 786436
  0.7 5.9 %copy-start.12 = (s32[288]{0:T(512)S(1)}, s32[288]{0:T(512)}, u32[]{:S(2)}) copy-start(s32[288]{0:T(512)} %columns.1) | copy-start | bytes 3460
  0.7 5.9 %copy-start.11 = (s32[288]{0:T(512)S(1)}, s32[288]{0:T(512)}, u32[]{:S(2)}) copy-start(s32[288]{0:T(512)} %rows.1) | copy-start | bytes 3460
  0.7 5.9 %copy-start.10 = (s32[2048]{0:T(1024)S(1)}, s32[2048]{0:T(1024)}, u32[]{:S(2)}) copy-start(s32[2048]{0:T(1024)} %param.14) | copy-start | bytes 24580
  0.7 5.9 %copy-start.9 = (s32[2048]{0:T(1024)S(1)}, s32[2048]{0:T(1024)}, u32[]{:S(2)}) copy-start(s32[2048]{0:T(1024)} %param.13) | copy-start | bytes 24580
  0.7 9.5 %copy-start = (bf16[288,128,128]{2,1,0:T(8,128)(2,1)S(1)}, bf16[288,128,128]{2,1,0:T(8,128)(2,1)}, u32[]{:S(2)}) copy-start(bf16[288,128,128]{2,1,0:T(8,128)(2,1)} %vals.7) | copy-start | bytes 28311556
  1.4 6.2 %collective-permute-start = (s32[64,256]{1,0:T(8,128)S(1)}, s32[64,256]{1,0:T(8,128)S(1)}, u32[]{:S(2)}, u32[]{:S(2)}) collective-permute-start(s32[64,256]{1,0:T(8,128)S(1)} %shard_map.123.after.refs_0_.ids.refs_4_), channel_id=1, source_target_pairs={{0,4},{4,0},{8,12},{12,8},{1,5},{5,1},{9,13},{13,9},{2,6},{6,2},{1... | collective-permute-start | bytes 196616 | tf_op jit(solution)/shard_map/ppermute | solution.py:357
  4.4 8.2 %collective-permute-start.2 = (s32[64,256]{1,0:T(8,128)S(1)}, s32[64,256]{1,0:T(8,128)S(1)}, u32[]{:S(2)}, u32[]{:S(2)}) collective-permute-start(s32[64,256]{1,0:T(8,128)S(1)} %shard_map.123.after.refs_0_.ids.refs_4_), channel_id=1, source_target_pairs={{0,2},{2,0},{1,3},{3,1},{4,6},{6,4},{5,7},{7,5},{8,10},{10,8},{9,1... | collective-permute-start | bytes 196616 | tf_op jit(solution)/shard_map/ppermute | solution.py:357
  7.6 9.1 %copy-start.2 = (s32[4,384]{1,0:T(4,128)}, s32[4,384]{1,0:T(4,128)S(1)}, u32[]{:S(2)}) copy-start(s32[4,384]{1,0:T(4,128)S(1)} %get-tuple-element.31.order) | copy-start | bytes 18436
  7.6 5.9 %collective-permute-start.1 = (s32[64,256]{1,0:T(8,128)S(1)}, s32[64,256]{1,0:T(8,128)S(1)}, u32[]{:S(2)}, u32[]{:S(2)}) collective-permute-start(s32[64,256]{1,0:T(8,128)S(1)} %shard_map.126), channel_id=1, source_target_pairs={{0,8},{4,12},{8,0},{12,4},{1,9},{5,13},{9,1},{13,5},{2,10},{6,14},... | collective-permute-start | bytes 196616 | tf_op jit(solution)/shard_map/ppermute | solution.py:357
  12.5 4.3 %collective-permute-start.4 = (f32[16,64,128]{2,1,0:T(8,128)S(1)}, f32[16,64,128]{2,1,0:T(8,128)S(1)}, u32[]{:S(2)}, u32[]{:S(2)}) collective-permute-start(f32[16,64,128]{2,1,0:T(8,128)S(1)} %shard_map.125.refs_0_.mine), channel_id=1, source_target_pairs={{0,1},{1,0},{2,3},{3,2},{4,5},{5,4},{6,7},{7,6},{8,9},{9,8},{10,11... | collective-permute-start | bytes 1572872 | tf_op jit(solution)/shard_map/ppermute | solution.py:357
  16.7 4.9 %collective-permute-start.3 = (f32[16,64,128]{2,1,0:T(8,128)S(1)}, f32[16,64,128]{2,1,0:T(8,128)S(1)}, u32[]{:S(2)}, u32[]{:S(2)}) collective-permute-start(f32[16,64,128]{2,1,0:T(8,128)S(1)} %shard_map.127.mine), channel_id=1, source_target_pairs={{0,1},{1,0},{2,3},{3,2},{4,5},{5,4},{6,7},{7,6},{8,9},{9,8},{10,11... | collective-permute-start | bytes 1572872 | tf_op jit(solution)/shard_map/ppermute | solution.py:357
  18.0 7.9 %collective-permute-start.6 = (f32[64,256]{1,0:T(8,128)S(1)}, f32[64,256]{1,0:T(8,128)S(1)}, u32[]{:S(2)}, u32[]{:S(2)}) collective-permute-start(f32[64,256]{1,0:T(8,128)S(1)} %get-tuple-element.38), channel_id=1, source_target_pairs={{0,8},{4,12},{8,0},{12,4},{1,9},{5,13},{9,1},{13,5},{2,10},{6,14},... | collective-permute-start | bytes 196616 | tf_op jit(solution)/shard_map/ppermute | solution.py:357
  19.3 6.7 %collective-permute-start.7 = (f32[64,256]{1,0:T(8,128)S(1)}, f32[64,256]{1,0:T(8,128)S(1)}, u32[]{:S(2)}, u32[]{:S(2)}) collective-permute-start(f32[64,256]{1,0:T(8,128)S(1)} %get-tuple-element.39), channel_id=1, source_target_pairs={{0,12},{4,8},{8,4},{12,0},{1,13},{5,9},{9,5},{13,1},{2,14},{6,10},... | collective-permute-start | bytes 196616 | tf_op jit(solution)/shard_map/ppermute | solution.py:357
  20.4 6.9 %collective-permute-start.8 = (f32[64,256]{1,0:T(8,128)S(1)}, f32[64,256]{1,0:T(8,128)S(1)}, u32[]{:S(2)}, u32[]{:S(2)}) collective-permute-start(f32[64,256]{1,0:T(8,128)S(1)} %get-tuple-element.40), channel_id=1, source_target_pairs={{0,4},{4,0},{8,12},{12,8},{1,5},{5,1},{9,13},{13,9},{2,6},{6,2},{1... | collective-permute-start | bytes 196616 | tf_op jit(solution)/shard_map/ppermute | solution.py:357
  22.2 5.1 %collective-permute-start.5 = (f32[64,256]{1,0:T(8,128)S(1)}, f32[64,256]{1,0:T(8,128)S(1)}, u32[]{:S(2)}, u32[]{:S(2)}) collective-permute-start(f32[64,256]{1,0:T(8,128)S(1)} %get-tuple-element.36), channel_id=1, source_target_pairs={{0,2},{2,0},{1,3},{3,1},{4,6},{6,4},{5,7},{7,5},{8,10},{10,8},{9,1... | collective-permute-start | bytes 196616 | tf_op jit(solution)/shard_map/ppermute | solution.py:357
  27.4 5.9 %collective-permute-start.11 = (f32[72,256]{1,0:T(8,128)S(1)}, f32[72,256]{1,0:T(8,128)S(1)}, u32[]{:S(2)}, u32[]{:S(2)}) collective-permute-start(f32[72,256]{1,0:T(8,128)S(1)} %get-tuple-element.42.refs_0_), channel_id=1, source_target_pairs={{0,3},{1,2},{2,1},{3,0},{4,7},{5,6},{6,5},{7,4},{8,11},{9,10},{10,... | collective-permute-start | bytes 221192 | tf_op jit(solution)/shard_map/ppermute | solution.py:456
  27.4 6.1 %collective-permute-start.10 = (f32[72,256]{1,0:T(8,128)S(1)}, f32[72,256]{1,0:T(8,128)S(1)}, u32[]{:S(2)}, u32[]{:S(2)}) collective-permute-start(f32[72,256]{1,0:T(8,128)S(1)} %get-tuple-element.42.refs_0_), channel_id=1, source_target_pairs={{0,2},{2,0},{1,3},{3,1},{4,6},{6,4},{5,7},{7,5},{8,10},{10,8},{9,1... | collective-permute-start | bytes 221192 | tf_op jit(solution)/shard_map/ppermute | solution.py:357
  29.1 4.5 %collective-permute-start.9 = (f32[72,256]{1,0:T(8,128)S(1)}, f32[72,256]{1,0:T(8,128)S(1)}, u32[]{:S(2)}, u32[]{:S(2)}) collective-permute-start(f32[72,256]{1,0:T(8,128)S(1)} %get-tuple-element.42.refs_0_), channel_id=1, source_target_pairs={{0,1},{1,0},{2,3},{3,2},{4,5},{5,4},{6,7},{7,6},{8,9},{9,8},{10,11... | collective-permute-start | bytes 221192 | tf_op jit(solution)/shard_map/ppermute | solution.py:357
  29.3 8.5 %collective-permute-start.14 = (f32[64,256]{1,0:T(8,128)S(1)}, f32[64,256]{1,0:T(8,128)S(1)}, u32[]{:S(2)}, u32[]{:S(2)}) collective-permute-start(f32[64,256]{1,0:T(8,128)S(1)} %get-tuple-element.45.refs_0_), channel_id=1, source_target_pairs={{0,8},{4,12},{8,0},{12,4},{1,9},{5,13},{9,1},{13,5},{2,10},{6,14},... | collective-permute-start | bytes 196616 | tf_op jit(solution)/shard_map/ppermute | solution.py:357
  30.9 6.9 %collective-permute-start.13 = (f32[64,256]{1,0:T(8,128)S(1)}, f32[64,256]{1,0:T(8,128)S(1)}, u32[]{:S(2)}, u32[]{:S(2)}) collective-permute-start(f32[64,256]{1,0:T(8,128)S(1)} %get-tuple-element.45.refs_0_), channel_id=1, source_target_pairs={{0,12},{4,8},{8,4},{12,0},{1,13},{5,9},{9,5},{13,1},{2,14},{6,10},... | collective-permute-start | bytes 196616 | tf_op jit(solution)/shard_map/ppermute | solution.py:357
  33.2 5.4 %collective-permute-start.12 = (f32[64,256]{1,0:T(8,128)S(1)}, f32[64,256]{1,0:T(8,128)S(1)}, u32[]{:S(2)}, u32[]{:S(2)}) collective-permute-start(f32[64,256]{1,0:T(8,128)S(1)} %get-tuple-element.45.refs_0_), channel_id=1, source_target_pairs={{0,4},{4,0},{8,12},{12,8},{1,5},{5,1},{9,13},{13,9},{2,6},{6,2},{1... | collective-permute-start | bytes 196616 | tf_op jit(solution)/shard_map/ppermute | solution.py:357
  37.3 2.9 %collective-permute-start.16 = (f32[16,32,128]{2,1,0:T(8,128)S(1)}, f32[16,32,128]{2,1,0:T(8,128)S(1)}, u32[]{:S(2)}, u32[]{:S(2)}) collective-permute-start(f32[16,32,128]{2,1,0:T(8,128)S(1)} %get-tuple-element.44.after), channel_id=1, source_target_pairs={{0,1},{1,0},{2,3},{3,2},{4,5},{5,4},{6,7},{7,6},{8,9},{9,8},{10,11... | collective-permute-start | bytes 786440 | tf_op jit(solution)/shard_map/ppermute | solution.py:357
  40.2 3.7 %collective-permute-start.15 = (f32[16,64,128]{2,1,0:T(8,128)S(1)}, f32[16,64,128]{2,1,0:T(8,128)S(1)}, u32[]{:S(2)}, u32[]{:S(2)}) collective-permute-start(f32[16,64,128]{2,1,0:T(8,128)S(1)} %shard_map.133.after.mine), channel_id=1, source_target_pairs={{0,1},{1,0},{2,3},{3,2},{4,5},{5,4},{6,7},{7,6},{8,9},{9,8},{10,11... | collective-permute-start | bytes 1572872 | tf_op jit(solution)/shard_map/ppermute | solution.py:357
  40.3 3.7 %copy-start.1 = (bf16[288,128,128]{2,1,0:T(8,128)(2,1)S(1)}, bf16[288,128,128]{2,1,0:T(8,128)(2,1)}, u32[]{:S(2)}) copy-start(bf16[288,128,128]{2,1,0:T(8,128)(2,1)} %vals.7) | copy-start | bytes 28311556
  40.3 3.7 %copy-start.3 = (s32[4,384]{1,0:T(4,128)S(1)}, s32[4,384]{1,0:T(4,128)}, u32[]{:S(2)}) copy-start(s32[4,384]{1,0:T(4,128)} %copy-done.2) | copy-start | bytes 18436
  40.4 8.4 %collective-permute-start.17 = (f32[4,32,128]{2,1,0:T(8,128)S(1)}, f32[4,32,128]{2,1,0:T(8,128)S(1)}, u32[]{:S(2)}, u32[]{:S(2)}) collective-permute-start(f32[4,32,128]{2,1,0:T(8,128)S(1)} %get-tuple-element.49), channel_id=1, source_target_pairs={{0,8},{4,12},{8,0},{12,4},{1,9},{5,13},{9,1},{13,5},{2,10},{6,14},... | collective-permute-start | bytes 196616 | tf_op jit(solution)/shard_map/ppermute | solution.py:357
  41.7 7.1 %collective-permute-start.18 = (f32[4,32,128]{2,1,0:T(8,128)S(1)}, f32[4,32,128]{2,1,0:T(8,128)S(1)}, u32[]{:S(2)}, u32[]{:S(2)}) collective-permute-start(f32[4,32,128]{2,1,0:T(8,128)S(1)} %get-tuple-element.50), channel_id=1, source_target_pairs={{0,12},{4,8},{8,4},{12,0},{1,13},{5,9},{9,5},{13,1},{2,14},{6,10},... | collective-permute-start | bytes 196616 | tf_op jit(solution)/shard_map/ppermute | solution.py:357
  43.4 6.6 %collective-permute-start.19 = (f32[4,32,128]{2,1,0:T(8,128)S(1)}, f32[4,32,128]{2,1,0:T(8,128)S(1)}, u32[]{:S(2)}, u32[]{:S(2)}) collective-permute-start(f32[4,32,128]{2,1,0:T(8,128)S(1)} %get-tuple-element.51), channel_id=1, source_target_pairs={{0,4},{4,0},{8,12},{12,8},{1,5},{5,1},{9,13},{13,9},{2,6},{6,2},{1... | collective-permute-start | bytes 196616 | tf_op jit(solution)/shard_map/ppermute | solution.py:357
  50.0 2.8 %collective-permute-start.23 = (f32[16,32,128]{2,1,0:T(8,128)S(1)}, f32[16,32,128]{2,1,0:T(8,128)S(1)}, u32[]{:S(2)}, u32[]{:S(2)}) collective-permute-start(f32[16,32,128]{2,1,0:T(8,128)S(1)} %shard_map.139), channel_id=1, source_target_pairs={{0,1},{1,0},{2,3},{3,2},{4,5},{5,4},{6,7},{7,6},{8,9},{9,8},{10,11... | collective-permute-start | bytes 786440 | tf_op jit(solution)/shard_map/ppermute | solution.py:357
  50.1 6.8 %collective-permute-start.20 = (f32[4,32,128]{2,1,0:T(8,128)S(1)}, f32[4,32,128]{2,1,0:T(8,128)S(1)}, u32[]{:S(2)}, u32[]{:S(2)}) collective-permute-start(f32[4,32,128]{2,1,0:T(8,128)S(1)} %shard_map.136.refs_0_), channel_id=1, source_target_pairs={{0,8},{4,12},{8,0},{12,4},{1,9},{5,13},{9,1},{13,5},{2,10},{6,14},... | collective-permute-start | bytes 196616 | tf_op jit(solution)/shard_map/ppermute | solution.py:357
  51.4 5.5 %collective-permute-start.21 = (f32[4,32,128]{2,1,0:T(8,128)S(1)}, f32[4,32,128]{2,1,0:T(8,128)S(1)}, u32[]{:S(2)}, u32[]{:S(2)}) collective-permute-start(f32[4,32,128]{2,1,0:T(8,128)S(1)} %shard_map.136.refs_0_), channel_id=1, source_target_pairs={{0,4},{4,0},{8,12},{12,8},{1,5},{5,1},{9,13},{13,9},{2,6},{6,2},{1... | collective-permute-start | bytes 196616 | tf_op jit(solution)/shard_map/ppermute | solution.py:357
  52.9 8.4 %collective-permute-start.24 = (f32[16,32,128]{2,1,0:T(8,128)S(1)}, f32[16,32,128]{2,1,0:T(8,128)S(1)}, u32[]{:S(2)}, u32[]{:S(2)}) collective-permute-start(f32[16,32,128]{2,1,0:T(8,128)S(1)} %shard_map.140.refs_1_), channel_id=1, source_target_pairs={{0,2},{2,0},{1,3},{3,1},{4,6},{6,4},{5,7},{7,5},{8,10},{10,8},{9,1... | collective-permute-start | bytes 786440 | tf_op jit(solution)/shard_map/ppermute | solution.py:357
  56.9 4.3 %collective-permute-start.22 = (f32[4,32,128]{2,1,0:T(8,128)S(1)}, f32[4,32,128]{2,1,0:T(8,128)S(1)}, u32[]{:S(2)}, u32[]{:S(2)}) collective-permute-start(f32[4,32,128]{2,1,0:T(8,128)S(1)} %shard_map.137.refs_1_), channel_id=1, source_target_pairs={{0,4},{4,0},{8,12},{12,8},{1,5},{5,1},{9,13},{13,9},{2,6},{6,2},{1... | collective-permute-start | bytes 196616 | tf_op jit(solution)/shard_map/ppermute | solution.py:357
  61.2 1.6 %collective-permute-start.26 = (f32[4,4,32,128]{3,2,1,0:T(8,128)S(1)}, f32[4,4,32,128]{3,2,1,0:T(8,128)S(1)}, u32[]{:S(2)}, u32[]{:S(2)}) collective-permute-start(f32[4,4,32,128]{3,2,1,0:T(8,128)S(1)} %shard_map.138.refs_0_.item_mine), channel_id=1, source_target_pairs={{0,1},{1,0},{2,3},{3,2},{4,5},{5,4},{6,7},{7,6},{8,9},{9,8},{10,11... | collective-permute-start | bytes 786440 | tf_op jit(solution)/shard_map/ppermute | solution.py:357
  61.3 1.8 %collective-permute-start.25 = (f32[16,32,128]{2,1,0:T(8,128)S(1)}, f32[16,32,128]{2,1,0:T(8,128)S(1)}, u32[]{:S(2)}, u32[]{:S(2)}) collective-permute-start(f32[16,32,128]{2,1,0:T(8,128)S(1)} %shard_map.141.user_mine), channel_id=1, source_target_pairs={{0,1},{1,0},{2,3},{3,2},{4,5},{5,4},{6,7},{7,6},{8,9},{9,8},{10,11... | collective-permute-start | bytes 786440 | tf_op jit(solution)/shard_map/ppermute | solution.py:357

commit v5 on v4

--- a/solution.py
+++ b/solution.py
@@ -11,7 +11,6 @@
 BF16 = jnp.bfloat16
 PACK = 4
 GROUP = 8
-ID_ROWS = 64
 HEAVY = 10 ** 11
 
 VMEM = pl.BlockSpec(memory_space=pltpu.VMEM)
@@ -371,7 +370,8 @@
     product_flops = 2 * slots * size * size * width
     product_bytes = slots * size * size * 2
     started = call(begin, shape(8, size), (), [], (), 16 * product_flops, product_bytes)
-    ids_shape = jax.ShapeDtypeStruct((ID_ROWS, trips), jnp.int32)
+    id_rows = max(16, -(-3 * users // 16) * 8)
+    ids_shape = jax.ShapeDtypeStruct((id_rows, trips), jnp.int32)
     ids = call(
         stack_ids, ids_shape,
         [each.reshape(1, trips) for each in (trip_user, trip_pos, trip_neg)] + [started],
@@ -407,12 +407,10 @@
         (item_order, block_vals, user_source, ids), [SMEM, VMEM, VMEM, ANY], (),
         product_flops, product_bytes,
     )
-    ids_here = [*held[1:], *ids_user[1:]]
     user_table = call(
         functools.partial(first_pass, True), shape(user_blocks, width, size),
-        (user_order, block_vals, item_source, item_table, *ids_here),
-        [SMEM, VMEM, VMEM] + [ANY] * (1 + len(ids_here)), (),
-        product_flops, product_bytes,
+        (user_order, block_vals, item_source, item_table), [SMEM, VMEM, VMEM, ANY], (),
+        HEAVY, product_bytes,
     )
 
     hot_flops = 2 * 3 * width * trips * size
@@ -424,7 +422,7 @@
             (table, swap(table), scale, after, *arrays),
             [VMEM] * 3 + [ANY] + [VMEM] * len(arrays),
             [pltpu.VMEM((3 * width, blocks * size), BF16)],
-            peers * blocks * hot_flops, 8 * blocks * width * size,
+            HEAVY if axis == "user" else 0, 8 * blocks * width * size,
         )
         return [dealt[0]] + [swap(part, axis, peers, o) for part, o in zip(dealt[1:], offsets)]
 
@@ -491,13 +489,13 @@
     item_own = call(functools.partial(sum_after, 1), shape(per, half, size), (user_keep, *parts),
                     [ANY] + [VMEM] * users,
                moved=4 * (users + 1) * per * half * size)
-    item_mine, step = {0: item_own}, users // 2
-    while step >= 1:
+    item_mine, step = {0: item_own}, 1
+    while step < users:
         for offset, part in list(item_mine.items()):
             item_mine[offset ^ step] = swap(part, "user", users, step)
-        if step > 1:
+        if 2 * step < users:
             item_mine[step] = hold(item_mine[step], flops=HEAVY)
-        step //= 2
+        step *= 2
     item_places = list(item_mine)
     item_mine = call(pack, shape(users, per, half, size), tuple(item_mine.values()),
                      [VMEM] * users, moved=8 * item_blocks * half * size)

time: 64.9 us -> 67.6 us (1.042)
  Pallas kernels: 18.5 us -> 23.4 us
  waiting for transfers between devices: 16.2 us -> 11.5 us
  starting transfers between devices: 27.2 us -> 29.6 us
    pallas_call x21, Pallas kernels: 18.5 us -> 23.4 us  [call(): pl.pallas_call(kernel, out_shape=outs, in_specs=specs, out_specs=jax.tree...]
    ppermute x26, waiting for transfers between devices: 16.2 us -> 11.5 us  [swap(): return lax.ppermute(values, axis, [(i, i ^ offset) for i in range(peers)])]
    ppermute x26, starting transfers between devices: 27.1 us -> 28.6 us  [swap(): return lax.ppermute(values, axis, [(i, i ^ offset) for i in range(peers)])]
    ppermute x1, starting transfers between devices: 0.07 us -> 0.92 us  [on_device(): lax.ppermute(pieces, ('item', 'rep'), [(i, i ^ 2 * offset + 1) for i in r...]
  transfers between devices with their start and end apart: 27 -> 27, of which waited for: 12 -> 12; matrix products, arithmetic and copies ran while one was open for 0% -> 0% of each run, Pallas kernels for 27% -> 31%
where the time goes in v5:
time: 67.6 us; the launch traced here: 67 us
  starting transfers between devices  29.6 us (44%)
  Pallas kernels  23.4 us (35%)
  waiting for transfers between devices  11.5 us (17%)
  between operations  1.78 us (3%)
  local copies, waits for them, and re-layouts  0.74 us (1%)
    ppermute x26, starting transfers between devices, swap(): return lax.ppermute(values, axis, [(i, i ^ offset) for i in range(peers)])  28.6 us
    pallas_call x21, Pallas kernels, call(): pl.pallas_call(kernel, out_shape=outs, in_specs=specs, out_specs=jax.tree...  23.4 us
    ppermute x26, waiting for transfers between devices, swap(): return lax.ppermute(values, axis, [(i, i ^ offset) for i in range(peers)])  11.5 us
  transfers between devices with their start and end apart: 27, of which 12 were waited for; matrix products, arithmetic and copies ran while one was open for 0% of the time, Pallas kernels for 31%

profile of v5, /device:TPU:0, one launch (start us, length us, event | category | flops | bytes accessed | tf_op | source)
XLA Modules:
  0.0 67.0 jit_solution(7251135147046621935)
XLA Ops:
  0.7 0.0 copy-start.15
  0.7 0.0 copy-start.13
  0.7 0.0 copy-start
  0.7 0.6 copy-done.12
  1.3 0.0 copy-done.11
  1.3 0.0 copy-done.10
  1.3 0.6 shard_map.123.after.refs_0_.ids.refs_4_
  2.0 2.9 %collective-permute-start.4 = (s32[16,256]{1,0:T(8,128)}, s32[16,256]{1,0:T(8,128)}, u32[]{:S(2)}, u32[]{:S(2)}) collective-permute-start(s32[16,256]{1,0:T(8,128)} %shard_map.123.after.refs_0_.ids.refs_4_), channel_id=1, source_target_pairs={{0,2},{2,0},{1,3},{3,1},{4,6},{6,4},{5,7},{7,5},{8,10},{10,8},{9,1... | collective-permute-start | bytes 49160 | tf_op jit(solution)/shard_map/ppermute | solution.py:356
  4.9 1.6 %collective-permute-start.2 = (s32[16,256]{1,0:T(8,128)}, s32[16,256]{1,0:T(8,128)S(1)}, u32[]{:S(2)}, u32[]{:S(2)}) collective-permute-start(s32[16,256]{1,0:T(8,128)} %shard_map.123.after.refs_0_.ids.refs_4_), channel_id=1, source_target_pairs={{0,4},{4,0},{8,12},{12,8},{1,5},{5,1},{9,13},{13,9},{2,6},{6,2},{1... | collective-permute-start | bytes 49160 | tf_op jit(solution)/shard_map/ppermute | solution.py:356
  7.2 0.9 %shard_map.124 = (bf16[17,64,128]{2,1,0:T(8,128)(2,1)S(1)}, bf16[17,64,128]{2,1,0:T(8,128)(2,1)S(1)}, f32[16,128]{1,0:T(8,128)S(1)}, f32[16,128]{1,0:T(8,128)S(1...) custom-call(s32[1]{0:T(128)S(6)} %copy.13.count, s32[288]{0:T(512)S(1)} %copy-done.19, s32[288]{0:T(512)S(1)} %copy-done.20, ...), custom_call_target="tpu_custom_call" | custom-call | flops 603979776 | bytes 9437184 | tf_op jit(solution)/shard_map/pallas_call | solution.py:23
  8.1 0.0 copy-start.6
  8.1 0.0 copy-start.4
  8.2 2.2 %shard_map.125.refs_0_.mine = f32[16,64,128]{2,1,0:T(8,128)S(1)} custom-call(s32[4,384]{1,0:T(4,128)S(1)} %get-tuple-element.28.order, bf16[288,128,128]{2,1,0:T(8,128)(2,1)S(1)} %copy-done, bf16[17,64,128]{2,1,0:T(8,128)(2,1)S(1)} %get-tuple-element.33.source, s32[16,256]{1,0:T(8,128)} %shard_map.123.after.refs_0_.ids.refs_4_), custom_call_target="tpu_custom_call" | custom-call | flops 603979776 | bytes 9437184 | tf_op jit(solution)/shard_map/pallas_call | solution.py:23
  10.4 0.1 collective-permute-start.1
  10.5 0.7 %shard_map.127 = s32[16,256]{1,0:T(8,128)S(1)} custom-call(s32[16,256]{1,0:T(8,128)} %shard_map.123.after.refs_0_.ids.refs_4_, s32[16,256]{1,0:T(8,128)S(1)} %collective-permute-done.2.refs_1_.refs_5_), custom_call_target="tpu_custom_call" | custom-call | tf_op jit(solution)/shard_map/pallas_call | solution.py:23
  11.2 2.6 %collective-permute-start.3 = (s32[16,256]{1,0:T(8,128)S(1)}, s32[16,256]{1,0:T(8,128)S(1)}, u32[]{:S(2)}, u32[]{:S(2)}) collective-permute-start(s32[16,256]{1,0:T(8,128)S(1)} %shard_map.127), channel_id=1, source_target_pairs={{0,8},{4,12},{8,0},{12,4},{1,9},{5,13},{9,1},{13,5},{2,10},{6,14},... | collective-permute-start | bytes 49160 | tf_op jit(solution)/shard_map/ppermute | solution.py:356
  13.8 3.1 %shard_map.126.mine = f32[16,64,128]{2,1,0:T(8,128)S(1)} custom-call(s32[4,384]{1,0:T(4,128)S(1)} %get-tuple-element.31.order, bf16[288,128,128]{2,1,0:T(8,128)(2,1)S(1)} %copy-done, bf16[17,64,128]{2,1,0:T(8,128)(2,1)S(1)} %get-tuple-element.32.source, f32[16,64,128]{2,1,0:T(8,128)S(1)} %shard_map.125.refs_0_.mine), custom_call_target="tpu_custom_call" | custom-call | flops 99999997952 | bytes 9437184 | tf_op jit(solution)/shard_map/pallas_call | solution.py:23
  16.9 0.1 collective-permute-start
  17.0 0.0 copy-start.14
  17.0 0.0 copy-start.16
  17.1 2.0 %shard_map.128 = (f32[64,256]{1,0:T(8,128)S(1)}, f32[64,256]{1,0:T(8,128)S(1)}, f32[64,256]{1,0:T(8,128)S(1)}, f32[64,256]{1,0:T(8,128)S(1)}) custom-call(f32[16,64,128]{2,1,0:T(8,128)S(1)} %shard_map.125.refs_0_.mine, f32[16,64,128]{2,1,0:T(8,128)S(1)} %collective-permute-done.1.other, f32[16,128]{1,0:T(8,128)S(1)} %get-tuple-element.30.scale.target_scale.source_scale, ...), custom_call_target="tpu_custom_call" | custom-call | flops 99999997952 | bytes 1048576 | tf_op jit(solution)/shard_map/pallas_call | solution.py:23
  19.1 1.5 %collective-permute-start.6 = (f32[64,256]{1,0:T(8,128)S(1)}, f32[64,256]{1,0:T(8,128)S(1)}, u32[]{:S(2)}, u32[]{:S(2)}) collective-permute-start(f32[64,256]{1,0:T(8,128)S(1)} %get-tuple-element.38), channel_id=1, source_target_pairs={{0,8},{4,12},{8,0},{12,4},{1,9},{5,13},{9,1},{13,5},{2,10},{6,14},... | collective-permute-start | bytes 196616 | tf_op jit(solution)/shard_map/ppermute | solution.py:356
  20.5 0.8 %collective-permute-start.7 = (f32[64,256]{1,0:T(8,128)S(1)}, f32[64,256]{1,0:T(8,128)S(1)}, u32[]{:S(2)}, u32[]{:S(2)}) collective-permute-start(f32[64,256]{1,0:T(8,128)S(1)} %get-tuple-element.39), channel_id=1, source_target_pairs={{0,12},{4,8},{8,4},{12,0},{1,13},{5,9},{9,5},{13,1},{2,14},{6,10},... | collective-permute-start | bytes 196616 | tf_op jit(solution)/shard_map/ppermute | solution.py:356
  21.3 1.3 %collective-permute-start.8 = (f32[64,256]{1,0:T(8,128)S(1)}, f32[64,256]{1,0:T(8,128)S(1)}, u32[]{:S(2)}, u32[]{:S(2)}) collective-permute-start(f32[64,256]{1,0:T(8,128)S(1)} %get-tuple-element.40), channel_id=1, source_target_pairs={{0,4},{4,0},{8,12},{12,8},{1,5},{5,1},{9,13},{13,9},{2,6},{6,2},{1... | collective-permute-start | bytes 196616 | tf_op jit(solution)/shard_map/ppermute | solution.py:356
  22.6 1.3 %shard_map.129 = (f32[64,256]{1,0:T(8,128)S(1)}, f32[64,256]{1,0:T(8,128)S(1)}) custom-call(f32[16,64,128]{2,1,0:T(8,128)S(1)} %shard_map.126.mine, f32[16,64,128]{2,1,0:T(8,128)S(1)} %collective-permute-done.other, f32[16,128]{1,0:T(8,128)S(1)} %get-tuple-element.29.scale.source_scale.target_scale, f32[64,256]{1,0:T(8,128)S(1)} %get-tuple-element.34.after.refs_3_, ...), custom_call_target="tpu_custom_call" | custom-call | bytes 1048576 | tf_op jit(solution)/shard_map/pallas_call | solution.py:23
  24.0 2.2 %collective-permute-start.5 = (f32[64,256]{1,0:T(8,128)S(1)}, f32[64,256]{1,0:T(8,128)S(1)}, u32[]{:S(2)}, u32[]{:S(2)}) collective-permute-start(f32[64,256]{1,0:T(8,128)S(1)} %get-tuple-element.36), channel_id=1, source_target_pairs={{0,2},{2,0},{1,3},{3,1},{4,6},{6,4},{5,7},{7,5},{8,10},{10,8},{9,1... | collective-permute-start | bytes 196616 | tf_op jit(solution)/shard_map/ppermute | solution.py:356
  26.2 1.2 %shard_map.130 = (f32[64,256]{1,0:T(8,128)S(1)}, f32[64,256]{1,0:T(8,128)S(1)}) custom-call(bf16[64,2048]{1,0:T(8,128)(2,1)S(1)} %copy-done.14, bf16[64,2048]{1,0:T(8,128)(2,1)S(1)} %copy-done.16, s32[16,256]{1,0:T(8,128)} %shard_map.123.after.refs_0_.ids.refs_4_), custom_call_target="tpu_custom_call" | custom-call | flops 268435456 | bytes 524288 | tf_op jit(solution)/shard_map/pallas_call | solution.py:23
  27.4 0.4 collective-permute-done.8.refs_6_
  27.8 0.6 collective-permute-done.5.refs_1_
  28.4 0.8 %shard_map.131 = (f32[72,256]{1,0:T(8,128)S(1)}, f32[64,256]{1,0:T(8,128)S(1)}) custom-call(s32[16,256]{1,0:T(8,128)} %shard_map.123.after.refs_0_.ids.refs_4_, f32[64,256]{1,0:T(8,128)S(1)} %get-tuple-element.35.refs_0_, f32[64,256]{1,0:T(8,128)S(1)} %collective-permute-done.5.refs_1_, f32[64,256]{1,0:T(8,128)S(1)} %get-tuple-element.37.refs_2_, ...), custom_call_target="tpu_custom_call" | custom-call | bytes 655360 | tf_op jit(solution)/shard_map/pallas_call | solution.py:23
  29.2 0.9 %collective-permute-start.11 = (f32[72,256]{1,0:T(8,128)S(1)}, f32[72,256]{1,0:T(8,128)S(1)}, u32[]{:S(2)}, u32[]{:S(2)}) collective-permute-start(f32[72,256]{1,0:T(8,128)S(1)} %get-tuple-element.42.refs_0_), channel_id=1, source_target_pairs={{0,3},{1,2},{2,1},{3,0},{4,7},{5,6},{6,5},{7,4},{8,11},{9,10},{10,... | collective-permute-start | bytes 221192 | tf_op jit(solution)/shard_map/ppermute | solution.py:454
  30.1 1.2 %collective-permute-start.10 = (f32[72,256]{1,0:T(8,128)S(1)}, f32[72,256]{1,0:T(8,128)S(1)}, u32[]{:S(2)}, u32[]{:S(2)}) collective-permute-start(f32[72,256]{1,0:T(8,128)S(1)} %get-tuple-element.42.refs_0_), channel_id=1, source_target_pairs={{0,2},{2,0},{1,3},{3,1},{4,6},{6,4},{5,7},{7,5},{8,10},{10,8},{9,1... | collective-permute-start | bytes 221192 | tf_op jit(solution)/shard_map/ppermute | solution.py:356
  31.4 0.0 collective-permute-start.9
  31.4 1.9 %collective-permute-start.14 = (f32[64,256]{1,0:T(8,128)S(1)}, f32[64,256]{1,0:T(8,128)S(1)}, u32[]{:S(2)}, u32[]{:S(2)}) collective-permute-start(f32[64,256]{1,0:T(8,128)S(1)} %get-tuple-element.45.refs_0_), channel_id=1, source_target_pairs={{0,8},{4,12},{8,0},{12,4},{1,9},{5,13},{9,1},{13,5},{2,10},{6,14},... | collective-permute-start | bytes 196616 | tf_op jit(solution)/shard_map/ppermute | solution.py:356
  33.3 2.5 %collective-permute-start.13 = (f32[64,256]{1,0:T(8,128)S(1)}, f32[64,256]{1,0:T(8,128)S(1)}, u32[]{:S(2)}, u32[]{:S(2)}) collective-permute-start(f32[64,256]{1,0:T(8,128)S(1)} %get-tuple-element.45.refs_0_), channel_id=1, source_target_pairs={{0,12},{4,8},{8,4},{12,0},{1,13},{5,9},{9,5},{13,1},{2,14},{6,10},... | collective-permute-start | bytes 196616 | tf_op jit(solution)/shard_map/ppermute | solution.py:356
  35.8 3.8 %shard_map.132 = (f32[16,64,128]{2,1,0:T(8,128)S(1)}, f32[16,32,128]{2,1,0:T(8,128)S(1)}, f32[16,32,128]{2,1,0:T(8,128)S(1)}) custom-call(s32[4,384]{1,0:T(4,128)S(1)} %copy-done.7, f32[16,128]{1,0:T(8,128)S(1)} %get-tuple-element.29.scale.source_scale.target_scale, f32[16,128]{1,0:T(8,128)S(1)} %get-tuple-element.30.scale.target_scale.source_scale, ...), custom_call_target="tpu_custom_call" | custom-call | flops 603979776 | bytes 9437184 | tf_op jit(solution)/shard_map/pallas_call | solution.py:23
  39.6 0.1 collective-permute-start.16
  39.7 0.2 collective-permute-done.14.refs_3_
  39.9 0.2 collective-permute-done.13.refs_2_
  40.1 0.9 %collective-permute-done.12.refs_1_ = f32[64,256]{1,0:T(8,128)S(1)} collective-permute-done((f32[64,256]{1,0:T(8,128)S(1)}, f32[64,256]{1,0:T(8,128)S(1)}, u32[]{:S(2)}, u32[]{:S(2)}) %collective-permute-start.12) | collective-permute-done | bytes 65568 | tf_op jit(solution)/shard_map/ppermute | solution.py:356
  41.0 2.2 %shard_map.133.after.mine = f32[16,64,128]{2,1,0:T(8,128)S(1)} custom-call(f32[16,32,128]{2,1,0:T(8,128)S(1)} %get-tuple-element.44.after, f32[64,256]{1,0:T(8,128)S(1)} %get-tuple-element.45.refs_0_, f32[64,256]{1,0:T(8,128)S(1)} %collective-permute-done.12.refs_1_, f32[64,256]{1,0:T(8,128)S(1)} %collective-permute-done.13.refs_2_, ...), custom_call_target="tpu_custom_call" | custom-call | flops 99999997952 | tf_op jit(solution)/shard_map/pallas_call | solution.py:23
  43.3 0.1 collective-permute-start.15
  43.4 0.0 copy-start.1
  43.4 0.0 copy-start.5
  43.5 1.1 %collective-permute-start.17 = (f32[4,32,128]{2,1,0:T(8,128)S(1)}, f32[4,32,128]{2,1,0:T(8,128)S(1)}, u32[]{:S(2)}, u32[]{:S(2)}) collective-permute-start(f32[4,32,128]{2,1,0:T(8,128)S(1)} %get-tuple-element.49), channel_id=1, source_target_pairs={{0,8},{4,12},{8,0},{12,4},{1,9},{5,13},{9,1},{13,5},{2,10},{6,14},... | collective-permute-start | bytes 196616 | tf_op jit(solution)/shard_map/ppermute | solution.py:356
  44.6 2.0 %collective-permute-start.18 = (f32[4,32,128]{2,1,0:T(8,128)S(1)}, f32[4,32,128]{2,1,0:T(8,128)S(1)}, u32[]{:S(2)}, u32[]{:S(2)}) collective-permute-start(f32[4,32,128]{2,1,0:T(8,128)S(1)} %get-tuple-element.50), channel_id=1, source_target_pairs={{0,12},{4,8},{8,4},{12,0},{1,13},{5,9},{9,5},{13,1},{2,14},{6,10},... | collective-permute-start | bytes 196616 | tf_op jit(solution)/shard_map/ppermute | solution.py:356
  46.5 0.5 collective-permute-start.19
  47.0 0.0 copy-done.1
  47.1 3.3 %shard_map.135 = (f32[16,64,128]{2,1,0:T(8,128)S(1)}, f32[16,32,128]{2,1,0:T(8,128)S(1)}, f32[16,32,128]{2,1,0:T(8,128)S(1)}) custom-call(s32[4,384]{1,0:T(4,128)S(1)} %copy-done.9, f32[16,64,128]{2,1,0:T(8,128)S(1)} %shard_map.133.after.mine, f32[16,64,128]{2,1,0:T(8,128)S(1)} %collective-permute-done.15.other, f32[16,128]{1,0:T(8,128)S(1)} %copy-done.5, ...), custom_call_target="tpu_custom_call" | custom-call | flops 603979776 | bytes 9437184 | tf_op jit(solution)/shard_map/pallas_call | solution.py:23
  50.3 1.4 %collective-permute-done.17.refs_2_ = f32[4,32,128]{2,1,0:T(8,128)S(1)} collective-permute-done((f32[4,32,128]{2,1,0:T(8,128)S(1)}, f32[4,32,128]{2,1,0:T(8,128)S(1)}, u32[]{:S(2)}, u32[]{:S(2)}) %collective-permute-start.17) | collective-permute-done | bytes 65568 | tf_op jit(solution)/shard_map/ppermute | solution.py:356
  51.8 1.3 %collective-permute-done.19.refs_4_ = f32[4,32,128]{2,1,0:T(8,128)S(1)} collective-permute-done((f32[4,32,128]{2,1,0:T(8,128)S(1)}, f32[4,32,128]{2,1,0:T(8,128)S(1)}, u32[]{:S(2)}, u32[]{:S(2)}) %collective-permute-start.19) | collective-permute-done | bytes 65568 | tf_op jit(solution)/shard_map/ppermute | solution.py:356
  53.1 0.1 collective-permute-start.23
  53.1 0.7 %collective-permute-start.20 = (f32[4,32,128]{2,1,0:T(8,128)S(1)}, f32[4,32,128]{2,1,0:T(8,128)S(1)}, u32[]{:S(2)}, u32[]{:S(2)}) collective-permute-start(f32[4,32,128]{2,1,0:T(8,128)S(1)} %shard_map.136.refs_0_), channel_id=1, source_target_pairs={{0,4},{4,0},{8,12},{12,8},{1,5},{5,1},{9,13},{13,9},{2,6},{6,2},{1... | collective-permute-start | bytes 196616 | tf_op jit(solution)/shard_map/ppermute | solution.py:356
  53.9 1.5 %collective-permute-start.21 = (f32[4,32,128]{2,1,0:T(8,128)S(1)}, f32[4,32,128]{2,1,0:T(8,128)S(1)}, u32[]{:S(2)}, u32[]{:S(2)}) collective-permute-start(f32[4,32,128]{2,1,0:T(8,128)S(1)} %shard_map.136.refs_0_), channel_id=1, source_target_pairs={{0,8},{4,12},{8,0},{12,4},{1,9},{5,13},{9,1},{13,5},{2,10},{6,14},... | collective-permute-start | bytes 196616 | tf_op jit(solution)/shard_map/ppermute | solution.py:356
  55.4 1.7 %collective-permute-start.24 = (f32[16,32,128]{2,1,0:T(8,128)S(1)}, f32[16,32,128]{2,1,0:T(8,128)S(1)}, u32[]{:S(2)}, u32[]{:S(2)}) collective-permute-start(f32[16,32,128]{2,1,0:T(8,128)S(1)} %shard_map.140.refs_1_), channel_id=1, source_target_pairs={{0,2},{2,0},{1,3},{3,1},{4,6},{6,4},{5,7},{7,5},{8,10},{10,8},{9,1... | collective-permute-start | bytes 786440 | tf_op jit(solution)/shard_map/ppermute | solution.py:356
  57.1 1.3 %collective-permute-done.20.values = f32[4,32,128]{2,1,0:T(8,128)S(1)} collective-permute-done((f32[4,32,128]{2,1,0:T(8,128)S(1)}, f32[4,32,128]{2,1,0:T(8,128)S(1)}, u32[]{:S(2)}, u32[]{:S(2)}) %collective-permute-start.20) | collective-permute-done | bytes 65568 | tf_op jit(solution)/shard_map/ppermute | solution.py:356
  58.5 1.6 %collective-permute-start.22 = (f32[4,32,128]{2,1,0:T(8,128)S(1)}, f32[4,32,128]{2,1,0:T(8,128)S(1)}, u32[]{:S(2)}, u32[]{:S(2)}) collective-permute-start(f32[4,32,128]{2,1,0:T(8,128)S(1)} %shard_map.137.refs_1_), channel_id=1, source_target_pairs={{0,8},{4,12},{8,0},{12,4},{1,9},{5,13},{9,1},{13,5},{2,10},{6,14},... | collective-permute-start | bytes 196616 | tf_op jit(solution)/shard_map/ppermute | solution.py:356
  60.1 0.3 collective-permute-done.21.refs_2_
  60.4 3.5 %collective-permute-done.22.refs_3_ = f32[4,32,128]{2,1,0:T(8,128)S(1)} collective-permute-done((f32[4,32,128]{2,1,0:T(8,128)S(1)}, f32[4,32,128]{2,1,0:T(8,128)S(1)}, u32[]{:S(2)}, u32[]{:S(2)}) %collective-permute-start.22) | collective-permute-done | bytes 65568 | tf_op jit(solution)/shard_map/ppermute | solution.py:356
  64.0 0.1 collective-permute-start.26
  64.1 0.5 collective-permute-start.25
  64.6 0.9 %collective-permute-done.26.item_other = f32[4,4,32,128]{3,2,1,0:T(8,128)S(1)} collective-permute-done((f32[4,4,32,128]{3,2,1,0:T(8,128)S(1)}, f32[4,4,32,128]{3,2,1,0:T(8,128)S(1)}, u32[]{:S(2)}, u32[]{:S(2)}) %collective-permute-start.26) | collective-permute-done | bytes 262176 | tf_op jit(solution)/shard_map/ppermute | solution.py:356
  65.6 0.4 collective-permute-done.25.user_other
  65.9 1.1 %shard_map.142 = (f32[64,2048]{1,0:T(8,128)}, f32[64,2048]{1,0:T(8,128)}) custom-call(f32[16,64,128]{2,1,0:T(8,128)S(1)} %get-tuple-element.43.user_half_grad, f32[16,32,128]{2,1,0:T(8,128)S(1)} %shard_map.141.user_mine, f32[16,32,128]{2,1,0:T(8,128)S(1)} %collective-permute-done.25.user_other, f32[16,64,128]{2,1,0:T(8,128)S(1)} %get-tuple-element.53.item_half_grad, ...), custom_call_target="tpu_custom_call" | custom-call | bytes 3145728 | tf_op jit(solution)/shard_map/pallas_call | solution.py:23
  (53 shorter events, 0.3 us)
Async XLA Ops:
  0.6 0.7 %copy-start.12 = (s32[256]{0:T(256)S(1)}, s32[256]{0:T(256)}, u32[]{:S(2)}) copy-start(s32[256]{0:T(256)} %param.21) | copy-start | bytes 3076
  0.6 0.7 %copy-start.11 = (s32[256]{0:T(256)S(1)}, s32[256]{0:T(256)}, u32[]{:S(2)}) copy-start(s32[256]{0:T(256)} %param.20) | copy-start | bytes 3076
  0.7 0.7 %copy-start.10 = (s32[256]{0:T(256)S(1)}, s32[256]{0:T(256)}, u32[]{:S(2)}) copy-start(s32[256]{0:T(256)} %param.19) | copy-start | bytes 3076
  0.7 6.5 %copy-start.15 = (bf16[64,2048]{1,0:T(8,128)(2,1)S(1)}, bf16[64,2048]{1,0:T(8,128)(2,1)}, u32[]{:S(2)}) copy-start(bf16[64,2048]{1,0:T(8,128)(2,1)} %item_emb.3) | copy-start | bytes 786436
  0.7 6.5 %copy-start.13 = (bf16[64,2048]{1,0:T(8,128)(2,1)S(1)}, bf16[64,2048]{1,0:T(8,128)(2,1)}, u32[]{:S(2)}) copy-start(bf16[64,2048]{1,0:T(8,128)(2,1)} %user_emb.3) | copy-start | bytes 786436
  0.7 6.5 %copy-start.20 = (s32[288]{0:T(512)S(1)}, s32[288]{0:T(512)}, u32[]{:S(2)}) copy-start(s32[288]{0:T(512)} %columns.1) | copy-start | bytes 3460
  0.7 6.5 %copy-start.19 = (s32[288]{0:T(512)S(1)}, s32[288]{0:T(512)}, u32[]{:S(2)}) copy-start(s32[288]{0:T(512)} %rows.1) | copy-start | bytes 3460
  0.7 6.5 %copy-start.18 = (s32[2048]{0:T(1024)S(1)}, s32[2048]{0:T(1024)}, u32[]{:S(2)}) copy-start(s32[2048]{0:T(1024)} %param.14) | copy-start | bytes 24580
  0.7 6.5 %copy-start.17 = (s32[2048]{0:T(1024)S(1)}, s32[2048]{0:T(1024)}, u32[]{:S(2)}) copy-start(s32[2048]{0:T(1024)} %param.13) | copy-start | bytes 24580
  0.7 7.4 %copy-start = (bf16[288,128,128]{2,1,0:T(8,128)(2,1)S(1)}, bf16[288,128,128]{2,1,0:T(8,128)(2,1)}, u32[]{:S(2)}) copy-start(bf16[288,128,128]{2,1,0:T(8,128)(2,1)} %vals.7) | copy-start | bytes 28311556
  2.0 20.7 %collective-permute-start.4 = (s32[16,256]{1,0:T(8,128)}, s32[16,256]{1,0:T(8,128)}, u32[]{:S(2)}, u32[]{:S(2)}) collective-permute-start(s32[16,256]{1,0:T(8,128)} %shard_map.123.after.refs_0_.ids.refs_4_), channel_id=1, source_target_pairs={{0,2},{2,0},{1,3},{3,1},{4,6},{6,4},{5,7},{7,5},{8,10},{10,8},{9,1... | collective-permute-start | bytes 49160 | tf_op jit(solution)/shard_map/ppermute | solution.py:356
  4.9 5.6 %collective-permute-start.2 = (s32[16,256]{1,0:T(8,128)}, s32[16,256]{1,0:T(8,128)S(1)}, u32[]{:S(2)}, u32[]{:S(2)}) collective-permute-start(s32[16,256]{1,0:T(8,128)} %shard_map.123.after.refs_0_.ids.refs_4_), channel_id=1, source_target_pairs={{0,4},{4,0},{8,12},{12,8},{1,5},{5,1},{9,13},{13,9},{2,6},{6,2},{1... | collective-permute-start | bytes 49160 | tf_op jit(solution)/shard_map/ppermute | solution.py:356
  8.1 8.8 %copy-start.6 = (s32[4,384]{1,0:T(4,128)}, s32[4,384]{1,0:T(4,128)S(1)}, u32[]{:S(2)}) copy-start(s32[4,384]{1,0:T(4,128)S(1)} %get-tuple-element.28.order) | copy-start | bytes 18436
  8.1 8.8 %copy-start.8 = (s32[4,384]{1,0:T(4,128)}, s32[4,384]{1,0:T(4,128)S(1)}, u32[]{:S(2)}) copy-start(s32[4,384]{1,0:T(4,128)S(1)} %get-tuple-element.31.order) | copy-start | bytes 18436
  8.1 27.7 %copy-start.2 = (f32[16,128]{1,0:T(8,128)}, f32[16,128]{1,0:T(8,128)S(1)}, u32[]{:S(2)}) copy-start(f32[16,128]{1,0:T(8,128)S(1)} %get-tuple-element.29.scale.source_scale.target_scale) | copy-start | bytes 24580
  8.1 27.7 %copy-start.4 = (f32[16,128]{1,0:T(8,128)}, f32[16,128]{1,0:T(8,128)S(1)}, u32[]{:S(2)}) copy-start(f32[16,128]{1,0:T(8,128)S(1)} %get-tuple-element.30.scale.target_scale.source_scale) | copy-start | bytes 24580
  10.4 6.6 %collective-permute-start.1 = (f32[16,64,128]{2,1,0:T(8,128)S(1)}, f32[16,64,128]{2,1,0:T(8,128)S(1)}, u32[]{:S(2)}, u32[]{:S(2)}) collective-permute-start(f32[16,64,128]{2,1,0:T(8,128)S(1)} %shard_map.125.refs_0_.mine), channel_id=1, source_target_pairs={{0,1},{1,0},{2,3},{3,2},{4,5},{5,4},{6,7},{7,6},{8,9},{9,8},{10,11... | collective-permute-start | bytes 1572872 | tf_op jit(solution)/shard_map/ppermute | solution.py:356
  11.2 5.8 %collective-permute-start.3 = (s32[16,256]{1,0:T(8,128)S(1)}, s32[16,256]{1,0:T(8,128)S(1)}, u32[]{:S(2)}, u32[]{:S(2)}) collective-permute-start(s32[16,256]{1,0:T(8,128)S(1)} %shard_map.127), channel_id=1, source_target_pairs={{0,8},{4,12},{8,0},{12,4},{1,9},{5,13},{9,1},{13,5},{2,10},{6,14},... | collective-permute-start | bytes 49160 | tf_op jit(solution)/shard_map/ppermute | solution.py:356
  16.9 5.7 %collective-permute-start = (f32[16,64,128]{2,1,0:T(8,128)S(1)}, f32[16,64,128]{2,1,0:T(8,128)S(1)}, u32[]{:S(2)}, u32[]{:S(2)}) collective-permute-start(f32[16,64,128]{2,1,0:T(8,128)S(1)} %shard_map.126.mine), channel_id=1, source_target_pairs={{0,1},{1,0},{2,3},{3,2},{4,5},{5,4},{6,7},{7,6},{8,9},{9,8},{10,11... | collective-permute-start | bytes 1572872 | tf_op jit(solution)/shard_map/ppermute | solution.py:356
  17.0 9.2 %copy-start.14 = (bf16[64,2048]{1,0:T(8,128)(2,1)S(1)}, bf16[64,2048]{1,0:T(8,128)(2,1)}, u32[]{:S(2)}) copy-start(bf16[64,2048]{1,0:T(8,128)(2,1)} %user_emb.3) | copy-start | bytes 786436
  17.0 9.1 %copy-start.16 = (bf16[64,2048]{1,0:T(8,128)(2,1)S(1)}, bf16[64,2048]{1,0:T(8,128)(2,1)}, u32[]{:S(2)}) copy-start(bf16[64,2048]{1,0:T(8,128)(2,1)} %item_emb.3) | copy-start | bytes 786436
  17.0 18.8 %copy-start.7 = (s32[4,384]{1,0:T(4,128)S(1)}, s32[4,384]{1,0:T(4,128)}, u32[]{:S(2)}) copy-start(s32[4,384]{1,0:T(4,128)} %copy-done.6) | copy-start | bytes 18436
  19.1 8.3 %collective-permute-start.6 = (f32[64,256]{1,0:T(8,128)S(1)}, f32[64,256]{1,0:T(8,128)S(1)}, u32[]{:S(2)}, u32[]{:S(2)}) collective-permute-start(f32[64,256]{1,0:T(8,128)S(1)} %get-tuple-element.38), channel_id=1, source_target_pairs={{0,8},{4,12},{8,0},{12,4},{1,9},{5,13},{9,1},{13,5},{2,10},{6,14},... | collective-permute-start | bytes 196616 | tf_op jit(solution)/shard_map/ppermute | solution.py:356
  20.5 6.8 %collective-permute-start.7 = (f32[64,256]{1,0:T(8,128)S(1)}, f32[64,256]{1,0:T(8,128)S(1)}, u32[]{:S(2)}, u32[]{:S(2)}) collective-permute-start(f32[64,256]{1,0:T(8,128)S(1)} %get-tuple-element.39), channel_id=1, source_target_pairs={{0,12},{4,8},{8,4},{12,0},{1,13},{5,9},{9,5},{13,1},{2,14},{6,10},... | collective-permute-start | bytes 196616 | tf_op jit(solution)/shard_map/ppermute | solution.py:356
  21.3 6.5 %collective-permute-start.8 = (f32[64,256]{1,0:T(8,128)S(1)}, f32[64,256]{1,0:T(8,128)S(1)}, u32[]{:S(2)}, u32[]{:S(2)}) collective-permute-start(f32[64,256]{1,0:T(8,128)S(1)} %get-tuple-element.40), channel_id=1, source_target_pairs={{0,4},{4,0},{8,12},{12,8},{1,5},{5,1},{9,13},{13,9},{2,6},{6,2},{1... | collective-permute-start | bytes 196616 | tf_op jit(solution)/shard_map/ppermute | solution.py:356
  24.0 4.5 %collective-permute-start.5 = (f32[64,256]{1,0:T(8,128)S(1)}, f32[64,256]{1,0:T(8,128)S(1)}, u32[]{:S(2)}, u32[]{:S(2)}) collective-permute-start(f32[64,256]{1,0:T(8,128)S(1)} %get-tuple-element.36), channel_id=1, source_target_pairs={{0,2},{2,0},{1,3},{3,1},{4,6},{6,4},{5,7},{7,5},{8,10},{10,8},{9,1... | collective-permute-start | bytes 196616 | tf_op jit(solution)/shard_map/ppermute | solution.py:356
  29.2 6.6 %collective-permute-start.11 = (f32[72,256]{1,0:T(8,128)S(1)}, f32[72,256]{1,0:T(8,128)S(1)}, u32[]{:S(2)}, u32[]{:S(2)}) collective-permute-start(f32[72,256]{1,0:T(8,128)S(1)} %get-tuple-element.42.refs_0_), channel_id=1, source_target_pairs={{0,3},{1,2},{2,1},{3,0},{4,7},{5,6},{6,5},{7,4},{8,11},{9,10},{10,... | collective-permute-start | bytes 221192 | tf_op jit(solution)/shard_map/ppermute | solution.py:454
  30.1 5.7 %collective-permute-start.10 = (f32[72,256]{1,0:T(8,128)S(1)}, f32[72,256]{1,0:T(8,128)S(1)}, u32[]{:S(2)}, u32[]{:S(2)}) collective-permute-start(f32[72,256]{1,0:T(8,128)S(1)} %get-tuple-element.42.refs_0_), channel_id=1, source_target_pairs={{0,2},{2,0},{1,3},{3,1},{4,6},{6,4},{5,7},{7,5},{8,10},{10,8},{9,1... | collective-permute-start | bytes 221192 | tf_op jit(solution)/shard_map/ppermute | solution.py:356
  31.4 4.4 %collective-permute-start.9 = (f32[72,256]{1,0:T(8,128)S(1)}, f32[72,256]{1,0:T(8,128)S(1)}, u32[]{:S(2)}, u32[]{:S(2)}) collective-permute-start(f32[72,256]{1,0:T(8,128)S(1)} %get-tuple-element.42.refs_0_), channel_id=1, source_target_pairs={{0,1},{1,0},{2,3},{3,2},{4,5},{5,4},{6,7},{7,6},{8,9},{9,8},{10,11... | collective-permute-start | bytes 221192 | tf_op jit(solution)/shard_map/ppermute | solution.py:356
  31.4 8.5 %collective-permute-start.14 = (f32[64,256]{1,0:T(8,128)S(1)}, f32[64,256]{1,0:T(8,128)S(1)}, u32[]{:S(2)}, u32[]{:S(2)}) collective-permute-start(f32[64,256]{1,0:T(8,128)S(1)} %get-tuple-element.45.refs_0_), channel_id=1, source_target_pairs={{0,8},{4,12},{8,0},{12,4},{1,9},{5,13},{9,1},{13,5},{2,10},{6,14},... | collective-permute-start | bytes 196616 | tf_op jit(solution)/shard_map/ppermute | solution.py:356
  33.3 6.8 %collective-permute-start.13 = (f32[64,256]{1,0:T(8,128)S(1)}, f32[64,256]{1,0:T(8,128)S(1)}, u32[]{:S(2)}, u32[]{:S(2)}) collective-permute-start(f32[64,256]{1,0:T(8,128)S(1)} %get-tuple-element.45.refs_0_), channel_id=1, source_target_pairs={{0,12},{4,8},{8,4},{12,0},{1,13},{5,9},{9,5},{13,1},{2,14},{6,10},... | collective-permute-start | bytes 196616 | tf_op jit(solution)/shard_map/ppermute | solution.py:356
  35.8 5.3 %collective-permute-start.12 = (f32[64,256]{1,0:T(8,128)S(1)}, f32[64,256]{1,0:T(8,128)S(1)}, u32[]{:S(2)}, u32[]{:S(2)}) collective-permute-start(f32[64,256]{1,0:T(8,128)S(1)} %get-tuple-element.45.refs_0_), channel_id=1, source_target_pairs={{0,4},{4,0},{8,12},{12,8},{1,5},{5,1},{9,13},{13,9},{2,6},{6,2},{1... | collective-permute-start | bytes 196616 | tf_op jit(solution)/shard_map/ppermute | solution.py:356
  39.6 3.8 %collective-permute-start.16 = (f32[16,32,128]{2,1,0:T(8,128)S(1)}, f32[16,32,128]{2,1,0:T(8,128)S(1)}, u32[]{:S(2)}, u32[]{:S(2)}) collective-permute-start(f32[16,32,128]{2,1,0:T(8,128)S(1)} %get-tuple-element.44.after), channel_id=1, source_target_pairs={{0,1},{1,0},{2,3},{3,2},{4,5},{5,4},{6,7},{7,6},{8,9},{9,8},{10,11... | collective-permute-start | bytes 786440 | tf_op jit(solution)/shard_map/ppermute | solution.py:356
  43.3 3.7 %collective-permute-start.15 = (f32[16,64,128]{2,1,0:T(8,128)S(1)}, f32[16,64,128]{2,1,0:T(8,128)S(1)}, u32[]{:S(2)}, u32[]{:S(2)}) collective-permute-start(f32[16,64,128]{2,1,0:T(8,128)S(1)} %shard_map.133.after.mine), channel_id=1, source_target_pairs={{0,1},{1,0},{2,3},{3,2},{4,5},{5,4},{6,7},{7,6},{8,9},{9,8},{10,11... | collective-permute-start | bytes 1572872 | tf_op jit(solution)/shard_map/ppermute | solution.py:356
  43.4 3.7 %copy-start.1 = (bf16[288,128,128]{2,1,0:T(8,128)(2,1)S(1)}, bf16[288,128,128]{2,1,0:T(8,128)(2,1)}, u32[]{:S(2)}) copy-start(bf16[288,128,128]{2,1,0:T(8,128)(2,1)} %vals.7) | copy-start | bytes 28311556
  43.4 3.7 %copy-start.3 = (f32[16,128]{1,0:T(8,128)S(1)}, f32[16,128]{1,0:T(8,128)}, u32[]{:S(2)}) copy-start(f32[16,128]{1,0:T(8,128)} %copy-done.2) | copy-start | bytes 24580
  43.4 3.7 %copy-start.5 = (f32[16,128]{1,0:T(8,128)S(1)}, f32[16,128]{1,0:T(8,128)}, u32[]{:S(2)}) copy-start(f32[16,128]{1,0:T(8,128)} %copy-done.4) | copy-start | bytes 24580
  43.4 3.7 %copy-start.9 = (s32[4,384]{1,0:T(4,128)S(1)}, s32[4,384]{1,0:T(4,128)}, u32[]{:S(2)}) copy-start(s32[4,384]{1,0:T(4,128)} %copy-done.8) | copy-start | bytes 18436
  43.5 8.3 %collective-permute-start.17 = (f32[4,32,128]{2,1,0:T(8,128)S(1)}, f32[4,32,128]{2,1,0:T(8,128)S(1)}, u32[]{:S(2)}, u32[]{:S(2)}) collective-permute-start(f32[4,32,128]{2,1,0:T(8,128)S(1)} %get-tuple-element.49), channel_id=1, source_target_pairs={{0,8},{4,12},{8,0},{12,4},{1,9},{5,13},{9,1},{13,5},{2,10},{6,14},... | collective-permute-start | bytes 196616 | tf_op jit(solution)/shard_map/ppermute | solution.py:356
  44.6 7.2 %collective-permute-start.18 = (f32[4,32,128]{2,1,0:T(8,128)S(1)}, f32[4,32,128]{2,1,0:T(8,128)S(1)}, u32[]{:S(2)}, u32[]{:S(2)}) collective-permute-start(f32[4,32,128]{2,1,0:T(8,128)S(1)} %get-tuple-element.50), channel_id=1, source_target_pairs={{0,12},{4,8},{8,4},{12,0},{1,13},{5,9},{9,5},{13,1},{2,14},{6,10},... | collective-permute-start | bytes 196616 | tf_op jit(solution)/shard_map/ppermute | solution.py:356
  46.5 6.5 %collective-permute-start.19 = (f32[4,32,128]{2,1,0:T(8,128)S(1)}, f32[4,32,128]{2,1,0:T(8,128)S(1)}, u32[]{:S(2)}, u32[]{:S(2)}) collective-permute-start(f32[4,32,128]{2,1,0:T(8,128)S(1)} %get-tuple-element.51), channel_id=1, source_target_pairs={{0,4},{4,0},{8,12},{12,8},{1,5},{5,1},{9,13},{13,9},{2,6},{6,2},{1... | collective-permute-start | bytes 196616 | tf_op jit(solution)/shard_map/ppermute | solution.py:356
  53.1 2.3 %collective-permute-start.23 = (f32[16,32,128]{2,1,0:T(8,128)S(1)}, f32[16,32,128]{2,1,0:T(8,128)S(1)}, u32[]{:S(2)}, u32[]{:S(2)}) collective-permute-start(f32[16,32,128]{2,1,0:T(8,128)S(1)} %shard_map.139), channel_id=1, source_target_pairs={{0,1},{1,0},{2,3},{3,2},{4,5},{5,4},{6,7},{7,6},{8,9},{9,8},{10,11... | collective-permute-start | bytes 786440 | tf_op jit(solution)/shard_map/ppermute | solution.py:356
  53.1 5.3 %collective-permute-start.20 = (f32[4,32,128]{2,1,0:T(8,128)S(1)}, f32[4,32,128]{2,1,0:T(8,128)S(1)}, u32[]{:S(2)}, u32[]{:S(2)}) collective-permute-start(f32[4,32,128]{2,1,0:T(8,128)S(1)} %shard_map.136.refs_0_), channel_id=1, source_target_pairs={{0,4},{4,0},{8,12},{12,8},{1,5},{5,1},{9,13},{13,9},{2,6},{6,2},{1... | collective-permute-start | bytes 196616 | tf_op jit(solution)/shard_map/ppermute | solution.py:356
  53.9 6.6 %collective-permute-start.21 = (f32[4,32,128]{2,1,0:T(8,128)S(1)}, f32[4,32,128]{2,1,0:T(8,128)S(1)}, u32[]{:S(2)}, u32[]{:S(2)}) collective-permute-start(f32[4,32,128]{2,1,0:T(8,128)S(1)} %shard_map.136.refs_0_), channel_id=1, source_target_pairs={{0,8},{4,12},{8,0},{12,4},{1,9},{5,13},{9,1},{13,5},{2,10},{6,14},... | collective-permute-start | bytes 196616 | tf_op jit(solution)/shard_map/ppermute | solution.py:356
  55.4 8.7 %collective-permute-start.24 = (f32[16,32,128]{2,1,0:T(8,128)S(1)}, f32[16,32,128]{2,1,0:T(8,128)S(1)}, u32[]{:S(2)}, u32[]{:S(2)}) collective-permute-start(f32[16,32,128]{2,1,0:T(8,128)S(1)} %shard_map.140.refs_1_), channel_id=1, source_target_pairs={{0,2},{2,0},{1,3},{3,1},{4,6},{6,4},{5,7},{7,5},{8,10},{10,8},{9,1... | collective-permute-start | bytes 786440 | tf_op jit(solution)/shard_map/ppermute | solution.py:356
  58.5 5.5 %collective-permute-start.22 = (f32[4,32,128]{2,1,0:T(8,128)S(1)}, f32[4,32,128]{2,1,0:T(8,128)S(1)}, u32[]{:S(2)}, u32[]{:S(2)}) collective-permute-start(f32[4,32,128]{2,1,0:T(8,128)S(1)} %shard_map.137.refs_1_), channel_id=1, source_target_pairs={{0,8},{4,12},{8,0},{12,4},{1,9},{5,13},{9,1},{13,5},{2,10},{6,14},... | collective-permute-start | bytes 196616 | tf_op jit(solution)/shard_map/ppermute | solution.py:356
  64.0 1.6 %collective-permute-start.26 = (f32[4,4,32,128]{3,2,1,0:T(8,128)S(1)}, f32[4,4,32,128]{3,2,1,0:T(8,128)S(1)}, u32[]{:S(2)}, u32[]{:S(2)}) collective-permute-start(f32[4,4,32,128]{3,2,1,0:T(8,128)S(1)} %shard_map.138.refs_0_.item_mine), channel_id=1, source_target_pairs={{0,1},{1,0},{2,3},{3,2},{4,5},{5,4},{6,7},{7,6},{8,9},{9,8},{10,11... | collective-permute-start | bytes 786440 | tf_op jit(solution)/shard_map/ppermute | solution.py:356
  64.1 1.8 %collective-permute-start.25 = (f32[16,32,128]{2,1,0:T(8,128)S(1)}, f32[16,32,128]{2,1,0:T(8,128)S(1)}, u32[]{:S(2)}, u32[]{:S(2)}) collective-permute-start(f32[16,32,128]{2,1,0:T(8,128)S(1)} %shard_map.141.user_mine), channel_id=1, source_target_pairs={{0,1},{1,0},{2,3},{3,2},{4,5},{5,4},{6,7},{7,6},{8,9},{9,8},{10,11... | collective-permute-start | bytes 786440 | tf_op jit(solution)/shard_map/ppermute | solution.py:356

commit v6 on v5

--- a/solution.py
+++ b/solution.py
@@ -409,7 +409,8 @@
     )
     user_table = call(
         functools.partial(first_pass, True), shape(user_blocks, width, size),
-        (user_order, block_vals, item_source, item_table), [SMEM, VMEM, VMEM, ANY], (),
+        (user_order, block_vals, item_source, item_table, *ids_user[1:]),
+        [SMEM, VMEM, VMEM] + [ANY] * items, (),
         HEAVY, product_bytes,
     )
 

time: 67.6 us -> 62.4 us (0.923)
  Pallas kernels: 23.4 us -> 14.7 us
  waiting for transfers between devices: 11.5 us -> 16.4 us
  starting transfers between devices: 29.6 us -> 28.4 us
    pallas_call x21, Pallas kernels: 23.4 us -> 14.7 us  [call(): pl.pallas_call(kernel, out_shape=outs, in_specs=specs, out_specs=jax.tree...]
    ppermute x26, waiting for transfers between devices: 11.5 us -> 16.4 us  [swap(): return lax.ppermute(values, axis, [(i, i ^ offset) for i in range(peers)])]
    ppermute x26, starting transfers between devices: 28.6 us -> 26.7 us  [swap(): return lax.ppermute(values, axis, [(i, i ^ offset) for i in range(peers)])]
    ppermute x1, starting transfers between devices: 0.92 us -> 1.69 us  [on_device(): lax.ppermute(pieces, ('item', 'rep'), [(i, i ^ 2 * offset + 1) for i in r...]
  transfers between devices with their start and end apart: 27 -> 27, of which waited for: 12 -> 15; matrix products, arithmetic and copies ran while one was open for 0% -> 0% of each run, Pallas kernels for 31% -> 22%
where the time goes in v6:
time: 62.4 us; the launch traced here: 61.9 us
  starting transfers between devices  28.4 us (46%)
  waiting for transfers between devices  16.4 us (26%)
  Pallas kernels  14.7 us (24%)
  between operations  1.68 us (3%)
  local copies, waits for them, and re-layouts  0.73 us (1%)
    ppermute x26, starting transfers between devices, swap(): return lax.ppermute(values, axis, [(i, i ^ offset) for i in range(peers)])  26.7 us
    ppermute x26, waiting for transfers between devices, swap(): return lax.ppermute(values, axis, [(i, i ^ offset) for i in range(peers)])  16.4 us
    pallas_call x21, Pallas kernels, call(): pl.pallas_call(kernel, out_shape=outs, in_specs=specs, out_specs=jax.tree...  14.7 us
    ppermute x1, starting transfers between devices, on_device(): lax.ppermute(pieces, ('item', 'rep'), [(i, i ^ 2 * offset + 1) for i in r...  1.69 us
  transfers between devices with their start and end apart: 27, of which 15 were waited for; matrix products, arithmetic and copies ran while one was open for 0% of the time, Pallas kernels for 22%

profile of v6, /device:TPU:0, one launch (start us, length us, event | category | flops | bytes accessed | tf_op | source)
XLA Modules:
  0.0 61.9 jit_solution(15786809626267632853)
XLA Ops:
  0.7 0.0 copy-start.11
  0.7 0.0 copy-start
  0.7 0.6 copy-done.10
  1.3 0.0 copy-done.9
  1.3 0.0 copy-done.8
  1.3 3.1 %collective-permute-start.3 = (s32[16,256]{1,0:T(8,128)S(1)}, s32[16,256]{1,0:T(8,128)S(1)}, u32[]{:S(2)}, u32[]{:S(2)}) collective-permute-start(s32[16,256]{1,0:T(8,128)S(1)} %shard_map.123.after.refs_0_.ids.refs_4_), channel_id=1, source_target_pairs={{0,4},{4,0},{8,12},{12,8},{1,5},{5,1},{9,13},{13,9},{2,6},{6,2},{1... | collective-permute-start | bytes 49160 | tf_op jit(solution)/shard_map/ppermute | solution.py:356
  4.4 1.5 %collective-permute-start = (s32[16,256]{1,0:T(8,128)S(1)}, s32[16,256]{1,0:T(8,128)S(1)}, u32[]{:S(2)}, u32[]{:S(2)}) collective-permute-start(s32[16,256]{1,0:T(8,128)S(1)} %shard_map.123.after.refs_0_.ids.refs_4_), channel_id=1, source_target_pairs={{0,2},{2,0},{1,3},{3,1},{4,6},{6,4},{5,7},{7,5},{8,10},{10,8},{9,1... | collective-permute-start | bytes 49160 | tf_op jit(solution)/shard_map/ppermute | solution.py:356
  6.6 0.9 %shard_map.124 = (bf16[17,64,128]{2,1,0:T(8,128)(2,1)S(1)}, bf16[17,64,128]{2,1,0:T(8,128)(2,1)S(1)}, f32[16,128]{1,0:T(8,128)S(1)}, f32[16,128]{1,0:T(8,128)S(1...) custom-call(s32[1]{0:T(128)S(6)} %copy.13.count, s32[288]{0:T(512)S(1)} %copy-done.16, s32[288]{0:T(512)S(1)} %copy-done.17, ...), custom_call_target="tpu_custom_call" | custom-call | flops 603979776 | bytes 9437184 | tf_op jit(solution)/shard_map/pallas_call | solution.py:23
  7.5 0.0 copy-start.4
  7.6 0.0 copy-start.2
  7.6 1.2 %shard_map.125.refs_0_.mine = f32[16,64,128]{2,1,0:T(8,128)S(1)} custom-call(s32[4,384]{1,0:T(4,128)S(1)} %get-tuple-element.28.order, bf16[288,128,128]{2,1,0:T(8,128)(2,1)S(1)} %copy-done, bf16[17,64,128]{2,1,0:T(8,128)(2,1)S(1)} %get-tuple-element.33.source, s32[16,256]{1,0:T(8,128)S(1)} %shard_map.123.after.refs_0_.ids.refs_4_), custom_call_target="tpu_custom_call" | custom-call | flops 603979776 | bytes 9437184 | tf_op jit(solution)/shard_map/pallas_call | solution.py:23
  8.8 0.1 collective-permute-start.2
  8.9 0.0 collective-permute-done.3.refs_1_.refs_5_
  8.9 3.2 %collective-permute-start.4 = (s32[16,256]{1,0:T(8,128)S(1)}, s32[16,256]{1,0:T(8,128)S(1)}, u32[]{:S(2)}, u32[]{:S(2)}) collective-permute-start(s32[16,256]{1,0:T(8,128)S(1)} %shard_map.127), channel_id=1, source_target_pairs={{0,8},{4,12},{8,0},{12,4},{1,9},{5,13},{9,1},{13,5},{2,10},{6,14},... | collective-permute-start | bytes 49160 | tf_op jit(solution)/shard_map/ppermute | solution.py:356
  12.1 0.0 collective-permute-done.refs_1_
  12.1 2.3 %shard_map.126.mine = f32[16,64,128]{2,1,0:T(8,128)S(1)} custom-call(s32[4,384]{1,0:T(4,128)S(1)} %get-tuple-element.31.order, bf16[288,128,128]{2,1,0:T(8,128)(2,1)S(1)} %copy-done, bf16[17,64,128]{2,1,0:T(8,128)(2,1)S(1)} %get-tuple-element.32.source, f32[16,64,128]{2,1,0:T(8,128)S(1)} %shard_map.125.refs_0_.mine, s32[16,256]{1,0:T(8,128)S(1)} %collective-permute-done.refs_1_), custom_call_target="tpu_custom_call" | custom-call | flops 99999997952 | bytes 9437184 | tf_op jit(solution)/shard_map/pallas_call | solution.py:23
  14.4 0.2 collective-permute-start.1
  14.6 0.0 copy-start.5
  14.6 1.2 %shard_map.128 = (f32[64,256]{1,0:T(8,128)S(1)}, f32[64,256]{1,0:T(8,128)S(1)}, f32[64,256]{1,0:T(8,128)S(1)}, f32[64,256]{1,0:T(8,128)S(1)}) custom-call(f32[16,64,128]{2,1,0:T(8,128)S(1)} %shard_map.125.refs_0_.mine, f32[16,64,128]{2,1,0:T(8,128)S(1)} %collective-permute-done.2.other, f32[16,128]{1,0:T(8,128)S(1)} %get-tuple-element.30.scale.target_scale.source_scale, ...), custom_call_target="tpu_custom_call" | custom-call | flops 99999997952 | bytes 1048576 | tf_op jit(solution)/shard_map/pallas_call | solution.py:23
  15.8 2.2 %collective-permute-start.6 = (f32[64,256]{1,0:T(8,128)S(1)}, f32[64,256]{1,0:T(8,128)S(1)}, u32[]{:S(2)}, u32[]{:S(2)}) collective-permute-start(f32[64,256]{1,0:T(8,128)S(1)} %get-tuple-element.38), channel_id=1, source_target_pairs={{0,8},{4,12},{8,0},{12,4},{1,9},{5,13},{9,1},{13,5},{2,10},{6,14},... | collective-permute-start | bytes 196616 | tf_op jit(solution)/shard_map/ppermute | solution.py:356
  18.0 2.3 %collective-permute-start.7 = (f32[64,256]{1,0:T(8,128)S(1)}, f32[64,256]{1,0:T(8,128)S(1)}, u32[]{:S(2)}, u32[]{:S(2)}) collective-permute-start(f32[64,256]{1,0:T(8,128)S(1)} %get-tuple-element.39), channel_id=1, source_target_pairs={{0,12},{4,8},{8,4},{12,0},{1,13},{5,9},{9,5},{13,1},{2,14},{6,10},... | collective-permute-start | bytes 196616 | tf_op jit(solution)/shard_map/ppermute | solution.py:356
  20.3 0.6 shard_map.129
  20.9 1.0 %collective-permute-start.5 = (f32[64,256]{1,0:T(8,128)S(1)}, f32[64,256]{1,0:T(8,128)S(1)}, u32[]{:S(2)}, u32[]{:S(2)}) collective-permute-start(f32[64,256]{1,0:T(8,128)S(1)} %get-tuple-element.36), channel_id=1, source_target_pairs={{0,2},{2,0},{1,3},{3,1},{4,6},{6,4},{5,7},{7,5},{8,10},{10,8},{9,1... | collective-permute-start | bytes 196616 | tf_op jit(solution)/shard_map/ppermute | solution.py:356
  21.9 0.5 shard_map.130
  22.4 2.2 %collective-permute-done.6.refs_4_ = f32[64,256]{1,0:T(8,128)S(1)} collective-permute-done((f32[64,256]{1,0:T(8,128)S(1)}, f32[64,256]{1,0:T(8,128)S(1)}, u32[]{:S(2)}, u32[]{:S(2)}) %collective-permute-start.6) | collective-permute-done | bytes 65568 | tf_op jit(solution)/shard_map/ppermute | solution.py:356
  24.6 0.6 collective-permute-done.8.refs_6_
  25.2 0.1 collective-permute-done.5.refs_1_
  25.2 0.1 shard_map.131
  25.3 1.7 %collective-permute-start.11 = (f32[72,256]{1,0:T(8,128)S(1)}, f32[72,256]{1,0:T(8,128)S(1)}, u32[]{:S(2)}, u32[]{:S(2)}) collective-permute-start(f32[72,256]{1,0:T(8,128)S(1)} %get-tuple-element.42.refs_0_), channel_id=1, source_target_pairs={{0,3},{1,2},{2,1},{3,0},{4,7},{5,6},{6,5},{7,4},{8,11},{9,10},{10,... | collective-permute-start | bytes 221192 | tf_op jit(solution)/shard_map/ppermute | solution.py:455
  27.0 0.5 collective-permute-start.10
  27.5 0.0 collective-permute-start.9
  27.5 2.3 %collective-permute-start.14 = (f32[64,256]{1,0:T(8,128)S(1)}, f32[64,256]{1,0:T(8,128)S(1)}, u32[]{:S(2)}, u32[]{:S(2)}) collective-permute-start(f32[64,256]{1,0:T(8,128)S(1)} %get-tuple-element.45.refs_0_), channel_id=1, source_target_pairs={{0,8},{4,12},{8,0},{12,4},{1,9},{5,13},{9,1},{13,5},{2,10},{6,14},... | collective-permute-start | bytes 196616 | tf_op jit(solution)/shard_map/ppermute | solution.py:356
  29.8 1.8 %collective-permute-start.13 = (f32[64,256]{1,0:T(8,128)S(1)}, f32[64,256]{1,0:T(8,128)S(1)}, u32[]{:S(2)}, u32[]{:S(2)}) collective-permute-start(f32[64,256]{1,0:T(8,128)S(1)} %get-tuple-element.45.refs_0_), channel_id=1, source_target_pairs={{0,12},{4,8},{8,4},{12,0},{1,13},{5,9},{9,5},{13,1},{2,14},{6,10},... | collective-permute-start | bytes 196616 | tf_op jit(solution)/shard_map/ppermute | solution.py:356
  31.6 0.1 collective-permute-done.10.refs_2_
  31.7 2.7 %shard_map.132 = (f32[16,64,128]{2,1,0:T(8,128)S(1)}, f32[16,32,128]{2,1,0:T(8,128)S(1)}, f32[16,32,128]{2,1,0:T(8,128)S(1)}) custom-call(s32[4,384]{1,0:T(4,128)S(1)} %copy-done.5, f32[16,128]{1,0:T(8,128)S(1)} %get-tuple-element.29.scale.source_scale.target_scale, f32[16,128]{1,0:T(8,128)S(1)} %get-tuple-element.30.scale.target_scale.source_scale, ...), custom_call_target="tpu_custom_call" | custom-call | flops 603979776 | bytes 9437184 | tf_op jit(solution)/shard_map/pallas_call | solution.py:23
  34.5 0.3 collective-permute-start.16
  34.8 0.9 %collective-permute-done.14.refs_3_ = f32[64,256]{1,0:T(8,128)S(1)} collective-permute-done((f32[64,256]{1,0:T(8,128)S(1)}, f32[64,256]{1,0:T(8,128)S(1)}, u32[]{:S(2)}, u32[]{:S(2)}) %collective-permute-start.14) | collective-permute-done | bytes 65568 | tf_op jit(solution)/shard_map/ppermute | solution.py:356
  35.7 0.8 %collective-permute-done.13.refs_2_ = f32[64,256]{1,0:T(8,128)S(1)} collective-permute-done((f32[64,256]{1,0:T(8,128)S(1)}, f32[64,256]{1,0:T(8,128)S(1)}, u32[]{:S(2)}, u32[]{:S(2)}) %collective-permute-start.13) | collective-permute-done | bytes 65568 | tf_op jit(solution)/shard_map/ppermute | solution.py:356
  36.5 0.4 collective-permute-done.12.refs_1_
  36.9 1.5 %shard_map.133.after.mine = f32[16,64,128]{2,1,0:T(8,128)S(1)} custom-call(f32[16,32,128]{2,1,0:T(8,128)S(1)} %get-tuple-element.44.after, f32[64,256]{1,0:T(8,128)S(1)} %get-tuple-element.45.refs_0_, f32[64,256]{1,0:T(8,128)S(1)} %collective-permute-done.12.refs_1_, f32[64,256]{1,0:T(8,128)S(1)} %collective-permute-done.13.refs_2_, ...), custom_call_target="tpu_custom_call" | custom-call | flops 99999997952 | tf_op jit(solution)/shard_map/pallas_call | solution.py:23
  38.4 0.1 collective-permute-start.15
  38.5 0.0 copy-start.1
  38.5 0.0 copy-start.3
  38.6 1.2 %collective-permute-start.17 = (f32[4,32,128]{2,1,0:T(8,128)S(1)}, f32[4,32,128]{2,1,0:T(8,128)S(1)}, u32[]{:S(2)}, u32[]{:S(2)}) collective-permute-start(f32[4,32,128]{2,1,0:T(8,128)S(1)} %get-tuple-element.49), channel_id=1, source_target_pairs={{0,8},{4,12},{8,0},{12,4},{1,9},{5,13},{9,1},{13,5},{2,10},{6,14},... | collective-permute-start | bytes 196616 | tf_op jit(solution)/shard_map/ppermute | solution.py:356
  39.8 2.0 %collective-permute-start.18 = (f32[4,32,128]{2,1,0:T(8,128)S(1)}, f32[4,32,128]{2,1,0:T(8,128)S(1)}, u32[]{:S(2)}, u32[]{:S(2)}) collective-permute-start(f32[4,32,128]{2,1,0:T(8,128)S(1)} %get-tuple-element.50), channel_id=1, source_target_pairs={{0,12},{4,8},{8,4},{12,0},{1,13},{5,9},{9,5},{13,1},{2,14},{6,10},... | collective-permute-start | bytes 196616 | tf_op jit(solution)/shard_map/ppermute | solution.py:356
  41.8 0.4 collective-permute-start.19
  42.2 0.0 copy-done.1
  42.2 2.5 %shard_map.135 = (f32[16,64,128]{2,1,0:T(8,128)S(1)}, f32[16,32,128]{2,1,0:T(8,128)S(1)}, f32[16,32,128]{2,1,0:T(8,128)S(1)}) custom-call(s32[4,384]{1,0:T(4,128)S(1)} %copy-done.7, f32[16,64,128]{2,1,0:T(8,128)S(1)} %shard_map.133.after.mine, f32[16,64,128]{2,1,0:T(8,128)S(1)} %collective-permute-done.15.other, ...), custom_call_target="tpu_custom_call" | custom-call | flops 603979776 | bytes 9437184 | tf_op jit(solution)/shard_map/pallas_call | solution.py:23
  44.7 2.5 %collective-permute-done.17.refs_2_ = f32[4,32,128]{2,1,0:T(8,128)S(1)} collective-permute-done((f32[4,32,128]{2,1,0:T(8,128)S(1)}, f32[4,32,128]{2,1,0:T(8,128)S(1)}, u32[]{:S(2)}, u32[]{:S(2)}) %collective-permute-start.17) | collective-permute-done | bytes 65568 | tf_op jit(solution)/shard_map/ppermute | solution.py:356
  47.2 1.0 %collective-permute-done.19.refs_4_ = f32[4,32,128]{2,1,0:T(8,128)S(1)} collective-permute-done((f32[4,32,128]{2,1,0:T(8,128)S(1)}, f32[4,32,128]{2,1,0:T(8,128)S(1)}, u32[]{:S(2)}, u32[]{:S(2)}) %collective-permute-start.19) | collective-permute-done | bytes 65568 | tf_op jit(solution)/shard_map/ppermute | solution.py:356
  48.3 0.1 collective-permute-start.23
  48.3 0.7 %collective-permute-start.20 = (f32[4,32,128]{2,1,0:T(8,128)S(1)}, f32[4,32,128]{2,1,0:T(8,128)S(1)}, u32[]{:S(2)}, u32[]{:S(2)}) collective-permute-start(f32[4,32,128]{2,1,0:T(8,128)S(1)} %shard_map.136.refs_0_), channel_id=1, source_target_pairs={{0,4},{4,0},{8,12},{12,8},{1,5},{5,1},{9,13},{13,9},{2,6},{6,2},{1... | collective-permute-start | bytes 196616 | tf_op jit(solution)/shard_map/ppermute | solution.py:356
  49.0 1.8 %collective-permute-start.21 = (f32[4,32,128]{2,1,0:T(8,128)S(1)}, f32[4,32,128]{2,1,0:T(8,128)S(1)}, u32[]{:S(2)}, u32[]{:S(2)}) collective-permute-start(f32[4,32,128]{2,1,0:T(8,128)S(1)} %shard_map.136.refs_0_), channel_id=1, source_target_pairs={{0,8},{4,12},{8,0},{12,4},{1,9},{5,13},{9,1},{13,5},{2,10},{6,14},... | collective-permute-start | bytes 196616 | tf_op jit(solution)/shard_map/ppermute | solution.py:356
  50.9 1.2 %collective-permute-start.24 = (f32[16,32,128]{2,1,0:T(8,128)S(1)}, f32[16,32,128]{2,1,0:T(8,128)S(1)}, u32[]{:S(2)}, u32[]{:S(2)}) collective-permute-start(f32[16,32,128]{2,1,0:T(8,128)S(1)} %shard_map.140.refs_1_), channel_id=1, source_target_pairs={{0,2},{2,0},{1,3},{3,1},{4,6},{6,4},{5,7},{7,5},{8,10},{10,8},{9,1... | collective-permute-start | bytes 786440 | tf_op jit(solution)/shard_map/ppermute | solution.py:356
  52.2 1.5 %collective-permute-done.20.values = f32[4,32,128]{2,1,0:T(8,128)S(1)} collective-permute-done((f32[4,32,128]{2,1,0:T(8,128)S(1)}, f32[4,32,128]{2,1,0:T(8,128)S(1)}, u32[]{:S(2)}, u32[]{:S(2)}) %collective-permute-start.20) | collective-permute-done | bytes 65568 | tf_op jit(solution)/shard_map/ppermute | solution.py:356
  53.7 0.3 collective-permute-start.22
  54.0 1.7 %collective-permute-done.21.refs_2_ = f32[4,32,128]{2,1,0:T(8,128)S(1)} collective-permute-done((f32[4,32,128]{2,1,0:T(8,128)S(1)}, f32[4,32,128]{2,1,0:T(8,128)S(1)}, u32[]{:S(2)}, u32[]{:S(2)}) %collective-permute-start.21) | collective-permute-done | bytes 65568 | tf_op jit(solution)/shard_map/ppermute | solution.py:356
  55.6 3.2 %collective-permute-done.22.refs_3_ = f32[4,32,128]{2,1,0:T(8,128)S(1)} collective-permute-done((f32[4,32,128]{2,1,0:T(8,128)S(1)}, f32[4,32,128]{2,1,0:T(8,128)S(1)}, u32[]{:S(2)}, u32[]{:S(2)}) %collective-permute-start.22) | collective-permute-done | bytes 65568 | tf_op jit(solution)/shard_map/ppermute | solution.py:356
  58.9 0.1 collective-permute-start.26
  58.9 0.1 collective-permute-done.24.refs_2_
  59.1 0.4 collective-permute-start.25
  59.5 0.9 %collective-permute-done.26.item_other = f32[4,4,32,128]{3,2,1,0:T(8,128)S(1)} collective-permute-done((f32[4,4,32,128]{3,2,1,0:T(8,128)S(1)}, f32[4,4,32,128]{3,2,1,0:T(8,128)S(1)}, u32[]{:S(2)}, u32[]{:S(2)}) %collective-permute-start.26) | collective-permute-done | bytes 262176 | tf_op jit(solution)/shard_map/ppermute | solution.py:356
  60.5 0.4 collective-permute-done.25.user_other
  60.8 1.1 %shard_map.142 = (f32[64,2048]{1,0:T(8,128)}, f32[64,2048]{1,0:T(8,128)}) custom-call(f32[16,64,128]{2,1,0:T(8,128)S(1)} %get-tuple-element.43.user_half_grad, f32[16,32,128]{2,1,0:T(8,128)S(1)} %shard_map.141.user_mine, f32[16,32,128]{2,1,0:T(8,128)S(1)} %collective-permute-done.25.user_other, f32[16,64,128]{2,1,0:T(8,128)S(1)} %get-tuple-element.53.item_half_grad, ...), custom_call_target="tpu_custom_call" | custom-call | bytes 3145728 | tf_op jit(solution)/shard_map/pallas_call | solution.py:23
  (47 shorter events, 0.3 us)
Async XLA Ops:
  0.6 0.7 %copy-start.10 = (s32[256]{0:T(256)S(1)}, s32[256]{0:T(256)}, u32[]{:S(2)}) copy-start(s32[256]{0:T(256)} %param.21) | copy-start | bytes 3076
  0.6 0.7 %copy-start.9 = (s32[256]{0:T(256)S(1)}, s32[256]{0:T(256)}, u32[]{:S(2)}) copy-start(s32[256]{0:T(256)} %param.20) | copy-start | bytes 3076
  0.7 0.7 %copy-start.8 = (s32[256]{0:T(256)S(1)}, s32[256]{0:T(256)}, u32[]{:S(2)}) copy-start(s32[256]{0:T(256)} %param.19) | copy-start | bytes 3076
  0.7 5.9 %copy-start.13 = (bf16[64,2048]{1,0:T(8,128)(2,1)S(1)}, bf16[64,2048]{1,0:T(8,128)(2,1)}, u32[]{:S(2)}) copy-start(bf16[64,2048]{1,0:T(8,128)(2,1)} %item_emb.3) | copy-start | bytes 786436
  0.7 5.9 %copy-start.11 = (bf16[64,2048]{1,0:T(8,128)(2,1)S(1)}, bf16[64,2048]{1,0:T(8,128)(2,1)}, u32[]{:S(2)}) copy-start(bf16[64,2048]{1,0:T(8,128)(2,1)} %user_emb.3) | copy-start | bytes 786436
  0.7 5.9 %copy-start.17 = (s32[288]{0:T(512)S(1)}, s32[288]{0:T(512)}, u32[]{:S(2)}) copy-start(s32[288]{0:T(512)} %columns.1) | copy-start | bytes 3460
  0.7 5.9 %copy-start.16 = (s32[288]{0:T(512)S(1)}, s32[288]{0:T(512)}, u32[]{:S(2)}) copy-start(s32[288]{0:T(512)} %rows.1) | copy-start | bytes 3460
  0.7 5.9 %copy-start.15 = (s32[2048]{0:T(1024)S(1)}, s32[2048]{0:T(1024)}, u32[]{:S(2)}) copy-start(s32[2048]{0:T(1024)} %param.14) | copy-start | bytes 24580
  0.7 5.9 %copy-start.14 = (s32[2048]{0:T(1024)S(1)}, s32[2048]{0:T(1024)}, u32[]{:S(2)}) copy-start(s32[2048]{0:T(1024)} %param.13) | copy-start | bytes 24580
  0.7 6.9 %copy-start = (bf16[288,128,128]{2,1,0:T(8,128)(2,1)S(1)}, bf16[288,128,128]{2,1,0:T(8,128)(2,1)}, u32[]{:S(2)}) copy-start(bf16[288,128,128]{2,1,0:T(8,128)(2,1)} %vals.7) | copy-start | bytes 28311556
  1.3 7.5 %collective-permute-start.3 = (s32[16,256]{1,0:T(8,128)S(1)}, s32[16,256]{1,0:T(8,128)S(1)}, u32[]{:S(2)}, u32[]{:S(2)}) collective-permute-start(s32[16,256]{1,0:T(8,128)S(1)} %shard_map.123.after.refs_0_.ids.refs_4_), channel_id=1, source_target_pairs={{0,4},{4,0},{8,12},{12,8},{1,5},{5,1},{9,13},{13,9},{2,6},{6,2},{1... | collective-permute-start | bytes 49160 | tf_op jit(solution)/shard_map/ppermute | solution.py:356
  4.4 7.7 %collective-permute-start = (s32[16,256]{1,0:T(8,128)S(1)}, s32[16,256]{1,0:T(8,128)S(1)}, u32[]{:S(2)}, u32[]{:S(2)}) collective-permute-start(s32[16,256]{1,0:T(8,128)S(1)} %shard_map.123.after.refs_0_.ids.refs_4_), channel_id=1, source_target_pairs={{0,2},{2,0},{1,3},{3,1},{4,6},{6,4},{5,7},{7,5},{8,10},{10,8},{9,1... | collective-permute-start | bytes 49160 | tf_op jit(solution)/shard_map/ppermute | solution.py:356
  7.5 4.5 %copy-start.4 = (s32[4,384]{1,0:T(4,128)}, s32[4,384]{1,0:T(4,128)S(1)}, u32[]{:S(2)}) copy-start(s32[4,384]{1,0:T(4,128)S(1)} %get-tuple-element.28.order) | copy-start | bytes 18436
  7.6 6.8 %copy-start.6 = (s32[4,384]{1,0:T(4,128)}, s32[4,384]{1,0:T(4,128)S(1)}, u32[]{:S(2)}) copy-start(s32[4,384]{1,0:T(4,128)S(1)} %get-tuple-element.31.order) | copy-start | bytes 18436
  7.6 24.1 %copy-start.2 = (f32[16,128]{1,0:T(8,128)}, f32[16,128]{1,0:T(8,128)S(1)}, u32[]{:S(2)}) copy-start(f32[16,128]{1,0:T(8,128)S(1)} %get-tuple-element.29.scale.source_scale.target_scale) | copy-start | bytes 24580
  8.8 5.8 %collective-permute-start.2 = (f32[16,64,128]{2,1,0:T(8,128)S(1)}, f32[16,64,128]{2,1,0:T(8,128)S(1)}, u32[]{:S(2)}, u32[]{:S(2)}) collective-permute-start(f32[16,64,128]{2,1,0:T(8,128)S(1)} %shard_map.125.refs_0_.mine), channel_id=1, source_target_pairs={{0,1},{1,0},{2,3},{3,2},{4,5},{5,4},{6,7},{7,6},{8,9},{9,8},{10,11... | collective-permute-start | bytes 1572872 | tf_op jit(solution)/shard_map/ppermute | solution.py:356
  8.9 5.7 %collective-permute-start.4 = (s32[16,256]{1,0:T(8,128)S(1)}, s32[16,256]{1,0:T(8,128)S(1)}, u32[]{:S(2)}, u32[]{:S(2)}) collective-permute-start(s32[16,256]{1,0:T(8,128)S(1)} %shard_map.127), channel_id=1, source_target_pairs={{0,8},{4,12},{8,0},{12,4},{1,9},{5,13},{9,1},{13,5},{2,10},{6,14},... | collective-permute-start | bytes 49160 | tf_op jit(solution)/shard_map/ppermute | solution.py:356
  14.4 5.9 %collective-permute-start.1 = (f32[16,64,128]{2,1,0:T(8,128)S(1)}, f32[16,64,128]{2,1,0:T(8,128)S(1)}, u32[]{:S(2)}, u32[]{:S(2)}) collective-permute-start(f32[16,64,128]{2,1,0:T(8,128)S(1)} %shard_map.126.mine), channel_id=1, source_target_pairs={{0,1},{1,0},{2,3},{3,2},{4,5},{5,4},{6,7},{7,6},{8,9},{9,8},{10,11... | collective-permute-start | bytes 1572872 | tf_op jit(solution)/shard_map/ppermute | solution.py:356
  14.6 7.3 %copy-start.12 = (bf16[64,2048]{1,0:T(8,128)(2,1)S(1)}, bf16[64,2048]{1,0:T(8,128)(2,1)}, u32[]{:S(2)}) copy-start(bf16[64,2048]{1,0:T(8,128)(2,1)} %user_emb.3) | copy-start | bytes 786436
  14.6 17.1 %copy-start.5 = (s32[4,384]{1,0:T(4,128)S(1)}, s32[4,384]{1,0:T(4,128)}, u32[]{:S(2)}) copy-start(s32[4,384]{1,0:T(4,128)} %copy-done.4) | copy-start | bytes 18436
  15.8 8.7 %collective-permute-start.6 = (f32[64,256]{1,0:T(8,128)S(1)}, f32[64,256]{1,0:T(8,128)S(1)}, u32[]{:S(2)}, u32[]{:S(2)}) collective-permute-start(f32[64,256]{1,0:T(8,128)S(1)} %get-tuple-element.38), channel_id=1, source_target_pairs={{0,8},{4,12},{8,0},{12,4},{1,9},{5,13},{9,1},{13,5},{2,10},{6,14},... | collective-permute-start | bytes 196616 | tf_op jit(solution)/shard_map/ppermute | solution.py:356
  18.0 6.5 %collective-permute-start.7 = (f32[64,256]{1,0:T(8,128)S(1)}, f32[64,256]{1,0:T(8,128)S(1)}, u32[]{:S(2)}, u32[]{:S(2)}) collective-permute-start(f32[64,256]{1,0:T(8,128)S(1)} %get-tuple-element.39), channel_id=1, source_target_pairs={{0,12},{4,8},{8,4},{12,0},{1,13},{5,9},{9,5},{13,1},{2,14},{6,10},... | collective-permute-start | bytes 196616 | tf_op jit(solution)/shard_map/ppermute | solution.py:356
  20.3 4.8 %collective-permute-start.8 = (f32[64,256]{1,0:T(8,128)S(1)}, f32[64,256]{1,0:T(8,128)S(1)}, u32[]{:S(2)}, u32[]{:S(2)}) collective-permute-start(f32[64,256]{1,0:T(8,128)S(1)} %get-tuple-element.40), channel_id=1, source_target_pairs={{0,4},{4,0},{8,12},{12,8},{1,5},{5,1},{9,13},{13,9},{2,6},{6,2},{1... | collective-permute-start | bytes 196616 | tf_op jit(solution)/shard_map/ppermute | solution.py:356
  20.9 4.3 %collective-permute-start.5 = (f32[64,256]{1,0:T(8,128)S(1)}, f32[64,256]{1,0:T(8,128)S(1)}, u32[]{:S(2)}, u32[]{:S(2)}) collective-permute-start(f32[64,256]{1,0:T(8,128)S(1)} %get-tuple-element.36), channel_id=1, source_target_pairs={{0,2},{2,0},{1,3},{3,1},{4,6},{6,4},{5,7},{7,5},{8,10},{10,8},{9,1... | collective-permute-start | bytes 196616 | tf_op jit(solution)/shard_map/ppermute | solution.py:356
  25.3 6.3 %collective-permute-start.11 = (f32[72,256]{1,0:T(8,128)S(1)}, f32[72,256]{1,0:T(8,128)S(1)}, u32[]{:S(2)}, u32[]{:S(2)}) collective-permute-start(f32[72,256]{1,0:T(8,128)S(1)} %get-tuple-element.42.refs_0_), channel_id=1, source_target_pairs={{0,3},{1,2},{2,1},{3,0},{4,7},{5,6},{6,5},{7,4},{8,11},{9,10},{10,... | collective-permute-start | bytes 221192 | tf_op jit(solution)/shard_map/ppermute | solution.py:455
  27.0 4.7 %collective-permute-start.10 = (f32[72,256]{1,0:T(8,128)S(1)}, f32[72,256]{1,0:T(8,128)S(1)}, u32[]{:S(2)}, u32[]{:S(2)}) collective-permute-start(f32[72,256]{1,0:T(8,128)S(1)} %get-tuple-element.42.refs_0_), channel_id=1, source_target_pairs={{0,2},{2,0},{1,3},{3,1},{4,6},{6,4},{5,7},{7,5},{8,10},{10,8},{9,1... | collective-permute-start | bytes 221192 | tf_op jit(solution)/shard_map/ppermute | solution.py:356
  27.5 4.2 %collective-permute-start.9 = (f32[72,256]{1,0:T(8,128)S(1)}, f32[72,256]{1,0:T(8,128)S(1)}, u32[]{:S(2)}, u32[]{:S(2)}) collective-permute-start(f32[72,256]{1,0:T(8,128)S(1)} %get-tuple-element.42.refs_0_), channel_id=1, source_target_pairs={{0,1},{1,0},{2,3},{3,2},{4,5},{5,4},{6,7},{7,6},{8,9},{9,8},{10,11... | collective-permute-start | bytes 221192 | tf_op jit(solution)/shard_map/ppermute | solution.py:356
  27.5 8.2 %collective-permute-start.14 = (f32[64,256]{1,0:T(8,128)S(1)}, f32[64,256]{1,0:T(8,128)S(1)}, u32[]{:S(2)}, u32[]{:S(2)}) collective-permute-start(f32[64,256]{1,0:T(8,128)S(1)} %get-tuple-element.45.refs_0_), channel_id=1, source_target_pairs={{0,8},{4,12},{8,0},{12,4},{1,9},{5,13},{9,1},{13,5},{2,10},{6,14},... | collective-permute-start | bytes 196616 | tf_op jit(solution)/shard_map/ppermute | solution.py:356
  29.8 6.7 %collective-permute-start.13 = (f32[64,256]{1,0:T(8,128)S(1)}, f32[64,256]{1,0:T(8,128)S(1)}, u32[]{:S(2)}, u32[]{:S(2)}) collective-permute-start(f32[64,256]{1,0:T(8,128)S(1)} %get-tuple-element.45.refs_0_), channel_id=1, source_target_pairs={{0,12},{4,8},{8,4},{12,0},{1,13},{5,9},{9,5},{13,1},{2,14},{6,10},... | collective-permute-start | bytes 196616 | tf_op jit(solution)/shard_map/ppermute | solution.py:356
  31.6 5.3 %collective-permute-start.12 = (f32[64,256]{1,0:T(8,128)S(1)}, f32[64,256]{1,0:T(8,128)S(1)}, u32[]{:S(2)}, u32[]{:S(2)}) collective-permute-start(f32[64,256]{1,0:T(8,128)S(1)} %get-tuple-element.45.refs_0_), channel_id=1, source_target_pairs={{0,4},{4,0},{8,12},{12,8},{1,5},{5,1},{9,13},{13,9},{2,6},{6,2},{1... | collective-permute-start | bytes 196616 | tf_op jit(solution)/shard_map/ppermute | solution.py:356
  34.5 4.1 %collective-permute-start.16 = (f32[16,32,128]{2,1,0:T(8,128)S(1)}, f32[16,32,128]{2,1,0:T(8,128)S(1)}, u32[]{:S(2)}, u32[]{:S(2)}) collective-permute-start(f32[16,32,128]{2,1,0:T(8,128)S(1)} %get-tuple-element.44.after), channel_id=1, source_target_pairs={{0,1},{1,0},{2,3},{3,2},{4,5},{5,4},{6,7},{7,6},{8,9},{9,8},{10,11... | collective-permute-start | bytes 786440 | tf_op jit(solution)/shard_map/ppermute | solution.py:356
  38.4 3.7 %collective-permute-start.15 = (f32[16,64,128]{2,1,0:T(8,128)S(1)}, f32[16,64,128]{2,1,0:T(8,128)S(1)}, u32[]{:S(2)}, u32[]{:S(2)}) collective-permute-start(f32[16,64,128]{2,1,0:T(8,128)S(1)} %shard_map.133.after.mine), channel_id=1, source_target_pairs={{0,1},{1,0},{2,3},{3,2},{4,5},{5,4},{6,7},{7,6},{8,9},{9,8},{10,11... | collective-permute-start | bytes 1572872 | tf_op jit(solution)/shard_map/ppermute | solution.py:356
  38.5 3.7 %copy-start.1 = (bf16[288,128,128]{2,1,0:T(8,128)(2,1)S(1)}, bf16[288,128,128]{2,1,0:T(8,128)(2,1)}, u32[]{:S(2)}) copy-start(bf16[288,128,128]{2,1,0:T(8,128)(2,1)} %vals.7) | copy-start | bytes 28311556
  38.5 3.7 %copy-start.3 = (f32[16,128]{1,0:T(8,128)S(1)}, f32[16,128]{1,0:T(8,128)}, u32[]{:S(2)}) copy-start(f32[16,128]{1,0:T(8,128)} %copy-done.2) | copy-start | bytes 24580
  38.6 3.7 %copy-start.7 = (s32[4,384]{1,0:T(4,128)S(1)}, s32[4,384]{1,0:T(4,128)}, u32[]{:S(2)}) copy-start(s32[4,384]{1,0:T(4,128)} %copy-done.6) | copy-start | bytes 18436
  38.6 8.6 %collective-permute-start.17 = (f32[4,32,128]{2,1,0:T(8,128)S(1)}, f32[4,32,128]{2,1,0:T(8,128)S(1)}, u32[]{:S(2)}, u32[]{:S(2)}) collective-permute-start(f32[4,32,128]{2,1,0:T(8,128)S(1)} %get-tuple-element.49), channel_id=1, source_target_pairs={{0,8},{4,12},{8,0},{12,4},{1,9},{5,13},{9,1},{13,5},{2,10},{6,14},... | collective-permute-start | bytes 196616 | tf_op jit(solution)/shard_map/ppermute | solution.py:356
  39.8 7.4 %collective-permute-start.18 = (f32[4,32,128]{2,1,0:T(8,128)S(1)}, f32[4,32,128]{2,1,0:T(8,128)S(1)}, u32[]{:S(2)}, u32[]{:S(2)}) collective-permute-start(f32[4,32,128]{2,1,0:T(8,128)S(1)} %get-tuple-element.50), channel_id=1, source_target_pairs={{0,12},{4,8},{8,4},{12,0},{1,13},{5,9},{9,5},{13,1},{2,14},{6,10},... | collective-permute-start | bytes 196616 | tf_op jit(solution)/shard_map/ppermute | solution.py:356
  41.8 6.4 %collective-permute-start.19 = (f32[4,32,128]{2,1,0:T(8,128)S(1)}, f32[4,32,128]{2,1,0:T(8,128)S(1)}, u32[]{:S(2)}, u32[]{:S(2)}) collective-permute-start(f32[4,32,128]{2,1,0:T(8,128)S(1)} %get-tuple-element.51), channel_id=1, source_target_pairs={{0,4},{4,0},{8,12},{12,8},{1,5},{5,1},{9,13},{13,9},{2,6},{6,2},{1... | collective-permute-start | bytes 196616 | tf_op jit(solution)/shard_map/ppermute | solution.py:356
  48.3 2.6 %collective-permute-start.23 = (f32[16,32,128]{2,1,0:T(8,128)S(1)}, f32[16,32,128]{2,1,0:T(8,128)S(1)}, u32[]{:S(2)}, u32[]{:S(2)}) collective-permute-start(f32[16,32,128]{2,1,0:T(8,128)S(1)} %shard_map.139), channel_id=1, source_target_pairs={{0,1},{1,0},{2,3},{3,2},{4,5},{5,4},{6,7},{7,6},{8,9},{9,8},{10,11... | collective-permute-start | bytes 786440 | tf_op jit(solution)/shard_map/ppermute | solution.py:356
  48.3 5.3 %collective-permute-start.20 = (f32[4,32,128]{2,1,0:T(8,128)S(1)}, f32[4,32,128]{2,1,0:T(8,128)S(1)}, u32[]{:S(2)}, u32[]{:S(2)}) collective-permute-start(f32[4,32,128]{2,1,0:T(8,128)S(1)} %shard_map.136.refs_0_), channel_id=1, source_target_pairs={{0,4},{4,0},{8,12},{12,8},{1,5},{5,1},{9,13},{13,9},{2,6},{6,2},{1... | collective-permute-start | bytes 196616 | tf_op jit(solution)/shard_map/ppermute | solution.py:356
  49.0 6.6 %collective-permute-start.21 = (f32[4,32,128]{2,1,0:T(8,128)S(1)}, f32[4,32,128]{2,1,0:T(8,128)S(1)}, u32[]{:S(2)}, u32[]{:S(2)}) collective-permute-start(f32[4,32,128]{2,1,0:T(8,128)S(1)} %shard_map.136.refs_0_), channel_id=1, source_target_pairs={{0,8},{4,12},{8,0},{12,4},{1,9},{5,13},{9,1},{13,5},{2,10},{6,14},... | collective-permute-start | bytes 196616 | tf_op jit(solution)/shard_map/ppermute | solution.py:356
  50.9 8.2 %collective-permute-start.24 = (f32[16,32,128]{2,1,0:T(8,128)S(1)}, f32[16,32,128]{2,1,0:T(8,128)S(1)}, u32[]{:S(2)}, u32[]{:S(2)}) collective-permute-start(f32[16,32,128]{2,1,0:T(8,128)S(1)} %shard_map.140.refs_1_), channel_id=1, source_target_pairs={{0,2},{2,0},{1,3},{3,1},{4,6},{6,4},{5,7},{7,5},{8,10},{10,8},{9,1... | collective-permute-start | bytes 786440 | tf_op jit(solution)/shard_map/ppermute | solution.py:356
  53.7 5.2 %collective-permute-start.22 = (f32[4,32,128]{2,1,0:T(8,128)S(1)}, f32[4,32,128]{2,1,0:T(8,128)S(1)}, u32[]{:S(2)}, u32[]{:S(2)}) collective-permute-start(f32[4,32,128]{2,1,0:T(8,128)S(1)} %shard_map.137.refs_1_), channel_id=1, source_target_pairs={{0,8},{4,12},{8,0},{12,4},{1,9},{5,13},{9,1},{13,5},{2,10},{6,14},... | collective-permute-start | bytes 196616 | tf_op jit(solution)/shard_map/ppermute | solution.py:356
  58.9 1.6 %collective-permute-start.26 = (f32[4,4,32,128]{3,2,1,0:T(8,128)S(1)}, f32[4,4,32,128]{3,2,1,0:T(8,128)S(1)}, u32[]{:S(2)}, u32[]{:S(2)}) collective-permute-start(f32[4,4,32,128]{3,2,1,0:T(8,128)S(1)} %shard_map.138.refs_0_.item_mine), channel_id=1, source_target_pairs={{0,1},{1,0},{2,3},{3,2},{4,5},{5,4},{6,7},{7,6},{8,9},{9,8},{10,11... | collective-permute-start | bytes 786440 | tf_op jit(solution)/shard_map/ppermute | solution.py:356
  59.1 1.7 %collective-permute-start.25 = (f32[16,32,128]{2,1,0:T(8,128)S(1)}, f32[16,32,128]{2,1,0:T(8,128)S(1)}, u32[]{:S(2)}, u32[]{:S(2)}) collective-permute-start(f32[16,32,128]{2,1,0:T(8,128)S(1)} %shard_map.141.user_mine), channel_id=1, source_target_pairs={{0,1},{1,0},{2,3},{3,2},{4,5},{5,4},{6,7},{7,6},{8,9},{9,8},{10,11... | collective-permute-start | bytes 786440 | tf_op jit(solution)/shard_map/ppermute | solution.py:356

commit v7 on v6

--- a/solution.py
+++ b/solution.py
@@ -12,6 +12,7 @@
 PACK = 4
 GROUP = 8
 HEAVY = 10 ** 11
+MEDIUM = 24 * 10 ** 8
 
 VMEM = pl.BlockSpec(memory_space=pltpu.VMEM)
 SMEM = pl.BlockSpec(memory_space=pltpu.SMEM)
@@ -490,20 +491,20 @@
     item_own = call(functools.partial(sum_after, 1), shape(per, half, size), (user_keep, *parts),
                     [ANY] + [VMEM] * users,
                moved=4 * (users + 1) * per * half * size)
-    item_mine, step = {0: item_own}, 1
-    while step < users:
-        for offset, part in list(item_mine.items()):
-            item_mine[offset ^ step] = swap(part, "user", users, step)
-        if 2 * step < users:
-            item_mine[step] = hold(item_mine[step], flops=HEAVY)
-        step *= 2
+    user_send = hold(user_send, item_own)
+
+    own = call(sum_parts, shape(user_blocks, half, size), (user_keep, swap(user_send)),
+               [VMEM, VMEM], moved=12 * user_blocks * half * size)
+    late = hold(item_own, own)
+    item_mine = {0: item_own}
+    for offset in [users - 1, *range(1, users - 1)] if users > 1 else []:
+        part = item_own if offset == users - 1 else late
+        item_mine[offset] = swap(part, "user", users, offset)
+    if users > 2:
+        item_mine[users - 1] = hold(item_mine[users - 1], flops=MEDIUM)
     item_places = list(item_mine)
     item_mine = call(pack, shape(users, per, half, size), tuple(item_mine.values()),
                      [VMEM] * users, moved=8 * item_blocks * half * size)
-    user_send = hold(user_send, item_own)
-
-    own = call(sum_parts, shape(user_blocks, half, size), (user_keep, swap(user_send)),
-               [VMEM, VMEM], moved=12 * user_blocks * half * size)
     mine = call(functools.partial(sum_after, 1), shape(user_blocks, half, size),
                 (item_mine, own, *[swap(own, "item", items, o) for o in range(1, items)]),
                 [ANY] + [VMEM] * items, moved=12 * user_blocks * half * size)

time: 62.4 us -> 62.2 us (level)
  waiting for transfers between devices: 16.4 us -> 12.6 us
  starting transfers between devices: 28.4 us -> 32.1 us
    ppermute x26, starting transfers between devices: 26.7 us -> 31.8 us  [swap(): return lax.ppermute(values, axis, [(i, i ^ offset) for i in range(peers)])]
    ppermute x26, waiting for transfers between devices: 16.4 us -> 12.6 us  [swap(): return lax.ppermute(values, axis, [(i, i ^ offset) for i in range(peers)])]
    ppermute x1, starting transfers between devices: 1.69 us -> 0.31 us  [on_device(): lax.ppermute(pieces, ('item', 'rep'), [(i, i ^ 2 * offset + 1) for i in r...]
    pallas_call x21 -> x22, Pallas kernels: 14.7 us -> 14.7 us  [call(): pl.pallas_call(kernel, out_shape=outs, in_specs=specs, out_specs=jax.tree...]
  transfers between devices with their start and end apart: 27 -> 27, of which waited for: 15 -> 13; matrix products, arithmetic and copies ran while one was open for 0% -> 0% of each run, Pallas kernels for 22% -> 22%
where the time goes in v7:
time: 62.2 us; the launch traced here: 62 us
  starting transfers between devices  32.1 us (52%)
  Pallas kernels  14.7 us (24%)
  waiting for transfers between devices  12.6 us (20%)
  between operations  1.71 us (3%)
  local copies, waits for them, and re-layouts  0.73 us (1%)
    ppermute x26, starting transfers between devices, swap(): return lax.ppermute(values, axis, [(i, i ^ offset) for i in range(peers)])  31.8 us
    pallas_call x22, Pallas kernels, call(): pl.pallas_call(kernel, out_shape=outs, in_specs=specs, out_specs=jax.tree...  14.7 us
    ppermute x26, waiting for transfers between devices, swap(): return lax.ppermute(values, axis, [(i, i ^ offset) for i in range(peers)])  12.6 us
  transfers between devices with their start and end apart: 27, of which 13 were waited for; matrix products, arithmetic and copies ran while one was open for 0% of the time, Pallas kernels for 22%

profile of v7, /device:TPU:0, one launch (start us, length us, event | category | flops | bytes accessed | tf_op | source)
XLA Modules:
  0.0 62.0 jit_solution(1060962045977796484)
XLA Ops:
  0.7 0.0 copy-start.11
  0.7 0.0 copy-start
  0.7 0.6 copy-done.10
  1.3 0.0 copy-done.9
  1.3 0.0 copy-done.8
  1.3 3.1 %collective-permute-start.3 = (s32[16,256]{1,0:T(8,128)S(1)}, s32[16,256]{1,0:T(8,128)S(1)}, u32[]{:S(2)}, u32[]{:S(2)}) collective-permute-start(s32[16,256]{1,0:T(8,128)S(1)} %shard_map.123.after.refs_0_.ids.refs_4_), channel_id=1, source_target_pairs={{0,4},{4,0},{8,12},{12,8},{1,5},{5,1},{9,13},{13,9},{2,6},{6,2},{1... | collective-permute-start | bytes 49160 | tf_op jit(solution)/shard_map/ppermute | solution.py:357
  4.4 1.5 %collective-permute-start = (s32[16,256]{1,0:T(8,128)S(1)}, s32[16,256]{1,0:T(8,128)S(1)}, u32[]{:S(2)}, u32[]{:S(2)}) collective-permute-start(s32[16,256]{1,0:T(8,128)S(1)} %shard_map.123.after.refs_0_.ids.refs_4_), channel_id=1, source_target_pairs={{0,2},{2,0},{1,3},{3,1},{4,6},{6,4},{5,7},{7,5},{8,10},{10,8},{9,1... | collective-permute-start | bytes 49160 | tf_op jit(solution)/shard_map/ppermute | solution.py:357
  6.6 0.9 %shard_map.124 = (bf16[17,64,128]{2,1,0:T(8,128)(2,1)S(1)}, bf16[17,64,128]{2,1,0:T(8,128)(2,1)S(1)}, f32[16,128]{1,0:T(8,128)S(1)}, f32[16,128]{1,0:T(8,128)S(1...) custom-call(s32[1]{0:T(128)S(6)} %copy.13.count, s32[288]{0:T(512)S(1)} %copy-done.16, s32[288]{0:T(512)S(1)} %copy-done.17, ...), custom_call_target="tpu_custom_call" | custom-call | flops 603979776 | bytes 9437184 | tf_op jit(solution)/shard_map/pallas_call | solution.py:24
  7.5 0.0 copy-start.4
  7.6 0.0 copy-start.2
  7.6 1.2 %shard_map.125.refs_0_.mine = f32[16,64,128]{2,1,0:T(8,128)S(1)} custom-call(s32[4,384]{1,0:T(4,128)S(1)} %get-tuple-element.28.order, bf16[288,128,128]{2,1,0:T(8,128)(2,1)S(1)} %copy-done, bf16[17,64,128]{2,1,0:T(8,128)(2,1)S(1)} %get-tuple-element.33.source, s32[16,256]{1,0:T(8,128)S(1)} %shard_map.123.after.refs_0_.ids.refs_4_), custom_call_target="tpu_custom_call" | custom-call | flops 603979776 | bytes 9437184 | tf_op jit(solution)/shard_map/pallas_call | solution.py:24
  8.8 0.1 collective-permute-start.2
  8.9 0.0 collective-permute-done.3.refs_1_.refs_5_
  8.9 3.2 %collective-permute-start.4 = (s32[16,256]{1,0:T(8,128)S(1)}, s32[16,256]{1,0:T(8,128)S(1)}, u32[]{:S(2)}, u32[]{:S(2)}) collective-permute-start(s32[16,256]{1,0:T(8,128)S(1)} %shard_map.127), channel_id=1, source_target_pairs={{0,8},{4,12},{8,0},{12,4},{1,9},{5,13},{9,1},{13,5},{2,10},{6,14},... | collective-permute-start | bytes 49160 | tf_op jit(solution)/shard_map/ppermute | solution.py:357
  12.1 0.0 collective-permute-done.refs_1_
  12.1 2.3 %shard_map.126.mine = f32[16,64,128]{2,1,0:T(8,128)S(1)} custom-call(s32[4,384]{1,0:T(4,128)S(1)} %get-tuple-element.31.order, bf16[288,128,128]{2,1,0:T(8,128)(2,1)S(1)} %copy-done, bf16[17,64,128]{2,1,0:T(8,128)(2,1)S(1)} %get-tuple-element.32.source, f32[16,64,128]{2,1,0:T(8,128)S(1)} %shard_map.125.refs_0_.mine, s32[16,256]{1,0:T(8,128)S(1)} %collective-permute-done.refs_1_), custom_call_target="tpu_custom_call" | custom-call | flops 99999997952 | bytes 9437184 | tf_op jit(solution)/shard_map/pallas_call | solution.py:24
  14.4 0.2 collective-permute-start.1
  14.6 0.0 collective-permute-done.4.refs_2_.refs_6_
  14.6 0.0 copy-start.5
  14.6 1.2 %shard_map.128 = (f32[64,256]{1,0:T(8,128)S(1)}, f32[64,256]{1,0:T(8,128)S(1)}, f32[64,256]{1,0:T(8,128)S(1)}, f32[64,256]{1,0:T(8,128)S(1)}) custom-call(f32[16,64,128]{2,1,0:T(8,128)S(1)} %shard_map.125.refs_0_.mine, f32[16,64,128]{2,1,0:T(8,128)S(1)} %collective-permute-done.2.other, f32[16,128]{1,0:T(8,128)S(1)} %get-tuple-element.30.scale.target_scale.source_scale, ...), custom_call_target="tpu_custom_call" | custom-call | flops 99999997952 | bytes 1048576 | tf_op jit(solution)/shard_map/pallas_call | solution.py:24
  15.9 2.1 %collective-permute-start.6 = (f32[64,256]{1,0:T(8,128)S(1)}, f32[64,256]{1,0:T(8,128)S(1)}, u32[]{:S(2)}, u32[]{:S(2)}) collective-permute-start(f32[64,256]{1,0:T(8,128)S(1)} %get-tuple-element.38), channel_id=1, source_target_pairs={{0,8},{4,12},{8,0},{12,4},{1,9},{5,13},{9,1},{13,5},{2,10},{6,14},... | collective-permute-start | bytes 196616 | tf_op jit(solution)/shard_map/ppermute | solution.py:357
  18.0 1.7 %collective-permute-start.7 = (f32[64,256]{1,0:T(8,128)S(1)}, f32[64,256]{1,0:T(8,128)S(1)}, u32[]{:S(2)}, u32[]{:S(2)}) collective-permute-start(f32[64,256]{1,0:T(8,128)S(1)} %get-tuple-element.39), channel_id=1, source_target_pairs={{0,12},{4,8},{8,4},{12,0},{1,13},{5,9},{9,5},{13,1},{2,14},{6,10},... | collective-permute-start | bytes 196616 | tf_op jit(solution)/shard_map/ppermute | solution.py:357
  19.7 0.0 collective-permute-start.8
  19.7 0.6 shard_map.129
  20.3 3.3 %collective-permute-start.5 = (f32[64,256]{1,0:T(8,128)S(1)}, f32[64,256]{1,0:T(8,128)S(1)}, u32[]{:S(2)}, u32[]{:S(2)}) collective-permute-start(f32[64,256]{1,0:T(8,128)S(1)} %get-tuple-element.36), channel_id=1, source_target_pairs={{0,2},{2,0},{1,3},{3,1},{4,6},{6,4},{5,7},{7,5},{8,10},{10,8},{9,1... | collective-permute-start | bytes 196616 | tf_op jit(solution)/shard_map/ppermute | solution.py:357
  23.6 0.5 shard_map.130
  24.1 0.5 collective-permute-done.6.refs_4_
  24.6 0.7 %collective-permute-done.8.refs_6_ = f32[64,256]{1,0:T(8,128)S(1)} collective-permute-done((f32[64,256]{1,0:T(8,128)S(1)}, f32[64,256]{1,0:T(8,128)S(1)}, u32[]{:S(2)}, u32[]{:S(2)}) %collective-permute-start.8) | collective-permute-done | bytes 65568 | tf_op jit(solution)/shard_map/ppermute | solution.py:357
  25.3 0.6 collective-permute-done.5.refs_1_
  25.8 0.1 shard_map.131
  25.9 0.3 collective-permute-start.11
  26.2 1.9 %collective-permute-start.10 = (f32[72,256]{1,0:T(8,128)S(1)}, f32[72,256]{1,0:T(8,128)S(1)}, u32[]{:S(2)}, u32[]{:S(2)}) collective-permute-start(f32[72,256]{1,0:T(8,128)S(1)} %get-tuple-element.42.refs_0_), channel_id=1, source_target_pairs={{0,2},{2,0},{1,3},{3,1},{4,6},{6,4},{5,7},{7,5},{8,10},{10,8},{9,1... | collective-permute-start | bytes 221192 | tf_op jit(solution)/shard_map/ppermute | solution.py:357
  28.1 0.0 collective-permute-start.9
  28.1 1.2 %collective-permute-start.14 = (f32[64,256]{1,0:T(8,128)S(1)}, f32[64,256]{1,0:T(8,128)S(1)}, u32[]{:S(2)}, u32[]{:S(2)}) collective-permute-start(f32[64,256]{1,0:T(8,128)S(1)} %get-tuple-element.45.refs_0_), channel_id=1, source_target_pairs={{0,8},{4,12},{8,0},{12,4},{1,9},{5,13},{9,1},{13,5},{2,10},{6,14},... | collective-permute-start | bytes 196616 | tf_op jit(solution)/shard_map/ppermute | solution.py:357
  29.3 3.2 %collective-permute-start.13 = (f32[64,256]{1,0:T(8,128)S(1)}, f32[64,256]{1,0:T(8,128)S(1)}, u32[]{:S(2)}, u32[]{:S(2)}) collective-permute-start(f32[64,256]{1,0:T(8,128)S(1)} %get-tuple-element.45.refs_0_), channel_id=1, source_target_pairs={{0,12},{4,8},{8,4},{12,0},{1,13},{5,9},{9,5},{13,1},{2,14},{6,10},... | collective-permute-start | bytes 196616 | tf_op jit(solution)/shard_map/ppermute | solution.py:357
  32.5 2.7 %shard_map.132 = (f32[16,64,128]{2,1,0:T(8,128)S(1)}, f32[16,32,128]{2,1,0:T(8,128)S(1)}, f32[16,32,128]{2,1,0:T(8,128)S(1)}) custom-call(s32[4,384]{1,0:T(4,128)S(1)} %copy-done.5, f32[16,128]{1,0:T(8,128)S(1)} %get-tuple-element.29.scale.source_scale.target_scale, f32[16,128]{1,0:T(8,128)S(1)} %get-tuple-element.30.scale.target_scale.source_scale, ...), custom_call_target="tpu_custom_call" | custom-call | flops 603979776 | bytes 9437184 | tf_op jit(solution)/shard_map/pallas_call | solution.py:24
  35.3 0.5 collective-permute-start.16
  35.8 0.8 %collective-permute-done.14.refs_3_ = f32[64,256]{1,0:T(8,128)S(1)} collective-permute-done((f32[64,256]{1,0:T(8,128)S(1)}, f32[64,256]{1,0:T(8,128)S(1)}, u32[]{:S(2)}, u32[]{:S(2)}) %collective-permute-start.14) | collective-permute-done | bytes 65568 | tf_op jit(solution)/shard_map/ppermute | solution.py:357
  36.6 0.2 collective-permute-done.13.refs_2_
  36.8 0.9 %collective-permute-done.12.refs_1_ = f32[64,256]{1,0:T(8,128)S(1)} collective-permute-done((f32[64,256]{1,0:T(8,128)S(1)}, f32[64,256]{1,0:T(8,128)S(1)}, u32[]{:S(2)}, u32[]{:S(2)}) %collective-permute-start.12) | collective-permute-done | bytes 65568 | tf_op jit(solution)/shard_map/ppermute | solution.py:357
  37.8 1.5 %shard_map.133.after.mine = f32[16,64,128]{2,1,0:T(8,128)S(1)} custom-call(f32[16,32,128]{2,1,0:T(8,128)S(1)} %get-tuple-element.44.after, f32[64,256]{1,0:T(8,128)S(1)} %get-tuple-element.45.refs_0_, f32[64,256]{1,0:T(8,128)S(1)} %collective-permute-done.12.refs_1_, f32[64,256]{1,0:T(8,128)S(1)} %collective-permute-done.13.refs_2_, ...), custom_call_target="tpu_custom_call" | custom-call | flops 99999997952 | tf_op jit(solution)/shard_map/pallas_call | solution.py:24
  39.3 0.1 collective-permute-start.15
  39.4 0.0 copy-start.1
  39.4 0.0 copy-start.3
  39.5 0.9 %collective-permute-start.17 = (f32[4,32,128]{2,1,0:T(8,128)S(1)}, f32[4,32,128]{2,1,0:T(8,128)S(1)}, u32[]{:S(2)}, u32[]{:S(2)}) collective-permute-start(f32[4,32,128]{2,1,0:T(8,128)S(1)} %get-tuple-element.49), channel_id=1, source_target_pairs={{0,8},{4,12},{8,0},{12,4},{1,9},{5,13},{9,1},{13,5},{2,10},{6,14},... | collective-permute-start | bytes 196616 | tf_op jit(solution)/shard_map/ppermute | solution.py:357
  40.3 2.7 %collective-permute-start.18 = (f32[4,32,128]{2,1,0:T(8,128)S(1)}, f32[4,32,128]{2,1,0:T(8,128)S(1)}, u32[]{:S(2)}, u32[]{:S(2)}) collective-permute-start(f32[4,32,128]{2,1,0:T(8,128)S(1)} %get-tuple-element.50), channel_id=1, source_target_pairs={{0,12},{4,8},{8,4},{12,0},{1,13},{5,9},{9,5},{13,1},{2,14},{6,10},... | collective-permute-start | bytes 196616 | tf_op jit(solution)/shard_map/ppermute | solution.py:357
  43.0 0.0 collective-permute-start.19
  43.0 0.0 copy-done.1
  43.1 2.5 %shard_map.135 = (f32[16,64,128]{2,1,0:T(8,128)S(1)}, f32[16,32,128]{2,1,0:T(8,128)S(1)}, f32[16,32,128]{2,1,0:T(8,128)S(1)}) custom-call(s32[4,384]{1,0:T(4,128)S(1)} %copy-done.7, f32[16,64,128]{2,1,0:T(8,128)S(1)} %shard_map.133.after.mine, f32[16,64,128]{2,1,0:T(8,128)S(1)} %collective-permute-done.15.other, ...), custom_call_target="tpu_custom_call" | custom-call | flops 603979776 | bytes 9437184 | tf_op jit(solution)/shard_map/pallas_call | solution.py:24
  45.5 2.4 %collective-permute-done.17.refs_2_ = f32[4,32,128]{2,1,0:T(8,128)S(1)} collective-permute-done((f32[4,32,128]{2,1,0:T(8,128)S(1)}, f32[4,32,128]{2,1,0:T(8,128)S(1)}, u32[]{:S(2)}, u32[]{:S(2)}) %collective-permute-start.17) | collective-permute-done | bytes 65568 | tf_op jit(solution)/shard_map/ppermute | solution.py:357
  48.0 0.8 %collective-permute-done.19.refs_4_ = f32[4,32,128]{2,1,0:T(8,128)S(1)} collective-permute-done((f32[4,32,128]{2,1,0:T(8,128)S(1)}, f32[4,32,128]{2,1,0:T(8,128)S(1)}, u32[]{:S(2)}, u32[]{:S(2)}) %collective-permute-start.19) | collective-permute-done | bytes 65568 | tf_op jit(solution)/shard_map/ppermute | solution.py:357
  48.9 0.1 collective-permute-start.21
  49.0 1.8 %collective-permute-start.20 = (f32[4,32,128]{2,1,0:T(8,128)S(1)}, f32[4,32,128]{2,1,0:T(8,128)S(1)}, u32[]{:S(2)}, u32[]{:S(2)}) collective-permute-start(f32[4,32,128]{2,1,0:T(8,128)S(1)} %shard_map.136.refs_0_.values), channel_id=1, source_target_pairs={{0,12},{4,8},{8,4},{12,0},{1,13},{5,9},{9,5},{13,1},{2,14},{6,10},... | collective-permute-start | bytes 196616 | tf_op jit(solution)/shard_map/ppermute | solution.py:357
  50.8 1.4 %collective-permute-start.24 = (f32[16,32,128]{2,1,0:T(8,128)S(1)}, f32[16,32,128]{2,1,0:T(8,128)S(1)}, u32[]{:S(2)}, u32[]{:S(2)}) collective-permute-start(f32[16,32,128]{2,1,0:T(8,128)S(1)} %shard_map.139.refs_0_.refs_1_), channel_id=1, source_target_pairs={{0,2},{2,0},{1,3},{3,1},{4,6},{6,4},{5,7},{7,5},{8,10},{10,8},{9,1... | collective-permute-start | bytes 786440 | tf_op jit(solution)/shard_map/ppermute | solution.py:357
  52.2 1.1 %collective-permute-start.23 = (f32[4,32,128]{2,1,0:T(8,128)S(1)}, f32[4,32,128]{2,1,0:T(8,128)S(1)}, u32[]{:S(2)}, u32[]{:S(2)}) collective-permute-start(f32[4,32,128]{2,1,0:T(8,128)S(1)} %shard_map.140), channel_id=1, source_target_pairs={{0,8},{4,12},{8,0},{12,4},{1,9},{5,13},{9,1},{13,5},{2,10},{6,14},... | collective-permute-start | bytes 196616 | tf_op jit(solution)/shard_map/ppermute | solution.py:357
  53.3 1.7 %collective-permute-start.22 = (f32[4,32,128]{2,1,0:T(8,128)S(1)}, f32[4,32,128]{2,1,0:T(8,128)S(1)}, u32[]{:S(2)}, u32[]{:S(2)}) collective-permute-start(f32[4,32,128]{2,1,0:T(8,128)S(1)} %shard_map.140), channel_id=1, source_target_pairs={{0,4},{4,0},{8,12},{12,8},{1,5},{5,1},{9,13},{13,9},{2,6},{6,2},{1... | collective-permute-start | bytes 196616 | tf_op jit(solution)/shard_map/ppermute | solution.py:357
  55.0 0.2 collective-permute-done.20.values
  55.3 3.1 %collective-permute-done.23.refs_3_ = f32[4,32,128]{2,1,0:T(8,128)S(1)} collective-permute-done((f32[4,32,128]{2,1,0:T(8,128)S(1)}, f32[4,32,128]{2,1,0:T(8,128)S(1)}, u32[]{:S(2)}, u32[]{:S(2)}) %collective-permute-start.23) | collective-permute-done | bytes 65568 | tf_op jit(solution)/shard_map/ppermute | solution.py:357
  58.4 0.1 collective-permute-start.26
  58.5 0.7 %collective-permute-done.24.refs_2_ = f32[16,32,128]{2,1,0:T(8,128)S(1)} collective-permute-done((f32[16,32,128]{2,1,0:T(8,128)S(1)}, f32[16,32,128]{2,1,0:T(8,128)S(1)}, u32[]{:S(2)}, u32[]{:S(2)}) %collective-permute-start.24) | collective-permute-done | bytes 262176 | tf_op jit(solution)/shard_map/ppermute | solution.py:357
  59.2 0.1 collective-permute-start.25
  59.3 0.7 %collective-permute-done.26.item_other = f32[4,4,32,128]{3,2,1,0:T(8,128)S(1)} collective-permute-done((f32[4,4,32,128]{3,2,1,0:T(8,128)S(1)}, f32[4,4,32,128]{3,2,1,0:T(8,128)S(1)}, u32[]{:S(2)}, u32[]{:S(2)}) %collective-permute-start.26) | collective-permute-done | bytes 262176 | tf_op jit(solution)/shard_map/ppermute | solution.py:357
  60.0 0.9 %collective-permute-done.25.user_other = f32[16,32,128]{2,1,0:T(8,128)S(1)} collective-permute-done((f32[16,32,128]{2,1,0:T(8,128)S(1)}, f32[16,32,128]{2,1,0:T(8,128)S(1)}, u32[]{:S(2)}, u32[]{:S(2)}) %collective-permute-start.25) | collective-permute-done | bytes 262176 | tf_op jit(solution)/shard_map/ppermute | solution.py:357
  60.9 1.1 %shard_map.143 = (f32[64,2048]{1,0:T(8,128)}, f32[64,2048]{1,0:T(8,128)}) custom-call(f32[16,64,128]{2,1,0:T(8,128)S(1)} %get-tuple-element.43.user_half_grad, f32[16,32,128]{2,1,0:T(8,128)S(1)} %shard_map.142.user_mine, f32[16,32,128]{2,1,0:T(8,128)S(1)} %collective-permute-done.25.user_other, f32[16,64,128]{2,1,0:T(8,128)S(1)} %get-tuple-element.53.item_half_grad, ...), custom_call_target="tpu_custom_call" | custom-call | bytes 3145728 | tf_op jit(solution)/shard_map/pallas_call | solution.py:24
  (48 shorter events, 0.3 us)
Async XLA Ops:
  0.6 0.7 %copy-start.10 = (s32[256]{0:T(256)S(1)}, s32[256]{0:T(256)}, u32[]{:S(2)}) copy-start(s32[256]{0:T(256)} %param.21) | copy-start | bytes 3076
  0.6 0.7 %copy-start.9 = (s32[256]{0:T(256)S(1)}, s32[256]{0:T(256)}, u32[]{:S(2)}) copy-start(s32[256]{0:T(256)} %param.20) | copy-start | bytes 3076
  0.7 0.7 %copy-start.8 = (s32[256]{0:T(256)S(1)}, s32[256]{0:T(256)}, u32[]{:S(2)}) copy-start(s32[256]{0:T(256)} %param.19) | copy-start | bytes 3076
  0.7 5.9 %copy-start.13 = (bf16[64,2048]{1,0:T(8,128)(2,1)S(1)}, bf16[64,2048]{1,0:T(8,128)(2,1)}, u32[]{:S(2)}) copy-start(bf16[64,2048]{1,0:T(8,128)(2,1)} %item_emb.3) | copy-start | bytes 786436
  0.7 5.9 %copy-start.11 = (bf16[64,2048]{1,0:T(8,128)(2,1)S(1)}, bf16[64,2048]{1,0:T(8,128)(2,1)}, u32[]{:S(2)}) copy-start(bf16[64,2048]{1,0:T(8,128)(2,1)} %user_emb.3) | copy-start | bytes 786436
  0.7 5.9 %copy-start.17 = (s32[288]{0:T(512)S(1)}, s32[288]{0:T(512)}, u32[]{:S(2)}) copy-start(s32[288]{0:T(512)} %columns.1) | copy-start | bytes 3460
  0.7 5.9 %copy-start.16 = (s32[288]{0:T(512)S(1)}, s32[288]{0:T(512)}, u32[]{:S(2)}) copy-start(s32[288]{0:T(512)} %rows.1) | copy-start | bytes 3460
  0.7 5.9 %copy-start.15 = (s32[2048]{0:T(1024)S(1)}, s32[2048]{0:T(1024)}, u32[]{:S(2)}) copy-start(s32[2048]{0:T(1024)} %param.14) | copy-start | bytes 24580
  0.7 5.9 %copy-start.14 = (s32[2048]{0:T(1024)S(1)}, s32[2048]{0:T(1024)}, u32[]{:S(2)}) copy-start(s32[2048]{0:T(1024)} %param.13) | copy-start | bytes 24580
  0.7 6.9 %copy-start = (bf16[288,128,128]{2,1,0:T(8,128)(2,1)S(1)}, bf16[288,128,128]{2,1,0:T(8,128)(2,1)}, u32[]{:S(2)}) copy-start(bf16[288,128,128]{2,1,0:T(8,128)(2,1)} %vals.7) | copy-start | bytes 28311556
  1.3 7.5 %collective-permute-start.3 = (s32[16,256]{1,0:T(8,128)S(1)}, s32[16,256]{1,0:T(8,128)S(1)}, u32[]{:S(2)}, u32[]{:S(2)}) collective-permute-start(s32[16,256]{1,0:T(8,128)S(1)} %shard_map.123.after.refs_0_.ids.refs_4_), channel_id=1, source_target_pairs={{0,4},{4,0},{8,12},{12,8},{1,5},{5,1},{9,13},{13,9},{2,6},{6,2},{1... | collective-permute-start | bytes 49160 | tf_op jit(solution)/shard_map/ppermute | solution.py:357
  4.4 7.7 %collective-permute-start = (s32[16,256]{1,0:T(8,128)S(1)}, s32[16,256]{1,0:T(8,128)S(1)}, u32[]{:S(2)}, u32[]{:S(2)}) collective-permute-start(s32[16,256]{1,0:T(8,128)S(1)} %shard_map.123.after.refs_0_.ids.refs_4_), channel_id=1, source_target_pairs={{0,2},{2,0},{1,3},{3,1},{4,6},{6,4},{5,7},{7,5},{8,10},{10,8},{9,1... | collective-permute-start | bytes 49160 | tf_op jit(solution)/shard_map/ppermute | solution.py:357
  7.5 4.5 %copy-start.4 = (s32[4,384]{1,0:T(4,128)}, s32[4,384]{1,0:T(4,128)S(1)}, u32[]{:S(2)}) copy-start(s32[4,384]{1,0:T(4,128)S(1)} %get-tuple-element.28.order) | copy-start | bytes 18436
  7.6 6.8 %copy-start.6 = (s32[4,384]{1,0:T(4,128)}, s32[4,384]{1,0:T(4,128)S(1)}, u32[]{:S(2)}) copy-start(s32[4,384]{1,0:T(4,128)S(1)} %get-tuple-element.31.order) | copy-start | bytes 18436
  7.6 25.0 %copy-start.2 = (f32[16,128]{1,0:T(8,128)}, f32[16,128]{1,0:T(8,128)S(1)}, u32[]{:S(2)}) copy-start(f32[16,128]{1,0:T(8,128)S(1)} %get-tuple-element.29.scale.source_scale.target_scale) | copy-start | bytes 24580
  8.8 5.8 %collective-permute-start.2 = (f32[16,64,128]{2,1,0:T(8,128)S(1)}, f32[16,64,128]{2,1,0:T(8,128)S(1)}, u32[]{:S(2)}, u32[]{:S(2)}) collective-permute-start(f32[16,64,128]{2,1,0:T(8,128)S(1)} %shard_map.125.refs_0_.mine), channel_id=1, source_target_pairs={{0,1},{1,0},{2,3},{3,2},{4,5},{5,4},{6,7},{7,6},{8,9},{9,8},{10,11... | collective-permute-start | bytes 1572872 | tf_op jit(solution)/shard_map/ppermute | solution.py:357
  8.9 5.7 %collective-permute-start.4 = (s32[16,256]{1,0:T(8,128)S(1)}, s32[16,256]{1,0:T(8,128)S(1)}, u32[]{:S(2)}, u32[]{:S(2)}) collective-permute-start(s32[16,256]{1,0:T(8,128)S(1)} %shard_map.127), channel_id=1, source_target_pairs={{0,8},{4,12},{8,0},{12,4},{1,9},{5,13},{9,1},{13,5},{2,10},{6,14},... | collective-permute-start | bytes 49160 | tf_op jit(solution)/shard_map/ppermute | solution.py:357
  14.4 5.3 %collective-permute-start.1 = (f32[16,64,128]{2,1,0:T(8,128)S(1)}, f32[16,64,128]{2,1,0:T(8,128)S(1)}, u32[]{:S(2)}, u32[]{:S(2)}) collective-permute-start(f32[16,64,128]{2,1,0:T(8,128)S(1)} %shard_map.126.mine), channel_id=1, source_target_pairs={{0,1},{1,0},{2,3},{3,2},{4,5},{5,4},{6,7},{7,6},{8,9},{9,8},{10,11... | collective-permute-start | bytes 1572872 | tf_op jit(solution)/shard_map/ppermute | solution.py:357
  14.6 9.0 %copy-start.12 = (bf16[64,2048]{1,0:T(8,128)(2,1)S(1)}, bf16[64,2048]{1,0:T(8,128)(2,1)}, u32[]{:S(2)}) copy-start(bf16[64,2048]{1,0:T(8,128)(2,1)} %user_emb.3) | copy-start | bytes 786436
  14.6 17.9 %copy-start.5 = (s32[4,384]{1,0:T(4,128)S(1)}, s32[4,384]{1,0:T(4,128)}, u32[]{:S(2)}) copy-start(s32[4,384]{1,0:T(4,128)} %copy-done.4) | copy-start | bytes 18436
  15.9 8.7 %collective-permute-start.6 = (f32[64,256]{1,0:T(8,128)S(1)}, f32[64,256]{1,0:T(8,128)S(1)}, u32[]{:S(2)}, u32[]{:S(2)}) collective-permute-start(f32[64,256]{1,0:T(8,128)S(1)} %get-tuple-element.38), channel_id=1, source_target_pairs={{0,8},{4,12},{8,0},{12,4},{1,9},{5,13},{9,1},{13,5},{2,10},{6,14},... | collective-permute-start | bytes 196616 | tf_op jit(solution)/shard_map/ppermute | solution.py:357
  18.0 6.5 %collective-permute-start.7 = (f32[64,256]{1,0:T(8,128)S(1)}, f32[64,256]{1,0:T(8,128)S(1)}, u32[]{:S(2)}, u32[]{:S(2)}) collective-permute-start(f32[64,256]{1,0:T(8,128)S(1)} %get-tuple-element.39), channel_id=1, source_target_pairs={{0,12},{4,8},{8,4},{12,0},{1,13},{5,9},{9,5},{13,1},{2,14},{6,10},... | collective-permute-start | bytes 196616 | tf_op jit(solution)/shard_map/ppermute | solution.py:357
  19.7 5.6 %collective-permute-start.8 = (f32[64,256]{1,0:T(8,128)S(1)}, f32[64,256]{1,0:T(8,128)S(1)}, u32[]{:S(2)}, u32[]{:S(2)}) collective-permute-start(f32[64,256]{1,0:T(8,128)S(1)} %get-tuple-element.40), channel_id=1, source_target_pairs={{0,4},{4,0},{8,12},{12,8},{1,5},{5,1},{9,13},{13,9},{2,6},{6,2},{1... | collective-permute-start | bytes 196616 | tf_op jit(solution)/shard_map/ppermute | solution.py:357
  20.3 5.6 %collective-permute-start.5 = (f32[64,256]{1,0:T(8,128)S(1)}, f32[64,256]{1,0:T(8,128)S(1)}, u32[]{:S(2)}, u32[]{:S(2)}) collective-permute-start(f32[64,256]{1,0:T(8,128)S(1)} %get-tuple-element.36), channel_id=1, source_target_pairs={{0,2},{2,0},{1,3},{3,1},{4,6},{6,4},{5,7},{7,5},{8,10},{10,8},{9,1... | collective-permute-start | bytes 196616 | tf_op jit(solution)/shard_map/ppermute | solution.py:357
  25.9 6.6 %collective-permute-start.11 = (f32[72,256]{1,0:T(8,128)S(1)}, f32[72,256]{1,0:T(8,128)S(1)}, u32[]{:S(2)}, u32[]{:S(2)}) collective-permute-start(f32[72,256]{1,0:T(8,128)S(1)} %get-tuple-element.42.refs_0_), channel_id=1, source_target_pairs={{0,3},{1,2},{2,1},{3,0},{4,7},{5,6},{6,5},{7,4},{8,11},{9,10},{10,... | collective-permute-start | bytes 221192 | tf_op jit(solution)/shard_map/ppermute | solution.py:456
  26.2 6.3 %collective-permute-start.10 = (f32[72,256]{1,0:T(8,128)S(1)}, f32[72,256]{1,0:T(8,128)S(1)}, u32[]{:S(2)}, u32[]{:S(2)}) collective-permute-start(f32[72,256]{1,0:T(8,128)S(1)} %get-tuple-element.42.refs_0_), channel_id=1, source_target_pairs={{0,2},{2,0},{1,3},{3,1},{4,6},{6,4},{5,7},{7,5},{8,10},{10,8},{9,1... | collective-permute-start | bytes 221192 | tf_op jit(solution)/shard_map/ppermute | solution.py:357
  28.1 4.4 %collective-permute-start.9 = (f32[72,256]{1,0:T(8,128)S(1)}, f32[72,256]{1,0:T(8,128)S(1)}, u32[]{:S(2)}, u32[]{:S(2)}) collective-permute-start(f32[72,256]{1,0:T(8,128)S(1)} %get-tuple-element.42.refs_0_), channel_id=1, source_target_pairs={{0,1},{1,0},{2,3},{3,2},{4,5},{5,4},{6,7},{7,6},{8,9},{9,8},{10,11... | collective-permute-start | bytes 221192 | tf_op jit(solution)/shard_map/ppermute | solution.py:357
  28.1 8.5 %collective-permute-start.14 = (f32[64,256]{1,0:T(8,128)S(1)}, f32[64,256]{1,0:T(8,128)S(1)}, u32[]{:S(2)}, u32[]{:S(2)}) collective-permute-start(f32[64,256]{1,0:T(8,128)S(1)} %get-tuple-element.45.refs_0_), channel_id=1, source_target_pairs={{0,8},{4,12},{8,0},{12,4},{1,9},{5,13},{9,1},{13,5},{2,10},{6,14},... | collective-permute-start | bytes 196616 | tf_op jit(solution)/shard_map/ppermute | solution.py:357
  29.3 7.5 %collective-permute-start.13 = (f32[64,256]{1,0:T(8,128)S(1)}, f32[64,256]{1,0:T(8,128)S(1)}, u32[]{:S(2)}, u32[]{:S(2)}) collective-permute-start(f32[64,256]{1,0:T(8,128)S(1)} %get-tuple-element.45.refs_0_), channel_id=1, source_target_pairs={{0,12},{4,8},{8,4},{12,0},{1,13},{5,9},{9,5},{13,1},{2,14},{6,10},... | collective-permute-start | bytes 196616 | tf_op jit(solution)/shard_map/ppermute | solution.py:357
  32.5 5.3 %collective-permute-start.12 = (f32[64,256]{1,0:T(8,128)S(1)}, f32[64,256]{1,0:T(8,128)S(1)}, u32[]{:S(2)}, u32[]{:S(2)}) collective-permute-start(f32[64,256]{1,0:T(8,128)S(1)} %get-tuple-element.45.refs_0_), channel_id=1, source_target_pairs={{0,4},{4,0},{8,12},{12,8},{1,5},{5,1},{9,13},{13,9},{2,6},{6,2},{1... | collective-permute-start | bytes 196616 | tf_op jit(solution)/shard_map/ppermute | solution.py:357
  35.3 4.1 %collective-permute-start.16 = (f32[16,32,128]{2,1,0:T(8,128)S(1)}, f32[16,32,128]{2,1,0:T(8,128)S(1)}, u32[]{:S(2)}, u32[]{:S(2)}) collective-permute-start(f32[16,32,128]{2,1,0:T(8,128)S(1)} %get-tuple-element.44.after), channel_id=1, source_target_pairs={{0,1},{1,0},{2,3},{3,2},{4,5},{5,4},{6,7},{7,6},{8,9},{9,8},{10,11... | collective-permute-start | bytes 786440 | tf_op jit(solution)/shard_map/ppermute | solution.py:357
  39.3 3.7 %collective-permute-start.15 = (f32[16,64,128]{2,1,0:T(8,128)S(1)}, f32[16,64,128]{2,1,0:T(8,128)S(1)}, u32[]{:S(2)}, u32[]{:S(2)}) collective-permute-start(f32[16,64,128]{2,1,0:T(8,128)S(1)} %shard_map.133.after.mine), channel_id=1, source_target_pairs={{0,1},{1,0},{2,3},{3,2},{4,5},{5,4},{6,7},{7,6},{8,9},{9,8},{10,11... | collective-permute-start | bytes 1572872 | tf_op jit(solution)/shard_map/ppermute | solution.py:357
  39.4 3.7 %copy-start.1 = (bf16[288,128,128]{2,1,0:T(8,128)(2,1)S(1)}, bf16[288,128,128]{2,1,0:T(8,128)(2,1)}, u32[]{:S(2)}) copy-start(bf16[288,128,128]{2,1,0:T(8,128)(2,1)} %vals.7) | copy-start | bytes 28311556
  39.4 3.7 %copy-start.3 = (f32[16,128]{1,0:T(8,128)S(1)}, f32[16,128]{1,0:T(8,128)}, u32[]{:S(2)}) copy-start(f32[16,128]{1,0:T(8,128)} %copy-done.2) | copy-start | bytes 24580
  39.4 3.7 %copy-start.7 = (s32[4,384]{1,0:T(4,128)S(1)}, s32[4,384]{1,0:T(4,128)}, u32[]{:S(2)}) copy-start(s32[4,384]{1,0:T(4,128)} %copy-done.6) | copy-start | bytes 18436
  39.5 8.5 %collective-permute-start.17 = (f32[4,32,128]{2,1,0:T(8,128)S(1)}, f32[4,32,128]{2,1,0:T(8,128)S(1)}, u32[]{:S(2)}, u32[]{:S(2)}) collective-permute-start(f32[4,32,128]{2,1,0:T(8,128)S(1)} %get-tuple-element.49), channel_id=1, source_target_pairs={{0,8},{4,12},{8,0},{12,4},{1,9},{5,13},{9,1},{13,5},{2,10},{6,14},... | collective-permute-start | bytes 196616 | tf_op jit(solution)/shard_map/ppermute | solution.py:357
  40.3 7.7 %collective-permute-start.18 = (f32[4,32,128]{2,1,0:T(8,128)S(1)}, f32[4,32,128]{2,1,0:T(8,128)S(1)}, u32[]{:S(2)}, u32[]{:S(2)}) collective-permute-start(f32[4,32,128]{2,1,0:T(8,128)S(1)} %get-tuple-element.50), channel_id=1, source_target_pairs={{0,12},{4,8},{8,4},{12,0},{1,13},{5,9},{9,5},{13,1},{2,14},{6,10},... | collective-permute-start | bytes 196616 | tf_op jit(solution)/shard_map/ppermute | solution.py:357
  43.0 5.8 %collective-permute-start.19 = (f32[4,32,128]{2,1,0:T(8,128)S(1)}, f32[4,32,128]{2,1,0:T(8,128)S(1)}, u32[]{:S(2)}, u32[]{:S(2)}) collective-permute-start(f32[4,32,128]{2,1,0:T(8,128)S(1)} %get-tuple-element.51), channel_id=1, source_target_pairs={{0,4},{4,0},{8,12},{12,8},{1,5},{5,1},{9,13},{13,9},{2,6},{6,2},{1... | collective-permute-start | bytes 196616 | tf_op jit(solution)/shard_map/ppermute | solution.py:357
  48.9 1.9 %collective-permute-start.21 = (f32[16,32,128]{2,1,0:T(8,128)S(1)}, f32[16,32,128]{2,1,0:T(8,128)S(1)}, u32[]{:S(2)}, u32[]{:S(2)}) collective-permute-start(f32[16,32,128]{2,1,0:T(8,128)S(1)} %shard_map.138), channel_id=1, source_target_pairs={{0,1},{1,0},{2,3},{3,2},{4,5},{5,4},{6,7},{7,6},{8,9},{9,8},{10,11... | collective-permute-start | bytes 786440 | tf_op jit(solution)/shard_map/ppermute | solution.py:357
  49.0 6.3 %collective-permute-start.20 = (f32[4,32,128]{2,1,0:T(8,128)S(1)}, f32[4,32,128]{2,1,0:T(8,128)S(1)}, u32[]{:S(2)}, u32[]{:S(2)}) collective-permute-start(f32[4,32,128]{2,1,0:T(8,128)S(1)} %shard_map.136.refs_0_.values), channel_id=1, source_target_pairs={{0,12},{4,8},{8,4},{12,0},{1,13},{5,9},{9,5},{13,1},{2,14},{6,10},... | collective-permute-start | bytes 196616 | tf_op jit(solution)/shard_map/ppermute | solution.py:357
  50.8 8.4 %collective-permute-start.24 = (f32[16,32,128]{2,1,0:T(8,128)S(1)}, f32[16,32,128]{2,1,0:T(8,128)S(1)}, u32[]{:S(2)}, u32[]{:S(2)}) collective-permute-start(f32[16,32,128]{2,1,0:T(8,128)S(1)} %shard_map.139.refs_0_.refs_1_), channel_id=1, source_target_pairs={{0,2},{2,0},{1,3},{3,1},{4,6},{6,4},{5,7},{7,5},{8,10},{10,8},{9,1... | collective-permute-start | bytes 786440 | tf_op jit(solution)/shard_map/ppermute | solution.py:357
  52.2 6.2 %collective-permute-start.23 = (f32[4,32,128]{2,1,0:T(8,128)S(1)}, f32[4,32,128]{2,1,0:T(8,128)S(1)}, u32[]{:S(2)}, u32[]{:S(2)}) collective-permute-start(f32[4,32,128]{2,1,0:T(8,128)S(1)} %shard_map.140), channel_id=1, source_target_pairs={{0,8},{4,12},{8,0},{12,4},{1,9},{5,13},{9,1},{13,5},{2,10},{6,14},... | collective-permute-start | bytes 196616 | tf_op jit(solution)/shard_map/ppermute | solution.py:357
  53.3 5.1 %collective-permute-start.22 = (f32[4,32,128]{2,1,0:T(8,128)S(1)}, f32[4,32,128]{2,1,0:T(8,128)S(1)}, u32[]{:S(2)}, u32[]{:S(2)}) collective-permute-start(f32[4,32,128]{2,1,0:T(8,128)S(1)} %shard_map.140), channel_id=1, source_target_pairs={{0,4},{4,0},{8,12},{12,8},{1,5},{5,1},{9,13},{13,9},{2,6},{6,2},{1... | collective-permute-start | bytes 196616 | tf_op jit(solution)/shard_map/ppermute | solution.py:357
  58.4 1.6 %collective-permute-start.26 = (f32[4,4,32,128]{3,2,1,0:T(8,128)S(1)}, f32[4,4,32,128]{3,2,1,0:T(8,128)S(1)}, u32[]{:S(2)}, u32[]{:S(2)}) collective-permute-start(f32[4,4,32,128]{3,2,1,0:T(8,128)S(1)} %shard_map.141.refs_0_.item_mine), channel_id=1, source_target_pairs={{0,1},{1,0},{2,3},{3,2},{4,5},{5,4},{6,7},{7,6},{8,9},{9,8},{10,11... | collective-permute-start | bytes 786440 | tf_op jit(solution)/shard_map/ppermute | solution.py:357
  59.2 1.6 %collective-permute-start.25 = (f32[16,32,128]{2,1,0:T(8,128)S(1)}, f32[16,32,128]{2,1,0:T(8,128)S(1)}, u32[]{:S(2)}, u32[]{:S(2)}) collective-permute-start(f32[16,32,128]{2,1,0:T(8,128)S(1)} %shard_map.142.user_mine), channel_id=1, source_target_pairs={{0,1},{1,0},{2,3},{3,2},{4,5},{5,4},{6,7},{7,6},{8,9},{9,8},{10,11... | collective-permute-start | bytes 786440 | tf_op jit(solution)/shard_map/ppermute | solution.py:357

commit v8 on v7

--- a/solution.py
+++ b/solution.py
@@ -231,7 +231,7 @@
             table, blocks, size, put)
 
 
-def gather_base(user_emb, item_emb, ids, user_out, item_out):
+def gather_base(user_emb, item_emb, ids, after, user_out, item_out):
     tile = ids.shape[1]
     user_out[...] = pick(user_emb, rows_of(ids, [0]), tile)
     item_out[...] = pick(item_emb, rows_of(ids, [1, 2]), tile)
@@ -417,28 +417,33 @@
 
     hot_flops = 2 * 3 * width * trips * size
 
-    def reduced(table, scale, arrays, places, axis, offsets, after):
-        peers, blocks = len(places), scale.shape[0]
-        dealt = call(
-            functools.partial(gather, places, len(arrays)), [shape(width, trips)] * peers,
-            (table, swap(table), scale, after, *arrays),
+    def picked(table, other, scale, arrays, places, after, flops):
+        return call(
+            functools.partial(gather, places, len(arrays)), [shape(width, trips)] * len(places),
+            (table, other, scale, after, *arrays),
             [VMEM] * 3 + [ANY] + [VMEM] * len(arrays),
-            [pltpu.VMEM((3 * width, blocks * size), BF16)],
-            HEAVY if axis == "user" else 0, 8 * blocks * width * size,
+            [pltpu.VMEM((3 * width, scale.shape[0] * size), BF16)], flops,
         )
-        return [dealt[0]] + [swap(part, axis, peers, o) for part, o in zip(dealt[1:], offsets)]
 
     def item_rows(offset):
         index, row = ids_item[offset]
         return index, [row + 1, row + 2]
 
-    item_parts = reduced(item_table, item_scale, held, [item_rows(o) for o in [0, *met]],
-                         "user", met, ids)
-    user_parts = reduced(user_table, user_scale, ids_user, [(o, [0]) for o in range(items)],
-                         "item", list(range(1, items)), item_parts[0])
+    other = swap(item_table)
+    first = picked(item_table, other, item_scale, held, [item_rows(o) for o in met[:1]], ids, 0)
+    rest = picked(item_table, other, item_scale, held, [item_rows(o) for o in [0, *met[1:]]],
+                  first[0] if first else ids, HEAVY)
+    item_parts = [rest[0]]
+    for offset, part in zip(met, [*first, *rest[1:]]):
+        come = swap(part, "user", users, offset)
+        item_parts.append(hold(come, flops=MEDIUM) if offset == met[0] else come)
+    dealt = picked(user_table, swap(user_table), user_scale, ids_user,
+                   [(o, [0]) for o in range(items)], rest[0], 0)
+    user_parts = [dealt[0]] + [
+        swap(part, "item", items, o) for o, part in zip(range(1, items), dealt[1:])]
     user_base, item_base = call(
-        gather_base, [shape(width, trips)] * 2, (user_emb, item_emb, ids),
-        [VMEM, VMEM, VMEM], (), 4 * width * trips * size * (user_blocks + item_blocks),
+        gather_base, [shape(width, trips)] * 2, (user_emb, item_emb, ids, dealt[0]),
+        [VMEM, VMEM, VMEM, ANY], (), 4 * width * trips * size * (user_blocks + item_blocks),
         2 * width * size * (user_blocks + item_blocks),
     )
     user_parts.append(user_base)

time: 62.2 us -> 62.6 us (level); the launches traced: 62 us -> 61.6 us
  starting transfers between devices: 32.1 us -> 29.4 us
  Pallas kernels: 14.7 us -> 16.2 us
  waiting for transfers between devices: 12.6 us -> 13.5 us
    ppermute x26, starting transfers between devices: 31.8 us -> 28.9 us  [swap(): return lax.ppermute(values, axis, [(i, i ^ offset) for i in range(peers)])]
    pallas_call x22 -> x24, Pallas kernels: 14.7 us -> 16.2 us  [call(): pl.pallas_call(kernel, out_shape=outs, in_specs=specs, out_specs=jax.tree...]
    ppermute x26, waiting for transfers between devices: 12.6 us -> 13.5 us  [swap(): return lax.ppermute(values, axis, [(i, i ^ offset) for i in range(peers)])]
  transfers between devices with their start and end apart: 27 -> 27, of which waited for: 13 -> 14; matrix products, arithmetic and copies ran while one was open for 0% -> 0% of each run, Pallas kernels for 22% -> 24%
where the time goes in v8:
time: 62.6 us; the launch traced here: 61.6 us
  starting transfers between devices  29.4 us (47%)
  Pallas kernels  16.2 us (26%)
  waiting for transfers between devices  13.5 us (22%)
  between operations  1.69 us (3%)
  local copies, waits for them, and re-layouts  0.74 us (1%)
    ppermute x26, starting transfers between devices, swap(): return lax.ppermute(values, axis, [(i, i ^ offset) for i in range(peers)])  28.9 us
    pallas_call x24, Pallas kernels, call(): pl.pallas_call(kernel, out_shape=outs, in_specs=specs, out_specs=jax.tree...  16.2 us
    ppermute x26, waiting for transfers between devices, swap(): return lax.ppermute(values, axis, [(i, i ^ offset) for i in range(peers)])  13.5 us
  transfers between devices with their start and end apart: 27, of which 14 were waited for; matrix products, arithmetic and copies ran while one was open for 0% of the time, Pallas kernels for 24%

profile of v8, /device:TPU:0, one launch (start us, length us, event | category | flops | bytes accessed | tf_op | source)
XLA Modules:
  0.0 61.6 jit_solution(6314944817161368343)
XLA Ops:
  0.7 0.0 copy-start.9
  0.7 0.0 copy-start
  0.7 0.6 copy-done.8
  1.3 0.0 copy-done.7
  1.3 0.0 copy-done.6
  1.3 3.1 %collective-permute-start.3 = (s32[16,256]{1,0:T(8,128)S(1)}, s32[16,256]{1,0:T(8,128)S(1)}, u32[]{:S(2)}, u32[]{:S(2)}) collective-permute-start(s32[16,256]{1,0:T(8,128)S(1)} %shard_map.123.after.refs_0_.ids.refs_4_), channel_id=1, source_target_pairs={{0,4},{4,0},{8,12},{12,8},{1,5},{5,1},{9,13},{13,9},{2,6},{6,2},{1... | collective-permute-start | bytes 49160 | tf_op jit(solution)/shard_map/ppermute | solution.py:357
  4.4 1.5 %collective-permute-start = (s32[16,256]{1,0:T(8,128)S(1)}, s32[16,256]{1,0:T(8,128)S(1)}, u32[]{:S(2)}, u32[]{:S(2)}) collective-permute-start(s32[16,256]{1,0:T(8,128)S(1)} %shard_map.123.after.refs_0_.ids.refs_4_), channel_id=1, source_target_pairs={{0,2},{2,0},{1,3},{3,1},{4,6},{6,4},{5,7},{7,5},{8,10},{10,8},{9,1... | collective-permute-start | bytes 49160 | tf_op jit(solution)/shard_map/ppermute | solution.py:357
  6.6 0.9 %shard_map.124 = (bf16[17,64,128]{2,1,0:T(8,128)(2,1)S(1)}, bf16[17,64,128]{2,1,0:T(8,128)(2,1)S(1)}, f32[16,128]{1,0:T(8,128)S(1)}, f32[16,128]{1,0:T(8,128)S(1...) custom-call(s32[1]{0:T(128)S(6)} %copy.13.count, s32[288]{0:T(512)S(1)} %copy-done.14, s32[288]{0:T(512)S(1)} %copy-done.15, ...), custom_call_target="tpu_custom_call" | custom-call | flops 603979776 | bytes 9437184 | tf_op jit(solution)/shard_map/pallas_call | solution.py:24
  7.5 0.0 copy-start.2
  7.6 0.0 copy-start.4
  7.6 1.7 %shard_map.125.refs_0_.mine = f32[16,64,128]{2,1,0:T(8,128)S(1)} custom-call(s32[4,384]{1,0:T(4,128)S(1)} %get-tuple-element.27.order, bf16[288,128,128]{2,1,0:T(8,128)(2,1)S(1)} %copy-done, bf16[17,64,128]{2,1,0:T(8,128)(2,1)S(1)} %get-tuple-element.32.source, s32[16,256]{1,0:T(8,128)S(1)} %shard_map.123.after.refs_0_.ids.refs_4_), custom_call_target="tpu_custom_call" | custom-call | flops 603979776 | bytes 9437184 | tf_op jit(solution)/shard_map/pallas_call | solution.py:24
  9.3 0.1 collective-permute-start.2
  9.4 3.2 %collective-permute-start.4 = (s32[16,256]{1,0:T(8,128)S(1)}, s32[16,256]{1,0:T(8,128)S(1)}, u32[]{:S(2)}, u32[]{:S(2)}) collective-permute-start(s32[16,256]{1,0:T(8,128)S(1)} %shard_map.127), channel_id=1, source_target_pairs={{0,8},{4,12},{8,0},{12,4},{1,9},{5,13},{9,1},{13,5},{2,10},{6,14},... | collective-permute-start | bytes 49160 | tf_op jit(solution)/shard_map/ppermute | solution.py:357
  12.6 2.3 %shard_map.126.mine = f32[16,64,128]{2,1,0:T(8,128)S(1)} custom-call(s32[4,384]{1,0:T(4,128)S(1)} %get-tuple-element.30.order, bf16[288,128,128]{2,1,0:T(8,128)(2,1)S(1)} %copy-done, bf16[17,64,128]{2,1,0:T(8,128)(2,1)S(1)} %get-tuple-element.31.source, f32[16,64,128]{2,1,0:T(8,128)S(1)} %shard_map.125.refs_0_.mine, s32[16,256]{1,0:T(8,128)S(1)} %collective-permute-done.refs_1_), custom_call_target="tpu_custom_call" | custom-call | flops 99999997952 | bytes 9437184 | tf_op jit(solution)/shard_map/pallas_call | solution.py:24
  14.9 0.2 collective-permute-start.1
  15.2 0.6 shard_map.128.after
  15.7 0.0 copy-start.10
  15.8 2.1 %collective-permute-start.6 = (f32[64,256]{1,0:T(8,128)S(1)}, f32[64,256]{1,0:T(8,128)S(1)}, u32[]{:S(2)}, u32[]{:S(2)}) collective-permute-start(f32[64,256]{1,0:T(8,128)S(1)} %shard_map.128.after), channel_id=1, source_target_pairs={{0,8},{4,12},{8,0},{12,4},{1,9},{5,13},{9,1},{13,5},{2,10},{6,14},... | collective-permute-start | bytes 196616 | tf_op jit(solution)/shard_map/ppermute | solution.py:357
  17.9 1.0 %shard_map.129 = (f32[64,256]{1,0:T(8,128)S(1)}, f32[64,256]{1,0:T(8,128)S(1)}, f32[64,256]{1,0:T(8,128)S(1)}) custom-call(f32[16,64,128]{2,1,0:T(8,128)S(1)} %shard_map.125.refs_0_.mine, f32[16,64,128]{2,1,0:T(8,128)S(1)} %collective-permute-done.2.other, f32[16,128]{1,0:T(8,128)S(1)} %get-tuple-element.29.scale.target_scale.source_scale, ...), custom_call_target="tpu_custom_call" | custom-call | flops 99999997952 | tf_op jit(solution)/shard_map/pallas_call | solution.py:24
  18.9 0.0 copy-start.3
  18.9 1.4 %collective-permute-start.7 = (f32[64,256]{1,0:T(8,128)S(1)}, f32[64,256]{1,0:T(8,128)S(1)}, u32[]{:S(2)}, u32[]{:S(2)}) collective-permute-start(f32[64,256]{1,0:T(8,128)S(1)} %get-tuple-element.37), channel_id=1, source_target_pairs={{0,12},{4,8},{8,4},{12,0},{1,13},{5,9},{9,5},{13,1},{2,14},{6,10},... | collective-permute-start | bytes 196616 | tf_op jit(solution)/shard_map/ppermute | solution.py:357
  20.3 0.1 collective-permute-start.8
  20.4 0.6 shard_map.130
  21.0 2.5 %collective-permute-start.5 = (f32[64,256]{1,0:T(8,128)S(1)}, f32[64,256]{1,0:T(8,128)S(1)}, u32[]{:S(2)}, u32[]{:S(2)}) collective-permute-start(f32[64,256]{1,0:T(8,128)S(1)} %get-tuple-element.35), channel_id=1, source_target_pairs={{0,2},{2,0},{1,3},{3,1},{4,6},{6,4},{5,7},{7,5},{8,10},{10,8},{9,1... | collective-permute-start | bytes 196616 | tf_op jit(solution)/shard_map/ppermute | solution.py:357
  23.5 0.5 shard_map.131
  24.1 1.2 %collective-permute-done.7.refs_5_ = f32[64,256]{1,0:T(8,128)S(1)} collective-permute-done((f32[64,256]{1,0:T(8,128)S(1)}, f32[64,256]{1,0:T(8,128)S(1)}, u32[]{:S(2)}, u32[]{:S(2)}) %collective-permute-start.7) | collective-permute-done | bytes 65568 | tf_op jit(solution)/shard_map/ppermute | solution.py:357
  25.2 0.3 collective-permute-done.8.refs_6_
  25.5 0.2 collective-permute-done.5.refs_1_
  25.8 0.1 shard_map.133
  25.9 0.5 collective-permute-start.11
  26.3 1.7 %collective-permute-start.10 = (f32[72,256]{1,0:T(8,128)S(1)}, f32[72,256]{1,0:T(8,128)S(1)}, u32[]{:S(2)}, u32[]{:S(2)}) collective-permute-start(f32[72,256]{1,0:T(8,128)S(1)} %get-tuple-element.40.refs_0_), channel_id=1, source_target_pairs={{0,2},{2,0},{1,3},{3,1},{4,6},{6,4},{5,7},{7,5},{8,10},{10,8},{9,1... | collective-permute-start | bytes 221192 | tf_op jit(solution)/shard_map/ppermute | solution.py:357
  28.0 0.0 collective-permute-start.9
  28.1 2.3 %collective-permute-start.14 = (f32[64,256]{1,0:T(8,128)S(1)}, f32[64,256]{1,0:T(8,128)S(1)}, u32[]{:S(2)}, u32[]{:S(2)}) collective-permute-start(f32[64,256]{1,0:T(8,128)S(1)} %get-tuple-element.43.refs_0_), channel_id=1, source_target_pairs={{0,8},{4,12},{8,0},{12,4},{1,9},{5,13},{9,1},{13,5},{2,10},{6,14},... | collective-permute-start | bytes 196616 | tf_op jit(solution)/shard_map/ppermute | solution.py:357
  30.3 1.3 %collective-permute-start.13 = (f32[64,256]{1,0:T(8,128)S(1)}, f32[64,256]{1,0:T(8,128)S(1)}, u32[]{:S(2)}, u32[]{:S(2)}) collective-permute-start(f32[64,256]{1,0:T(8,128)S(1)} %get-tuple-element.43.refs_0_), channel_id=1, source_target_pairs={{0,12},{4,8},{8,4},{12,0},{1,13},{5,9},{9,5},{13,1},{2,14},{6,10},... | collective-permute-start | bytes 196616 | tf_op jit(solution)/shard_map/ppermute | solution.py:357
  31.6 0.2 collective-permute-done.10.refs_2_
  31.9 3.3 %shard_map.134 = (f32[16,64,128]{2,1,0:T(8,128)S(1)}, f32[16,32,128]{2,1,0:T(8,128)S(1)}, f32[16,32,128]{2,1,0:T(8,128)S(1)}) custom-call(s32[4,384]{1,0:T(4,128)S(1)} %copy-done.3, f32[16,128]{1,0:T(8,128)S(1)} %get-tuple-element.28.scale.source_scale.target_scale, f32[16,128]{1,0:T(8,128)S(1)} %get-tuple-element.29.scale.target_scale.source_scale, ...), custom_call_target="tpu_custom_call" | custom-call | flops 603979776 | bytes 9437184 | tf_op jit(solution)/shard_map/pallas_call | solution.py:24
  35.2 0.2 collective-permute-start.16
  35.3 1.3 %collective-permute-done.14.refs_3_ = f32[64,256]{1,0:T(8,128)S(1)} collective-permute-done((f32[64,256]{1,0:T(8,128)S(1)}, f32[64,256]{1,0:T(8,128)S(1)}, u32[]{:S(2)}, u32[]{:S(2)}) %collective-permute-start.14) | collective-permute-done | bytes 65568 | tf_op jit(solution)/shard_map/ppermute | solution.py:357
  36.6 0.8 %collective-permute-done.12.refs_1_ = f32[64,256]{1,0:T(8,128)S(1)} collective-permute-done((f32[64,256]{1,0:T(8,128)S(1)}, f32[64,256]{1,0:T(8,128)S(1)}, u32[]{:S(2)}, u32[]{:S(2)}) %collective-permute-start.12) | collective-permute-done | bytes 65568 | tf_op jit(solution)/shard_map/ppermute | solution.py:357
  37.4 1.5 %shard_map.135.after.mine = f32[16,64,128]{2,1,0:T(8,128)S(1)} custom-call(f32[16,32,128]{2,1,0:T(8,128)S(1)} %get-tuple-element.42.after, f32[64,256]{1,0:T(8,128)S(1)} %get-tuple-element.43.refs_0_, f32[64,256]{1,0:T(8,128)S(1)} %collective-permute-done.12.refs_1_, f32[64,256]{1,0:T(8,128)S(1)} %collective-permute-done.13.refs_2_, ...), custom_call_target="tpu_custom_call" | custom-call | flops 99999997952 | tf_op jit(solution)/shard_map/pallas_call | solution.py:24
  39.0 0.1 collective-permute-start.15
  39.1 0.0 copy-start.1
  39.1 0.0 copy-start.5
  39.1 1.7 %collective-permute-start.17 = (f32[4,32,128]{2,1,0:T(8,128)S(1)}, f32[4,32,128]{2,1,0:T(8,128)S(1)}, u32[]{:S(2)}, u32[]{:S(2)}) collective-permute-start(f32[4,32,128]{2,1,0:T(8,128)S(1)} %get-tuple-element.47), channel_id=1, source_target_pairs={{0,8},{4,12},{8,0},{12,4},{1,9},{5,13},{9,1},{13,5},{2,10},{6,14},... | collective-permute-start | bytes 196616 | tf_op jit(solution)/shard_map/ppermute | solution.py:357
  40.8 1.6 %collective-permute-start.18 = (f32[4,32,128]{2,1,0:T(8,128)S(1)}, f32[4,32,128]{2,1,0:T(8,128)S(1)}, u32[]{:S(2)}, u32[]{:S(2)}) collective-permute-start(f32[4,32,128]{2,1,0:T(8,128)S(1)} %get-tuple-element.48), channel_id=1, source_target_pairs={{0,12},{4,8},{8,4},{12,0},{1,13},{5,9},{9,5},{13,1},{2,14},{6,10},... | collective-permute-start | bytes 196616 | tf_op jit(solution)/shard_map/ppermute | solution.py:357
  42.4 0.3 collective-permute-start.19
  42.7 0.1 copy-done.1
  42.7 2.5 %shard_map.137 = (f32[16,64,128]{2,1,0:T(8,128)S(1)}, f32[16,32,128]{2,1,0:T(8,128)S(1)}, f32[16,32,128]{2,1,0:T(8,128)S(1)}) custom-call(s32[4,384]{1,0:T(4,128)S(1)} %copy-done.5, f32[16,64,128]{2,1,0:T(8,128)S(1)} %shard_map.135.after.mine, f32[16,64,128]{2,1,0:T(8,128)S(1)} %collective-permute-done.15.other, ...), custom_call_target="tpu_custom_call" | custom-call | flops 603979776 | bytes 9437184 | tf_op jit(solution)/shard_map/pallas_call | solution.py:24
  45.2 2.5 %collective-permute-done.17.refs_2_ = f32[4,32,128]{2,1,0:T(8,128)S(1)} collective-permute-done((f32[4,32,128]{2,1,0:T(8,128)S(1)}, f32[4,32,128]{2,1,0:T(8,128)S(1)}, u32[]{:S(2)}, u32[]{:S(2)}) %collective-permute-start.17) | collective-permute-done | bytes 65568 | tf_op jit(solution)/shard_map/ppermute | solution.py:357
  47.7 1.0 %collective-permute-done.19.refs_4_ = f32[4,32,128]{2,1,0:T(8,128)S(1)} collective-permute-done((f32[4,32,128]{2,1,0:T(8,128)S(1)}, f32[4,32,128]{2,1,0:T(8,128)S(1)}, u32[]{:S(2)}, u32[]{:S(2)}) %collective-permute-start.19) | collective-permute-done | bytes 65568 | tf_op jit(solution)/shard_map/ppermute | solution.py:357
  48.8 0.1 collective-permute-start.21
  48.8 1.4 %collective-permute-start.20 = (f32[4,32,128]{2,1,0:T(8,128)S(1)}, f32[4,32,128]{2,1,0:T(8,128)S(1)}, u32[]{:S(2)}, u32[]{:S(2)}) collective-permute-start(f32[4,32,128]{2,1,0:T(8,128)S(1)} %shard_map.138.refs_0_.values), channel_id=1, source_target_pairs={{0,12},{4,8},{8,4},{12,0},{1,13},{5,9},{9,5},{13,1},{2,14},{6,10},... | collective-permute-start | bytes 196616 | tf_op jit(solution)/shard_map/ppermute | solution.py:357
  50.3 0.1 collective-permute-done.21.refs_1_
  50.4 1.1 %collective-permute-start.24 = (f32[16,32,128]{2,1,0:T(8,128)S(1)}, f32[16,32,128]{2,1,0:T(8,128)S(1)}, u32[]{:S(2)}, u32[]{:S(2)}) collective-permute-start(f32[16,32,128]{2,1,0:T(8,128)S(1)} %shard_map.141.refs_0_.refs_1_), channel_id=1, source_target_pairs={{0,2},{2,0},{1,3},{3,1},{4,6},{6,4},{5,7},{7,5},{8,10},{10,8},{9,1... | collective-permute-start | bytes 786440 | tf_op jit(solution)/shard_map/ppermute | solution.py:357
  51.5 0.7 %collective-permute-start.23 = (f32[4,32,128]{2,1,0:T(8,128)S(1)}, f32[4,32,128]{2,1,0:T(8,128)S(1)}, u32[]{:S(2)}, u32[]{:S(2)}) collective-permute-start(f32[4,32,128]{2,1,0:T(8,128)S(1)} %shard_map.142), channel_id=1, source_target_pairs={{0,8},{4,12},{8,0},{12,4},{1,9},{5,13},{9,1},{13,5},{2,10},{6,14},... | collective-permute-start | bytes 196616 | tf_op jit(solution)/shard_map/ppermute | solution.py:357
  52.2 2.2 %collective-permute-start.22 = (f32[4,32,128]{2,1,0:T(8,128)S(1)}, f32[4,32,128]{2,1,0:T(8,128)S(1)}, u32[]{:S(2)}, u32[]{:S(2)}) collective-permute-start(f32[4,32,128]{2,1,0:T(8,128)S(1)} %shard_map.142), channel_id=1, source_target_pairs={{0,4},{4,0},{8,12},{12,8},{1,5},{5,1},{9,13},{13,9},{2,6},{6,2},{1... | collective-permute-start | bytes 196616 | tf_op jit(solution)/shard_map/ppermute | solution.py:357
  54.4 0.9 %collective-permute-done.20.values = f32[4,32,128]{2,1,0:T(8,128)S(1)} collective-permute-done((f32[4,32,128]{2,1,0:T(8,128)S(1)}, f32[4,32,128]{2,1,0:T(8,128)S(1)}, u32[]{:S(2)}, u32[]{:S(2)}) %collective-permute-start.20) | collective-permute-done | bytes 65568 | tf_op jit(solution)/shard_map/ppermute | solution.py:357
  55.4 2.6 %collective-permute-done.23.refs_3_ = f32[4,32,128]{2,1,0:T(8,128)S(1)} collective-permute-done((f32[4,32,128]{2,1,0:T(8,128)S(1)}, f32[4,32,128]{2,1,0:T(8,128)S(1)}, u32[]{:S(2)}, u32[]{:S(2)}) %collective-permute-start.23) | collective-permute-done | bytes 65568 | tf_op jit(solution)/shard_map/ppermute | solution.py:357
  58.0 0.1 collective-permute-start.26
  58.1 0.8 %collective-permute-done.24.refs_2_ = f32[16,32,128]{2,1,0:T(8,128)S(1)} collective-permute-done((f32[16,32,128]{2,1,0:T(8,128)S(1)}, f32[16,32,128]{2,1,0:T(8,128)S(1)}, u32[]{:S(2)}, u32[]{:S(2)}) %collective-permute-start.24) | collective-permute-done | bytes 262176 | tf_op jit(solution)/shard_map/ppermute | solution.py:357
  58.9 0.1 collective-permute-start.25
  58.9 0.7 %collective-permute-done.26.item_other = f32[4,4,32,128]{3,2,1,0:T(8,128)S(1)} collective-permute-done((f32[4,4,32,128]{3,2,1,0:T(8,128)S(1)}, f32[4,4,32,128]{3,2,1,0:T(8,128)S(1)}, u32[]{:S(2)}, u32[]{:S(2)}) %collective-permute-start.26) | collective-permute-done | bytes 262176 | tf_op jit(solution)/shard_map/ppermute | solution.py:357
  59.6 0.9 %collective-permute-done.25.user_other = f32[16,32,128]{2,1,0:T(8,128)S(1)} collective-permute-done((f32[16,32,128]{2,1,0:T(8,128)S(1)}, f32[16,32,128]{2,1,0:T(8,128)S(1)}, u32[]{:S(2)}, u32[]{:S(2)}) %collective-permute-start.25) | collective-permute-done | bytes 262176 | tf_op jit(solution)/shard_map/ppermute | solution.py:357
  60.5 1.1 %shard_map.145 = (f32[64,2048]{1,0:T(8,128)}, f32[64,2048]{1,0:T(8,128)}) custom-call(f32[16,64,128]{2,1,0:T(8,128)S(1)} %get-tuple-element.41.user_half_grad, f32[16,32,128]{2,1,0:T(8,128)S(1)} %shard_map.144.user_mine, f32[16,32,128]{2,1,0:T(8,128)S(1)} %collective-permute-done.25.user_other, f32[16,64,128]{2,1,0:T(8,128)S(1)} %get-tuple-element.51.item_half_grad, ...), custom_call_target="tpu_custom_call" | custom-call | bytes 3145728 | tf_op jit(solution)/shard_map/pallas_call | solution.py:24
  (46 shorter events, 0.3 us)
Async XLA Ops:
  0.6 0.7 %copy-start.8 = (s32[256]{0:T(256)S(1)}, s32[256]{0:T(256)}, u32[]{:S(2)}) copy-start(s32[256]{0:T(256)} %param.21) | copy-start | bytes 3076
  0.6 0.7 %copy-start.7 = (s32[256]{0:T(256)S(1)}, s32[256]{0:T(256)}, u32[]{:S(2)}) copy-start(s32[256]{0:T(256)} %param.20) | copy-start | bytes 3076
  0.7 0.7 %copy-start.6 = (s32[256]{0:T(256)S(1)}, s32[256]{0:T(256)}, u32[]{:S(2)}) copy-start(s32[256]{0:T(256)} %param.19) | copy-start | bytes 3076
  0.7 5.9 %copy-start.11 = (bf16[64,2048]{1,0:T(8,128)(2,1)S(1)}, bf16[64,2048]{1,0:T(8,128)(2,1)}, u32[]{:S(2)}) copy-start(bf16[64,2048]{1,0:T(8,128)(2,1)} %item_emb.3) | copy-start | bytes 786436
  0.7 5.9 %copy-start.9 = (bf16[64,2048]{1,0:T(8,128)(2,1)S(1)}, bf16[64,2048]{1,0:T(8,128)(2,1)}, u32[]{:S(2)}) copy-start(bf16[64,2048]{1,0:T(8,128)(2,1)} %user_emb.3) | copy-start | bytes 786436
  0.7 5.9 %copy-start.15 = (s32[288]{0:T(512)S(1)}, s32[288]{0:T(512)}, u32[]{:S(2)}) copy-start(s32[288]{0:T(512)} %columns.1) | copy-start | bytes 3460
  0.7 5.9 %copy-start.14 = (s32[288]{0:T(512)S(1)}, s32[288]{0:T(512)}, u32[]{:S(2)}) copy-start(s32[288]{0:T(512)} %rows.1) | copy-start | bytes 3460
  0.7 5.9 %copy-start.13 = (s32[2048]{0:T(1024)S(1)}, s32[2048]{0:T(1024)}, u32[]{:S(2)}) copy-start(s32[2048]{0:T(1024)} %param.14) | copy-start | bytes 24580
  0.7 5.9 %copy-start.12 = (s32[2048]{0:T(1024)S(1)}, s32[2048]{0:T(1024)}, u32[]{:S(2)}) copy-start(s32[2048]{0:T(1024)} %param.13) | copy-start | bytes 24580
  0.7 6.9 %copy-start = (bf16[288,128,128]{2,1,0:T(8,128)(2,1)S(1)}, bf16[288,128,128]{2,1,0:T(8,128)(2,1)}, u32[]{:S(2)}) copy-start(bf16[288,128,128]{2,1,0:T(8,128)(2,1)} %vals.7) | copy-start | bytes 28311556
  1.3 8.1 %collective-permute-start.3 = (s32[16,256]{1,0:T(8,128)S(1)}, s32[16,256]{1,0:T(8,128)S(1)}, u32[]{:S(2)}, u32[]{:S(2)}) collective-permute-start(s32[16,256]{1,0:T(8,128)S(1)} %shard_map.123.after.refs_0_.ids.refs_4_), channel_id=1, source_target_pairs={{0,4},{4,0},{8,12},{12,8},{1,5},{5,1},{9,13},{13,9},{2,6},{6,2},{1... | collective-permute-start | bytes 49160 | tf_op jit(solution)/shard_map/ppermute | solution.py:357
  4.4 8.2 %collective-permute-start = (s32[16,256]{1,0:T(8,128)S(1)}, s32[16,256]{1,0:T(8,128)S(1)}, u32[]{:S(2)}, u32[]{:S(2)}) collective-permute-start(s32[16,256]{1,0:T(8,128)S(1)} %shard_map.123.after.refs_0_.ids.refs_4_), channel_id=1, source_target_pairs={{0,2},{2,0},{1,3},{3,1},{4,6},{6,4},{5,7},{7,5},{8,10},{10,8},{9,1... | collective-permute-start | bytes 49160 | tf_op jit(solution)/shard_map/ppermute | solution.py:357
  7.5 5.1 %copy-start.2 = (s32[4,384]{1,0:T(4,128)}, s32[4,384]{1,0:T(4,128)S(1)}, u32[]{:S(2)}) copy-start(s32[4,384]{1,0:T(4,128)S(1)} %get-tuple-element.27.order) | copy-start | bytes 18436
  7.6 7.4 %copy-start.4 = (s32[4,384]{1,0:T(4,128)}, s32[4,384]{1,0:T(4,128)S(1)}, u32[]{:S(2)}) copy-start(s32[4,384]{1,0:T(4,128)S(1)} %get-tuple-element.30.order) | copy-start | bytes 18436
  9.3 5.8 %collective-permute-start.2 = (f32[16,64,128]{2,1,0:T(8,128)S(1)}, f32[16,64,128]{2,1,0:T(8,128)S(1)}, u32[]{:S(2)}, u32[]{:S(2)}) collective-permute-start(f32[16,64,128]{2,1,0:T(8,128)S(1)} %shard_map.125.refs_0_.mine), channel_id=1, source_target_pairs={{0,1},{1,0},{2,3},{3,2},{4,5},{5,4},{6,7},{7,6},{8,9},{9,8},{10,11... | collective-permute-start | bytes 1572872 | tf_op jit(solution)/shard_map/ppermute | solution.py:357
  9.4 5.7 %collective-permute-start.4 = (s32[16,256]{1,0:T(8,128)S(1)}, s32[16,256]{1,0:T(8,128)S(1)}, u32[]{:S(2)}, u32[]{:S(2)}) collective-permute-start(s32[16,256]{1,0:T(8,128)S(1)} %shard_map.127), channel_id=1, source_target_pairs={{0,8},{4,12},{8,0},{12,4},{1,9},{5,13},{9,1},{13,5},{2,10},{6,14},... | collective-permute-start | bytes 49160 | tf_op jit(solution)/shard_map/ppermute | solution.py:357
  14.9 5.5 %collective-permute-start.1 = (f32[16,64,128]{2,1,0:T(8,128)S(1)}, f32[16,64,128]{2,1,0:T(8,128)S(1)}, u32[]{:S(2)}, u32[]{:S(2)}) collective-permute-start(f32[16,64,128]{2,1,0:T(8,128)S(1)} %shard_map.126.mine), channel_id=1, source_target_pairs={{0,1},{1,0},{2,3},{3,2},{4,5},{5,4},{6,7},{7,6},{8,9},{9,8},{10,11... | collective-permute-start | bytes 1572872 | tf_op jit(solution)/shard_map/ppermute | solution.py:357
  15.7 7.8 %copy-start.10 = (bf16[64,2048]{1,0:T(8,128)(2,1)S(1)}, bf16[64,2048]{1,0:T(8,128)(2,1)}, u32[]{:S(2)}) copy-start(bf16[64,2048]{1,0:T(8,128)(2,1)} %user_emb.3) | copy-start | bytes 786436
  15.8 8.3 %collective-permute-start.6 = (f32[64,256]{1,0:T(8,128)S(1)}, f32[64,256]{1,0:T(8,128)S(1)}, u32[]{:S(2)}, u32[]{:S(2)}) collective-permute-start(f32[64,256]{1,0:T(8,128)S(1)} %shard_map.128.after), channel_id=1, source_target_pairs={{0,8},{4,12},{8,0},{12,4},{1,9},{5,13},{9,1},{13,5},{2,10},{6,14},... | collective-permute-start | bytes 196616 | tf_op jit(solution)/shard_map/ppermute | solution.py:357
  18.9 12.9 %copy-start.3 = (s32[4,384]{1,0:T(4,128)S(1)}, s32[4,384]{1,0:T(4,128)}, u32[]{:S(2)}) copy-start(s32[4,384]{1,0:T(4,128)} %copy-done.2) | copy-start | bytes 18436
  18.9 6.3 %collective-permute-start.7 = (f32[64,256]{1,0:T(8,128)S(1)}, f32[64,256]{1,0:T(8,128)S(1)}, u32[]{:S(2)}, u32[]{:S(2)}) collective-permute-start(f32[64,256]{1,0:T(8,128)S(1)} %get-tuple-element.37), channel_id=1, source_target_pairs={{0,12},{4,8},{8,4},{12,0},{1,13},{5,9},{9,5},{13,1},{2,14},{6,10},... | collective-permute-start | bytes 196616 | tf_op jit(solution)/shard_map/ppermute | solution.py:357
  20.3 5.2 %collective-permute-start.8 = (f32[64,256]{1,0:T(8,128)S(1)}, f32[64,256]{1,0:T(8,128)S(1)}, u32[]{:S(2)}, u32[]{:S(2)}) collective-permute-start(f32[64,256]{1,0:T(8,128)S(1)} %get-tuple-element.38), channel_id=1, source_target_pairs={{0,4},{4,0},{8,12},{12,8},{1,5},{5,1},{9,13},{13,9},{2,6},{6,2},{1... | collective-permute-start | bytes 196616 | tf_op jit(solution)/shard_map/ppermute | solution.py:357
  21.0 4.8 %collective-permute-start.5 = (f32[64,256]{1,0:T(8,128)S(1)}, f32[64,256]{1,0:T(8,128)S(1)}, u32[]{:S(2)}, u32[]{:S(2)}) collective-permute-start(f32[64,256]{1,0:T(8,128)S(1)} %get-tuple-element.35), channel_id=1, source_target_pairs={{0,2},{2,0},{1,3},{3,1},{4,6},{6,4},{5,7},{7,5},{8,10},{10,8},{9,1... | collective-permute-start | bytes 196616 | tf_op jit(solution)/shard_map/ppermute | solution.py:357
  25.9 5.8 %collective-permute-start.11 = (f32[72,256]{1,0:T(8,128)S(1)}, f32[72,256]{1,0:T(8,128)S(1)}, u32[]{:S(2)}, u32[]{:S(2)}) collective-permute-start(f32[72,256]{1,0:T(8,128)S(1)} %get-tuple-element.40.refs_0_), channel_id=1, source_target_pairs={{0,3},{1,2},{2,1},{3,0},{4,7},{5,6},{6,5},{7,4},{8,11},{9,10},{10,... | collective-permute-start | bytes 221192 | tf_op jit(solution)/shard_map/ppermute | solution.py:461
  26.3 5.5 %collective-permute-start.10 = (f32[72,256]{1,0:T(8,128)S(1)}, f32[72,256]{1,0:T(8,128)S(1)}, u32[]{:S(2)}, u32[]{:S(2)}) collective-permute-start(f32[72,256]{1,0:T(8,128)S(1)} %get-tuple-element.40.refs_0_), channel_id=1, source_target_pairs={{0,2},{2,0},{1,3},{3,1},{4,6},{6,4},{5,7},{7,5},{8,10},{10,8},{9,1... | collective-permute-start | bytes 221192 | tf_op jit(solution)/shard_map/ppermute | solution.py:357
  28.0 3.9 %collective-permute-start.9 = (f32[72,256]{1,0:T(8,128)S(1)}, f32[72,256]{1,0:T(8,128)S(1)}, u32[]{:S(2)}, u32[]{:S(2)}) collective-permute-start(f32[72,256]{1,0:T(8,128)S(1)} %get-tuple-element.40.refs_0_), channel_id=1, source_target_pairs={{0,1},{1,0},{2,3},{3,2},{4,5},{5,4},{6,7},{7,6},{8,9},{9,8},{10,11... | collective-permute-start | bytes 221192 | tf_op jit(solution)/shard_map/ppermute | solution.py:357
  28.1 8.6 %collective-permute-start.14 = (f32[64,256]{1,0:T(8,128)S(1)}, f32[64,256]{1,0:T(8,128)S(1)}, u32[]{:S(2)}, u32[]{:S(2)}) collective-permute-start(f32[64,256]{1,0:T(8,128)S(1)} %get-tuple-element.43.refs_0_), channel_id=1, source_target_pairs={{0,8},{4,12},{8,0},{12,4},{1,9},{5,13},{9,1},{13,5},{2,10},{6,14},... | collective-permute-start | bytes 196616 | tf_op jit(solution)/shard_map/ppermute | solution.py:357
  30.3 6.3 %collective-permute-start.13 = (f32[64,256]{1,0:T(8,128)S(1)}, f32[64,256]{1,0:T(8,128)S(1)}, u32[]{:S(2)}, u32[]{:S(2)}) collective-permute-start(f32[64,256]{1,0:T(8,128)S(1)} %get-tuple-element.43.refs_0_), channel_id=1, source_target_pairs={{0,12},{4,8},{8,4},{12,0},{1,13},{5,9},{9,5},{13,1},{2,14},{6,10},... | collective-permute-start | bytes 196616 | tf_op jit(solution)/shard_map/ppermute | solution.py:357
  31.6 5.8 %collective-permute-start.12 = (f32[64,256]{1,0:T(8,128)S(1)}, f32[64,256]{1,0:T(8,128)S(1)}, u32[]{:S(2)}, u32[]{:S(2)}) collective-permute-start(f32[64,256]{1,0:T(8,128)S(1)} %get-tuple-element.43.refs_0_), channel_id=1, source_target_pairs={{0,4},{4,0},{8,12},{12,8},{1,5},{5,1},{9,13},{13,9},{2,6},{6,2},{1... | collective-permute-start | bytes 196616 | tf_op jit(solution)/shard_map/ppermute | solution.py:357
  35.2 3.9 %collective-permute-start.16 = (f32[16,32,128]{2,1,0:T(8,128)S(1)}, f32[16,32,128]{2,1,0:T(8,128)S(1)}, u32[]{:S(2)}, u32[]{:S(2)}) collective-permute-start(f32[16,32,128]{2,1,0:T(8,128)S(1)} %get-tuple-element.42.after), channel_id=1, source_target_pairs={{0,1},{1,0},{2,3},{3,2},{4,5},{5,4},{6,7},{7,6},{8,9},{9,8},{10,11... | collective-permute-start | bytes 786440 | tf_op jit(solution)/shard_map/ppermute | solution.py:357
  39.0 3.7 %collective-permute-start.15 = (f32[16,64,128]{2,1,0:T(8,128)S(1)}, f32[16,64,128]{2,1,0:T(8,128)S(1)}, u32[]{:S(2)}, u32[]{:S(2)}) collective-permute-start(f32[16,64,128]{2,1,0:T(8,128)S(1)} %shard_map.135.after.mine), channel_id=1, source_target_pairs={{0,1},{1,0},{2,3},{3,2},{4,5},{5,4},{6,7},{7,6},{8,9},{9,8},{10,11... | collective-permute-start | bytes 1572872 | tf_op jit(solution)/shard_map/ppermute | solution.py:357
  39.1 3.7 %copy-start.1 = (bf16[288,128,128]{2,1,0:T(8,128)(2,1)S(1)}, bf16[288,128,128]{2,1,0:T(8,128)(2,1)}, u32[]{:S(2)}) copy-start(bf16[288,128,128]{2,1,0:T(8,128)(2,1)} %vals.7) | copy-start | bytes 28311556
  39.1 3.7 %copy-start.5 = (s32[4,384]{1,0:T(4,128)S(1)}, s32[4,384]{1,0:T(4,128)}, u32[]{:S(2)}) copy-start(s32[4,384]{1,0:T(4,128)} %copy-done.4) | copy-start | bytes 18436
  39.1 8.6 %collective-permute-start.17 = (f32[4,32,128]{2,1,0:T(8,128)S(1)}, f32[4,32,128]{2,1,0:T(8,128)S(1)}, u32[]{:S(2)}, u32[]{:S(2)}) collective-permute-start(f32[4,32,128]{2,1,0:T(8,128)S(1)} %get-tuple-element.47), channel_id=1, source_target_pairs={{0,8},{4,12},{8,0},{12,4},{1,9},{5,13},{9,1},{13,5},{2,10},{6,14},... | collective-permute-start | bytes 196616 | tf_op jit(solution)/shard_map/ppermute | solution.py:357
  40.8 6.9 %collective-permute-start.18 = (f32[4,32,128]{2,1,0:T(8,128)S(1)}, f32[4,32,128]{2,1,0:T(8,128)S(1)}, u32[]{:S(2)}, u32[]{:S(2)}) collective-permute-start(f32[4,32,128]{2,1,0:T(8,128)S(1)} %get-tuple-element.48), channel_id=1, source_target_pairs={{0,12},{4,8},{8,4},{12,0},{1,13},{5,9},{9,5},{13,1},{2,14},{6,10},... | collective-permute-start | bytes 196616 | tf_op jit(solution)/shard_map/ppermute | solution.py:357
  42.4 6.3 %collective-permute-start.19 = (f32[4,32,128]{2,1,0:T(8,128)S(1)}, f32[4,32,128]{2,1,0:T(8,128)S(1)}, u32[]{:S(2)}, u32[]{:S(2)}) collective-permute-start(f32[4,32,128]{2,1,0:T(8,128)S(1)} %get-tuple-element.49), channel_id=1, source_target_pairs={{0,4},{4,0},{8,12},{12,8},{1,5},{5,1},{9,13},{13,9},{2,6},{6,2},{1... | collective-permute-start | bytes 196616 | tf_op jit(solution)/shard_map/ppermute | solution.py:357
  48.8 1.6 %collective-permute-start.21 = (f32[16,32,128]{2,1,0:T(8,128)S(1)}, f32[16,32,128]{2,1,0:T(8,128)S(1)}, u32[]{:S(2)}, u32[]{:S(2)}) collective-permute-start(f32[16,32,128]{2,1,0:T(8,128)S(1)} %shard_map.140), channel_id=1, source_target_pairs={{0,1},{1,0},{2,3},{3,2},{4,5},{5,4},{6,7},{7,6},{8,9},{9,8},{10,11... | collective-permute-start | bytes 786440 | tf_op jit(solution)/shard_map/ppermute | solution.py:357
  48.8 6.5 %collective-permute-start.20 = (f32[4,32,128]{2,1,0:T(8,128)S(1)}, f32[4,32,128]{2,1,0:T(8,128)S(1)}, u32[]{:S(2)}, u32[]{:S(2)}) collective-permute-start(f32[4,32,128]{2,1,0:T(8,128)S(1)} %shard_map.138.refs_0_.values), channel_id=1, source_target_pairs={{0,12},{4,8},{8,4},{12,0},{1,13},{5,9},{9,5},{13,1},{2,14},{6,10},... | collective-permute-start | bytes 196616 | tf_op jit(solution)/shard_map/ppermute | solution.py:357
  50.4 8.4 %collective-permute-start.24 = (f32[16,32,128]{2,1,0:T(8,128)S(1)}, f32[16,32,128]{2,1,0:T(8,128)S(1)}, u32[]{:S(2)}, u32[]{:S(2)}) collective-permute-start(f32[16,32,128]{2,1,0:T(8,128)S(1)} %shard_map.141.refs_0_.refs_1_), channel_id=1, source_target_pairs={{0,2},{2,0},{1,3},{3,1},{4,6},{6,4},{5,7},{7,5},{8,10},{10,8},{9,1... | collective-permute-start | bytes 786440 | tf_op jit(solution)/shard_map/ppermute | solution.py:357
  51.5 6.4 %collective-permute-start.23 = (f32[4,32,128]{2,1,0:T(8,128)S(1)}, f32[4,32,128]{2,1,0:T(8,128)S(1)}, u32[]{:S(2)}, u32[]{:S(2)}) collective-permute-start(f32[4,32,128]{2,1,0:T(8,128)S(1)} %shard_map.142), channel_id=1, source_target_pairs={{0,8},{4,12},{8,0},{12,4},{1,9},{5,13},{9,1},{13,5},{2,10},{6,14},... | collective-permute-start | bytes 196616 | tf_op jit(solution)/shard_map/ppermute | solution.py:357
  52.2 5.7 %collective-permute-start.22 = (f32[4,32,128]{2,1,0:T(8,128)S(1)}, f32[4,32,128]{2,1,0:T(8,128)S(1)}, u32[]{:S(2)}, u32[]{:S(2)}) collective-permute-start(f32[4,32,128]{2,1,0:T(8,128)S(1)} %shard_map.142), channel_id=1, source_target_pairs={{0,4},{4,0},{8,12},{12,8},{1,5},{5,1},{9,13},{13,9},{2,6},{6,2},{1... | collective-permute-start | bytes 196616 | tf_op jit(solution)/shard_map/ppermute | solution.py:357
  58.0 1.6 %collective-permute-start.26 = (f32[4,4,32,128]{3,2,1,0:T(8,128)S(1)}, f32[4,4,32,128]{3,2,1,0:T(8,128)S(1)}, u32[]{:S(2)}, u32[]{:S(2)}) collective-permute-start(f32[4,4,32,128]{3,2,1,0:T(8,128)S(1)} %shard_map.143.refs_0_.item_mine), channel_id=1, source_target_pairs={{0,1},{1,0},{2,3},{3,2},{4,5},{5,4},{6,7},{7,6},{8,9},{9,8},{10,11... | collective-permute-start | bytes 786440 | tf_op jit(solution)/shard_map/ppermute | solution.py:357
  58.9 1.6 %collective-permute-start.25 = (f32[16,32,128]{2,1,0:T(8,128)S(1)}, f32[16,32,128]{2,1,0:T(8,128)S(1)}, u32[]{:S(2)}, u32[]{:S(2)}) collective-permute-start(f32[16,32,128]{2,1,0:T(8,128)S(1)} %shard_map.144.user_mine), channel_id=1, source_target_pairs={{0,1},{1,0},{2,3},{3,2},{4,5},{5,4},{6,7},{7,6},{8,9},{9,8},{10,11... | collective-permute-start | bytes 786440 | tf_op jit(solution)/shard_map/ppermute | solution.py:357

commit v9 on v7

--- a/solution.py
+++ b/solution.py
@@ -267,7 +267,7 @@
 
 def second_items(parts, order, source_scale, target_scale, vals, *refs):
     pieces = refs[:parts]
-    half_grad, keep, send, source, total, table = refs[parts:]
+    half_grad, keep, send, source, total, table = refs[-6:]
     blocks, width, size = half_grad.shape
 
     def put(block, grad):
@@ -455,21 +455,27 @@
         arrays.append(swap(pieces, "item", items, offset))
         arrays.append(lax.ppermute(pieces, ("item", "rep"), [
             (i, i ^ (2 * offset + 1)) for i in range(2 * items)]))
+    shared, step = {0: pushed}, 1
+    while step < users:
+        for offset, part in list(shared.items()):
+            shared[offset ^ step] = swap(part, "user", users, step)
+        if 2 * step < users:
+            shared[step] = hold(shared[step], flops=0)
+        step *= 2
     user_half_grad, item_keep, item_send = call(
         functools.partial(second_items, len(arrays)),
         [shape(user_blocks, width, size)] + [shape(item_blocks, half, size)] * 2,
-        (item_order, user_scale, item_scale, block_vals, *arrays),
-        [SMEM] + [VMEM] * (3 + len(arrays)),
+        (item_order, user_scale, item_scale, block_vals, *arrays, *list(shared.values())[1:2]),
+        [SMEM] + [VMEM] * (3 + len(arrays)) + [ANY] * min(1, users - 1),
         [pltpu.VMEM((user_blocks + 1, width, size), BF16),
          pltpu.VMEM((item_blocks, width, size), F32),
          pltpu.VMEM((len(arrays), 3 * width, trips), BF16)],
         product_flops, product_bytes,
     )
-    arrays = [pushed] + [swap(pushed, "user", users, o) for o in back]
     item_grad = call(
-        functools.partial(scatter_items, [item_rows(o) for o in [0, *back]]),
+        functools.partial(scatter_items, [item_rows(o) for o in shared]),
         shape(item_blocks, width, size),
-        (item_send, *arrays, *held), [ANY] + [VMEM] * (users + len(held)),
+        (item_send, *shared.values(), *held), [ANY] + [VMEM] * (users + len(held)),
         [pltpu.VMEM((users, 3 * width, trips), BF16)], HEAVY, 0,
     )
 

time: 62.2 us -> 62.6 us (level)
  Pallas kernels: 14.7 us -> 23.8 us
  starting transfers between devices: 32.1 us -> 23.5 us
    pallas_call x22 -> x23, Pallas kernels: 14.7 us -> 23.8 us  [call(): pl.pallas_call(kernel, out_shape=outs, in_specs=specs, out_specs=jax.tree...]
    ppermute x26, starting transfers between devices: 31.8 us -> 23.5 us  [swap(): return lax.ppermute(values, axis, [(i, i ^ offset) for i in range(peers)])]
  transfers between devices with their start and end apart: 27 -> 27, of which waited for: 13 -> 11; matrix products, arithmetic and copies ran while one was open for 0% -> 0% of each run, Pallas kernels for 22% -> 36%
where the time goes in v9:
time: 62.6 us; the launch traced here: 62.7 us
  Pallas kernels  23.8 us (38%)
  starting transfers between devices  23.5 us (38%)
  waiting for transfers between devices  13 us (21%)
  between operations  1.73 us (3%)
  local copies, waits for them, and re-layouts  0.75 us (1%)
    pallas_call x23, Pallas kernels, call(): pl.pallas_call(kernel, out_shape=outs, in_specs=specs, out_specs=jax.tree...  23.8 us
    ppermute x26, starting transfers between devices, swap(): return lax.ppermute(values, axis, [(i, i ^ offset) for i in range(peers)])  23.5 us
    ppermute x26, waiting for transfers between devices, swap(): return lax.ppermute(values, axis, [(i, i ^ offset) for i in range(peers)])  13 us
  transfers between devices with their start and end apart: 27, of which 11 were waited for; matrix products, arithmetic and copies ran while one was open for 0% of the time, Pallas kernels for 36%

profile of v9, /device:TPU:0, one launch (start us, length us, event | category | flops | bytes accessed | tf_op | source)
XLA Modules:
  0.0 62.7 jit_solution(11154211855378014170)
XLA Ops:
  0.7 0.0 copy-start.11
  0.7 0.0 copy-start
  0.7 0.6 copy-done.10
  1.3 0.0 copy-done.9
  1.3 0.0 copy-done.8
  1.3 3.1 %collective-permute-start.3 = (s32[16,256]{1,0:T(8,128)S(1)}, s32[16,256]{1,0:T(8,128)S(1)}, u32[]{:S(2)}, u32[]{:S(2)}) collective-permute-start(s32[16,256]{1,0:T(8,128)S(1)} %shard_map.123.after.refs_0_.ids.refs_4_), channel_id=1, source_target_pairs={{0,4},{4,0},{8,12},{12,8},{1,5},{5,1},{9,13},{13,9},{2,6},{6,2},{1... | collective-permute-start | bytes 49160 | tf_op jit(solution)/shard_map/ppermute | solution.py:357
  4.4 1.5 %collective-permute-start = (s32[16,256]{1,0:T(8,128)S(1)}, s32[16,256]{1,0:T(8,128)S(1)}, u32[]{:S(2)}, u32[]{:S(2)}) collective-permute-start(s32[16,256]{1,0:T(8,128)S(1)} %shard_map.123.after.refs_0_.ids.refs_4_), channel_id=1, source_target_pairs={{0,2},{2,0},{1,3},{3,1},{4,6},{6,4},{5,7},{7,5},{8,10},{10,8},{9,1... | collective-permute-start | bytes 49160 | tf_op jit(solution)/shard_map/ppermute | solution.py:357
  6.6 0.9 %shard_map.124 = (bf16[17,64,128]{2,1,0:T(8,128)(2,1)S(1)}, bf16[17,64,128]{2,1,0:T(8,128)(2,1)S(1)}, f32[16,128]{1,0:T(8,128)S(1)}, f32[16,128]{1,0:T(8,128)S(1...) custom-call(s32[1]{0:T(128)S(6)} %copy.13.count, s32[288]{0:T(512)S(1)} %copy-done.16, s32[288]{0:T(512)S(1)} %copy-done.17, ...), custom_call_target="tpu_custom_call" | custom-call | flops 603979776 | bytes 9437184 | tf_op jit(solution)/shard_map/pallas_call | solution.py:24
  7.5 0.0 copy-start.4
  7.6 0.0 copy-start.2
  7.6 3.3 %shard_map.125.refs_0_.mine = f32[16,64,128]{2,1,0:T(8,128)S(1)} custom-call(s32[4,384]{1,0:T(4,128)S(1)} %get-tuple-element.28.order, bf16[288,128,128]{2,1,0:T(8,128)(2,1)S(1)} %copy-done, bf16[17,64,128]{2,1,0:T(8,128)(2,1)S(1)} %get-tuple-element.33.source, s32[16,256]{1,0:T(8,128)S(1)} %shard_map.123.after.refs_0_.ids.refs_4_), custom_call_target="tpu_custom_call" | custom-call | flops 603979776 | bytes 9437184 | tf_op jit(solution)/shard_map/pallas_call | solution.py:24
  10.9 0.1 collective-permute-start.2
  11.0 0.0 collective-permute-done.3.refs_1_.refs_5_
  11.0 1.1 %collective-permute-start.4 = (s32[16,256]{1,0:T(8,128)S(1)}, s32[16,256]{1,0:T(8,128)S(1)}, u32[]{:S(2)}, u32[]{:S(2)}) collective-permute-start(s32[16,256]{1,0:T(8,128)S(1)} %shard_map.127), channel_id=1, source_target_pairs={{0,8},{4,12},{8,0},{12,4},{1,9},{5,13},{9,1},{13,5},{2,10},{6,14},... | collective-permute-start | bytes 49160 | tf_op jit(solution)/shard_map/ppermute | solution.py:357
  12.1 0.0 collective-permute-done.refs_1_
  12.1 4.7 %shard_map.126.mine = f32[16,64,128]{2,1,0:T(8,128)S(1)} custom-call(s32[4,384]{1,0:T(4,128)S(1)} %get-tuple-element.31.order, bf16[288,128,128]{2,1,0:T(8,128)(2,1)S(1)} %copy-done, bf16[17,64,128]{2,1,0:T(8,128)(2,1)S(1)} %get-tuple-element.32.source, f32[16,64,128]{2,1,0:T(8,128)S(1)} %shard_map.125.refs_0_.mine, s32[16,256]{1,0:T(8,128)S(1)} %collective-permute-done.refs_1_), custom_call_target="tpu_custom_call" | custom-call | flops 99999997952 | bytes 9437184 | tf_op jit(solution)/shard_map/pallas_call | solution.py:24
  16.8 0.1 collective-permute-start.1
  16.9 0.0 collective-permute-done.4.refs_2_.refs_6_
  16.9 0.0 copy-start.12
  16.9 0.0 copy-start.5
  16.9 1.2 %shard_map.128 = (f32[64,256]{1,0:T(8,128)S(1)}, f32[64,256]{1,0:T(8,128)S(1)}, f32[64,256]{1,0:T(8,128)S(1)}, f32[64,256]{1,0:T(8,128)S(1)}) custom-call(f32[16,64,128]{2,1,0:T(8,128)S(1)} %shard_map.125.refs_0_.mine, f32[16,64,128]{2,1,0:T(8,128)S(1)} %collective-permute-done.2.other, f32[16,128]{1,0:T(8,128)S(1)} %get-tuple-element.30.scale.target_scale.source_scale, ...), custom_call_target="tpu_custom_call" | custom-call | flops 99999997952 | bytes 1048576 | tf_op jit(solution)/shard_map/pallas_call | solution.py:24
  18.1 0.1 collective-permute-start.6
  18.2 2.1 %collective-permute-start.7 = (f32[64,256]{1,0:T(8,128)S(1)}, f32[64,256]{1,0:T(8,128)S(1)}, u32[]{:S(2)}, u32[]{:S(2)}) collective-permute-start(f32[64,256]{1,0:T(8,128)S(1)} %get-tuple-element.39), channel_id=1, source_target_pairs={{0,12},{4,8},{8,4},{12,0},{1,13},{5,9},{9,5},{13,1},{2,14},{6,10},... | collective-permute-start | bytes 196616 | tf_op jit(solution)/shard_map/ppermute | solution.py:357
  20.3 1.4 %collective-permute-start.8 = (f32[64,256]{1,0:T(8,128)S(1)}, f32[64,256]{1,0:T(8,128)S(1)}, u32[]{:S(2)}, u32[]{:S(2)}) collective-permute-start(f32[64,256]{1,0:T(8,128)S(1)} %get-tuple-element.40), channel_id=1, source_target_pairs={{0,4},{4,0},{8,12},{12,8},{1,5},{5,1},{9,13},{13,9},{2,6},{6,2},{1... | collective-permute-start | bytes 196616 | tf_op jit(solution)/shard_map/ppermute | solution.py:357
  21.7 0.0 collective-permute-done.1.other
  21.7 0.6 shard_map.129
  22.3 0.1 collective-permute-start.5
  22.4 0.5 shard_map.130
  22.9 2.7 %collective-permute-done.6.refs_4_ = f32[64,256]{1,0:T(8,128)S(1)} collective-permute-done((f32[64,256]{1,0:T(8,128)S(1)}, f32[64,256]{1,0:T(8,128)S(1)}, u32[]{:S(2)}, u32[]{:S(2)}) %collective-permute-start.6) | collective-permute-done | bytes 65568 | tf_op jit(solution)/shard_map/ppermute | solution.py:357
  25.6 1.3 %collective-permute-done.8.refs_6_ = f32[64,256]{1,0:T(8,128)S(1)} collective-permute-done((f32[64,256]{1,0:T(8,128)S(1)}, f32[64,256]{1,0:T(8,128)S(1)}, u32[]{:S(2)}, u32[]{:S(2)}) %collective-permute-start.8) | collective-permute-done | bytes 65568 | tf_op jit(solution)/shard_map/ppermute | solution.py:357
  26.9 0.1 shard_map.131
  26.9 0.7 %collective-permute-start.12 = (f32[64,256]{1,0:T(8,128)S(1)}, f32[64,256]{1,0:T(8,128)S(1)}, u32[]{:S(2)}, u32[]{:S(2)}) collective-permute-start(f32[64,256]{1,0:T(8,128)S(1)} %get-tuple-element.43.refs_0_), channel_id=1, source_target_pairs={{0,4},{4,0},{8,12},{12,8},{1,5},{5,1},{9,13},{13,9},{2,6},{6,2},{1... | collective-permute-start | bytes 196616 | tf_op jit(solution)/shard_map/ppermute | solution.py:357
  27.6 1.4 %collective-permute-start.10 = (f32[72,256]{1,0:T(8,128)S(1)}, f32[72,256]{1,0:T(8,128)S(1)}, u32[]{:S(2)}, u32[]{:S(2)}) collective-permute-start(f32[72,256]{1,0:T(8,128)S(1)} %get-tuple-element.42.refs_0_), channel_id=1, source_target_pairs={{0,2},{2,0},{1,3},{3,1},{4,6},{6,4},{5,7},{7,5},{8,10},{10,8},{9,1... | collective-permute-start | bytes 221192 | tf_op jit(solution)/shard_map/ppermute | solution.py:357
  29.0 0.4 collective-permute-start.9
  29.5 1.2 %collective-permute-start.13 = (f32[64,256]{1,0:T(8,128)S(1)}, f32[64,256]{1,0:T(8,128)S(1)}, u32[]{:S(2)}, u32[]{:S(2)}) collective-permute-start(f32[64,256]{1,0:T(8,128)S(1)} %get-tuple-element.43.refs_0_), channel_id=1, source_target_pairs={{0,8},{4,12},{8,0},{12,4},{1,9},{5,13},{9,1},{13,5},{2,10},{6,14},... | collective-permute-start | bytes 196616 | tf_op jit(solution)/shard_map/ppermute | solution.py:357
  30.6 0.6 collective-permute-done.12.values
  31.3 1.2 %collective-permute-start.14 = (f32[64,256]{1,0:T(8,128)S(1)}, f32[64,256]{1,0:T(8,128)S(1)}, u32[]{:S(2)}, u32[]{:S(2)}) collective-permute-start(f32[64,256]{1,0:T(8,128)S(1)} %shard_map.132.refs_4_.refs_1_), channel_id=1, source_target_pairs={{0,8},{4,12},{8,0},{12,4},{1,9},{5,13},{9,1},{13,5},{2,10},{6,14},... | collective-permute-start | bytes 196616 | tf_op jit(solution)/shard_map/ppermute | solution.py:357
  32.5 1.2 %collective-permute-done.10.refs_2_ = f32[72,256]{1,0:T(8,128)S(1)} collective-permute-done((f32[72,256]{1,0:T(8,128)S(1)}, f32[72,256]{1,0:T(8,128)S(1)}, u32[]{:S(2)}, u32[]{:S(2)}) %collective-permute-start.10) | collective-permute-done | bytes 73760 | tf_op jit(solution)/shard_map/ppermute | solution.py:357
  33.7 0.0 collective-permute-done.9.refs_1_
  33.7 4.8 %shard_map.133 = (f32[16,64,128]{2,1,0:T(8,128)S(1)}, f32[16,32,128]{2,1,0:T(8,128)S(1)}, f32[16,32,128]{2,1,0:T(8,128)S(1)}) custom-call(s32[4,384]{1,0:T(4,128)S(1)} %copy-done.5, f32[16,128]{1,0:T(8,128)S(1)} %get-tuple-element.29.scale.source_scale.target_scale, f32[16,128]{1,0:T(8,128)S(1)} %get-tuple-element.30.scale.target_scale.source_scale, ...), custom_call_target="tpu_custom_call" | custom-call | flops 603979776 | bytes 9437184 | tf_op jit(solution)/shard_map/pallas_call | solution.py:24
  38.5 0.1 collective-permute-start.16
  38.6 0.1 collective-permute-done.14.refs_3_
  38.7 1.5 %shard_map.134.after.mine = f32[16,64,128]{2,1,0:T(8,128)S(1)} custom-call(f32[16,32,128]{2,1,0:T(8,128)S(1)} %get-tuple-element.45.after, f32[64,256]{1,0:T(8,128)S(1)} %get-tuple-element.43.refs_0_, f32[64,256]{1,0:T(8,128)S(1)} %shard_map.132.refs_4_.refs_1_, f32[64,256]{1,0:T(8,128)S(1)} %collective-permute-done.13.refs_2_, ...), custom_call_target="tpu_custom_call" | custom-call | flops 99999997952 | tf_op jit(solution)/shard_map/pallas_call | solution.py:24
  40.3 0.4 collective-permute-start.15
  40.7 0.0 collective-permute-done.16.received
  40.7 0.1 collective-permute-start.17
  40.8 2.6 %collective-permute-start.18 = (f32[4,32,128]{2,1,0:T(8,128)S(1)}, f32[4,32,128]{2,1,0:T(8,128)S(1)}, u32[]{:S(2)}, u32[]{:S(2)}) collective-permute-start(f32[4,32,128]{2,1,0:T(8,128)S(1)} %get-tuple-element.50), channel_id=1, source_target_pairs={{0,12},{4,8},{8,4},{12,0},{1,13},{5,9},{9,5},{13,1},{2,14},{6,10},... | collective-permute-start | bytes 196616 | tf_op jit(solution)/shard_map/ppermute | solution.py:357
  43.4 0.8 %collective-permute-start.19 = (f32[4,32,128]{2,1,0:T(8,128)S(1)}, f32[4,32,128]{2,1,0:T(8,128)S(1)}, u32[]{:S(2)}, u32[]{:S(2)}) collective-permute-start(f32[4,32,128]{2,1,0:T(8,128)S(1)} %get-tuple-element.51), channel_id=1, source_target_pairs={{0,4},{4,0},{8,12},{12,8},{1,5},{5,1},{9,13},{13,9},{2,6},{6,2},{1... | collective-permute-start | bytes 196616 | tf_op jit(solution)/shard_map/ppermute | solution.py:357
  44.3 0.1 copy-done.1
  44.4 4.9 %shard_map.136 = (f32[16,64,128]{2,1,0:T(8,128)S(1)}, f32[16,32,128]{2,1,0:T(8,128)S(1)}, f32[16,32,128]{2,1,0:T(8,128)S(1)}) custom-call(s32[4,384]{1,0:T(4,128)S(1)} %copy-done.7, f32[16,64,128]{2,1,0:T(8,128)S(1)} %shard_map.134.after.mine, f32[16,64,128]{2,1,0:T(8,128)S(1)} %collective-permute-done.15.other, ...), custom_call_target="tpu_custom_call" | custom-call | flops 603979776 | bytes 9437184 | tf_op jit(solution)/shard_map/pallas_call | solution.py:24
  49.3 0.1 collective-permute-done.19.refs_4_
  49.5 0.1 collective-permute-start.21
  49.6 1.9 %collective-permute-start.20 = (f32[4,32,128]{2,1,0:T(8,128)S(1)}, f32[4,32,128]{2,1,0:T(8,128)S(1)}, u32[]{:S(2)}, u32[]{:S(2)}) collective-permute-start(f32[4,32,128]{2,1,0:T(8,128)S(1)} %shard_map.137.refs_0_.values), channel_id=1, source_target_pairs={{0,12},{4,8},{8,4},{12,0},{1,13},{5,9},{9,5},{13,1},{2,14},{6,10},... | collective-permute-start | bytes 196616 | tf_op jit(solution)/shard_map/ppermute | solution.py:357
  51.5 0.8 %collective-permute-start.24 = (f32[16,32,128]{2,1,0:T(8,128)S(1)}, f32[16,32,128]{2,1,0:T(8,128)S(1)}, u32[]{:S(2)}, u32[]{:S(2)}) collective-permute-start(f32[16,32,128]{2,1,0:T(8,128)S(1)} %shard_map.140.refs_0_.refs_1_), channel_id=1, source_target_pairs={{0,2},{2,0},{1,3},{3,1},{4,6},{6,4},{5,7},{7,5},{8,10},{10,8},{9,1... | collective-permute-start | bytes 786440 | tf_op jit(solution)/shard_map/ppermute | solution.py:357
  52.3 0.6 collective-permute-start.23
  52.9 1.6 %collective-permute-start.22 = (f32[4,32,128]{2,1,0:T(8,128)S(1)}, f32[4,32,128]{2,1,0:T(8,128)S(1)}, u32[]{:S(2)}, u32[]{:S(2)}) collective-permute-start(f32[4,32,128]{2,1,0:T(8,128)S(1)} %shard_map.141), channel_id=1, source_target_pairs={{0,4},{4,0},{8,12},{12,8},{1,5},{5,1},{9,13},{13,9},{2,6},{6,2},{1... | collective-permute-start | bytes 196616 | tf_op jit(solution)/shard_map/ppermute | solution.py:357
  54.5 1.9 %collective-permute-done.20.values = f32[4,32,128]{2,1,0:T(8,128)S(1)} collective-permute-done((f32[4,32,128]{2,1,0:T(8,128)S(1)}, f32[4,32,128]{2,1,0:T(8,128)S(1)}, u32[]{:S(2)}, u32[]{:S(2)}) %collective-permute-start.20) | collective-permute-done | bytes 65568 | tf_op jit(solution)/shard_map/ppermute | solution.py:357
  56.4 2.3 %collective-permute-done.23.refs_3_ = f32[4,32,128]{2,1,0:T(8,128)S(1)} collective-permute-done((f32[4,32,128]{2,1,0:T(8,128)S(1)}, f32[4,32,128]{2,1,0:T(8,128)S(1)}, u32[]{:S(2)}, u32[]{:S(2)}) %collective-permute-start.23) | collective-permute-done | bytes 65568 | tf_op jit(solution)/shard_map/ppermute | solution.py:357
  58.7 0.1 collective-permute-start.26
  58.8 1.2 %collective-permute-done.24.refs_2_ = f32[16,32,128]{2,1,0:T(8,128)S(1)} collective-permute-done((f32[16,32,128]{2,1,0:T(8,128)S(1)}, f32[16,32,128]{2,1,0:T(8,128)S(1)}, u32[]{:S(2)}, u32[]{:S(2)}) %collective-permute-start.24) | collective-permute-done | bytes 262176 | tf_op jit(solution)/shard_map/ppermute | solution.py:357
  60.0 0.1 collective-permute-start.25
  60.0 0.3 collective-permute-done.26.item_other
  60.3 1.3 %collective-permute-done.25.user_other = f32[16,32,128]{2,1,0:T(8,128)S(1)} collective-permute-done((f32[16,32,128]{2,1,0:T(8,128)S(1)}, f32[16,32,128]{2,1,0:T(8,128)S(1)}, u32[]{:S(2)}, u32[]{:S(2)}) %collective-permute-start.25) | collective-permute-done | bytes 262176 | tf_op jit(solution)/shard_map/ppermute | solution.py:357
  61.6 1.1 %shard_map.144 = (f32[64,2048]{1,0:T(8,128)}, f32[64,2048]{1,0:T(8,128)}) custom-call(f32[16,64,128]{2,1,0:T(8,128)S(1)} %get-tuple-element.44.user_half_grad, f32[16,32,128]{2,1,0:T(8,128)S(1)} %shard_map.143.user_mine, f32[16,32,128]{2,1,0:T(8,128)S(1)} %collective-permute-done.25.user_other, f32[16,64,128]{2,1,0:T(8,128)S(1)} %get-tuple-element.53.item_half_grad, ...), custom_call_target="tpu_custom_call" | custom-call | bytes 3145728 | tf_op jit(solution)/shard_map/pallas_call | solution.py:24
  (49 shorter events, 0.3 us)
Async XLA Ops:
  0.6 0.7 %copy-start.10 = (s32[256]{0:T(256)S(1)}, s32[256]{0:T(256)}, u32[]{:S(2)}) copy-start(s32[256]{0:T(256)} %param.21) | copy-start | bytes 3076
  0.6 0.7 %copy-start.9 = (s32[256]{0:T(256)S(1)}, s32[256]{0:T(256)}, u32[]{:S(2)}) copy-start(s32[256]{0:T(256)} %param.20) | copy-start | bytes 3076
  0.7 0.7 %copy-start.8 = (s32[256]{0:T(256)S(1)}, s32[256]{0:T(256)}, u32[]{:S(2)}) copy-start(s32[256]{0:T(256)} %param.19) | copy-start | bytes 3076
  0.7 5.9 %copy-start.13 = (bf16[64,2048]{1,0:T(8,128)(2,1)S(1)}, bf16[64,2048]{1,0:T(8,128)(2,1)}, u32[]{:S(2)}) copy-start(bf16[64,2048]{1,0:T(8,128)(2,1)} %item_emb.3) | copy-start | bytes 786436
  0.7 5.9 %copy-start.11 = (bf16[64,2048]{1,0:T(8,128)(2,1)S(1)}, bf16[64,2048]{1,0:T(8,128)(2,1)}, u32[]{:S(2)}) copy-start(bf16[64,2048]{1,0:T(8,128)(2,1)} %user_emb.3) | copy-start | bytes 786436
  0.7 5.9 %copy-start.17 = (s32[288]{0:T(512)S(1)}, s32[288]{0:T(512)}, u32[]{:S(2)}) copy-start(s32[288]{0:T(512)} %columns.1) | copy-start | bytes 3460
  0.7 5.9 %copy-start.16 = (s32[288]{0:T(512)S(1)}, s32[288]{0:T(512)}, u32[]{:S(2)}) copy-start(s32[288]{0:T(512)} %rows.1) | copy-start | bytes 3460
  0.7 5.9 %copy-start.15 = (s32[2048]{0:T(1024)S(1)}, s32[2048]{0:T(1024)}, u32[]{:S(2)}) copy-start(s32[2048]{0:T(1024)} %param.14) | copy-start | bytes 24580
  0.7 5.9 %copy-start.14 = (s32[2048]{0:T(1024)S(1)}, s32[2048]{0:T(1024)}, u32[]{:S(2)}) copy-start(s32[2048]{0:T(1024)} %param.13) | copy-start | bytes 24580
  0.7 6.9 %copy-start = (bf16[288,128,128]{2,1,0:T(8,128)(2,1)S(1)}, bf16[288,128,128]{2,1,0:T(8,128)(2,1)}, u32[]{:S(2)}) copy-start(bf16[288,128,128]{2,1,0:T(8,128)(2,1)} %vals.7) | copy-start | bytes 28311556
  1.3 9.6 %collective-permute-start.3 = (s32[16,256]{1,0:T(8,128)S(1)}, s32[16,256]{1,0:T(8,128)S(1)}, u32[]{:S(2)}, u32[]{:S(2)}) collective-permute-start(s32[16,256]{1,0:T(8,128)S(1)} %shard_map.123.after.refs_0_.ids.refs_4_), channel_id=1, source_target_pairs={{0,4},{4,0},{8,12},{12,8},{1,5},{5,1},{9,13},{13,9},{2,6},{6,2},{1... | collective-permute-start | bytes 49160 | tf_op jit(solution)/shard_map/ppermute | solution.py:357
  4.4 7.7 %collective-permute-start = (s32[16,256]{1,0:T(8,128)S(1)}, s32[16,256]{1,0:T(8,128)S(1)}, u32[]{:S(2)}, u32[]{:S(2)}) collective-permute-start(s32[16,256]{1,0:T(8,128)S(1)} %shard_map.123.after.refs_0_.ids.refs_4_), channel_id=1, source_target_pairs={{0,2},{2,0},{1,3},{3,1},{4,6},{6,4},{5,7},{7,5},{8,10},{10,8},{9,1... | collective-permute-start | bytes 49160 | tf_op jit(solution)/shard_map/ppermute | solution.py:357
  7.5 4.5 %copy-start.4 = (s32[4,384]{1,0:T(4,128)}, s32[4,384]{1,0:T(4,128)S(1)}, u32[]{:S(2)}) copy-start(s32[4,384]{1,0:T(4,128)S(1)} %get-tuple-element.28.order) | copy-start | bytes 18436
  7.6 9.2 %copy-start.6 = (s32[4,384]{1,0:T(4,128)}, s32[4,384]{1,0:T(4,128)S(1)}, u32[]{:S(2)}) copy-start(s32[4,384]{1,0:T(4,128)S(1)} %get-tuple-element.31.order) | copy-start | bytes 18436
  7.6 26.1 %copy-start.2 = (f32[16,128]{1,0:T(8,128)}, f32[16,128]{1,0:T(8,128)S(1)}, u32[]{:S(2)}) copy-start(f32[16,128]{1,0:T(8,128)S(1)} %get-tuple-element.29.scale.source_scale.target_scale) | copy-start | bytes 24580
  10.9 6.0 %collective-permute-start.2 = (f32[16,64,128]{2,1,0:T(8,128)S(1)}, f32[16,64,128]{2,1,0:T(8,128)S(1)}, u32[]{:S(2)}, u32[]{:S(2)}) collective-permute-start(f32[16,64,128]{2,1,0:T(8,128)S(1)} %shard_map.125.refs_0_.mine), channel_id=1, source_target_pairs={{0,1},{1,0},{2,3},{3,2},{4,5},{5,4},{6,7},{7,6},{8,9},{9,8},{10,11... | collective-permute-start | bytes 1572872 | tf_op jit(solution)/shard_map/ppermute | solution.py:357
  11.0 5.8 %collective-permute-start.4 = (s32[16,256]{1,0:T(8,128)S(1)}, s32[16,256]{1,0:T(8,128)S(1)}, u32[]{:S(2)}, u32[]{:S(2)}) collective-permute-start(s32[16,256]{1,0:T(8,128)S(1)} %shard_map.127), channel_id=1, source_target_pairs={{0,8},{4,12},{8,0},{12,4},{1,9},{5,13},{9,1},{13,5},{2,10},{6,14},... | collective-permute-start | bytes 49160 | tf_op jit(solution)/shard_map/ppermute | solution.py:357
  16.8 4.9 %collective-permute-start.1 = (f32[16,64,128]{2,1,0:T(8,128)S(1)}, f32[16,64,128]{2,1,0:T(8,128)S(1)}, u32[]{:S(2)}, u32[]{:S(2)}) collective-permute-start(f32[16,64,128]{2,1,0:T(8,128)S(1)} %shard_map.126.mine), channel_id=1, source_target_pairs={{0,1},{1,0},{2,3},{3,2},{4,5},{5,4},{6,7},{7,6},{8,9},{9,8},{10,11... | collective-permute-start | bytes 1572872 | tf_op jit(solution)/shard_map/ppermute | solution.py:357
  16.9 5.5 %copy-start.12 = (bf16[64,2048]{1,0:T(8,128)(2,1)S(1)}, bf16[64,2048]{1,0:T(8,128)(2,1)}, u32[]{:S(2)}) copy-start(bf16[64,2048]{1,0:T(8,128)(2,1)} %user_emb.3) | copy-start | bytes 786436
  16.9 16.8 %copy-start.5 = (s32[4,384]{1,0:T(4,128)S(1)}, s32[4,384]{1,0:T(4,128)}, u32[]{:S(2)}) copy-start(s32[4,384]{1,0:T(4,128)} %copy-done.4) | copy-start | bytes 18436
  18.1 7.4 %collective-permute-start.6 = (f32[64,256]{1,0:T(8,128)S(1)}, f32[64,256]{1,0:T(8,128)S(1)}, u32[]{:S(2)}, u32[]{:S(2)}) collective-permute-start(f32[64,256]{1,0:T(8,128)S(1)} %get-tuple-element.38), channel_id=1, source_target_pairs={{0,8},{4,12},{8,0},{12,4},{1,9},{5,13},{9,1},{13,5},{2,10},{6,14},... | collective-permute-start | bytes 196616 | tf_op jit(solution)/shard_map/ppermute | solution.py:357
  18.2 7.3 %collective-permute-start.7 = (f32[64,256]{1,0:T(8,128)S(1)}, f32[64,256]{1,0:T(8,128)S(1)}, u32[]{:S(2)}, u32[]{:S(2)}) collective-permute-start(f32[64,256]{1,0:T(8,128)S(1)} %get-tuple-element.39), channel_id=1, source_target_pairs={{0,12},{4,8},{8,4},{12,0},{1,13},{5,9},{9,5},{13,1},{2,14},{6,10},... | collective-permute-start | bytes 196616 | tf_op jit(solution)/shard_map/ppermute | solution.py:357
  20.3 6.5 %collective-permute-start.8 = (f32[64,256]{1,0:T(8,128)S(1)}, f32[64,256]{1,0:T(8,128)S(1)}, u32[]{:S(2)}, u32[]{:S(2)}) collective-permute-start(f32[64,256]{1,0:T(8,128)S(1)} %get-tuple-element.40), channel_id=1, source_target_pairs={{0,4},{4,0},{8,12},{12,8},{1,5},{5,1},{9,13},{13,9},{2,6},{6,2},{1... | collective-permute-start | bytes 196616 | tf_op jit(solution)/shard_map/ppermute | solution.py:357
  22.3 4.6 %collective-permute-start.5 = (f32[64,256]{1,0:T(8,128)S(1)}, f32[64,256]{1,0:T(8,128)S(1)}, u32[]{:S(2)}, u32[]{:S(2)}) collective-permute-start(f32[64,256]{1,0:T(8,128)S(1)} %get-tuple-element.36), channel_id=1, source_target_pairs={{0,2},{2,0},{1,3},{3,1},{4,6},{6,4},{5,7},{7,5},{8,10},{10,8},{9,1... | collective-permute-start | bytes 196616 | tf_op jit(solution)/shard_map/ppermute | solution.py:357
  26.9 4.3 %collective-permute-start.12 = (f32[64,256]{1,0:T(8,128)S(1)}, f32[64,256]{1,0:T(8,128)S(1)}, u32[]{:S(2)}, u32[]{:S(2)}) collective-permute-start(f32[64,256]{1,0:T(8,128)S(1)} %get-tuple-element.43.refs_0_), channel_id=1, source_target_pairs={{0,4},{4,0},{8,12},{12,8},{1,5},{5,1},{9,13},{13,9},{2,6},{6,2},{1... | collective-permute-start | bytes 196616 | tf_op jit(solution)/shard_map/ppermute | solution.py:357
  27.6 4.9 %collective-permute-start.11 = (f32[72,256]{1,0:T(8,128)S(1)}, f32[72,256]{1,0:T(8,128)S(1)}, u32[]{:S(2)}, u32[]{:S(2)}) collective-permute-start(f32[72,256]{1,0:T(8,128)S(1)} %get-tuple-element.42.refs_0_), channel_id=1, source_target_pairs={{0,3},{1,2},{2,1},{3,0},{4,7},{5,6},{6,5},{7,4},{8,11},{9,10},{10,... | collective-permute-start | bytes 221192 | tf_op jit(solution)/shard_map/ppermute | solution.py:456
  27.6 6.1 %collective-permute-start.10 = (f32[72,256]{1,0:T(8,128)S(1)}, f32[72,256]{1,0:T(8,128)S(1)}, u32[]{:S(2)}, u32[]{:S(2)}) collective-permute-start(f32[72,256]{1,0:T(8,128)S(1)} %get-tuple-element.42.refs_0_), channel_id=1, source_target_pairs={{0,2},{2,0},{1,3},{3,1},{4,6},{6,4},{5,7},{7,5},{8,10},{10,8},{9,1... | collective-permute-start | bytes 221192 | tf_op jit(solution)/shard_map/ppermute | solution.py:357
  29.0 4.7 %collective-permute-start.9 = (f32[72,256]{1,0:T(8,128)S(1)}, f32[72,256]{1,0:T(8,128)S(1)}, u32[]{:S(2)}, u32[]{:S(2)}) collective-permute-start(f32[72,256]{1,0:T(8,128)S(1)} %get-tuple-element.42.refs_0_), channel_id=1, source_target_pairs={{0,1},{1,0},{2,3},{3,2},{4,5},{5,4},{6,7},{7,6},{8,9},{9,8},{10,11... | collective-permute-start | bytes 221192 | tf_op jit(solution)/shard_map/ppermute | solution.py:357
  29.5 9.1 %collective-permute-start.13 = (f32[64,256]{1,0:T(8,128)S(1)}, f32[64,256]{1,0:T(8,128)S(1)}, u32[]{:S(2)}, u32[]{:S(2)}) collective-permute-start(f32[64,256]{1,0:T(8,128)S(1)} %get-tuple-element.43.refs_0_), channel_id=1, source_target_pairs={{0,8},{4,12},{8,0},{12,4},{1,9},{5,13},{9,1},{13,5},{2,10},{6,14},... | collective-permute-start | bytes 196616 | tf_op jit(solution)/shard_map/ppermute | solution.py:357
  31.3 7.5 %collective-permute-start.14 = (f32[64,256]{1,0:T(8,128)S(1)}, f32[64,256]{1,0:T(8,128)S(1)}, u32[]{:S(2)}, u32[]{:S(2)}) collective-permute-start(f32[64,256]{1,0:T(8,128)S(1)} %shard_map.132.refs_4_.refs_1_), channel_id=1, source_target_pairs={{0,8},{4,12},{8,0},{12,4},{1,9},{5,13},{9,1},{13,5},{2,10},{6,14},... | collective-permute-start | bytes 196616 | tf_op jit(solution)/shard_map/ppermute | solution.py:357
  38.5 2.2 %collective-permute-start.16 = (f32[16,32,128]{2,1,0:T(8,128)S(1)}, f32[16,32,128]{2,1,0:T(8,128)S(1)}, u32[]{:S(2)}, u32[]{:S(2)}) collective-permute-start(f32[16,32,128]{2,1,0:T(8,128)S(1)} %get-tuple-element.45.after), channel_id=1, source_target_pairs={{0,1},{1,0},{2,3},{3,2},{4,5},{5,4},{6,7},{7,6},{8,9},{9,8},{10,11... | collective-permute-start | bytes 786440 | tf_op jit(solution)/shard_map/ppermute | solution.py:357
  40.3 4.0 %collective-permute-start.15 = (f32[16,64,128]{2,1,0:T(8,128)S(1)}, f32[16,64,128]{2,1,0:T(8,128)S(1)}, u32[]{:S(2)}, u32[]{:S(2)}) collective-permute-start(f32[16,64,128]{2,1,0:T(8,128)S(1)} %shard_map.134.after.mine), channel_id=1, source_target_pairs={{0,1},{1,0},{2,3},{3,2},{4,5},{5,4},{6,7},{7,6},{8,9},{9,8},{10,11... | collective-permute-start | bytes 1572872 | tf_op jit(solution)/shard_map/ppermute | solution.py:357
  40.7 3.7 %copy-start.1 = (bf16[288,128,128]{2,1,0:T(8,128)(2,1)S(1)}, bf16[288,128,128]{2,1,0:T(8,128)(2,1)}, u32[]{:S(2)}) copy-start(bf16[288,128,128]{2,1,0:T(8,128)(2,1)} %vals.7) | copy-start | bytes 28311556
  40.7 3.7 %copy-start.3 = (f32[16,128]{1,0:T(8,128)S(1)}, f32[16,128]{1,0:T(8,128)}, u32[]{:S(2)}) copy-start(f32[16,128]{1,0:T(8,128)} %copy-done.2) | copy-start | bytes 24580
  40.7 3.7 %copy-start.7 = (s32[4,384]{1,0:T(4,128)S(1)}, s32[4,384]{1,0:T(4,128)}, u32[]{:S(2)}) copy-start(s32[4,384]{1,0:T(4,128)} %copy-done.6) | copy-start | bytes 18436
  40.7 8.5 %collective-permute-start.17 = (f32[4,32,128]{2,1,0:T(8,128)S(1)}, f32[4,32,128]{2,1,0:T(8,128)S(1)}, u32[]{:S(2)}, u32[]{:S(2)}) collective-permute-start(f32[4,32,128]{2,1,0:T(8,128)S(1)} %get-tuple-element.49), channel_id=1, source_target_pairs={{0,8},{4,12},{8,0},{12,4},{1,9},{5,13},{9,1},{13,5},{2,10},{6,14},... | collective-permute-start | bytes 196616 | tf_op jit(solution)/shard_map/ppermute | solution.py:357
  40.8 8.5 %collective-permute-start.18 = (f32[4,32,128]{2,1,0:T(8,128)S(1)}, f32[4,32,128]{2,1,0:T(8,128)S(1)}, u32[]{:S(2)}, u32[]{:S(2)}) collective-permute-start(f32[4,32,128]{2,1,0:T(8,128)S(1)} %get-tuple-element.50), channel_id=1, source_target_pairs={{0,12},{4,8},{8,4},{12,0},{1,13},{5,9},{9,5},{13,1},{2,14},{6,10},... | collective-permute-start | bytes 196616 | tf_op jit(solution)/shard_map/ppermute | solution.py:357
  43.4 6.0 %collective-permute-start.19 = (f32[4,32,128]{2,1,0:T(8,128)S(1)}, f32[4,32,128]{2,1,0:T(8,128)S(1)}, u32[]{:S(2)}, u32[]{:S(2)}) collective-permute-start(f32[4,32,128]{2,1,0:T(8,128)S(1)} %get-tuple-element.51), channel_id=1, source_target_pairs={{0,4},{4,0},{8,12},{12,8},{1,5},{5,1},{9,13},{13,9},{2,6},{6,2},{1... | collective-permute-start | bytes 196616 | tf_op jit(solution)/shard_map/ppermute | solution.py:357
  49.5 2.0 %collective-permute-start.21 = (f32[16,32,128]{2,1,0:T(8,128)S(1)}, f32[16,32,128]{2,1,0:T(8,128)S(1)}, u32[]{:S(2)}, u32[]{:S(2)}) collective-permute-start(f32[16,32,128]{2,1,0:T(8,128)S(1)} %shard_map.139), channel_id=1, source_target_pairs={{0,1},{1,0},{2,3},{3,2},{4,5},{5,4},{6,7},{7,6},{8,9},{9,8},{10,11... | collective-permute-start | bytes 786440 | tf_op jit(solution)/shard_map/ppermute | solution.py:357
  49.6 6.8 %collective-permute-start.20 = (f32[4,32,128]{2,1,0:T(8,128)S(1)}, f32[4,32,128]{2,1,0:T(8,128)S(1)}, u32[]{:S(2)}, u32[]{:S(2)}) collective-permute-start(f32[4,32,128]{2,1,0:T(8,128)S(1)} %shard_map.137.refs_0_.values), channel_id=1, source_target_pairs={{0,12},{4,8},{8,4},{12,0},{1,13},{5,9},{9,5},{13,1},{2,14},{6,10},... | collective-permute-start | bytes 196616 | tf_op jit(solution)/shard_map/ppermute | solution.py:357
  51.5 8.4 %collective-permute-start.24 = (f32[16,32,128]{2,1,0:T(8,128)S(1)}, f32[16,32,128]{2,1,0:T(8,128)S(1)}, u32[]{:S(2)}, u32[]{:S(2)}) collective-permute-start(f32[16,32,128]{2,1,0:T(8,128)S(1)} %shard_map.140.refs_0_.refs_1_), channel_id=1, source_target_pairs={{0,2},{2,0},{1,3},{3,1},{4,6},{6,4},{5,7},{7,5},{8,10},{10,8},{9,1... | collective-permute-start | bytes 786440 | tf_op jit(solution)/shard_map/ppermute | solution.py:357
  52.3 6.4 %collective-permute-start.23 = (f32[4,32,128]{2,1,0:T(8,128)S(1)}, f32[4,32,128]{2,1,0:T(8,128)S(1)}, u32[]{:S(2)}, u32[]{:S(2)}) collective-permute-start(f32[4,32,128]{2,1,0:T(8,128)S(1)} %shard_map.141), channel_id=1, source_target_pairs={{0,8},{4,12},{8,0},{12,4},{1,9},{5,13},{9,1},{13,5},{2,10},{6,14},... | collective-permute-start | bytes 196616 | tf_op jit(solution)/shard_map/ppermute | solution.py:357
  52.9 5.8 %collective-permute-start.22 = (f32[4,32,128]{2,1,0:T(8,128)S(1)}, f32[4,32,128]{2,1,0:T(8,128)S(1)}, u32[]{:S(2)}, u32[]{:S(2)}) collective-permute-start(f32[4,32,128]{2,1,0:T(8,128)S(1)} %shard_map.141), channel_id=1, source_target_pairs={{0,4},{4,0},{8,12},{12,8},{1,5},{5,1},{9,13},{13,9},{2,6},{6,2},{1... | collective-permute-start | bytes 196616 | tf_op jit(solution)/shard_map/ppermute | solution.py:357
  58.7 1.6 %collective-permute-start.26 = (f32[4,4,32,128]{3,2,1,0:T(8,128)S(1)}, f32[4,4,32,128]{3,2,1,0:T(8,128)S(1)}, u32[]{:S(2)}, u32[]{:S(2)}) collective-permute-start(f32[4,4,32,128]{3,2,1,0:T(8,128)S(1)} %shard_map.142.refs_0_.item_mine), channel_id=1, source_target_pairs={{0,1},{1,0},{2,3},{3,2},{4,5},{5,4},{6,7},{7,6},{8,9},{9,8},{10,11... | collective-permute-start | bytes 786440 | tf_op jit(solution)/shard_map/ppermute | solution.py:357
  60.0 1.6 %collective-permute-start.25 = (f32[16,32,128]{2,1,0:T(8,128)S(1)}, f32[16,32,128]{2,1,0:T(8,128)S(1)}, u32[]{:S(2)}, u32[]{:S(2)}) collective-permute-start(f32[16,32,128]{2,1,0:T(8,128)S(1)} %shard_map.143.user_mine), channel_id=1, source_target_pairs={{0,1},{1,0},{2,3},{3,2},{4,5},{5,4},{6,7},{7,6},{8,9},{9,8},{10,11... | collective-permute-start | bytes 786440 | tf_op jit(solution)/shard_map/ppermute | solution.py:357

commit v10 on v7

--- a/solution.py
+++ b/solution.py
@@ -323,13 +323,7 @@
         refs[-1][place] = ref[...]
 
 
-def finish(offsets, user_half_grad, user_mine, user_other, item_half_grad, item_mine, item_other,
-           user_out, item_out):
-    finish_users(user_half_grad, user_mine, user_other, user_out)
-    finish_items(offsets, item_half_grad, item_mine, item_other, item_out)
-
-
-def finish_users(half_grad, mine, other, out):
+def finish_users(half_grad, mine, other, after, out):
     me = lax.axis_index("rep")
     blocks, width, size = half_grad.shape
     half = width // 2
@@ -508,12 +502,17 @@
     mine = call(functools.partial(sum_after, 1), shape(user_blocks, half, size),
                 (item_mine, own, *[swap(own, "item", items, o) for o in range(1, items)]),
                 [ANY] + [VMEM] * items, moved=12 * user_blocks * half * size)
-    return call(
-        functools.partial(finish, item_places),
-        (shape(width, user_blocks * size), shape(width, item_blocks * size)),
-        (user_half_grad, mine, swap(mine), item_half_grad, item_mine, swap(item_mine)),
-        [VMEM] * 6, moved=12 * (user_blocks + item_blocks) * width * size,
-    )
+    grad_item = call(
+        functools.partial(finish_items, item_places), shape(width, item_blocks * size),
+        (item_half_grad, item_mine, swap(item_mine)), [VMEM] * 3,
+        moved=12 * item_blocks * width * size,
+    )
+    grad_user = call(
+        finish_users, shape(width, user_blocks * size),
+        (user_half_grad, mine, swap(mine), item_mine), [VMEM] * 3 + [ANY],
+        moved=12 * user_blocks * width * size,
+    )
+    return (grad_user, grad_item)
 
 
 def solution(mesh):

time: 62.2 us -> 63.1 us (1.014)
  starting transfers between devices: 32.1 us -> 28.6 us
  waiting for transfers between devices: 12.6 us -> 15.3 us
  Pallas kernels: 14.7 us -> 16.5 us
    ppermute x26, starting transfers between devices: 31.8 us -> 28.6 us  [swap(): return lax.ppermute(values, axis, [(i, i ^ offset) for i in range(peers)])]
    ppermute x26, waiting for transfers between devices: 12.6 us -> 15.3 us  [swap(): return lax.ppermute(values, axis, [(i, i ^ offset) for i in range(peers)])]
    pallas_call x22 -> x23, Pallas kernels: 14.7 us -> 16.5 us  [call(): pl.pallas_call(kernel, out_shape=outs, in_specs=specs, out_specs=jax.tree...]
  transfers between devices with their start and end apart: 27 -> 27, of which waited for: 13 -> 11; matrix products, arithmetic and copies ran while one was open for 0% -> 0% of each run, Pallas kernels for 22% -> 25%
where the time goes in v10:
time: 63.1 us; the launch traced here: 62.8 us
  starting transfers between devices  28.6 us (45%)
  Pallas kernels  16.5 us (26%)
  waiting for transfers between devices  15.3 us (24%)
  between operations  1.74 us (3%)
  local copies, waits for them, and re-layouts  0.7 us (1%)
    ppermute x26, starting transfers between devices, swap(): return lax.ppermute(values, axis, [(i, i ^ offset) for i in range(peers)])  28.6 us
    pallas_call x23, Pallas kernels, call(): pl.pallas_call(kernel, out_shape=outs, in_specs=specs, out_specs=jax.tree...  16.5 us
    ppermute x26, waiting for transfers between devices, swap(): return lax.ppermute(values, axis, [(i, i ^ offset) for i in range(peers)])  15.3 us
  transfers between devices with their start and end apart: 27, of which 11 were waited for; matrix products, arithmetic and copies ran while one was open for 0% of the time, Pallas kernels for 25%

profile of v10, /device:TPU:0, one launch (start us, length us, event | category | flops | bytes accessed | tf_op | source)
XLA Modules:
  0.0 62.8 jit_solution(6423010574991065494)
XLA Ops:
  0.7 0.0 copy-start.11
  0.7 0.0 copy-start
  0.7 0.6 copy-done.10
  1.3 0.0 copy-done.9
  1.3 0.0 copy-done.8
  1.3 3.1 %collective-permute-start.3 = (s32[16,256]{1,0:T(8,128)S(1)}, s32[16,256]{1,0:T(8,128)S(1)}, u32[]{:S(2)}, u32[]{:S(2)}) collective-permute-start(s32[16,256]{1,0:T(8,128)S(1)} %shard_map.123.after.refs_0_.ids.refs_4_), channel_id=1, source_target_pairs={{0,4},{4,0},{8,12},{12,8},{1,5},{5,1},{9,13},{13,9},{2,6},{6,2},{1... | collective-permute-start | bytes 49160 | tf_op jit(solution)/shard_map/ppermute | solution.py:351
  4.4 1.5 %collective-permute-start = (s32[16,256]{1,0:T(8,128)S(1)}, s32[16,256]{1,0:T(8,128)S(1)}, u32[]{:S(2)}, u32[]{:S(2)}) collective-permute-start(s32[16,256]{1,0:T(8,128)S(1)} %shard_map.123.after.refs_0_.ids.refs_4_), channel_id=1, source_target_pairs={{0,2},{2,0},{1,3},{3,1},{4,6},{6,4},{5,7},{7,5},{8,10},{10,8},{9,1... | collective-permute-start | bytes 49160 | tf_op jit(solution)/shard_map/ppermute | solution.py:351
  6.6 0.9 %shard_map.124 = (bf16[17,64,128]{2,1,0:T(8,128)(2,1)S(1)}, bf16[17,64,128]{2,1,0:T(8,128)(2,1)S(1)}, f32[16,128]{1,0:T(8,128)S(1)}, f32[16,128]{1,0:T(8,128)S(1...) custom-call(s32[1]{0:T(128)S(6)} %copy.13.count, s32[288]{0:T(512)S(1)} %copy-done.16, s32[288]{0:T(512)S(1)} %copy-done.17, ...), custom_call_target="tpu_custom_call" | custom-call | flops 603979776 | bytes 9437184 | tf_op jit(solution)/shard_map/pallas_call | solution.py:24
  7.5 0.0 copy-start.4
  7.6 0.0 copy-start.2
  7.6 1.7 %shard_map.125.refs_0_.mine = f32[16,64,128]{2,1,0:T(8,128)S(1)} custom-call(s32[4,384]{1,0:T(4,128)S(1)} %get-tuple-element.28.order, bf16[288,128,128]{2,1,0:T(8,128)(2,1)S(1)} %copy-done, bf16[17,64,128]{2,1,0:T(8,128)(2,1)S(1)} %get-tuple-element.33.source, s32[16,256]{1,0:T(8,128)S(1)} %shard_map.123.after.refs_0_.ids.refs_4_), custom_call_target="tpu_custom_call" | custom-call | flops 603979776 | bytes 9437184 | tf_op jit(solution)/shard_map/pallas_call | solution.py:24
  9.3 0.1 collective-permute-start.2
  9.4 0.0 collective-permute-done.3.refs_1_.refs_5_
  9.4 4.2 %collective-permute-start.4 = (s32[16,256]{1,0:T(8,128)S(1)}, s32[16,256]{1,0:T(8,128)S(1)}, u32[]{:S(2)}, u32[]{:S(2)}) collective-permute-start(s32[16,256]{1,0:T(8,128)S(1)} %shard_map.127), channel_id=1, source_target_pairs={{0,8},{4,12},{8,0},{12,4},{1,9},{5,13},{9,1},{13,5},{2,10},{6,14},... | collective-permute-start | bytes 49160 | tf_op jit(solution)/shard_map/ppermute | solution.py:351
  13.7 2.3 %shard_map.126.mine = f32[16,64,128]{2,1,0:T(8,128)S(1)} custom-call(s32[4,384]{1,0:T(4,128)S(1)} %get-tuple-element.31.order, bf16[288,128,128]{2,1,0:T(8,128)(2,1)S(1)} %copy-done, bf16[17,64,128]{2,1,0:T(8,128)(2,1)S(1)} %get-tuple-element.32.source, f32[16,64,128]{2,1,0:T(8,128)S(1)} %shard_map.125.refs_0_.mine, s32[16,256]{1,0:T(8,128)S(1)} %collective-permute-done.refs_1_), custom_call_target="tpu_custom_call" | custom-call | flops 99999997952 | bytes 9437184 | tf_op jit(solution)/shard_map/pallas_call | solution.py:24
  16.0 1.0 %collective-permute-start.1 = (f32[16,64,128]{2,1,0:T(8,128)S(1)}, f32[16,64,128]{2,1,0:T(8,128)S(1)}, u32[]{:S(2)}, u32[]{:S(2)}) collective-permute-start(f32[16,64,128]{2,1,0:T(8,128)S(1)} %shard_map.126.mine), channel_id=1, source_target_pairs={{0,1},{1,0},{2,3},{3,2},{4,5},{5,4},{6,7},{7,6},{8,9},{9,8},{10,11... | collective-permute-start | bytes 1572872 | tf_op jit(solution)/shard_map/ppermute | solution.py:351
  17.0 0.0 collective-permute-done.4.refs_2_.refs_6_
  17.1 0.0 collective-permute-done.2.other
  17.1 0.0 copy-start.5
  17.1 1.2 %shard_map.128 = (f32[64,256]{1,0:T(8,128)S(1)}, f32[64,256]{1,0:T(8,128)S(1)}, f32[64,256]{1,0:T(8,128)S(1)}, f32[64,256]{1,0:T(8,128)S(1)}) custom-call(f32[16,64,128]{2,1,0:T(8,128)S(1)} %shard_map.125.refs_0_.mine, f32[16,64,128]{2,1,0:T(8,128)S(1)} %collective-permute-done.2.other, f32[16,128]{1,0:T(8,128)S(1)} %get-tuple-element.30.scale.target_scale.source_scale, ...), custom_call_target="tpu_custom_call" | custom-call | flops 99999997952 | bytes 1048576 | tf_op jit(solution)/shard_map/pallas_call | solution.py:24
  18.3 1.6 %collective-permute-start.6 = (f32[64,256]{1,0:T(8,128)S(1)}, f32[64,256]{1,0:T(8,128)S(1)}, u32[]{:S(2)}, u32[]{:S(2)}) collective-permute-start(f32[64,256]{1,0:T(8,128)S(1)} %get-tuple-element.38), channel_id=1, source_target_pairs={{0,8},{4,12},{8,0},{12,4},{1,9},{5,13},{9,1},{13,5},{2,10},{6,14},... | collective-permute-start | bytes 196616 | tf_op jit(solution)/shard_map/ppermute | solution.py:351
  19.9 0.0 collective-permute-start.7
  19.9 1.9 %collective-permute-start.8 = (f32[64,256]{1,0:T(8,128)S(1)}, f32[64,256]{1,0:T(8,128)S(1)}, u32[]{:S(2)}, u32[]{:S(2)}) collective-permute-start(f32[64,256]{1,0:T(8,128)S(1)} %get-tuple-element.40), channel_id=1, source_target_pairs={{0,4},{4,0},{8,12},{12,8},{1,5},{5,1},{9,13},{13,9},{2,6},{6,2},{1... | collective-permute-start | bytes 196616 | tf_op jit(solution)/shard_map/ppermute | solution.py:351
  21.9 0.6 shard_map.129
  22.5 0.1 collective-permute-start.5
  22.6 0.5 shard_map.130
  23.0 1.0 %collective-permute-done.6.refs_4_ = f32[64,256]{1,0:T(8,128)S(1)} collective-permute-done((f32[64,256]{1,0:T(8,128)S(1)}, f32[64,256]{1,0:T(8,128)S(1)}, u32[]{:S(2)}, u32[]{:S(2)}) %collective-permute-start.6) | collective-permute-done | bytes 65568 | tf_op jit(solution)/shard_map/ppermute | solution.py:351
  24.0 2.6 %collective-permute-done.7.refs_5_ = f32[64,256]{1,0:T(8,128)S(1)} collective-permute-done((f32[64,256]{1,0:T(8,128)S(1)}, f32[64,256]{1,0:T(8,128)S(1)}, u32[]{:S(2)}, u32[]{:S(2)}) %collective-permute-start.7) | collective-permute-done | bytes 65568 | tf_op jit(solution)/shard_map/ppermute | solution.py:351
  26.6 0.2 collective-permute-done.5.refs_1_
  26.8 0.1 shard_map.131
  26.9 0.1 collective-permute-start.11
  26.9 0.1 collective-permute-start.10
  27.0 1.8 %collective-permute-start.9 = (f32[72,256]{1,0:T(8,128)S(1)}, f32[72,256]{1,0:T(8,128)S(1)}, u32[]{:S(2)}, u32[]{:S(2)}) collective-permute-start(f32[72,256]{1,0:T(8,128)S(1)} %get-tuple-element.42.refs_0_), channel_id=1, source_target_pairs={{0,1},{1,0},{2,3},{3,2},{4,5},{5,4},{6,7},{7,6},{8,9},{9,8},{10,11... | collective-permute-start | bytes 221192 | tf_op jit(solution)/shard_map/ppermute | solution.py:351
  28.8 2.5 %collective-permute-start.14 = (f32[64,256]{1,0:T(8,128)S(1)}, f32[64,256]{1,0:T(8,128)S(1)}, u32[]{:S(2)}, u32[]{:S(2)}) collective-permute-start(f32[64,256]{1,0:T(8,128)S(1)} %get-tuple-element.45.refs_0_), channel_id=1, source_target_pairs={{0,8},{4,12},{8,0},{12,4},{1,9},{5,13},{9,1},{13,5},{2,10},{6,14},... | collective-permute-start | bytes 196616 | tf_op jit(solution)/shard_map/ppermute | solution.py:351
  31.2 0.4 collective-permute-start.13
  31.6 0.0 collective-permute-done.11.refs_3_
  31.6 0.7 %collective-permute-start.12 = (f32[64,256]{1,0:T(8,128)S(1)}, f32[64,256]{1,0:T(8,128)S(1)}, u32[]{:S(2)}, u32[]{:S(2)}) collective-permute-start(f32[64,256]{1,0:T(8,128)S(1)} %get-tuple-element.45.refs_0_), channel_id=1, source_target_pairs={{0,4},{4,0},{8,12},{12,8},{1,5},{5,1},{9,13},{13,9},{2,6},{6,2},{1... | collective-permute-start | bytes 196616 | tf_op jit(solution)/shard_map/ppermute | solution.py:351
  32.3 3.3 %shard_map.132 = (f32[16,64,128]{2,1,0:T(8,128)S(1)}, f32[16,32,128]{2,1,0:T(8,128)S(1)}, f32[16,32,128]{2,1,0:T(8,128)S(1)}) custom-call(s32[4,384]{1,0:T(4,128)S(1)} %copy-done.5, f32[16,128]{1,0:T(8,128)S(1)} %get-tuple-element.29.scale.source_scale.target_scale, f32[16,128]{1,0:T(8,128)S(1)} %get-tuple-element.30.scale.target_scale.source_scale, ...), custom_call_target="tpu_custom_call" | custom-call | flops 603979776 | bytes 9437184 | tf_op jit(solution)/shard_map/pallas_call | solution.py:24
  35.6 0.1 collective-permute-start.16
  35.7 1.9 %collective-permute-done.13.refs_2_ = f32[64,256]{1,0:T(8,128)S(1)} collective-permute-done((f32[64,256]{1,0:T(8,128)S(1)}, f32[64,256]{1,0:T(8,128)S(1)}, u32[]{:S(2)}, u32[]{:S(2)}) %collective-permute-start.13) | collective-permute-done | bytes 65568 | tf_op jit(solution)/shard_map/ppermute | solution.py:351
  37.6 1.5 %shard_map.133.after.mine = f32[16,64,128]{2,1,0:T(8,128)S(1)} custom-call(f32[16,32,128]{2,1,0:T(8,128)S(1)} %get-tuple-element.44.after, f32[64,256]{1,0:T(8,128)S(1)} %get-tuple-element.45.refs_0_, f32[64,256]{1,0:T(8,128)S(1)} %collective-permute-done.12.refs_1_, f32[64,256]{1,0:T(8,128)S(1)} %collective-permute-done.13.refs_2_, ...), custom_call_target="tpu_custom_call" | custom-call | flops 99999997952 | tf_op jit(solution)/shard_map/pallas_call | solution.py:24
  39.1 0.1 collective-permute-start.15
  39.2 0.0 copy-start.1
  39.2 0.0 copy-start.3
  39.3 3.5 %collective-permute-start.17 = (f32[4,32,128]{2,1,0:T(8,128)S(1)}, f32[4,32,128]{2,1,0:T(8,128)S(1)}, u32[]{:S(2)}, u32[]{:S(2)}) collective-permute-start(f32[4,32,128]{2,1,0:T(8,128)S(1)} %get-tuple-element.49), channel_id=1, source_target_pairs={{0,8},{4,12},{8,0},{12,4},{1,9},{5,13},{9,1},{13,5},{2,10},{6,14},... | collective-permute-start | bytes 196616 | tf_op jit(solution)/shard_map/ppermute | solution.py:351
  42.8 0.6 %collective-permute-start.19 = (f32[4,32,128]{2,1,0:T(8,128)S(1)}, f32[4,32,128]{2,1,0:T(8,128)S(1)}, u32[]{:S(2)}, u32[]{:S(2)}) collective-permute-start(f32[4,32,128]{2,1,0:T(8,128)S(1)} %get-tuple-element.51), channel_id=1, source_target_pairs={{0,4},{4,0},{8,12},{12,8},{1,5},{5,1},{9,13},{13,9},{2,6},{6,2},{1... | collective-permute-start | bytes 196616 | tf_op jit(solution)/shard_map/ppermute | solution.py:351
  43.4 2.5 %shard_map.135 = (f32[16,64,128]{2,1,0:T(8,128)S(1)}, f32[16,32,128]{2,1,0:T(8,128)S(1)}, f32[16,32,128]{2,1,0:T(8,128)S(1)}) custom-call(s32[4,384]{1,0:T(4,128)S(1)} %copy-done.7, f32[16,64,128]{2,1,0:T(8,128)S(1)} %shard_map.133.after.mine, f32[16,64,128]{2,1,0:T(8,128)S(1)} %collective-permute-done.15.other, ...), custom_call_target="tpu_custom_call" | custom-call | flops 603979776 | bytes 9437184 | tf_op jit(solution)/shard_map/pallas_call | solution.py:24
  45.9 0.5 collective-permute-done.17.refs_2_
  46.4 2.7 %collective-permute-done.18.refs_3_ = f32[4,32,128]{2,1,0:T(8,128)S(1)} collective-permute-done((f32[4,32,128]{2,1,0:T(8,128)S(1)}, f32[4,32,128]{2,1,0:T(8,128)S(1)}, u32[]{:S(2)}, u32[]{:S(2)}) %collective-permute-start.18) | collective-permute-done | bytes 65568 | tf_op jit(solution)/shard_map/ppermute | solution.py:351
  49.1 0.0 collective-permute-done.19.refs_4_
  49.2 0.1 collective-permute-start.21
  49.3 2.2 %collective-permute-start.20 = (f32[4,32,128]{2,1,0:T(8,128)S(1)}, f32[4,32,128]{2,1,0:T(8,128)S(1)}, u32[]{:S(2)}, u32[]{:S(2)}) collective-permute-start(f32[4,32,128]{2,1,0:T(8,128)S(1)} %shard_map.136.refs_0_.values), channel_id=1, source_target_pairs={{0,12},{4,8},{8,4},{12,0},{1,13},{5,9},{9,5},{13,1},{2,14},{6,10},... | collective-permute-start | bytes 196616 | tf_op jit(solution)/shard_map/ppermute | solution.py:351
  51.5 0.8 %collective-permute-start.24 = (f32[16,32,128]{2,1,0:T(8,128)S(1)}, f32[16,32,128]{2,1,0:T(8,128)S(1)}, u32[]{:S(2)}, u32[]{:S(2)}) collective-permute-start(f32[16,32,128]{2,1,0:T(8,128)S(1)} %shard_map.139.refs_0_.refs_1_), channel_id=1, source_target_pairs={{0,2},{2,0},{1,3},{3,1},{4,6},{6,4},{5,7},{7,5},{8,10},{10,8},{9,1... | collective-permute-start | bytes 786440 | tf_op jit(solution)/shard_map/ppermute | solution.py:351
  52.3 1.7 %collective-permute-start.23 = (f32[4,32,128]{2,1,0:T(8,128)S(1)}, f32[4,32,128]{2,1,0:T(8,128)S(1)}, u32[]{:S(2)}, u32[]{:S(2)}) collective-permute-start(f32[4,32,128]{2,1,0:T(8,128)S(1)} %shard_map.140), channel_id=1, source_target_pairs={{0,8},{4,12},{8,0},{12,4},{1,9},{5,13},{9,1},{13,5},{2,10},{6,14},... | collective-permute-start | bytes 196616 | tf_op jit(solution)/shard_map/ppermute | solution.py:351
  54.0 0.4 collective-permute-start.22
  54.4 1.2 %collective-permute-done.20.values = f32[4,32,128]{2,1,0:T(8,128)S(1)} collective-permute-done((f32[4,32,128]{2,1,0:T(8,128)S(1)}, f32[4,32,128]{2,1,0:T(8,128)S(1)}, u32[]{:S(2)}, u32[]{:S(2)}) %collective-permute-start.20) | collective-permute-done | bytes 65568 | tf_op jit(solution)/shard_map/ppermute | solution.py:351
  55.7 3.7 %collective-permute-done.23.refs_3_ = f32[4,32,128]{2,1,0:T(8,128)S(1)} collective-permute-done((f32[4,32,128]{2,1,0:T(8,128)S(1)}, f32[4,32,128]{2,1,0:T(8,128)S(1)}, u32[]{:S(2)}, u32[]{:S(2)}) %collective-permute-start.23) | collective-permute-done | bytes 65568 | tf_op jit(solution)/shard_map/ppermute | solution.py:351
  59.4 0.1 collective-permute-done.22.refs_2_
  59.5 0.1 collective-permute-start.26
  59.6 0.4 collective-permute-done.24.refs_2_
  60.0 0.2 collective-permute-start.25
  60.2 0.9 %collective-permute-done.26.other = f32[4,4,32,128]{3,2,1,0:T(8,128)S(1)} collective-permute-done((f32[4,4,32,128]{3,2,1,0:T(8,128)S(1)}, f32[4,4,32,128]{3,2,1,0:T(8,128)S(1)}, u32[]{:S(2)}, u32[]{:S(2)}) %collective-permute-start.26) | collective-permute-done | bytes 262176 | tf_op jit(solution)/shard_map/ppermute | solution.py:351
  61.1 0.9 %shard_map.144 = f32[64,2048]{1,0:T(8,128)} custom-call(f32[16,64,128]{2,1,0:T(8,128)S(1)} %get-tuple-element.53.half_grad, f32[4,4,32,128]{3,2,1,0:T(8,128)S(1)} %shard_map.141.refs_0_.after.mine, f32[4,4,32,128]{3,2,1,0:T(8,128)S(1)} %collective-permute-done.26.other), custom_call_target="tpu_custom_call" | custom-call | bytes 1572864 | tf_op jit(solution)/shard_map/pallas_call | solution.py:24
  62.0 0.8 %shard_map.143 = f32[64,2048]{1,0:T(8,128)} custom-call(f32[16,64,128]{2,1,0:T(8,128)S(1)} %get-tuple-element.43.half_grad, f32[16,32,128]{2,1,0:T(8,128)S(1)} %shard_map.142.mine, f32[16,32,128]{2,1,0:T(8,128)S(1)} %collective-permute-done.25.other, f32[4,4,32,128]{3,2,1,0:T(8,128)S(1)} %shard_map.141.refs_0_.after.mine), custom_call_target="tpu_custom_call" | custom-call | bytes 1572864 | tf_op jit(solution)/shard_map/pallas_call | solution.py:24
  (49 shorter events, 0.3 us)
Async XLA Ops:
  0.6 0.7 %copy-start.10 = (s32[256]{0:T(256)S(1)}, s32[256]{0:T(256)}, u32[]{:S(2)}) copy-start(s32[256]{0:T(256)} %param.21) | copy-start | bytes 3076
  0.6 0.7 %copy-start.9 = (s32[256]{0:T(256)S(1)}, s32[256]{0:T(256)}, u32[]{:S(2)}) copy-start(s32[256]{0:T(256)} %param.20) | copy-start | bytes 3076
  0.7 0.7 %copy-start.8 = (s32[256]{0:T(256)S(1)}, s32[256]{0:T(256)}, u32[]{:S(2)}) copy-start(s32[256]{0:T(256)} %param.19) | copy-start | bytes 3076
  0.7 5.9 %copy-start.13 = (bf16[64,2048]{1,0:T(8,128)(2,1)S(1)}, bf16[64,2048]{1,0:T(8,128)(2,1)}, u32[]{:S(2)}) copy-start(bf16[64,2048]{1,0:T(8,128)(2,1)} %item_emb.3) | copy-start | bytes 786436
  0.7 5.9 %copy-start.11 = (bf16[64,2048]{1,0:T(8,128)(2,1)S(1)}, bf16[64,2048]{1,0:T(8,128)(2,1)}, u32[]{:S(2)}) copy-start(bf16[64,2048]{1,0:T(8,128)(2,1)} %user_emb.3) | copy-start | bytes 786436
  0.7 5.9 %copy-start.17 = (s32[288]{0:T(512)S(1)}, s32[288]{0:T(512)}, u32[]{:S(2)}) copy-start(s32[288]{0:T(512)} %columns.1) | copy-start | bytes 3460
  0.7 5.9 %copy-start.16 = (s32[288]{0:T(512)S(1)}, s32[288]{0:T(512)}, u32[]{:S(2)}) copy-start(s32[288]{0:T(512)} %rows.1) | copy-start | bytes 3460
  0.7 5.9 %copy-start.15 = (s32[2048]{0:T(1024)S(1)}, s32[2048]{0:T(1024)}, u32[]{:S(2)}) copy-start(s32[2048]{0:T(1024)} %param.14) | copy-start | bytes 24580
  0.7 5.9 %copy-start.14 = (s32[2048]{0:T(1024)S(1)}, s32[2048]{0:T(1024)}, u32[]{:S(2)}) copy-start(s32[2048]{0:T(1024)} %param.13) | copy-start | bytes 24580
  0.7 6.9 %copy-start = (bf16[288,128,128]{2,1,0:T(8,128)(2,1)S(1)}, bf16[288,128,128]{2,1,0:T(8,128)(2,1)}, u32[]{:S(2)}) copy-start(bf16[288,128,128]{2,1,0:T(8,128)(2,1)} %vals.7) | copy-start | bytes 28311556
  1.3 8.1 %collective-permute-start.3 = (s32[16,256]{1,0:T(8,128)S(1)}, s32[16,256]{1,0:T(8,128)S(1)}, u32[]{:S(2)}, u32[]{:S(2)}) collective-permute-start(s32[16,256]{1,0:T(8,128)S(1)} %shard_map.123.after.refs_0_.ids.refs_4_), channel_id=1, source_target_pairs={{0,4},{4,0},{8,12},{12,8},{1,5},{5,1},{9,13},{13,9},{2,6},{6,2},{1... | collective-permute-start | bytes 49160 | tf_op jit(solution)/shard_map/ppermute | solution.py:351
  4.4 9.2 %collective-permute-start = (s32[16,256]{1,0:T(8,128)S(1)}, s32[16,256]{1,0:T(8,128)S(1)}, u32[]{:S(2)}, u32[]{:S(2)}) collective-permute-start(s32[16,256]{1,0:T(8,128)S(1)} %shard_map.123.after.refs_0_.ids.refs_4_), channel_id=1, source_target_pairs={{0,2},{2,0},{1,3},{3,1},{4,6},{6,4},{5,7},{7,5},{8,10},{10,8},{9,1... | collective-permute-start | bytes 49160 | tf_op jit(solution)/shard_map/ppermute | solution.py:351
  7.5 6.1 %copy-start.4 = (s32[4,384]{1,0:T(4,128)}, s32[4,384]{1,0:T(4,128)S(1)}, u32[]{:S(2)}) copy-start(s32[4,384]{1,0:T(4,128)S(1)} %get-tuple-element.28.order) | copy-start | bytes 18436
  7.6 8.4 %copy-start.6 = (s32[4,384]{1,0:T(4,128)}, s32[4,384]{1,0:T(4,128)S(1)}, u32[]{:S(2)}) copy-start(s32[4,384]{1,0:T(4,128)S(1)} %get-tuple-element.31.order) | copy-start | bytes 18436
  7.6 24.7 %copy-start.2 = (f32[16,128]{1,0:T(8,128)}, f32[16,128]{1,0:T(8,128)S(1)}, u32[]{:S(2)}) copy-start(f32[16,128]{1,0:T(8,128)S(1)} %get-tuple-element.29.scale.source_scale.target_scale) | copy-start | bytes 24580
  9.3 7.7 %collective-permute-start.2 = (f32[16,64,128]{2,1,0:T(8,128)S(1)}, f32[16,64,128]{2,1,0:T(8,128)S(1)}, u32[]{:S(2)}, u32[]{:S(2)}) collective-permute-start(f32[16,64,128]{2,1,0:T(8,128)S(1)} %shard_map.125.refs_0_.mine), channel_id=1, source_target_pairs={{0,1},{1,0},{2,3},{3,2},{4,5},{5,4},{6,7},{7,6},{8,9},{9,8},{10,11... | collective-permute-start | bytes 1572872 | tf_op jit(solution)/shard_map/ppermute | solution.py:351
  9.4 7.6 %collective-permute-start.4 = (s32[16,256]{1,0:T(8,128)S(1)}, s32[16,256]{1,0:T(8,128)S(1)}, u32[]{:S(2)}, u32[]{:S(2)}) collective-permute-start(s32[16,256]{1,0:T(8,128)S(1)} %shard_map.127), channel_id=1, source_target_pairs={{0,8},{4,12},{8,0},{12,4},{1,9},{5,13},{9,1},{13,5},{2,10},{6,14},... | collective-permute-start | bytes 49160 | tf_op jit(solution)/shard_map/ppermute | solution.py:351
  16.0 5.9 %collective-permute-start.1 = (f32[16,64,128]{2,1,0:T(8,128)S(1)}, f32[16,64,128]{2,1,0:T(8,128)S(1)}, u32[]{:S(2)}, u32[]{:S(2)}) collective-permute-start(f32[16,64,128]{2,1,0:T(8,128)S(1)} %shard_map.126.mine), channel_id=1, source_target_pairs={{0,1},{1,0},{2,3},{3,2},{4,5},{5,4},{6,7},{7,6},{8,9},{9,8},{10,11... | collective-permute-start | bytes 1572872 | tf_op jit(solution)/shard_map/ppermute | solution.py:351
  17.1 5.5 %copy-start.12 = (bf16[64,2048]{1,0:T(8,128)(2,1)S(1)}, bf16[64,2048]{1,0:T(8,128)(2,1)}, u32[]{:S(2)}) copy-start(bf16[64,2048]{1,0:T(8,128)(2,1)} %user_emb.3) | copy-start | bytes 786436
  17.1 15.2 %copy-start.5 = (s32[4,384]{1,0:T(4,128)S(1)}, s32[4,384]{1,0:T(4,128)}, u32[]{:S(2)}) copy-start(s32[4,384]{1,0:T(4,128)} %copy-done.4) | copy-start | bytes 18436
  18.3 5.7 %collective-permute-start.6 = (f32[64,256]{1,0:T(8,128)S(1)}, f32[64,256]{1,0:T(8,128)S(1)}, u32[]{:S(2)}, u32[]{:S(2)}) collective-permute-start(f32[64,256]{1,0:T(8,128)S(1)} %get-tuple-element.38), channel_id=1, source_target_pairs={{0,8},{4,12},{8,0},{12,4},{1,9},{5,13},{9,1},{13,5},{2,10},{6,14},... | collective-permute-start | bytes 196616 | tf_op jit(solution)/shard_map/ppermute | solution.py:351
  19.9 6.7 %collective-permute-start.7 = (f32[64,256]{1,0:T(8,128)S(1)}, f32[64,256]{1,0:T(8,128)S(1)}, u32[]{:S(2)}, u32[]{:S(2)}) collective-permute-start(f32[64,256]{1,0:T(8,128)S(1)} %get-tuple-element.39), channel_id=1, source_target_pairs={{0,12},{4,8},{8,4},{12,0},{1,13},{5,9},{9,5},{13,1},{2,14},{6,10},... | collective-permute-start | bytes 196616 | tf_op jit(solution)/shard_map/ppermute | solution.py:351
  19.9 6.7 %collective-permute-start.8 = (f32[64,256]{1,0:T(8,128)S(1)}, f32[64,256]{1,0:T(8,128)S(1)}, u32[]{:S(2)}, u32[]{:S(2)}) collective-permute-start(f32[64,256]{1,0:T(8,128)S(1)} %get-tuple-element.40), channel_id=1, source_target_pairs={{0,4},{4,0},{8,12},{12,8},{1,5},{5,1},{9,13},{13,9},{2,6},{6,2},{1... | collective-permute-start | bytes 196616 | tf_op jit(solution)/shard_map/ppermute | solution.py:351
  22.5 4.3 %collective-permute-start.5 = (f32[64,256]{1,0:T(8,128)S(1)}, f32[64,256]{1,0:T(8,128)S(1)}, u32[]{:S(2)}, u32[]{:S(2)}) collective-permute-start(f32[64,256]{1,0:T(8,128)S(1)} %get-tuple-element.36), channel_id=1, source_target_pairs={{0,2},{2,0},{1,3},{3,1},{4,6},{6,4},{5,7},{7,5},{8,10},{10,8},{9,1... | collective-permute-start | bytes 196616 | tf_op jit(solution)/shard_map/ppermute | solution.py:351
  26.9 4.8 %collective-permute-start.11 = (f32[72,256]{1,0:T(8,128)S(1)}, f32[72,256]{1,0:T(8,128)S(1)}, u32[]{:S(2)}, u32[]{:S(2)}) collective-permute-start(f32[72,256]{1,0:T(8,128)S(1)} %get-tuple-element.42.refs_0_), channel_id=1, source_target_pairs={{0,3},{1,2},{2,1},{3,0},{4,7},{5,6},{6,5},{7,4},{8,11},{9,10},{10,... | collective-permute-start | bytes 221192 | tf_op jit(solution)/shard_map/ppermute | solution.py:450
  26.9 5.3 %collective-permute-start.10 = (f32[72,256]{1,0:T(8,128)S(1)}, f32[72,256]{1,0:T(8,128)S(1)}, u32[]{:S(2)}, u32[]{:S(2)}) collective-permute-start(f32[72,256]{1,0:T(8,128)S(1)} %get-tuple-element.42.refs_0_), channel_id=1, source_target_pairs={{0,2},{2,0},{1,3},{3,1},{4,6},{6,4},{5,7},{7,5},{8,10},{10,8},{9,1... | collective-permute-start | bytes 221192 | tf_op jit(solution)/shard_map/ppermute | solution.py:351
  27.0 5.3 %collective-permute-start.9 = (f32[72,256]{1,0:T(8,128)S(1)}, f32[72,256]{1,0:T(8,128)S(1)}, u32[]{:S(2)}, u32[]{:S(2)}) collective-permute-start(f32[72,256]{1,0:T(8,128)S(1)} %get-tuple-element.42.refs_0_), channel_id=1, source_target_pairs={{0,1},{1,0},{2,3},{3,2},{4,5},{5,4},{6,7},{7,6},{8,9},{9,8},{10,11... | collective-permute-start | bytes 221192 | tf_op jit(solution)/shard_map/ppermute | solution.py:351
  28.8 6.9 %collective-permute-start.14 = (f32[64,256]{1,0:T(8,128)S(1)}, f32[64,256]{1,0:T(8,128)S(1)}, u32[]{:S(2)}, u32[]{:S(2)}) collective-permute-start(f32[64,256]{1,0:T(8,128)S(1)} %get-tuple-element.45.refs_0_), channel_id=1, source_target_pairs={{0,8},{4,12},{8,0},{12,4},{1,9},{5,13},{9,1},{13,5},{2,10},{6,14},... | collective-permute-start | bytes 196616 | tf_op jit(solution)/shard_map/ppermute | solution.py:351
  31.2 6.4 %collective-permute-start.13 = (f32[64,256]{1,0:T(8,128)S(1)}, f32[64,256]{1,0:T(8,128)S(1)}, u32[]{:S(2)}, u32[]{:S(2)}) collective-permute-start(f32[64,256]{1,0:T(8,128)S(1)} %get-tuple-element.45.refs_0_), channel_id=1, source_target_pairs={{0,12},{4,8},{8,4},{12,0},{1,13},{5,9},{9,5},{13,1},{2,14},{6,10},... | collective-permute-start | bytes 196616 | tf_op jit(solution)/shard_map/ppermute | solution.py:351
  31.6 6.0 %collective-permute-start.12 = (f32[64,256]{1,0:T(8,128)S(1)}, f32[64,256]{1,0:T(8,128)S(1)}, u32[]{:S(2)}, u32[]{:S(2)}) collective-permute-start(f32[64,256]{1,0:T(8,128)S(1)} %get-tuple-element.45.refs_0_), channel_id=1, source_target_pairs={{0,4},{4,0},{8,12},{12,8},{1,5},{5,1},{9,13},{13,9},{2,6},{6,2},{1... | collective-permute-start | bytes 196616 | tf_op jit(solution)/shard_map/ppermute | solution.py:351
  35.6 3.7 %collective-permute-start.16 = (f32[16,32,128]{2,1,0:T(8,128)S(1)}, f32[16,32,128]{2,1,0:T(8,128)S(1)}, u32[]{:S(2)}, u32[]{:S(2)}) collective-permute-start(f32[16,32,128]{2,1,0:T(8,128)S(1)} %get-tuple-element.44.after), channel_id=1, source_target_pairs={{0,1},{1,0},{2,3},{3,2},{4,5},{5,4},{6,7},{7,6},{8,9},{9,8},{10,11... | collective-permute-start | bytes 786440 | tf_op jit(solution)/shard_map/ppermute | solution.py:351
  39.1 4.3 %collective-permute-start.15 = (f32[16,64,128]{2,1,0:T(8,128)S(1)}, f32[16,64,128]{2,1,0:T(8,128)S(1)}, u32[]{:S(2)}, u32[]{:S(2)}) collective-permute-start(f32[16,64,128]{2,1,0:T(8,128)S(1)} %shard_map.133.after.mine), channel_id=1, source_target_pairs={{0,1},{1,0},{2,3},{3,2},{4,5},{5,4},{6,7},{7,6},{8,9},{9,8},{10,11... | collective-permute-start | bytes 1572872 | tf_op jit(solution)/shard_map/ppermute | solution.py:351
  39.2 4.2 %copy-start.1 = (bf16[288,128,128]{2,1,0:T(8,128)(2,1)S(1)}, bf16[288,128,128]{2,1,0:T(8,128)(2,1)}, u32[]{:S(2)}) copy-start(bf16[288,128,128]{2,1,0:T(8,128)(2,1)} %vals.7) | copy-start | bytes 28311556
  39.2 4.2 %copy-start.3 = (f32[16,128]{1,0:T(8,128)S(1)}, f32[16,128]{1,0:T(8,128)}, u32[]{:S(2)}) copy-start(f32[16,128]{1,0:T(8,128)} %copy-done.2) | copy-start | bytes 24580
  39.3 4.2 %copy-start.7 = (s32[4,384]{1,0:T(4,128)S(1)}, s32[4,384]{1,0:T(4,128)}, u32[]{:S(2)}) copy-start(s32[4,384]{1,0:T(4,128)} %copy-done.6) | copy-start | bytes 18436
  39.3 7.1 %collective-permute-start.17 = (f32[4,32,128]{2,1,0:T(8,128)S(1)}, f32[4,32,128]{2,1,0:T(8,128)S(1)}, u32[]{:S(2)}, u32[]{:S(2)}) collective-permute-start(f32[4,32,128]{2,1,0:T(8,128)S(1)} %get-tuple-element.49), channel_id=1, source_target_pairs={{0,8},{4,12},{8,0},{12,4},{1,9},{5,13},{9,1},{13,5},{2,10},{6,14},... | collective-permute-start | bytes 196616 | tf_op jit(solution)/shard_map/ppermute | solution.py:351
  42.8 6.3 %collective-permute-start.18 = (f32[4,32,128]{2,1,0:T(8,128)S(1)}, f32[4,32,128]{2,1,0:T(8,128)S(1)}, u32[]{:S(2)}, u32[]{:S(2)}) collective-permute-start(f32[4,32,128]{2,1,0:T(8,128)S(1)} %get-tuple-element.50), channel_id=1, source_target_pairs={{0,12},{4,8},{8,4},{12,0},{1,13},{5,9},{9,5},{13,1},{2,14},{6,10},... | collective-permute-start | bytes 196616 | tf_op jit(solution)/shard_map/ppermute | solution.py:351
  42.8 6.4 %collective-permute-start.19 = (f32[4,32,128]{2,1,0:T(8,128)S(1)}, f32[4,32,128]{2,1,0:T(8,128)S(1)}, u32[]{:S(2)}, u32[]{:S(2)}) collective-permute-start(f32[4,32,128]{2,1,0:T(8,128)S(1)} %get-tuple-element.51), channel_id=1, source_target_pairs={{0,4},{4,0},{8,12},{12,8},{1,5},{5,1},{9,13},{13,9},{2,6},{6,2},{1... | collective-permute-start | bytes 196616 | tf_op jit(solution)/shard_map/ppermute | solution.py:351
  49.2 2.3 %collective-permute-start.21 = (f32[16,32,128]{2,1,0:T(8,128)S(1)}, f32[16,32,128]{2,1,0:T(8,128)S(1)}, u32[]{:S(2)}, u32[]{:S(2)}) collective-permute-start(f32[16,32,128]{2,1,0:T(8,128)S(1)} %shard_map.138), channel_id=1, source_target_pairs={{0,1},{1,0},{2,3},{3,2},{4,5},{5,4},{6,7},{7,6},{8,9},{9,8},{10,11... | collective-permute-start | bytes 786440 | tf_op jit(solution)/shard_map/ppermute | solution.py:351
  49.3 6.4 %collective-permute-start.20 = (f32[4,32,128]{2,1,0:T(8,128)S(1)}, f32[4,32,128]{2,1,0:T(8,128)S(1)}, u32[]{:S(2)}, u32[]{:S(2)}) collective-permute-start(f32[4,32,128]{2,1,0:T(8,128)S(1)} %shard_map.136.refs_0_.values), channel_id=1, source_target_pairs={{0,12},{4,8},{8,4},{12,0},{1,13},{5,9},{9,5},{13,1},{2,14},{6,10},... | collective-permute-start | bytes 196616 | tf_op jit(solution)/shard_map/ppermute | solution.py:351
  51.5 8.4 %collective-permute-start.24 = (f32[16,32,128]{2,1,0:T(8,128)S(1)}, f32[16,32,128]{2,1,0:T(8,128)S(1)}, u32[]{:S(2)}, u32[]{:S(2)}) collective-permute-start(f32[16,32,128]{2,1,0:T(8,128)S(1)} %shard_map.139.refs_0_.refs_1_), channel_id=1, source_target_pairs={{0,2},{2,0},{1,3},{3,1},{4,6},{6,4},{5,7},{7,5},{8,10},{10,8},{9,1... | collective-permute-start | bytes 786440 | tf_op jit(solution)/shard_map/ppermute | solution.py:351
  52.3 7.0 %collective-permute-start.23 = (f32[4,32,128]{2,1,0:T(8,128)S(1)}, f32[4,32,128]{2,1,0:T(8,128)S(1)}, u32[]{:S(2)}, u32[]{:S(2)}) collective-permute-start(f32[4,32,128]{2,1,0:T(8,128)S(1)} %shard_map.140), channel_id=1, source_target_pairs={{0,8},{4,12},{8,0},{12,4},{1,9},{5,13},{9,1},{13,5},{2,10},{6,14},... | collective-permute-start | bytes 196616 | tf_op jit(solution)/shard_map/ppermute | solution.py:351
  54.0 5.5 %collective-permute-start.22 = (f32[4,32,128]{2,1,0:T(8,128)S(1)}, f32[4,32,128]{2,1,0:T(8,128)S(1)}, u32[]{:S(2)}, u32[]{:S(2)}) collective-permute-start(f32[4,32,128]{2,1,0:T(8,128)S(1)} %shard_map.140), channel_id=1, source_target_pairs={{0,4},{4,0},{8,12},{12,8},{1,5},{5,1},{9,13},{13,9},{2,6},{6,2},{1... | collective-permute-start | bytes 196616 | tf_op jit(solution)/shard_map/ppermute | solution.py:351
  59.5 1.6 %collective-permute-start.26 = (f32[4,4,32,128]{3,2,1,0:T(8,128)S(1)}, f32[4,4,32,128]{3,2,1,0:T(8,128)S(1)}, u32[]{:S(2)}, u32[]{:S(2)}) collective-permute-start(f32[4,4,32,128]{3,2,1,0:T(8,128)S(1)} %shard_map.141.refs_0_.after.mine), channel_id=1, source_target_pairs={{0,1},{1,0},{2,3},{3,2},{4,5},{5,4},{6,7},{7,6},{8,9},{9,8},{10,11... | collective-permute-start | bytes 786440 | tf_op jit(solution)/shard_map/ppermute | solution.py:351
  60.0 2.0 %collective-permute-start.25 = (f32[16,32,128]{2,1,0:T(8,128)S(1)}, f32[16,32,128]{2,1,0:T(8,128)S(1)}, u32[]{:S(2)}, u32[]{:S(2)}) collective-permute-start(f32[16,32,128]{2,1,0:T(8,128)S(1)} %shard_map.142.mine), channel_id=1, source_target_pairs={{0,1},{1,0},{2,3},{3,2},{4,5},{5,4},{6,7},{7,6},{8,9},{9,8},{10,11... | collective-permute-start | bytes 786440 | tf_op jit(solution)/shard_map/ppermute | solution.py:351
